TPU v7x, 32 devices: a whole 2x2x4 slice. The times are simulated.
32 devices in a mesh: row: 16 (over z, y, core), ch: 2 (over x).
Axes of the slice: x: 2, y: 2, z: 4, core: 2. Of those that a mesh axis runs over, the one named last changes fastest.
Arguments:
- pair_act: bfloat16 [256, 256, 128], P('row', 'ch'), may hold values from -6 to 6
- valid_count: int32 [1], replicated, may hold values from 129 to 256
- edge_proj: bfloat16 [128, 256], replicated, may hold values from -0.5 to 0.5
- edge_gate: bfloat16 [128, 256], replicated, may hold values from -0.5 to 0.5
- tri_gate: bfloat16 [128, 128], replicated, may hold values from -0.5 to 0.5
- tri_out: bfloat16 [128, 128], replicated, may hold values from -0.5 to 0.5
- attn_proj: bfloat16 [128, 512], replicated, may hold values from -0.5 to 0.5
- bias_proj: bfloat16 [128, 4], replicated, may hold values from -24 to 24, as said below
- attn_out: bfloat16 [128, 128], replicated, may hold values from -0.5 to 0.5
Outputs:
- pair_out: bfloat16 [256, 256, 128], P('row', 'ch')
Inputs may be any that keep to these rules, and one draw needn't show every extreme that they name: `bias_proj`: biases' projection; its columns differ in scale.
All inputs are finite; a program needn't handle non-finite values.
Results may differ from a plain program's by a relative error of at most 0.038.
Values may be sent and summed in bfloat16 or wider, within the bound.
No kernel may reach another device: no remote copies, remote signals or barrier semaphores. Data moves between devices by JAX's collectives and lax.ppermute only.
A program may use at most 128 MiB of HBM per device.

v0:
```python
import jax
import jax.numpy as jnp
from jax import lax
from jax.sharding import PartitionSpec as P

EPS = 1e-05


def layer_norm(values):
    centre = values - jnp.mean(values, axis=-1, keepdims=True)
    spread = jnp.mean(centre * centre, axis=-1, keepdims=True)
    return centre * lax.rsqrt(spread + EPS)


def local(
    pair_act, valid_count, edge_proj, edge_gate, tri_gate, tri_out, attn_proj, bias_proj, attn_out
):
    row_count = pair_act.shape[0]
    col_count = pair_act.shape[1]
    channels = pair_act.shape[2]
    head_count = bias_proj.shape[1]
    head_size = channels // head_count
    row_devices = lax.axis_size("row")
    col_devices = lax.axis_size("ch")
    tokens = row_count * row_devices
    row_offset = lax.axis_index("row") * row_count
    col_offset = lax.axis_index("ch") * col_count
    length = valid_count[0]
    row_valid = (row_offset + jnp.arange(row_count) < length).astype(jnp.float32)
    col_valid = (col_offset + jnp.arange(col_count) < length).astype(jnp.float32)
    key_valid = (jnp.arange(tokens) < length).astype(jnp.float32)
    pair_valid = row_valid[:, None] * col_valid[None, :]
    source = pair_act.astype(jnp.float32)
    normed = layer_norm(source).astype(jnp.bfloat16)
    projected = jnp.dot(normed, edge_proj, preferred_element_type=jnp.float32)
    gating = jnp.dot(normed, edge_gate, preferred_element_type=jnp.float32)
    edges = (jax.nn.sigmoid(gating) * projected * pair_valid[:, :, None]).astype(jnp.bfloat16)
    left_edges = edges[:, :, :channels]
    right_edges = edges[:, :, channels:]
    partial_sums = jnp.einsum(
        "ikc,jkc->ijc",
        left_edges,
        lax.all_gather(right_edges, "row", axis=0, tiled=True),
        preferred_element_type=jnp.float32,
    )
    triangle = lax.psum_scatter(partial_sums, "ch", scatter_dimension=1, tiled=True)
    tri_normed = layer_norm(triangle).astype(jnp.bfloat16)
    update = jax.nn.sigmoid(
        jnp.dot(normed, tri_gate, preferred_element_type=jnp.float32)
    ) * jnp.dot(tri_normed, tri_out, preferred_element_type=jnp.float32)
    updated = (source + update).astype(jnp.bfloat16)
    attn_normed = layer_norm(updated.astype(jnp.float32)).astype(jnp.bfloat16)
    mixed = jnp.dot(attn_normed, attn_proj, preferred_element_type=jnp.float32)
    query = mixed[..., :channels].astype(jnp.bfloat16)
    keys = mixed[..., channels : 2 * channels].astype(jnp.bfloat16)
    values = mixed[..., 2 * channels : 3 * channels].astype(jnp.bfloat16)
    attn_gate = jax.nn.sigmoid(mixed[..., 3 * channels :])
    local_bias = jnp.transpose(
        jnp.dot(attn_normed, bias_proj, preferred_element_type=jnp.float32), (2, 0, 1)
    ).astype(jnp.bfloat16)
    key_rows, value_rows = (
        lax.all_gather(keys, "ch", axis=1, tiled=True),
        lax.all_gather(values, "ch", axis=1, tiled=True),
    )
    gathered = lax.all_gather(local_bias, ("row", "ch"), axis=1, tiled=True)
    gathered = gathered.reshape(head_count, row_devices, col_devices, row_count, col_count)
    full_bias = jnp.transpose(gathered, (0, 1, 3, 2, 4)).reshape(head_count, tokens, tokens)
    own_bias = lax.dynamic_slice_in_dim(full_bias, col_offset, col_count, 1)
    my_bias = own_bias.astype(jnp.float32)
    key_term = (key_valid - 1.0) * 1000000000.0
    score_scale = head_size ** (-0.5)
    group = 4
    blocks = row_count // group

    def attend(block):
        query_part, key_part, value_part = block
        query_heads = query_part.reshape(group, col_count, head_count, head_size)
        key_heads = key_part.reshape(group, tokens, head_count, head_size)
        value_heads = value_part.reshape(group, tokens, head_count, head_size)
        logits = (
            jnp.einsum(
                "ijhd,ikhd->ihjk", query_heads, key_heads, preferred_element_type=jnp.float32
            )
            * score_scale
        )
        logits = logits + my_bias[None] + key_term[None, None, None, :]
        attn_weights = jax.nn.softmax(logits, axis=-1).astype(jnp.bfloat16)
        output = jnp.einsum(
            "ihjk,ikhd->ijhd", attn_weights, value_heads, preferred_element_type=jnp.float32
        )
        return output.reshape(group, col_count, channels)

    attended = lax.map(
        attend,
        (
            query.reshape(blocks, group, col_count, channels),
            key_rows.reshape(blocks, group, tokens, channels),
            value_rows.reshape(blocks, group, tokens, channels),
        ),
    )
    attended = attended.reshape(row_count, col_count, channels)
    gated = (attended * attn_gate).astype(jnp.bfloat16)
    return (
        updated.astype(jnp.float32) + jnp.dot(gated, attn_out, preferred_element_type=jnp.float32)
    ).astype(jnp.bfloat16)


def solution(mesh):
    placed = (P("row", "ch", None), P(), P(), P(), P(), P(), P(), P(), P())
    return jax.shard_map(
        local, mesh=mesh, in_specs=placed, out_specs=P("row", "ch", None), check_vma=False
    )
```

profile of v0, /device:TPU:0, one launch (start us, length us, event | category | flops | bytes accessed | tf_op | source)
XLA Modules:
  0.0 254.5 jit_solution(18356648243666427325)
XLA Ops:
  6.5 1.4 copy.29
  10.3 1.1 fusion.56
  11.8 77.3 %all-gather.4.cloned.1.call-done = bf16[256,128,128]{2,1,0:T(8,128)(2,1)} async-done(((bf16[16,128,128]{2,1,0:T(8,128)(2,1)}), bf16[256,128,128]{2,1,0:T(8,128)(2,1)}) %all-gather.4.cloned.1.call-update) | async-done | bytes 8388624 | tf_op jit(solution)/shard_map/all_gather | solution.py:43
  89.1 11.8 %copy.34 = bf16[256,128,128]{1,0,2:T(8,128)(2,1)} copy(bf16[256,128,128]{2,1,0:T(8,128)(2,1)} %all-gather.4.cloned.1.call-done) | data formatting | bytes 16777216 | tf_op jit(solution)/shard_map/all_gather | solution.py:43
  100.9 7.1 %convolution_bitcast_fusion = f32[16,256,128]{1,0,2:T(8,128)} fusion(bf16[256,128,128]{1,0,2:T(8,128)(2,1)} %copy.34, bf16[16,128,128]{1,0,2:T(8,128)(2,1)S(1)} %copy.35), kind=kOutput, calls=%fused_computation.22 | convolution fusion | flops 134217728 | bytes 11010048 | tf_op jit(solution)/shard_map/ikc,jkc->ijc/dot_general | solution.py:40
  108.0 30.1 %reduce-scatter.2.cloned.1.call-done = f32[16,128,128]{1,0,2:T(8,128)} async-done(((f32[16,256,128]{1,0,2:T(8,128)}), f32[16,128,128]{1,0,2:T(8,128)}) %reduce-scatter.2.cloned.1.call-update) | async-done | bytes 1048592 | tf_op jit(solution)/shard_map/reduce_scatter | solution.py:46
  138.2 1.5 reduce_sum.65
  139.7 1.4 multiply_reduce_fusion
  142.4 2.7 %fusion.57 = (bf16[16,128,512]{2,1,0:T(8,128)(2,1)S(1)}, f32[16,128,512]{2,1,0:T(8,128)}) fusion(bf16[128,512]{1,0:T(8,128)(2,1)S(1)} %copy-done, bf16[16,128,128]{1,2,0:T(8,128)(2,1)S(1)} %get-tuple-element.96, f32[16,128]{1,0:T(8,128)S(1)} %add_rsqrt_fusion, f32[16,128]{1,0:T(8,128)S(1)} %broadcast_multiply_fusion.1), kind=kOutput, calls=%fused_computation.80 | convolution fusion | flops 270532608 | bytes 6963200 | tf_op jit(solution)/shard_map/dot_general | solution.py:53
  145.0 1.4 fusion.55
  147.3 70.4 %all_gather.15 = bf16[4,512,128]{2,0,1:T(4,128)(2,1)S(1)} all-gather(bf16[4,16,128]{2,0,1:T(4,128)(2,1)S(1)} %fusion.26), channel_id=1, replica_groups=mesh['row'=16,'ch'=2] {'row','ch'}, dimensions={1}, use_global_device_ids=true | all-gather | bytes 540672 | tf_op jit(solution)/shard_map/all_gather | solution.py:65
  218.2 1.2 reshape.115
  219.4 1.4 slice.32
  221.2 23.8 %while.11 = (s32[]{:T(128)}, f32[4,4,128,128]{2,3,1,0:T(8,128)}, bf16[4,4,256,128]{3,2,1,0:T(8,128)(2,1)}, bf16[4,4,128,128]{3,2,1,0:T(8,128)(2,1)}, bf16[4,4,25...) while((s32[]{:T(128)}, f32[4,4,128,128]{2,3,1,0:T(8,128)}, ...), condition=%wide.region_10.11_spmd.clone, body=%wide.region_7.10_spmd.clone.sunk | while | flops 106434048 | bytes 5525089 | solution.py:93
  221.2 1.1 constant_dynamic-slice_fusion.5
  225.3 1.1 fusion.81
  227.2 1.1 constant_dynamic-slice_fusion.5
  231.3 1.1 fusion.81
  233.1 1.1 constant_dynamic-slice_fusion.5
  237.2 1.1 fusion.81
  239.1 1.1 constant_dynamic-slice_fusion.5
  243.2 1.1 fusion.81
  245.1 1.5 fusion.31
  246.9 1.0 copy.47
  (79 shorter events, 20.5 us)
Async XLA Ops:
  6.5 135.8 %copy-start = (bf16[128,512]{1,0:T(8,128)(2,1)S(1)}, bf16[128,512]{1,0:T(8,128)(2,1)}, u32[]{:S(2)}) copy-start(bf16[128,512]{1,0:T(8,128)(2,1)} %param.17) | copy-start | bytes 393220
  6.5 2.4 copy-start.3
  6.5 82.6 %all-gather.4.cloned.1.call-start = ((), (), s32[]{:S(2)}) async-start(), calls=%async_computation.1 | async-start | bytes 8912896 | tf_op jit(solution)/shard_map/all_gather | solution.py:43
  7.9 1.5 copy-start.6
  11.4 126.8 %reduce-scatter.2.cloned.1.call-start = ((), (), s32[]{:S(2)}) async-start(), calls=%async_computation.2 | async-start | bytes 3145728 | tf_op jit(solution)/shard_map/reduce_scatter | solution.py:46
  108.0 33.2 %copy-start.4 = (bf16[128,128]{1,0:T(8,128)(2,1)S(1)}, bf16[128,128]{1,0:T(8,128)(2,1)}, u32[]{:S(2)}) copy-start(bf16[128,128]{1,0:T(8,128)(2,1)} %param.16) | copy-start | bytes 98308
  108.0 113.2 %all-gather.6.cloned.1.call-start = ((), (), s32[]{:S(2)}) async-start(), calls=%async_computation.3 | async-start | bytes 1572864 | tf_op jit(solution)/shard_map/all_gather | solution.py:63
  138.2 2.9 %copy-start.1 = (f32[16,128,128]{1,0,2:T(8,128)S(1)}, f32[16,128,128]{1,0,2:T(8,128)}, u32[]{:S(2)}) copy-start(f32[16,128,128]{1,0,2:T(8,128)} %reduce-scatter.2.cloned.1.call-done) | copy-start | bytes 3145732
  139.6 1.9 copy-start.7
  145.0 2.0 copy-start.8
  146.4 74.8 %all-gather.8.cloned.1.call-start = ((), (), s32[]{:S(2)}) async-start(), calls=%async_computation.4 | async-start | bytes 1572864 | tf_op jit(solution)/shard_map/all_gather | solution.py:62
  219.4 1.7 copy-start.2
  245.1 1.5 copy-start.5
Sparse Core Ops, SparseCore 0:
  11.5 77.5 all-gather.3
  108.1 30.0 reduce-scatter.1
  146.5 23.7 all-gather.5
  171.8 23.3 all-gather.7
where the time goes:
time: 255 us; the launch traced here: 254 us
  waiting for transfers between devices  108 us (42%)
  blocking collectives  70.4 us (28%)
  local copies, waits for them, and re-layouts  33.1 us (13%)
  matrix products  21 us (8%)
  between operations  14 us (5%)
  other arithmetic  7.64 us (3%)
    all_gather x1, waiting for transfers between devices, local(): lax.all_gather(right_edges, 'row', axis=0, tiled=True)  77.3 us
    all_gather x1, blocking collectives, local(): gathered = lax.all_gather(local_bias, ('row', 'ch'), axis=1, tiled=True)  70.4 us
    reduce_scatter x1, waiting for transfers between devices, local(): lax.psum_scatter(partial_sums, 'ch', scatter_dimension=1, tiled=True)  30.1 us
    all_gather x1, local copies, waits for them, and re-layouts, local(): lax.all_gather(right_edges, 'row', axis=0, tiled=True)  11.8 us
    dynamic_slice x20, local copies, waits for them, and re-layouts, local(): lax.map(attend, (query.reshape(blocks, group, col_count, channels), key_r...  9.64 us
    dot_general x1, matrix products, local(): jnp.einsum('ikc,jkc->ijc', left_edges, lax.all_gather(right_edges, 'row',...  7.07 us
  transfers between devices with their start and end apart: 4, of which 2 were waited for; matrix products, arithmetic and copies ran while one was open for 2% of the time, Pallas kernels for 0%

commit v1 on v0

v1 whole, which is shorter than its diff:
```python
import functools
import math

import jax
import jax.numpy as jnp
from jax import lax
from jax.experimental import pallas as pl
from jax.experimental.pallas import tpu as pltpu
from jax.sharding import PartitionSpec as P

EPS = 1e-05
BOTH = ("row", "ch")
F32 = jnp.float32
BF16 = jnp.bfloat16
VMEM = pl.BlockSpec(memory_space=pltpu.VMEM)
SMEM = pl.BlockSpec(memory_space=pltpu.SMEM)
HBM = pl.BlockSpec(memory_space=pltpu.HBM)
ANY = pl.BlockSpec(memory_space=pl.ANY)


def layer_norm(values, axis):
    centre = values - jnp.mean(values, axis=axis, keepdims=True)
    spread = jnp.mean(centre * centre, axis=axis, keepdims=True)
    return centre * lax.rsqrt(spread + EPS)


def in_hbm(array):
    return pltpu.with_memory_space_constraint(array, pltpu.HBM)


def sigmoid(values):
    return 0.5 * jnp.tanh(0.5 * values) + 0.5


def dot(a, b, dims):
    return lax.dot_general(a, b, ((dims[:1], dims[1:]), ((), ())), preferred_element_type=F32)


def call(body, name, outs, ins, scratch=(), flops=1e8, smem=0, space=VMEM, out_space=VMEM, specs=None):
    sizes = [math.prod(a.shape) * a.dtype.itemsize for a in outs]
    if out_space is HBM:
        outs = [pltpu.HBM(a.shape, a.dtype) for a in outs]
    return pl.pallas_call(
        body,
        out_shape=outs,
        in_specs=specs or [SMEM] * smem + [space] * (ins - smem),
        out_specs=[out_space] * len(outs),
        scratch_shapes=list(scratch),
        compiler_params=pltpu.CompilerParams(vmem_limit_bytes=16 * 2**20),
        cost_estimate=pl.CostEstimate(
            flops=int(flops), bytes_accessed=2 * sum(sizes), transcendentals=0
        ),
        name=name,
    )


def turned(weights):
    return weights.astype(F32).T.astype(BF16)


def run(copies):
    for copy in copies:
        copy.start()
    for copy in copies:
        copy.wait()


def place():
    per_half = lax.axis_size("row") // 2
    columns = lax.axis_size("ch")
    row = lax.rem(lax.axis_index("row"), per_half)
    core = lax.rem(row, 2)
    return (row - core) * columns + lax.axis_index("ch"), core


def chip_offsets():
    columns = lax.axis_size("ch")
    share = lax.axis_size("row") // 2 * columns
    return [o for o in range(share) if o // columns % 2 == 0]


def chunked(pairs, sems, first, chunks):
    rows = pairs[0][0].shape[0]
    size = rows // chunks
    return [
        [
            pltpu.make_async_copy(
                source.at[pl.ds(chunk * size, size)],
                target.at[pl.ds(chunk * size, size)],
                sems.at[first + k, chunk],
            )
            for k, (source, target) in enumerate(pairs)
        ]
        for chunk in range(chunks)
    ]


def edges_body(length, source_hbm, proj_hbm, gate_hbm, *rest, side):
    outs = rest[:-6]
    source, proj, gate, held, out, sems = rest[-6:]
    rows, cols, channels = source.shape
    share, own = out.shape[:2]
    columns = lax.axis_size("ch")
    span = pl.ds(side * channels, channels)
    fetches = [
        pltpu.make_async_copy(proj_hbm.at[:, span], proj, sems.at[0, 2]),
        pltpu.make_async_copy(gate_hbm.at[:, span], gate, sems.at[0, 3]),
    ]
    chunks = chunked([(source_hbm, source)], sems, 0, 2)
    for copy in fetches + chunks[0] + chunks[1]:
        copy.start()
    row_offset = lax.axis_index("row") * rows
    col_offset = lax.axis_index("ch") * cols
    count = length[0]
    tokens = col_offset + lax.broadcasted_iota(jnp.int32, (1, cols), 1)
    col_valid = jnp.where(tokens < count, 0.5, 0.0)
    for copy in fetches:
        copy.wait()
    weights = jnp.concatenate([turned(proj[...]), turned(gate[...])], axis=0)

    def step(row, carry):
        values = source[row]
        if side:
            values = layer_norm(values.astype(F32), -1).astype(BF16)
            source[row] = values
        mixed = dot(weights, values, (1, 1))
        valid = col_valid * (row_offset + row < count).astype(F32)
        twice = jnp.tanh(0.5 * mixed[channels:]) + 1.0
        held[pl.ds(row, channels, stride=rows), :] = twice * (mixed[:channels] * valid)
        return carry

    for (copy,) in chunks:
        copy.wait()
    lax.fori_loop(0, rows, step, 0, unroll=rows)
    sends = []
    if side:
        sends.append(pltpu.make_async_copy(source, outs[1], sems.at[1, 0]))
        sends[0].start()
    group = share // 4
    for device in range(share):
        part = held[device * own * rows : (device + 1) * own * rows, :].astype(BF16)
        position = share - 1 - device
        out[position] = part.reshape(own, rows, cols)
        if side and device % group == group - 1:
            for k in range(2):
                source_part = out.at[pl.ds(position, group)]
                target = outs[0].at[pl.ds(k * share + position, group)]
                sends.append(
                    pltpu.make_async_copy(source_part, target, sems.at[1 + k, 1 + device // group])
                )
                sends[-1].start()
    if not side:
        chip, core = place()
        for k, offset in enumerate(chip_offsets()):
            for other in range(2):
                index = jnp.bitwise_xor(chip, offset) + lax.rem(core + other, 2) * columns
                outs[other][k] = out[index]
    for copy in sends:
        copy.wait()


def pack_body(mine, sibling, *outs):
    _, core = place()
    for k, out in enumerate(outs):
        out[core] = mine[k]
        out[1 - core] = sibling[k]


def gate_body(pair, normed, weights, out, source):
    turned_weights = turned(weights[...])

    def step(row, carry):
        out[row] = sigmoid(dot(turned_weights, normed[row], (1, 1))).astype(BF16)
        source[row] = pair[row].astype(F32).T.astype(BF16)
        return carry

    lax.fori_loop(0, pair.shape[0], step, 0, unroll=2)


def triangle_body(right, *rest):
    parts, out, held, sent = rest[:-3], rest[-3], rest[-2], rest[-1]
    row_devices, col_devices, own, rows, cols = right.shape
    chip, _ = place()
    chip_row = lax.div(chip, col_devices)
    me = lax.axis_index("ch")
    groups = [(first, core) for first in range(0, row_devices // 2, 2) for core in range(2)]
    offsets = chip_offsets()
    for channel in range(own):
        left, whole = [], []
        for flip in range(col_devices):
            left.append(
                jnp.concatenate(
                    [
                        parts[offsets.index(first * col_devices + flip)][core, channel]
                        for first, core in groups
                    ],
                    axis=0,
                )
            )
            whole.append(right[:, jnp.bitwise_xor(me, flip), channel].reshape(-1, cols))
        triangle = dot(
            jnp.concatenate(left, axis=1), jnp.concatenate(whole, axis=1), (1, 1)
        ).astype(BF16)
        for k, (first, core) in enumerate(groups):
            for part in range(col_devices):
                row = row_devices // 2 - 1 - core - jnp.bitwise_xor(chip_row, first)
                held[row, col_devices - 1 - part, channel] = triangle[
                    k * rows : (k + 1) * rows, part * cols : (part + 1) * cols
                ]
    run([pltpu.make_async_copy(held, out, sent)])


def copies_body(bias, out):
    for k in range(out.shape[0]):
        out[k] = bias[...]


def spread_sum(values):
    lead = 8
    split = values.reshape((values.shape[0] // lead, lead) + values.shape[1:])
    return jnp.sum(jnp.sum(split, axis=0), axis=0, keepdims=True)


def update_body(triangle, source, gate, tri_out, bias_proj, updated, bias, held, bias_held):
    channels, rows, cols = triangle.shape
    heads = bias_proj.shape[1]
    values = triangle[...].astype(F32)
    centre = values - spread_sum(values) * (1.0 / channels)
    spread = spread_sum(centre * centre) * (1.0 / channels)
    held[...] = (centre * lax.rsqrt(spread + EPS)).reshape(channels * rows, cols)
    out_weights = turned(tri_out[...])
    bias_weights = turned(bias_proj[...])

    def step(row, carry):
        tri_normed = held[pl.ds(row, channels, stride=rows), :].astype(BF16)
        update = gate[row].astype(F32) * dot(out_weights, tri_normed, (1, 0))
        mine = (source[row].astype(F32) + update).astype(BF16)
        updated[row] = mine
        normed = layer_norm(mine.astype(F32), 0).astype(BF16)
        bias_held[pl.ds(row, heads, stride=rows), :] = dot(bias_weights, normed, (1, 0))
        return carry

    lax.fori_loop(0, rows, step, 0, unroll=8)
    bias[...] = bias_held[...].astype(BF16).reshape(heads, rows, cols)


def project(updated, attn_proj, mixed, row, score_scale):
    channels = updated.shape[1]
    values = updated[row].astype(F32)
    normed = layer_norm(values, 0)
    natural = normed.T.astype(BF16)

    def put(block, array):
        mixed[row, :, block * channels : (block + 1) * channels] = array.astype(BF16)

    put(0, dot(turned(attn_proj[:, channels : 2 * channels]), normed.astype(BF16), (1, 0)))
    put(1, dot(natural, attn_proj[:, 2 * channels : 3 * channels], (1, 0)))
    if score_scale is not None:
        put(2, dot(natural, attn_proj[:, :channels], (1, 0)) * score_scale)
        put(3, sigmoid(dot(natural, attn_proj[:, 3 * channels :], (1, 0))))
        put(4, values.T)


def own_body(updated, attn_proj, mixed_hbm, mixed, sems, *, score_scale):
    rows = updated.shape[0]

    def step(row, carry):
        project(updated, attn_proj, mixed, row, score_scale)
        return carry

    sends = chunked([(mixed, mixed_hbm)], sems, 0, 2)
    for chunk in range(2):
        lax.fori_loop(chunk * rows // 2, (chunk + 1) * rows // 2, step, 0, unroll=rows // 2)
        sends[chunk][0].start()
    for (copy,) in sends:
        copy.wait()


def other_body(mixed_hbm, attn_proj, *rest):
    pieces = (len(rest) - 2) // 2
    others, mixed, keys, sem = rest[:pieces], rest[pieces], rest[pieces + 1 : -1], rest[-1]
    fetch = pltpu.make_async_copy(mixed_hbm, mixed, sem)
    fetch.start()
    rows = mixed.shape[0]
    for updated, target in zip(others, keys):

        def step(row, carry):
            project(updated, attn_proj, target, row, None)
            return carry

        lax.fori_loop(0, rows, step, 0, unroll=rows // 2)
    fetch.wait()


def attend_body(length, mine, sibling, attn_out, *rest):
    mixed, (out_hbm, out, bias_held, sems) = rest[:-4], rest[-4:]
    pieces = len(mixed)
    rows, cols, channels = out.shape
    heads = mine.shape[1]
    me = lax.axis_index("ch")
    its_core = lax.rem(lax.axis_index("row"), 2)
    head_of = lax.broadcasted_iota(jnp.int32, (1, channels), 1) // (channels // heads)
    count = sems.shape[1]
    sends = chunked([(out, out_hbm)], sems, 0, count)
    chips = cols // rows // 2
    for piece in range(pieces):
        block = lax.rem(me + piece, pieces)
        token = block * cols + lax.broadcasted_iota(jnp.int32, (1, cols), 1)
        key_term = jnp.where(token < length[0], 0.0, -1e9)
        for part, core in ((mine, its_core), (sibling, 1 - its_core)):
            for chip in range(chips):
                tiles = part[(me * chips + chip) * pieces + block]
                for head in range(heads):
                    first = pl.multiple_of(head * cols + (chip * 2 + core) * rows, rows)
                    bias_held[pl.ds(first, rows), piece * cols : (piece + 1) * cols] = (
                        tiles[head].astype(F32) + key_term
                    )
    both_of = jnp.concatenate([head_of, head_of], axis=1)
    masks = [(head_of == head).astype(BF16) for head in range(heads)]
    ones = jnp.ones((pieces * cols, channels), BF16)

    def load(row):
        keys = jnp.concatenate([part[row, :, :channels] for part in mixed], axis=1)
        values = jnp.concatenate([part[row, :, channels : 2 * channels] for part in mixed], axis=0)
        values = jnp.concatenate([values, ones], axis=1)
        return keys, values, mixed[0][row, :, 2 * channels : 3 * channels]

    def finish(row, total):
        attended = total[:, :channels] / total[:, channels:]
        gate = mixed[0][row, :, 3 * channels : 4 * channels].astype(F32)
        gated = (attended * gate).astype(BF16)
        residual = mixed[0][row, :, 4 * channels :].astype(F32)
        out[row] = (residual + dot(gated, attn_out[...], (1, 0))).astype(BF16)

    per_chunk = rows // count
    loaded, logits, weights = {}, {}, {}
    for time in range(rows + 2):
        row = time
        if row < rows:
            loaded[row] = load(row)
            keys, _, query = loaded[row]
            queries = jnp.concatenate([query * mask for mask in masks], axis=0)
            logits[row] = dot(queries, keys, (1, 0)) + bias_held[...]
        row = time - 1
        if 0 <= row < rows:
            scores = logits.pop(row)
            top = jnp.max(scores, axis=-1, keepdims=True)
            weights[row] = jnp.exp((scores - top).astype(BF16))
        row = time - 2
        if row >= 0:
            sums = dot(weights.pop(row), loaded.pop(row)[1], (1, 0))
            total = sums[:cols]
            for head in range(1, heads):
                total = jnp.where(both_of == head, sums[head * cols : (head + 1) * cols], total)
            finish(row, total)
            chunk, place_in = divmod(row, per_chunk)
            if place_in == per_chunk - 1:
                for copy in sends[chunk]:
                    copy.start()
    for send in sends:
        for copy in send:
            copy.wait()


def local(
    pair_act, valid_count, edge_proj, edge_gate, tri_gate, tri_out, attn_proj, bias_proj, attn_out
):
    rows, cols, channels = pair_act.shape
    heads = bias_proj.shape[1]
    row_devices = lax.axis_size("row")
    col_devices = lax.axis_size("ch")
    devices = row_devices * col_devices
    share = devices // 2
    own = channels // share
    everyone = list(reversed(range(devices)))
    halves = [everyone[share:], everyone[:share]]
    shape = jax.ShapeDtypeStruct
    block = (rows, cols, channels)
    turned_block = (rows, channels, cols)

    def in_half(array):
        return lax.all_to_all(
            array, BOTH, split_axis=0, concat_axis=0, axis_index_groups=halves, tiled=True
        )


    weight = pltpu.VMEM((channels, channels), BF16)
    offsets = chip_offsets()
    tile = (own, rows, cols)

    def edges(side, source):
        outs = [shape((devices,) + tile, BF16), shape(block, BF16)]
        return call(
            functools.partial(edges_body, side=side),
            "right_edges" if side else "left_edges",
            outs if side else [shape((len(offsets),) + tile, BF16)] * 2,
            4,
            [
                pltpu.VMEM(block, BF16),
                weight,
                weight,
                pltpu.VMEM((channels * rows, cols), F32),
                pltpu.VMEM((share,) + tile, BF16),
                pltpu.SemaphoreType.DMA((3, 5)),
            ],
            smem=1,
            space=HBM,
            out_space=HBM if side else VMEM,
            flops=3e9,
        )(valid_count, *[in_hbm(a) for a in (source, edge_proj, edge_gate)])

    def flipped(array, bits):
        return lax.ppermute(array, BOTH, [(d, d ^ bits) for d in range(devices)])

    right, normed = edges(1, pair_act)
    right = lax.all_to_all(right, BOTH, split_axis=0, concat_axis=0, tiled=True)
    mine, theirs = edges(0, normed)
    left = call(pack_body, "pack", [shape((2,) + tile, BF16)] * len(offsets), 2)(
        mine, flipped(theirs, col_devices)
    )
    left = [flipped(part, offset) if offset else part for part, offset in zip(left, offsets)]
    tri_gating, source = call(
        gate_body, "tri_gate", [shape(turned_block, BF16)] * 2, 3, flops=2e9
    )(pair_act, normed, tri_gate)
    triangle_shape = (row_devices // 2, col_devices, own, rows, cols)
    (triangle,) = call(
        triangle_body,
        "triangle",
        [shape(triangle_shape, BF16)],
        1 + len(left),
        [pltpu.VMEM(triangle_shape, BF16), pltpu.SemaphoreType.DMA(())],
        out_space=HBM,
        flops=2e9,
    )(right.reshape((row_devices,) + triangle_shape[1:]), *left)
    triangle = in_half(triangle.reshape(share, own, rows, cols))
    bias_shape = (heads, rows, cols)
    updated, bias = call(
        update_body,
        "update",
        [shape(turned_block, BF16), shape(bias_shape, BF16)],
        5,
        [pltpu.VMEM((channels * rows, cols), F32), pltpu.VMEM((heads * rows, cols), F32)],
        flops=2e9,
    )(triangle.reshape(channels, rows, cols), source, tri_gating, tri_out, bias_proj)
    one_core = [
        [d for d in range(devices) if d // col_devices % 2 == core] for core in range(2)
    ]
    (copies,) = call(
        copies_body,
        "bias_copies",
        [shape((share,) + bias_shape, BF16)],
        1,
        flops=1e9,
    )(bias)

    others = [
        lax.ppermute(updated, "ch", [((c + s) % col_devices, c) for c in range(col_devices)])
        for s in range(1, col_devices)
    ]
    bias = lax.all_to_all(
        copies, BOTH, split_axis=0, concat_axis=0, axis_index_groups=one_core, tiled=True
    )

    mixed_shape = (rows, cols, 5 * channels)
    key_shape = (rows, cols, 2 * channels)
    (mixed,) = call(
        functools.partial(own_body, score_scale=(channels // heads) ** (-0.5)),
        "own_projections",
        [shape(mixed_shape, BF16)],
        2,
        [pltpu.VMEM(mixed_shape, BF16), pltpu.SemaphoreType.DMA((1, 2))],
        out_space=HBM,
        flops=3e9,
    )(updated, attn_proj)
    bias, *others = lax.optimization_barrier((bias, *others))
    mixed = call(
        other_body,
        "other_keys",
        [shape(mixed_shape, BF16)] + [shape(key_shape, BF16)] * len(others),
        2 + len(others),
        [pltpu.SemaphoreType.DMA(())],
        specs=[HBM] + [VMEM] * (1 + len(others)),
        flops=3e9,
    )(in_hbm(mixed), attn_proj, *others)
    (result,) = call(
        attend_body,
        "attend",
        [shape(block, BF16)],
        4 + col_devices,
        [
            pltpu.VMEM(block, BF16),
            pltpu.VMEM((heads * cols, col_devices * cols), F32),
            pltpu.SemaphoreType.DMA((1, rows // 2)),
        ],
        smem=1,
        out_space=HBM,
    )(valid_count, bias, flipped(bias, col_devices), attn_out, *mixed)
    return result


def solution(mesh):
    placed = (P("row", "ch", None), P(), P(), P(), P(), P(), P(), P(), P())
    return jax.shard_map(
        local, mesh=mesh, in_specs=placed, out_specs=P("row", "ch", None), check_vma=False
    )
```

time: 255 us -> 78 us (0.31)
  waiting for transfers between devices: 108 us -> 29.5 us
  blocking collectives: 70.4 us -> 0 us
  local copies, waits for them, and re-layouts: 33.1 us -> 0.17 us
  starting transfers between devices: 0.13 us -> 27.7 us
  matrix products: 21 us -> 0 us
  Pallas kernels: 0 us -> 19.2 us
  between operations: 14 us -> 0.81 us
  other arithmetic: 7.64 us -> 0 us
    all_gather x3 -> x0, waiting for transfers between devices: 77.3 us -> none  [the longest x1 77.3 us: local(): lax.all_gather(right_edges, 'row', axis=0, tiled=True)]
    all_gather x1 -> x0, blocking collectives: 70.4 us -> none  [local(): gathered = lax.all_gather(local_bias, ('row', 'ch'), axis=1, tiled=True)]
    reduce_scatter x1 -> x0, waiting for transfers between devices: 30.1 us -> none  [local(): lax.psum_scatter(partial_sums, 'ch', scatter_dimension=1, tiled=True)]
    pallas_call x0 -> x10, Pallas kernels: none -> 19.2 us  [the longest x2 5.34 us: edges(): call(functools.partial(edges_body, side=side), 'right_edges' if side else...]
    all_to_all x0 -> x3, starting transfers between devices: none -> 17.6 us  [the longest x1 7.3 us: local(): right = lax.all_to_all(right, BOTH, split_axis=0, concat_axis=0, tiled=True)]
    dot_general x12 -> x0, matrix products: 17 us -> none  [the longest x1 7.07 us: local(): jnp.einsum('ikc,jkc->ijc', left_edges, lax.all_gather(right_edges, 'row',...]
    ppermute x0 -> x10, waiting for transfers between devices: none -> 15.9 us  [the longest x9 15.9 us: flipped(): return lax.ppermute(array, BOTH, [(d, d ^ bits) for d in range(devices)])]
    all_to_all x0 -> x3, waiting for transfers between devices: none -> 13.6 us  [the longest x1 8.18 us: local(): lax.all_to_all(copies, BOTH, split_axis=0, concat_axis=0, axis_index_grou...]
  transfers between devices with their start and end apart: 4 -> 13, of which waited for: 2 -> 9; matrix products, arithmetic and copies ran while one was open for 2% -> 0% of each run, Pallas kernels for 0% -> 11%
where the time goes in v1:
time: 78 us; the launch traced here: 77.5 us
  waiting for transfers between devices  29.5 us (38%)
  starting transfers between devices  27.7 us (36%)
  Pallas kernels  19.2 us (25%)
  between operations  0.81 us (1%)
    ppermute x9, waiting for transfers between devices, flipped(): return lax.ppermute(array, BOTH, [(d, d ^ bits) for d in range(devices)])  15.9 us
    ppermute x9, starting transfers between devices, flipped(): return lax.ppermute(array, BOTH, [(d, d ^ bits) for d in range(devices)])  8.45 us
    all_to_all x1, waiting for transfers between devices, local(): lax.all_to_all(copies, BOTH, split_axis=0, concat_axis=0, axis_index_grou...  8.18 us
    all_to_all x1, starting transfers between devices, local(): right = lax.all_to_all(right, BOTH, split_axis=0, concat_axis=0, tiled=True)  7.3 us
    all_to_all x1, waiting for transfers between devices, in_half(): lax.all_to_all(array, BOTH, split_axis=0, concat_axis=0, axis_index_group...  5.42 us
    pallas_call x2, Pallas kernels, edges(): call(functools.partial(edges_body, side=side), 'right_edges' if side else...  5.34 us
    all_to_all x1, starting transfers between devices, local(): lax.all_to_all(copies, BOTH, split_axis=0, concat_axis=0, axis_index_grou...  5.14 us
    all_to_all x1, starting transfers between devices, in_half(): lax.all_to_all(array, BOTH, split_axis=0, concat_axis=0, axis_index_group...  5.11 us
  transfers between devices with their start and end apart: 13, of which 9 were waited for; matrix products, arithmetic and copies ran while one was open for 0% of the time, Pallas kernels for 11%

profile of v1, /device:TPU:0, one launch (start us, length us, event | category | flops | bytes accessed | tf_op | source)
XLA Modules:
  0.0 77.5 jit_solution(27912560547877675)
XLA Ops:
  0.7 3.4 %right_edges.1 = (bf16[32,8,16,128]{3,2,1,0:T(8,128)(2,1)}, bf16[16,128,128]{2,1,0:T(8,128)(2,1)}) custom-call(s32[1]{0:T(128)S(6)} %copy.11.length, bf16[16,128,128]{2,1,0:T(8,128)(2,1)} %pair.1, bf16[128,256]{1,0:T(8,128)(2,1)} %proj_hbm.3, bf16[128,256]{1,0:T(8,128)(2,1)} %gate_hbm.3), custom_call_target="tpu_custom_call" | custom-call | flops 3000000000 | bytes 3145728 | tf_op jit(solution)/shard_map/right_edges/pallas_call | solution.py:393
  4.0 7.3 %all-to-all-start = ((bf16[32,8,16,128]{3,2,1,0:T(8,128)(2,1)}), bf16[32,8,16,128]{3,2,1,0:T(8,128)(2,1)S(1)}, u32[]{:S(2)}, u32[]{:S(2)}) async-start(bf16[32,8,16,128]{3,2,1,0:T(8,128)(2,1)} %get-tuple-element.25), calls=%async_computation | async-start | bytes 2097152 | tf_op jit(solution)/shard_map/all_to_all | solution.py:416
  11.3 2.0 %left_edges.1 = (bf16[8,8,16,128]{3,2,1,0:T(8,128)(2,1)S(1)}, bf16[8,8,16,128]{3,2,1,0:T(8,128)(2,1)S(1)}) custom-call(s32[1]{0:T(128)S(6)} %copy.11.length, bf16[16,128,128]{2,1,0:T(8,128)(2,1)} %get-tuple-element.26.source_hbm.normed, bf16[128,256]{1,0:T(8,128)(2,1)} %proj_hbm.3, bf16[128,256]{1,0:T(8,128)(2,1)} %gate_hbm.3), custom_call_target="tpu_custom_call" | custom-call | flops 3000000000 | bytes 1048576 | tf_op jit(solution)/shard_map/left_edges/pallas_call | solution.py:393
  13.6 1.3 %collective-permute-done.sibling = bf16[8,8,16,128]{3,2,1,0:T(8,128)(2,1)S(1)} collective-permute-done((bf16[8,8,16,128]{3,2,1,0:T(8,128)(2,1)S(1)}, bf16[8,8,16,128]{3,2,1,0:T(8,128)(2,1)S(1)}, u32[]{:S(2)}, u32[]{:S(2)}) %collective-permute-start) | collective-permute-done | bytes 262176 | tf_op jit(solution)/shard_map/ppermute | solution.py:413
  15.0 1.8 %collective-permute-start.1 = (bf16[2,8,16,128]{3,2,1,0:T(8,128)(2,1)S(1)}, bf16[2,8,16,128]{3,2,1,0:T(8,128)(2,1)S(1)}, u32[]{:S(2)}, u32[]{:S(2)}) collective-permute-start(bf16[2,8,16,128]{3,2,1,0:T(8,128)(2,1)S(1)} %get-tuple-element.30), channel_id=1, source_target_pairs={{0,1},{1,0},{2,3},{3,2},{4,5},{5,4},{6,7},{7,6},{8,9},{9,8},{10,11... | collective-permute-start | bytes 196616 | tf_op jit(solution)/shard_map/ppermute | solution.py:413
  16.8 1.5 %collective-permute-start.2 = (bf16[2,8,16,128]{3,2,1,0:T(8,128)(2,1)S(1)}, bf16[2,8,16,128]{3,2,1,0:T(8,128)(2,1)S(1)}, u32[]{:S(2)}, u32[]{:S(2)}) collective-permute-start(bf16[2,8,16,128]{3,2,1,0:T(8,128)(2,1)S(1)} %get-tuple-element.31), channel_id=1, source_target_pairs={{0,4},{1,5},{2,6},{3,7},{4,0},{5,1},{6,2},{7,3},{8,12},{9,13},{10,... | collective-permute-start | bytes 196616 | tf_op jit(solution)/shard_map/ppermute | solution.py:413
  18.5 1.8 %collective-permute-start.4 = (bf16[2,8,16,128]{3,2,1,0:T(8,128)(2,1)S(1)}, bf16[2,8,16,128]{3,2,1,0:T(8,128)(2,1)S(1)}, u32[]{:S(2)}, u32[]{:S(2)}) collective-permute-start(bf16[2,8,16,128]{3,2,1,0:T(8,128)(2,1)S(1)} %get-tuple-element.33), channel_id=1, source_target_pairs={{0,8},{1,9},{2,10},{3,11},{4,12},{5,13},{6,14},{7,15},{8,0},{9,1},... | collective-permute-start | bytes 196616 | tf_op jit(solution)/shard_map/ppermute | solution.py:413
  20.3 1.5 %collective-permute-start.5 = (bf16[2,8,16,128]{3,2,1,0:T(8,128)(2,1)S(1)}, bf16[2,8,16,128]{3,2,1,0:T(8,128)(2,1)S(1)}, u32[]{:S(2)}, u32[]{:S(2)}) collective-permute-start(bf16[2,8,16,128]{3,2,1,0:T(8,128)(2,1)S(1)} %get-tuple-element.34), channel_id=1, source_target_pairs={{0,9},{1,8},{2,11},{3,10},{4,13},{5,12},{6,15},{7,14},{8,1},{9,0},... | collective-permute-start | bytes 196616 | tf_op jit(solution)/shard_map/ppermute | solution.py:413
  21.8 1.6 %collective-permute-done.1.rest_1_ = bf16[2,8,16,128]{3,2,1,0:T(8,128)(2,1)S(1)} collective-permute-done((bf16[2,8,16,128]{3,2,1,0:T(8,128)(2,1)S(1)}, bf16[2,8,16,128]{3,2,1,0:T(8,128)(2,1)S(1)}, u32[]{:S(2)}, u32[]{:S(2)}) %collective-permute-start.1) | collective-permute-done | bytes 65568 | tf_op jit(solution)/shard_map/ppermute | solution.py:413
  25.9 4.8 %collective-permute-done.4.rest_4_ = bf16[2,8,16,128]{3,2,1,0:T(8,128)(2,1)S(1)} collective-permute-done((bf16[2,8,16,128]{3,2,1,0:T(8,128)(2,1)S(1)}, bf16[2,8,16,128]{3,2,1,0:T(8,128)(2,1)S(1)}, u32[]{:S(2)}, u32[]{:S(2)}) %collective-permute-start.4) | collective-permute-done | bytes 65568 | tf_op jit(solution)/shard_map/ppermute | solution.py:413
  30.7 1.5 %collective-permute-done.5.rest_5_ = bf16[2,8,16,128]{3,2,1,0:T(8,128)(2,1)S(1)} collective-permute-done((bf16[2,8,16,128]{3,2,1,0:T(8,128)(2,1)S(1)}, bf16[2,8,16,128]{3,2,1,0:T(8,128)(2,1)S(1)}, u32[]{:S(2)}, u32[]{:S(2)}) %collective-permute-start.5) | collective-permute-done | bytes 65568 | tf_op jit(solution)/shard_map/ppermute | solution.py:413
  32.2 2.7 %collective-permute-done.6.rest_6_ = bf16[2,8,16,128]{3,2,1,0:T(8,128)(2,1)S(1)} collective-permute-done((bf16[2,8,16,128]{3,2,1,0:T(8,128)(2,1)S(1)}, bf16[2,8,16,128]{3,2,1,0:T(8,128)(2,1)S(1)}, u32[]{:S(2)}, u32[]{:S(2)}) %collective-permute-start.6) | collective-permute-done | bytes 65568 | tf_op jit(solution)/shard_map/ppermute | solution.py:413
  34.9 2.9 %collective-permute-done.7.rest_7_ = bf16[2,8,16,128]{3,2,1,0:T(8,128)(2,1)S(1)} collective-permute-done((bf16[2,8,16,128]{3,2,1,0:T(8,128)(2,1)S(1)}, bf16[2,8,16,128]{3,2,1,0:T(8,128)(2,1)S(1)}, u32[]{:S(2)}, u32[]{:S(2)}) %collective-permute-start.7) | collective-permute-done | bytes 65568 | tf_op jit(solution)/shard_map/ppermute | solution.py:413
  37.8 1.3 %triangle.1 = bf16[8,2,8,16,128]{4,3,2,1,0:T(8,128)(2,1)} custom-call(bf16[16,2,8,16,128]{4,3,2,1,0:T(8,128)(2,1)S(1)} %bitcast.3, bf16[2,8,16,128]{3,2,1,0:T(8,128)(2,1)S(1)} %get-tuple-element.29.rest_0_, bf16[2,8,16,128]{3,2,1,0:T(8,128)(2,1)S(1)} %collective-permute-done.1.rest_1_, bf16[2,8,16,128]{3,2,1,0:T(8,128)(2,1)S(1)} %collective-permute-done.2.rest_2_, ...), custom_call_target="tpu_custom_call" | custom-call | flops 2000000000 | bytes 1048576 | tf_op jit(solution)/shard_map/triangle/pallas_call | solution.py:426
  39.1 5.1 %all-to-all-start.1 = ((bf16[16,8,16,128]{3,2,1,0:T(8,128)(2,1)}), bf16[16,8,16,128]{3,2,1,0:T(8,128)(2,1)S(1)}, u32[]{:S(2)}, u32[]{:S(2)}) async-start(bf16[16,8,16,128]{3,2,1,0:T(8,128)(2,1)} %bitcast.5), calls=%async_computation.1 | async-start | bytes 1048576 | tf_op jit(solution)/shard_map/all_to_all | solution.py:382
  44.4 1.6 %tri_gate.1 = (bf16[16,128,128]{2,1,0:T(8,128)(2,1)S(1)}, bf16[16,128,128]{2,1,0:T(8,128)(2,1)S(1)}) custom-call(bf16[16,128,128]{2,1,0:T(8,128)(2,1)S(1)} %copy-done.1, bf16[16,128,128]{2,1,0:T(8,128)(2,1)S(1)} %copy-done.5, bf16[128,128]{1,0:T(8,128)(2,1)S(1)} %copy-done.3), custom_call_target="tpu_custom_call" | custom-call | flops 2000000000 | bytes 2097152 | tf_op jit(solution)/shard_map/tri_gate/pallas_call | solution.py:422
  46.0 5.4 %all-to-all-done.1 = bf16[16,8,16,128]{3,2,1,0:T(8,128)(2,1)S(1)} async-done(((bf16[16,8,16,128]{3,2,1,0:T(8,128)(2,1)}), bf16[16,8,16,128]{3,2,1,0:T(8,128)(2,1)S(1)}, u32[]{:S(2)}, u32[]{:S(2)}) %all-to-all-start.1) | async-done | bytes 524320 | tf_op jit(solution)/shard_map/all_to_all | solution.py:382
  51.4 1.5 %update.1 = (bf16[16,128,128]{2,1,0:T(8,128)(2,1)S(1)}, bf16[4,16,128]{2,1,0:T(8,128)(2,1)S(1)}) custom-call(bf16[128,16,128]{2,1,0:T(8,128)(2,1)S(1)} %bitcast.4, bf16[16,128,128]{2,1,0:T(8,128)(2,1)S(1)} %get-tuple-element.37.source, bf16[16,128,128]{2,1,0:T(8,128)(2,1)S(1)} %get-tuple-element.38.gate, bf16[128,128]{1,0:T(8,128)(2,1)S(1)} %copy-done.4, ...), custom_call_target="tpu_custom_call" | custom-call | flops 2000000000 | bytes 1081344 | tf_op jit(solution)/shard_map/update/pallas_call | solution.py:437
  52.9 1.7 %collective-permute-start.8 = (bf16[16,128,128]{2,1,0:T(8,128)(2,1)S(1)}, bf16[16,128,128]{2,1,0:T(8,128)(2,1)S(1)}, u32[]{:S(2)}, u32[]{:S(2)}) collective-permute-start(bf16[16,128,128]{2,1,0:T(8,128)(2,1)S(1)} %get-tuple-element.40.updated), channel_id=1, source_target_pairs={{1,0},{0,1},{3,2},{2,3},{5,4},{4,5},{7,6},{6,7},{9,8},{8,9},{11,10... | collective-permute-start | bytes 1572872 | tf_op jit(solution)/shard_map/ppermute | solution.py:457
  55.4 5.1 %all-to-all-start.2 = ((bf16[16,4,16,128]{3,2,1,0:T(8,128)(2,1)}), bf16[16,4,16,128]{3,2,1,0:T(8,128)(2,1)S(1)}, u32[]{:S(2)}, u32[]{:S(2)}) async-start(bf16[16,4,16,128]{3,2,1,0:T(8,128)(2,1)} %bias_copies.1), calls=%async_computation.2 | async-start | bytes 524288 | tf_op jit(solution)/shard_map/all_to_all | solution.py:460
  60.6 2.3 %own_projections.1.mixed_hbm = bf16[16,128,640]{2,1,0:T(8,128)(2,1)} custom-call(bf16[16,128,128]{2,1,0:T(8,128)(2,1)S(1)} %get-tuple-element.40.updated, bf16[128,512]{1,0:T(8,128)(2,1)S(1)} %copy-done.2), custom_call_target="tpu_custom_call" | custom-call | flops 3000000000 | bytes 5242880 | tf_op jit(solution)/shard_map/own_projections/pallas_call | solution.py:466
  62.9 8.2 %all-to-all-done.2.mine = bf16[16,4,16,128]{3,2,1,0:T(8,128)(2,1)S(1)} async-done(((bf16[16,4,16,128]{3,2,1,0:T(8,128)(2,1)}), bf16[16,4,16,128]{3,2,1,0:T(8,128)(2,1)S(1)}, u32[]{:S(2)}, u32[]{:S(2)}) %all-to-all-start.2) | async-done | bytes 262176 | tf_op jit(solution)/shard_map/all_to_all | solution.py:460
  71.0 1.7 %other_keys.1 = (bf16[16,128,640]{2,1,0:T(8,128)(2,1)S(1)}, bf16[16,128,256]{2,1,0:T(8,128)(2,1)S(1)}) custom-call(bf16[16,128,640]{2,1,0:T(8,128)(2,1)} %own_projections.1.mixed_hbm, bf16[128,512]{1,0:T(8,128)(2,1)S(1)} %copy-done.2, bf16[16,128,128]{2,1,0:T(8,128)(2,1)S(1)} %collective-permute-done.8.rest_0_), custom_call_target="tpu_custom_call" | custom-call | flops 3000000000 | bytes 7340032 | tf_op jit(solution)/shard_map/other_keys/pallas_call | solution.py:476
  72.8 4.7 %attend.1 = bf16[16,128,128]{2,1,0:T(8,128)(2,1)} custom-call(s32[1]{0:T(128)S(6)} %copy.11.length, bf16[16,4,16,128]{3,2,1,0:T(8,128)(2,1)S(1)} %all-to-all-done.2.mine, bf16[16,4,16,128]{3,2,1,0:T(8,128)(2,1)S(1)} %collective-permute-done.9.sibling, bf16[128,128]{1,0:T(8,128)(2,1)S(1)} %copy-done, bf16[16,128,640]{2,1,0:T(8,128)(2,1)S(1)} %get-tuple-element.43.rest_0_, ...), custom_call_target="tpu_custom_call" | custom-call | flops 100000000 | bytes 1048576 | tf_op jit(solution)/shard_map/attend/pallas_call | solution.py:485
  (27 shorter events, 4.0 us)
Async XLA Ops:
  4.0 33.7 %all-to-all-start = ((bf16[32,8,16,128]{3,2,1,0:T(8,128)(2,1)}), bf16[32,8,16,128]{3,2,1,0:T(8,128)(2,1)S(1)}, u32[]{:S(2)}, u32[]{:S(2)}) async-start(bf16[32,8,16,128]{3,2,1,0:T(8,128)(2,1)} %get-tuple-element.25), calls=%async_computation | async-start | bytes 2097152 | tf_op jit(solution)/shard_map/all_to_all | solution.py:416
  13.3 1.6 %collective-permute-start = (bf16[8,8,16,128]{3,2,1,0:T(8,128)(2,1)S(1)}, bf16[8,8,16,128]{3,2,1,0:T(8,128)(2,1)S(1)}, u32[]{:S(2)}, u32[]{:S(2)}) collective-permute-start(bf16[8,8,16,128]{3,2,1,0:T(8,128)(2,1)S(1)} %get-tuple-element.28), channel_id=1, source_target_pairs={{0,2},{1,3},{2,0},{3,1},{4,6},{5,7},{6,4},{7,5},{8,10},{9,11},{10,... | collective-permute-start | bytes 786440 | tf_op jit(solution)/shard_map/ppermute | solution.py:413
  15.0 8.4 %collective-permute-start.1 = (bf16[2,8,16,128]{3,2,1,0:T(8,128)(2,1)S(1)}, bf16[2,8,16,128]{3,2,1,0:T(8,128)(2,1)S(1)}, u32[]{:S(2)}, u32[]{:S(2)}) collective-permute-start(bf16[2,8,16,128]{3,2,1,0:T(8,128)(2,1)S(1)} %get-tuple-element.30), channel_id=1, source_target_pairs={{0,1},{1,0},{2,3},{3,2},{4,5},{5,4},{6,7},{7,6},{8,9},{9,8},{10,11... | collective-permute-start | bytes 196616 | tf_op jit(solution)/shard_map/ppermute | solution.py:413
  16.8 8.5 %collective-permute-start.2 = (bf16[2,8,16,128]{3,2,1,0:T(8,128)(2,1)S(1)}, bf16[2,8,16,128]{3,2,1,0:T(8,128)(2,1)S(1)}, u32[]{:S(2)}, u32[]{:S(2)}) collective-permute-start(bf16[2,8,16,128]{3,2,1,0:T(8,128)(2,1)S(1)} %get-tuple-element.31), channel_id=1, source_target_pairs={{0,4},{1,5},{2,6},{3,7},{4,0},{5,1},{6,2},{7,3},{8,12},{9,13},{10,... | collective-permute-start | bytes 196616 | tf_op jit(solution)/shard_map/ppermute | solution.py:413
  18.3 7.6 %collective-permute-start.3 = (bf16[2,8,16,128]{3,2,1,0:T(8,128)(2,1)S(1)}, bf16[2,8,16,128]{3,2,1,0:T(8,128)(2,1)S(1)}, u32[]{:S(2)}, u32[]{:S(2)}) collective-permute-start(bf16[2,8,16,128]{3,2,1,0:T(8,128)(2,1)S(1)} %get-tuple-element.32), channel_id=1, source_target_pairs={{0,5},{1,4},{2,7},{3,6},{4,1},{5,0},{6,3},{7,2},{8,13},{9,12},{10,... | collective-permute-start | bytes 196616 | tf_op jit(solution)/shard_map/ppermute | solution.py:413
  18.5 12.2 %collective-permute-start.4 = (bf16[2,8,16,128]{3,2,1,0:T(8,128)(2,1)S(1)}, bf16[2,8,16,128]{3,2,1,0:T(8,128)(2,1)S(1)}, u32[]{:S(2)}, u32[]{:S(2)}) collective-permute-start(bf16[2,8,16,128]{3,2,1,0:T(8,128)(2,1)S(1)} %get-tuple-element.33), channel_id=1, source_target_pairs={{0,8},{1,9},{2,10},{3,11},{4,12},{5,13},{6,14},{7,15},{8,0},{9,1},... | collective-permute-start | bytes 196616 | tf_op jit(solution)/shard_map/ppermute | solution.py:413
  20.3 11.9 %collective-permute-start.5 = (bf16[2,8,16,128]{3,2,1,0:T(8,128)(2,1)S(1)}, bf16[2,8,16,128]{3,2,1,0:T(8,128)(2,1)S(1)}, u32[]{:S(2)}, u32[]{:S(2)}) collective-permute-start(bf16[2,8,16,128]{3,2,1,0:T(8,128)(2,1)S(1)} %get-tuple-element.34), channel_id=1, source_target_pairs={{0,9},{1,8},{2,11},{3,10},{4,13},{5,12},{6,15},{7,14},{8,1},{9,0},... | collective-permute-start | bytes 196616 | tf_op jit(solution)/shard_map/ppermute | solution.py:413
  23.3 11.5 %collective-permute-start.6 = (bf16[2,8,16,128]{3,2,1,0:T(8,128)(2,1)S(1)}, bf16[2,8,16,128]{3,2,1,0:T(8,128)(2,1)S(1)}, u32[]{:S(2)}, u32[]{:S(2)}) collective-permute-start(bf16[2,8,16,128]{3,2,1,0:T(8,128)(2,1)S(1)} %get-tuple-element.35), channel_id=1, source_target_pairs={{0,12},{1,13},{2,14},{3,15},{4,8},{5,9},{6,10},{7,11},{8,4},{9,5},... | collective-permute-start | bytes 196616 | tf_op jit(solution)/shard_map/ppermute | solution.py:413
  25.3 12.5 %collective-permute-start.7 = (bf16[2,8,16,128]{3,2,1,0:T(8,128)(2,1)S(1)}, bf16[2,8,16,128]{3,2,1,0:T(8,128)(2,1)S(1)}, u32[]{:S(2)}, u32[]{:S(2)}) collective-permute-start(bf16[2,8,16,128]{3,2,1,0:T(8,128)(2,1)S(1)} %get-tuple-element.36), channel_id=1, source_target_pairs={{0,13},{1,12},{2,15},{3,14},{4,9},{5,8},{6,11},{7,10},{8,5},{9,4},... | collective-permute-start | bytes 196616 | tf_op jit(solution)/shard_map/ppermute | solution.py:413
  37.8 6.5 %copy-start.6 = (bf16[128,4]{0,1:T(4,128)(2,1)S(1)}, bf16[128,4]{0,1:T(4,128)(2,1)}, u32[]{:S(2)}) copy-start(bf16[128,4]{0,1:T(4,128)(2,1)} %param.16) | copy-start | bytes 3076
  37.8 6.6 %copy-start.1 = (bf16[16,128,128]{2,1,0:T(8,128)(2,1)S(1)}, bf16[16,128,128]{2,1,0:T(8,128)(2,1)}, u32[]{:S(2)}) copy-start(bf16[16,128,128]{2,1,0:T(8,128)(2,1)} %pair.1) | copy-start | bytes 1572868
  37.8 6.6 %copy-start.3 = (bf16[128,128]{1,0:T(8,128)(2,1)S(1)}, bf16[128,128]{1,0:T(8,128)(2,1)}, u32[]{:S(2)}) copy-start(bf16[128,128]{1,0:T(8,128)(2,1)} %weights.1) | copy-start | bytes 98308
  37.8 6.6 %copy-start.5 = (bf16[16,128,128]{2,1,0:T(8,128)(2,1)S(1)}, bf16[16,128,128]{2,1,0:T(8,128)(2,1)}, u32[]{:S(2)}) copy-start(bf16[16,128,128]{2,1,0:T(8,128)(2,1)} %get-tuple-element.26.source_hbm.normed) | copy-start | bytes 1572868
  39.1 12.3 %all-to-all-start.1 = ((bf16[16,8,16,128]{3,2,1,0:T(8,128)(2,1)}), bf16[16,8,16,128]{3,2,1,0:T(8,128)(2,1)S(1)}, u32[]{:S(2)}, u32[]{:S(2)}) async-start(bf16[16,8,16,128]{3,2,1,0:T(8,128)(2,1)} %bitcast.5), calls=%async_computation.1 | async-start | bytes 1048576 | tf_op jit(solution)/shard_map/all_to_all | solution.py:382
  44.4 7.0 %copy-start.4 = (bf16[128,128]{1,0:T(8,128)(2,1)S(1)}, bf16[128,128]{1,0:T(8,128)(2,1)}, u32[]{:S(2)}) copy-start(bf16[128,128]{1,0:T(8,128)(2,1)} %tri_out.1) | copy-start | bytes 98308
  52.9 7.6 %copy-start.2 = (bf16[128,512]{1,0:T(8,128)(2,1)S(1)}, bf16[128,512]{1,0:T(8,128)(2,1)}, u32[]{:S(2)}) copy-start(bf16[128,512]{1,0:T(8,128)(2,1)} %attn_proj.3) | copy-start | bytes 393220
  52.9 18.1 %collective-permute-start.8 = (bf16[16,128,128]{2,1,0:T(8,128)(2,1)S(1)}, bf16[16,128,128]{2,1,0:T(8,128)(2,1)S(1)}, u32[]{:S(2)}, u32[]{:S(2)}) collective-permute-start(bf16[16,128,128]{2,1,0:T(8,128)(2,1)S(1)} %get-tuple-element.40.updated), channel_id=1, source_target_pairs={{1,0},{0,1},{3,2},{2,3},{5,4},{4,5},{7,6},{6,7},{9,8},{8,9},{11,10... | collective-permute-start | bytes 1572872 | tf_op jit(solution)/shard_map/ppermute | solution.py:457
  55.4 15.6 %all-to-all-start.2 = ((bf16[16,4,16,128]{3,2,1,0:T(8,128)(2,1)}), bf16[16,4,16,128]{3,2,1,0:T(8,128)(2,1)S(1)}, u32[]{:S(2)}, u32[]{:S(2)}) async-start(bf16[16,4,16,128]{3,2,1,0:T(8,128)(2,1)} %bias_copies.1), calls=%async_computation.2 | async-start | bytes 524288 | tf_op jit(solution)/shard_map/all_to_all | solution.py:460
  62.8 10.0 %copy-start = (bf16[128,128]{1,0:T(8,128)(2,1)S(1)}, bf16[128,128]{1,0:T(8,128)(2,1)}, u32[]{:S(2)}) copy-start(bf16[128,128]{1,0:T(8,128)(2,1)} %attn_out.1) | copy-start | bytes 98308
  71.0 1.8 %collective-permute-start.9 = (bf16[16,4,16,128]{3,2,1,0:T(8,128)(2,1)S(1)}, bf16[16,4,16,128]{3,2,1,0:T(8,128)(2,1)S(1)}, u32[]{:S(2)}, u32[]{:S(2)}) collective-permute-start(bf16[16,4,16,128]{3,2,1,0:T(8,128)(2,1)S(1)} %all-to-all-done.2.mine), channel_id=1, source_target_pairs={{0,2},{1,3},{2,0},{3,1},{4,6},{5,7},{6,4},{7,5},{8,10},{9,11},{10,... | collective-permute-start | bytes 786440 | tf_op jit(solution)/shard_map/ppermute | solution.py:413

commit v2 on v1

--- a/solution.py
+++ b/solution.py
@@ -210,9 +210,17 @@
     run([pltpu.make_async_copy(held, out, sent)])
 
 
-def copies_body(bias, out):
-    for k in range(out.shape[0]):
-        out[k] = bias[...]
+def deal_body(*refs):
+    parts, out = refs[:-1], refs[-1]
+    columns = len(parts)
+    per_part = lax.axis_size("row") // columns
+    part = lax.div(lax.axis_index("row"), per_part)
+    for col in range(columns):
+        value = parts[0][...]
+        for flip in range(1, columns):
+            value = jnp.where(jnp.bitwise_xor(part, col) == flip, parts[flip][...], value)
+        for chip in range(out.shape[0] // columns):
+            out[chip * columns + col] = value
 
 
 def spread_sum(values):
@@ -309,7 +317,7 @@
         key_term = jnp.where(token < length[0], 0.0, -1e9)
         for part, core in ((mine, its_core), (sibling, 1 - its_core)):
             for chip in range(chips):
-                tiles = part[(me * chips + chip) * pieces + block]
+                tiles = part[chip * pieces + block]
                 for head in range(heads):
                     first = pl.multiple_of(head * cols + (chip * 2 + core) * rows, rows)
                     bias_held[pl.ds(first, rows), piece * cols : (piece + 1) * cols] = (
@@ -442,23 +450,25 @@
         [pltpu.VMEM((channels * rows, cols), F32), pltpu.VMEM((heads * rows, cols), F32)],
         flops=2e9,
     )(triangle.reshape(channels, rows, cols), source, tri_gating, tri_out, bias_proj)
-    one_core = [
-        [d for d in range(devices) if d // col_devices % 2 == core] for core in range(2)
+    per_part = row_devices // col_devices
+    parts = [bias] + [
+        flipped(bias, flip * per_part * col_devices) for flip in range(1, col_devices)
     ]
-    (copies,) = call(
-        copies_body,
-        "bias_copies",
-        [shape((share,) + bias_shape, BF16)],
-        1,
-        flops=1e9,
-    )(bias)
+    (dealt,) = call(
+        deal_body, "deal_bias", [shape((per_part // 2 * col_devices,) + bias_shape, BF16)], col_devices
+    )(*parts)
+    one_core = []
+    for part in range(col_devices):
+        for core in range(2):
+            members = range(part * per_part + core, (part + 1) * per_part, 2)
+            one_core.append([r * col_devices + c for r in members for c in range(col_devices)])
 
     others = [
         lax.ppermute(updated, "ch", [((c + s) % col_devices, c) for c in range(col_devices)])
         for s in range(1, col_devices)
     ]
     bias = lax.all_to_all(
-        copies, BOTH, split_axis=0, concat_axis=0, axis_index_groups=one_core, tiled=True
+        dealt, BOTH, split_axis=0, concat_axis=0, axis_index_groups=one_core, tiled=True
     )
 
     mixed_shape = (rows, cols, 5 * channels)

time: 78 us -> 76.4 us (0.979)
  waiting for transfers between devices: 29.5 us -> 26.8 us
  starting transfers between devices: 27.7 us -> 28.9 us
    all_to_all x1, waiting for transfers between devices: 8.18 us -> 3.73 us  [local(): lax.all_to_all(dealt, BOTH, split_axis=0, concat_axis=0, axis_index_group...]
    ppermute x9 -> x10, starting transfers between devices: 8.45 us -> 11.4 us  [flipped(): return lax.ppermute(array, BOTH, [(d, d ^ bits) for d in range(devices)])]
    all_to_all x1, starting transfers between devices: 5.14 us -> 3.37 us  [local(): lax.all_to_all(dealt, BOTH, split_axis=0, concat_axis=0, axis_index_group...]
    ppermute x9 -> x10, waiting for transfers between devices: 15.9 us -> 17.6 us  [flipped(): return lax.ppermute(array, BOTH, [(d, d ^ bits) for d in range(devices)])]
  transfers between devices with their start and end apart: 13 -> 14, of which waited for: 9 -> 10; matrix products, arithmetic and copies ran while one was open for 0% -> 0% of each run, Pallas kernels for 11% -> 11%
where the time goes in v2:
time: 76.4 us; the launch traced here: 75.9 us
  starting transfers between devices  28.9 us (38%)
  waiting for transfers between devices  26.8 us (35%)
  Pallas kernels  19.2 us (25%)
  between operations  0.81 us (1%)
    ppermute x10, waiting for transfers between devices, flipped(): return lax.ppermute(array, BOTH, [(d, d ^ bits) for d in range(devices)])  17.6 us
    ppermute x10, starting transfers between devices, flipped(): return lax.ppermute(array, BOTH, [(d, d ^ bits) for d in range(devices)])  11.4 us
    all_to_all x1, starting transfers between devices, local(): right = lax.all_to_all(right, BOTH, split_axis=0, concat_axis=0, tiled=True)  7.3 us
    all_to_all x1, waiting for transfers between devices, in_half(): lax.all_to_all(array, BOTH, split_axis=0, concat_axis=0, axis_index_group...  5.43 us
    pallas_call x2, Pallas kernels, edges(): call(functools.partial(edges_body, side=side), 'right_edges' if side else...  5.34 us
    all_to_all x1, starting transfers between devices, in_half(): lax.all_to_all(array, BOTH, split_axis=0, concat_axis=0, axis_index_group...  5.12 us
    pallas_call x1, Pallas kernels, local(): call(attend_body, 'attend', [shape(block, BF16)], 4 + col_devices, [pltpu...  4.67 us
    all_to_all x1, waiting for transfers between devices, local(): lax.all_to_all(dealt, BOTH, split_axis=0, concat_axis=0, axis_index_group...  3.73 us
  transfers between devices with their start and end apart: 14, of which 10 were waited for; matrix products, arithmetic and copies ran while one was open for 0% of the time, Pallas kernels for 11%

profile of v2, /device:TPU:0, one launch (start us, length us, event | category | flops | bytes accessed | tf_op | source)
XLA Modules:
  0.0 75.9 jit_solution(10944422602499353464)
XLA Ops:
  0.7 3.3 %right_edges.1 = (bf16[32,8,16,128]{3,2,1,0:T(8,128)(2,1)}, bf16[16,128,128]{2,1,0:T(8,128)(2,1)}) custom-call(s32[1]{0:T(128)S(6)} %copy.11.length, bf16[16,128,128]{2,1,0:T(8,128)(2,1)} %pair.1, bf16[128,256]{1,0:T(8,128)(2,1)} %proj_hbm.3, bf16[128,256]{1,0:T(8,128)(2,1)} %gate_hbm.3), custom_call_target="tpu_custom_call" | custom-call | flops 3000000000 | bytes 3145728 | tf_op jit(solution)/shard_map/right_edges/pallas_call | solution.py:401
  4.0 7.3 %all-to-all-start = ((bf16[32,8,16,128]{3,2,1,0:T(8,128)(2,1)}), bf16[32,8,16,128]{3,2,1,0:T(8,128)(2,1)S(1)}, u32[]{:S(2)}, u32[]{:S(2)}) async-start(bf16[32,8,16,128]{3,2,1,0:T(8,128)(2,1)} %get-tuple-element.25), calls=%async_computation | async-start | bytes 2097152 | tf_op jit(solution)/shard_map/all_to_all | solution.py:424
  11.3 2.0 %left_edges.1 = (bf16[8,8,16,128]{3,2,1,0:T(8,128)(2,1)S(1)}, bf16[8,8,16,128]{3,2,1,0:T(8,128)(2,1)S(1)}) custom-call(s32[1]{0:T(128)S(6)} %copy.11.length, bf16[16,128,128]{2,1,0:T(8,128)(2,1)} %get-tuple-element.26.source_hbm.normed, bf16[128,256]{1,0:T(8,128)(2,1)} %proj_hbm.3, bf16[128,256]{1,0:T(8,128)(2,1)} %gate_hbm.3), custom_call_target="tpu_custom_call" | custom-call | flops 3000000000 | bytes 1048576 | tf_op jit(solution)/shard_map/left_edges/pallas_call | solution.py:401
  15.0 1.8 %collective-permute-start.1 = (bf16[2,8,16,128]{3,2,1,0:T(8,128)(2,1)S(1)}, bf16[2,8,16,128]{3,2,1,0:T(8,128)(2,1)S(1)}, u32[]{:S(2)}, u32[]{:S(2)}) collective-permute-start(bf16[2,8,16,128]{3,2,1,0:T(8,128)(2,1)S(1)} %get-tuple-element.30), channel_id=1, source_target_pairs={{0,1},{1,0},{2,3},{3,2},{4,5},{5,4},{6,7},{7,6},{8,9},{9,8},{10,11... | collective-permute-start | bytes 196616 | tf_op jit(solution)/shard_map/ppermute | solution.py:421
  16.8 1.5 %collective-permute-start.2 = (bf16[2,8,16,128]{3,2,1,0:T(8,128)(2,1)S(1)}, bf16[2,8,16,128]{3,2,1,0:T(8,128)(2,1)S(1)}, u32[]{:S(2)}, u32[]{:S(2)}) collective-permute-start(bf16[2,8,16,128]{3,2,1,0:T(8,128)(2,1)S(1)} %get-tuple-element.31), channel_id=1, source_target_pairs={{0,4},{1,5},{2,6},{3,7},{4,0},{5,1},{6,2},{7,3},{8,12},{9,13},{10,... | collective-permute-start | bytes 196616 | tf_op jit(solution)/shard_map/ppermute | solution.py:421
  18.5 1.8 %collective-permute-start.4 = (bf16[2,8,16,128]{3,2,1,0:T(8,128)(2,1)S(1)}, bf16[2,8,16,128]{3,2,1,0:T(8,128)(2,1)S(1)}, u32[]{:S(2)}, u32[]{:S(2)}) collective-permute-start(bf16[2,8,16,128]{3,2,1,0:T(8,128)(2,1)S(1)} %get-tuple-element.33), channel_id=1, source_target_pairs={{0,8},{1,9},{2,10},{3,11},{4,12},{5,13},{6,14},{7,15},{8,0},{9,1},... | collective-permute-start | bytes 196616 | tf_op jit(solution)/shard_map/ppermute | solution.py:421
  20.3 1.5 %collective-permute-start.5 = (bf16[2,8,16,128]{3,2,1,0:T(8,128)(2,1)S(1)}, bf16[2,8,16,128]{3,2,1,0:T(8,128)(2,1)S(1)}, u32[]{:S(2)}, u32[]{:S(2)}) collective-permute-start(bf16[2,8,16,128]{3,2,1,0:T(8,128)(2,1)S(1)} %get-tuple-element.34), channel_id=1, source_target_pairs={{0,9},{1,8},{2,11},{3,10},{4,13},{5,12},{6,15},{7,14},{8,1},{9,0},... | collective-permute-start | bytes 196616 | tf_op jit(solution)/shard_map/ppermute | solution.py:421
  21.8 1.6 %collective-permute-done.1.rest_1_ = bf16[2,8,16,128]{3,2,1,0:T(8,128)(2,1)S(1)} collective-permute-done((bf16[2,8,16,128]{3,2,1,0:T(8,128)(2,1)S(1)}, bf16[2,8,16,128]{3,2,1,0:T(8,128)(2,1)S(1)}, u32[]{:S(2)}, u32[]{:S(2)}) %collective-permute-start.1) | collective-permute-done | bytes 65568 | tf_op jit(solution)/shard_map/ppermute | solution.py:421
  25.9 4.9 %collective-permute-done.4.rest_4_ = bf16[2,8,16,128]{3,2,1,0:T(8,128)(2,1)S(1)} collective-permute-done((bf16[2,8,16,128]{3,2,1,0:T(8,128)(2,1)S(1)}, bf16[2,8,16,128]{3,2,1,0:T(8,128)(2,1)S(1)}, u32[]{:S(2)}, u32[]{:S(2)}) %collective-permute-start.4) | collective-permute-done | bytes 65568 | tf_op jit(solution)/shard_map/ppermute | solution.py:421
  30.7 1.5 %collective-permute-done.5.rest_5_ = bf16[2,8,16,128]{3,2,1,0:T(8,128)(2,1)S(1)} collective-permute-done((bf16[2,8,16,128]{3,2,1,0:T(8,128)(2,1)S(1)}, bf16[2,8,16,128]{3,2,1,0:T(8,128)(2,1)S(1)}, u32[]{:S(2)}, u32[]{:S(2)}) %collective-permute-start.5) | collective-permute-done | bytes 65568 | tf_op jit(solution)/shard_map/ppermute | solution.py:421
  32.2 2.7 %collective-permute-done.6.rest_6_ = bf16[2,8,16,128]{3,2,1,0:T(8,128)(2,1)S(1)} collective-permute-done((bf16[2,8,16,128]{3,2,1,0:T(8,128)(2,1)S(1)}, bf16[2,8,16,128]{3,2,1,0:T(8,128)(2,1)S(1)}, u32[]{:S(2)}, u32[]{:S(2)}) %collective-permute-start.6) | collective-permute-done | bytes 65568 | tf_op jit(solution)/shard_map/ppermute | solution.py:421
  34.9 2.9 %collective-permute-done.7.rest_7_ = bf16[2,8,16,128]{3,2,1,0:T(8,128)(2,1)S(1)} collective-permute-done((bf16[2,8,16,128]{3,2,1,0:T(8,128)(2,1)S(1)}, bf16[2,8,16,128]{3,2,1,0:T(8,128)(2,1)S(1)}, u32[]{:S(2)}, u32[]{:S(2)}) %collective-permute-start.7) | collective-permute-done | bytes 65568 | tf_op jit(solution)/shard_map/ppermute | solution.py:421
  39.1 5.1 %all-to-all-start.1 = ((bf16[16,8,16,128]{3,2,1,0:T(8,128)(2,1)}), bf16[16,8,16,128]{3,2,1,0:T(8,128)(2,1)S(1)}, u32[]{:S(2)}, u32[]{:S(2)}) async-start(bf16[16,8,16,128]{3,2,1,0:T(8,128)(2,1)} %bitcast.5), calls=%async_computation.1 | async-start | bytes 1048576 | tf_op jit(solution)/shard_map/all_to_all | solution.py:390
  44.4 1.6 %tri_gate.1 = (bf16[16,128,128]{2,1,0:T(8,128)(2,1)S(1)}, bf16[16,128,128]{2,1,0:T(8,128)(2,1)S(1)}) custom-call(bf16[16,128,128]{2,1,0:T(8,128)(2,1)S(1)} %copy-done.1, bf16[16,128,128]{2,1,0:T(8,128)(2,1)S(1)} %copy-done.5, bf16[128,128]{1,0:T(8,128)(2,1)S(1)} %copy-done.3), custom_call_target="tpu_custom_call" | custom-call | flops 2000000000 | bytes 2097152 | tf_op jit(solution)/shard_map/tri_gate/pallas_call | solution.py:430
  46.0 5.4 %all-to-all-done.1 = bf16[16,8,16,128]{3,2,1,0:T(8,128)(2,1)S(1)} async-done(((bf16[16,8,16,128]{3,2,1,0:T(8,128)(2,1)}), bf16[16,8,16,128]{3,2,1,0:T(8,128)(2,1)S(1)}, u32[]{:S(2)}, u32[]{:S(2)}) %all-to-all-start.1) | async-done | bytes 524320 | tf_op jit(solution)/shard_map/all_to_all | solution.py:390
  51.4 1.5 %update.1 = (bf16[16,128,128]{2,1,0:T(8,128)(2,1)S(1)}, bf16[4,16,128]{2,1,0:T(8,128)(2,1)S(1)}) custom-call(bf16[128,16,128]{2,1,0:T(8,128)(2,1)S(1)} %bitcast.4, bf16[16,128,128]{2,1,0:T(8,128)(2,1)S(1)} %get-tuple-element.37.source, bf16[16,128,128]{2,1,0:T(8,128)(2,1)S(1)} %get-tuple-element.38.gate, bf16[128,128]{1,0:T(8,128)(2,1)S(1)} %copy-done.4, ...), custom_call_target="tpu_custom_call" | custom-call | flops 2000000000 | bytes 1081344 | tf_op jit(solution)/shard_map/update/pallas_call | solution.py:445
  52.9 1.7 %collective-permute-start.9 = (bf16[16,128,128]{2,1,0:T(8,128)(2,1)S(1)}, bf16[16,128,128]{2,1,0:T(8,128)(2,1)S(1)}, u32[]{:S(2)}, u32[]{:S(2)}) collective-permute-start(bf16[16,128,128]{2,1,0:T(8,128)(2,1)S(1)} %get-tuple-element.40.updated), channel_id=1, source_target_pairs={{1,0},{0,1},{3,2},{2,3},{5,4},{4,5},{7,6},{6,7},{9,8},{8,9},{11,10... | collective-permute-start | bytes 1572872 | tf_op jit(solution)/shard_map/ppermute | solution.py:467
  54.7 3.0 %collective-permute-start.8 = (bf16[4,16,128]{2,1,0:T(8,128)(2,1)S(1)}, bf16[4,16,128]{2,1,0:T(8,128)(2,1)S(1)}, u32[]{:S(2)}, u32[]{:S(2)}) collective-permute-start(bf16[4,16,128]{2,1,0:T(8,128)(2,1)S(1)} %get-tuple-element.39.refs_0_), channel_id=1, source_target_pairs={{0,16},{1,17},{2,18},{3,19},{4,20},{5,21},{6,22},{7,23},{8,24},{9,... | collective-permute-start | bytes 49160 | tf_op jit(solution)/shard_map/ppermute | solution.py:421
  57.6 1.7 %collective-permute-done.8.refs_1_ = bf16[4,16,128]{2,1,0:T(8,128)(2,1)S(1)} collective-permute-done((bf16[4,16,128]{2,1,0:T(8,128)(2,1)S(1)}, bf16[4,16,128]{2,1,0:T(8,128)(2,1)S(1)}, u32[]{:S(2)}, u32[]{:S(2)}) %collective-permute-start.8) | collective-permute-done | bytes 16416 | tf_op jit(solution)/shard_map/ppermute | solution.py:421
  60.0 3.4 %all-to-all-start.2 = ((bf16[8,4,16,128]{3,2,1,0:T(8,128)(2,1)}), bf16[8,4,16,128]{3,2,1,0:T(8,128)(2,1)S(1)}, u32[]{:S(2)}, u32[]{:S(2)}) async-start(bf16[8,4,16,128]{3,2,1,0:T(8,128)(2,1)} %deal_bias.1), calls=%async_computation.2 | async-start | bytes 262144 | tf_op jit(solution)/shard_map/all_to_all | solution.py:470
  63.4 2.3 %own_projections.1.mixed_hbm = bf16[16,128,640]{2,1,0:T(8,128)(2,1)} custom-call(bf16[16,128,128]{2,1,0:T(8,128)(2,1)S(1)} %get-tuple-element.40.updated, bf16[128,512]{1,0:T(8,128)(2,1)S(1)} %copy-done.2), custom_call_target="tpu_custom_call" | custom-call | flops 3000000000 | bytes 5242880 | tf_op jit(solution)/shard_map/own_projections/pallas_call | solution.py:476
  65.7 3.7 %all-to-all-done.2.mine = bf16[8,4,16,128]{3,2,1,0:T(8,128)(2,1)S(1)} async-done(((bf16[8,4,16,128]{3,2,1,0:T(8,128)(2,1)}), bf16[8,4,16,128]{3,2,1,0:T(8,128)(2,1)S(1)}, u32[]{:S(2)}, u32[]{:S(2)}) %all-to-all-start.2) | async-done | bytes 131104 | tf_op jit(solution)/shard_map/all_to_all | solution.py:470
  69.4 1.7 %other_keys.1 = (bf16[16,128,640]{2,1,0:T(8,128)(2,1)S(1)}, bf16[16,128,256]{2,1,0:T(8,128)(2,1)S(1)}) custom-call(bf16[16,128,640]{2,1,0:T(8,128)(2,1)} %own_projections.1.mixed_hbm, bf16[128,512]{1,0:T(8,128)(2,1)S(1)} %copy-done.2, bf16[16,128,128]{2,1,0:T(8,128)(2,1)S(1)} %collective-permute-done.9.rest_0_), custom_call_target="tpu_custom_call" | custom-call | flops 3000000000 | bytes 7340032 | tf_op jit(solution)/shard_map/other_keys/pallas_call | solution.py:486
  71.2 4.7 %attend.1 = bf16[16,128,128]{2,1,0:T(8,128)(2,1)} custom-call(s32[1]{0:T(128)S(6)} %copy.11.length, bf16[8,4,16,128]{3,2,1,0:T(8,128)(2,1)S(1)} %all-to-all-done.2.mine, bf16[8,4,16,128]{3,2,1,0:T(8,128)(2,1)S(1)} %collective-permute-done.10.sibling, bf16[128,128]{1,0:T(8,128)(2,1)S(1)} %copy-done, bf16[16,128,640]{2,1,0:T(8,128)(2,1)S(1)} %get-tuple-element.43.rest_0_, ...), custom_call_target="tpu_custom_call" | custom-call | flops 100000000 | bytes 1048576 | tf_op jit(solution)/shard_map/attend/pallas_call | solution.py:495
  (29 shorter events, 6.6 us)
Async XLA Ops:
  4.0 33.7 %all-to-all-start = ((bf16[32,8,16,128]{3,2,1,0:T(8,128)(2,1)}), bf16[32,8,16,128]{3,2,1,0:T(8,128)(2,1)S(1)}, u32[]{:S(2)}, u32[]{:S(2)}) async-start(bf16[32,8,16,128]{3,2,1,0:T(8,128)(2,1)} %get-tuple-element.25), calls=%async_computation | async-start | bytes 2097152 | tf_op jit(solution)/shard_map/all_to_all | solution.py:424
  13.3 1.6 %collective-permute-start = (bf16[8,8,16,128]{3,2,1,0:T(8,128)(2,1)S(1)}, bf16[8,8,16,128]{3,2,1,0:T(8,128)(2,1)S(1)}, u32[]{:S(2)}, u32[]{:S(2)}) collective-permute-start(bf16[8,8,16,128]{3,2,1,0:T(8,128)(2,1)S(1)} %get-tuple-element.28), channel_id=1, source_target_pairs={{0,2},{1,3},{2,0},{3,1},{4,6},{5,7},{6,4},{7,5},{8,10},{9,11},{10,... | collective-permute-start | bytes 786440 | tf_op jit(solution)/shard_map/ppermute | solution.py:421
  15.0 8.4 %collective-permute-start.1 = (bf16[2,8,16,128]{3,2,1,0:T(8,128)(2,1)S(1)}, bf16[2,8,16,128]{3,2,1,0:T(8,128)(2,1)S(1)}, u32[]{:S(2)}, u32[]{:S(2)}) collective-permute-start(bf16[2,8,16,128]{3,2,1,0:T(8,128)(2,1)S(1)} %get-tuple-element.30), channel_id=1, source_target_pairs={{0,1},{1,0},{2,3},{3,2},{4,5},{5,4},{6,7},{7,6},{8,9},{9,8},{10,11... | collective-permute-start | bytes 196616 | tf_op jit(solution)/shard_map/ppermute | solution.py:421
  16.8 8.5 %collective-permute-start.2 = (bf16[2,8,16,128]{3,2,1,0:T(8,128)(2,1)S(1)}, bf16[2,8,16,128]{3,2,1,0:T(8,128)(2,1)S(1)}, u32[]{:S(2)}, u32[]{:S(2)}) collective-permute-start(bf16[2,8,16,128]{3,2,1,0:T(8,128)(2,1)S(1)} %get-tuple-element.31), channel_id=1, source_target_pairs={{0,4},{1,5},{2,6},{3,7},{4,0},{5,1},{6,2},{7,3},{8,12},{9,13},{10,... | collective-permute-start | bytes 196616 | tf_op jit(solution)/shard_map/ppermute | solution.py:421
  18.3 7.6 %collective-permute-start.3 = (bf16[2,8,16,128]{3,2,1,0:T(8,128)(2,1)S(1)}, bf16[2,8,16,128]{3,2,1,0:T(8,128)(2,1)S(1)}, u32[]{:S(2)}, u32[]{:S(2)}) collective-permute-start(bf16[2,8,16,128]{3,2,1,0:T(8,128)(2,1)S(1)} %get-tuple-element.32), channel_id=1, source_target_pairs={{0,5},{1,4},{2,7},{3,6},{4,1},{5,0},{6,3},{7,2},{8,13},{9,12},{10,... | collective-permute-start | bytes 196616 | tf_op jit(solution)/shard_map/ppermute | solution.py:421
  18.5 12.2 %collective-permute-start.4 = (bf16[2,8,16,128]{3,2,1,0:T(8,128)(2,1)S(1)}, bf16[2,8,16,128]{3,2,1,0:T(8,128)(2,1)S(1)}, u32[]{:S(2)}, u32[]{:S(2)}) collective-permute-start(bf16[2,8,16,128]{3,2,1,0:T(8,128)(2,1)S(1)} %get-tuple-element.33), channel_id=1, source_target_pairs={{0,8},{1,9},{2,10},{3,11},{4,12},{5,13},{6,14},{7,15},{8,0},{9,1},... | collective-permute-start | bytes 196616 | tf_op jit(solution)/shard_map/ppermute | solution.py:421
  20.3 11.9 %collective-permute-start.5 = (bf16[2,8,16,128]{3,2,1,0:T(8,128)(2,1)S(1)}, bf16[2,8,16,128]{3,2,1,0:T(8,128)(2,1)S(1)}, u32[]{:S(2)}, u32[]{:S(2)}) collective-permute-start(bf16[2,8,16,128]{3,2,1,0:T(8,128)(2,1)S(1)} %get-tuple-element.34), channel_id=1, source_target_pairs={{0,9},{1,8},{2,11},{3,10},{4,13},{5,12},{6,15},{7,14},{8,1},{9,0},... | collective-permute-start | bytes 196616 | tf_op jit(solution)/shard_map/ppermute | solution.py:421
  23.3 11.5 %collective-permute-start.6 = (bf16[2,8,16,128]{3,2,1,0:T(8,128)(2,1)S(1)}, bf16[2,8,16,128]{3,2,1,0:T(8,128)(2,1)S(1)}, u32[]{:S(2)}, u32[]{:S(2)}) collective-permute-start(bf16[2,8,16,128]{3,2,1,0:T(8,128)(2,1)S(1)} %get-tuple-element.35), channel_id=1, source_target_pairs={{0,12},{1,13},{2,14},{3,15},{4,8},{5,9},{6,10},{7,11},{8,4},{9,5},... | collective-permute-start | bytes 196616 | tf_op jit(solution)/shard_map/ppermute | solution.py:421
  25.3 12.5 %collective-permute-start.7 = (bf16[2,8,16,128]{3,2,1,0:T(8,128)(2,1)S(1)}, bf16[2,8,16,128]{3,2,1,0:T(8,128)(2,1)S(1)}, u32[]{:S(2)}, u32[]{:S(2)}) collective-permute-start(bf16[2,8,16,128]{3,2,1,0:T(8,128)(2,1)S(1)} %get-tuple-element.36), channel_id=1, source_target_pairs={{0,13},{1,12},{2,15},{3,14},{4,9},{5,8},{6,11},{7,10},{8,5},{9,4},... | collective-permute-start | bytes 196616 | tf_op jit(solution)/shard_map/ppermute | solution.py:421
  37.8 6.5 %copy-start.6 = (bf16[128,4]{0,1:T(4,128)(2,1)S(1)}, bf16[128,4]{0,1:T(4,128)(2,1)}, u32[]{:S(2)}) copy-start(bf16[128,4]{0,1:T(4,128)(2,1)} %param.16) | copy-start | bytes 3076
  37.8 6.6 %copy-start.1 = (bf16[16,128,128]{2,1,0:T(8,128)(2,1)S(1)}, bf16[16,128,128]{2,1,0:T(8,128)(2,1)}, u32[]{:S(2)}) copy-start(bf16[16,128,128]{2,1,0:T(8,128)(2,1)} %pair.1) | copy-start | bytes 1572868
  37.8 6.6 %copy-start.3 = (bf16[128,128]{1,0:T(8,128)(2,1)S(1)}, bf16[128,128]{1,0:T(8,128)(2,1)}, u32[]{:S(2)}) copy-start(bf16[128,128]{1,0:T(8,128)(2,1)} %weights.1) | copy-start | bytes 98308
  37.8 6.6 %copy-start.5 = (bf16[16,128,128]{2,1,0:T(8,128)(2,1)S(1)}, bf16[16,128,128]{2,1,0:T(8,128)(2,1)}, u32[]{:S(2)}) copy-start(bf16[16,128,128]{2,1,0:T(8,128)(2,1)} %get-tuple-element.26.source_hbm.normed) | copy-start | bytes 1572868
  39.1 12.3 %all-to-all-start.1 = ((bf16[16,8,16,128]{3,2,1,0:T(8,128)(2,1)}), bf16[16,8,16,128]{3,2,1,0:T(8,128)(2,1)S(1)}, u32[]{:S(2)}, u32[]{:S(2)}) async-start(bf16[16,8,16,128]{3,2,1,0:T(8,128)(2,1)} %bitcast.5), calls=%async_computation.1 | async-start | bytes 1048576 | tf_op jit(solution)/shard_map/all_to_all | solution.py:390
  44.4 7.0 %copy-start.4 = (bf16[128,128]{1,0:T(8,128)(2,1)S(1)}, bf16[128,128]{1,0:T(8,128)(2,1)}, u32[]{:S(2)}) copy-start(bf16[128,128]{1,0:T(8,128)(2,1)} %tri_out.1) | copy-start | bytes 98308
  51.4 12.0 %copy-start.2 = (bf16[128,512]{1,0:T(8,128)(2,1)S(1)}, bf16[128,512]{1,0:T(8,128)(2,1)}, u32[]{:S(2)}) copy-start(bf16[128,512]{1,0:T(8,128)(2,1)} %attn_proj.3) | copy-start | bytes 393220
  52.9 16.5 %collective-permute-start.9 = (bf16[16,128,128]{2,1,0:T(8,128)(2,1)S(1)}, bf16[16,128,128]{2,1,0:T(8,128)(2,1)S(1)}, u32[]{:S(2)}, u32[]{:S(2)}) collective-permute-start(bf16[16,128,128]{2,1,0:T(8,128)(2,1)S(1)} %get-tuple-element.40.updated), channel_id=1, source_target_pairs={{1,0},{0,1},{3,2},{2,3},{5,4},{4,5},{7,6},{6,7},{9,8},{8,9},{11,10... | collective-permute-start | bytes 1572872 | tf_op jit(solution)/shard_map/ppermute | solution.py:467
  54.7 4.7 %collective-permute-start.8 = (bf16[4,16,128]{2,1,0:T(8,128)(2,1)S(1)}, bf16[4,16,128]{2,1,0:T(8,128)(2,1)S(1)}, u32[]{:S(2)}, u32[]{:S(2)}) collective-permute-start(bf16[4,16,128]{2,1,0:T(8,128)(2,1)S(1)} %get-tuple-element.39.refs_0_), channel_id=1, source_target_pairs={{0,16},{1,17},{2,18},{3,19},{4,20},{5,21},{6,22},{7,23},{8,24},{9,... | collective-permute-start | bytes 49160 | tf_op jit(solution)/shard_map/ppermute | solution.py:421
  60.0 9.4 %all-to-all-start.2 = ((bf16[8,4,16,128]{3,2,1,0:T(8,128)(2,1)}), bf16[8,4,16,128]{3,2,1,0:T(8,128)(2,1)S(1)}, u32[]{:S(2)}, u32[]{:S(2)}) async-start(bf16[8,4,16,128]{3,2,1,0:T(8,128)(2,1)} %deal_bias.1), calls=%async_computation.2 | async-start | bytes 262144 | tf_op jit(solution)/shard_map/all_to_all | solution.py:470
  65.7 5.5 %copy-start = (bf16[128,128]{1,0:T(8,128)(2,1)S(1)}, bf16[128,128]{1,0:T(8,128)(2,1)}, u32[]{:S(2)}) copy-start(bf16[128,128]{1,0:T(8,128)(2,1)} %attn_out.1) | copy-start | bytes 98308
  69.4 1.8 %collective-permute-start.10 = (bf16[8,4,16,128]{3,2,1,0:T(8,128)(2,1)S(1)}, bf16[8,4,16,128]{3,2,1,0:T(8,128)(2,1)S(1)}, u32[]{:S(2)}, u32[]{:S(2)}) collective-permute-start(bf16[8,4,16,128]{3,2,1,0:T(8,128)(2,1)S(1)} %all-to-all-done.2.mine), channel_id=1, source_target_pairs={{0,2},{1,3},{2,0},{3,1},{4,6},{5,7},{6,4},{7,5},{8,10},{9,11},{10,... | collective-permute-start | bytes 393224 | tf_op jit(solution)/shard_map/ppermute | solution.py:421

commit v3 on v2

--- a/solution.py
+++ b/solution.py
@@ -38,13 +38,13 @@
 
 def call(body, name, outs, ins, scratch=(), flops=1e8, smem=0, space=VMEM, out_space=VMEM, specs=None):
     sizes = [math.prod(a.shape) * a.dtype.itemsize for a in outs]
-    if out_space is HBM:
-        outs = [pltpu.HBM(a.shape, a.dtype) for a in outs]
+    spaces = out_space if isinstance(out_space, list) else [out_space] * len(outs)
+    outs = [pltpu.HBM(a.shape, a.dtype) if b is HBM else a for a, b in zip(outs, spaces)]
     return pl.pallas_call(
         body,
         out_shape=outs,
         in_specs=specs or [SMEM] * smem + [space] * (ins - smem),
-        out_specs=[out_space] * len(outs),
+        out_specs=spaces,
         scratch_shapes=list(scratch),
         compiler_params=pltpu.CompilerParams(vmem_limit_bytes=16 * 2**20),
         cost_estimate=pl.CostEstimate(
@@ -252,31 +252,31 @@
     bias[...] = bias_held[...].astype(BF16).reshape(heads, rows, cols)
 
 
-def project(updated, attn_proj, mixed, row, score_scale):
+def project(updated, attn_proj, mixed, row, score_scale, late=None):
     channels = updated.shape[1]
     values = updated[row].astype(F32)
     normed = layer_norm(values, 0)
     natural = normed.T.astype(BF16)
 
-    def put(block, array):
-        mixed[row, :, block * channels : (block + 1) * channels] = array.astype(BF16)
-
-    put(0, dot(turned(attn_proj[:, channels : 2 * channels]), normed.astype(BF16), (1, 0)))
-    put(1, dot(natural, attn_proj[:, 2 * channels : 3 * channels], (1, 0)))
-    if score_scale is not None:
-        put(2, dot(natural, attn_proj[:, :channels], (1, 0)) * score_scale)
-        put(3, sigmoid(dot(natural, attn_proj[:, 3 * channels :], (1, 0))))
-        put(4, values.T)
-
-
-def own_body(updated, attn_proj, mixed_hbm, mixed, sems, *, score_scale):
+    def put(target, block, array):
+        target[row, :, block * channels : (block + 1) * channels] = array.astype(BF16)
+
+    put(mixed, 0, dot(turned(attn_proj[:, channels : 2 * channels]), normed.astype(BF16), (1, 0)))
+    put(mixed, 1, dot(natural, attn_proj[:, 2 * channels : 3 * channels], (1, 0)))
+    if late is not None:
+        put(mixed, 2, dot(natural, attn_proj[:, :channels], (1, 0)) * score_scale)
+        put(late, 0, sigmoid(dot(natural, attn_proj[:, 3 * channels :], (1, 0))))
+        put(late, 1, values.T)
+
+
+def own_body(updated, attn_proj, mixed, late_hbm, late, sems, *, score_scale):
     rows = updated.shape[0]
 
     def step(row, carry):
-        project(updated, attn_proj, mixed, row, score_scale)
+        project(updated, attn_proj, mixed, row, score_scale, late)
         return carry
 
-    sends = chunked([(mixed, mixed_hbm)], sems, 0, 2)
+    sends = chunked([(late, late_hbm)], sems, 0, 2)
     for chunk in range(2):
         lax.fori_loop(chunk * rows // 2, (chunk + 1) * rows // 2, step, 0, unroll=rows // 2)
         sends[chunk][0].start()
@@ -284,12 +284,12 @@
         copy.wait()
 
 
-def other_body(mixed_hbm, attn_proj, *rest):
+def other_body(late_hbm, attn_proj, *rest):
     pieces = (len(rest) - 2) // 2
-    others, mixed, keys, sem = rest[:pieces], rest[pieces], rest[pieces + 1 : -1], rest[-1]
-    fetch = pltpu.make_async_copy(mixed_hbm, mixed, sem)
+    others, late, keys, sem = rest[:pieces], rest[pieces], rest[pieces + 1 : -1], rest[-1]
+    fetch = pltpu.make_async_copy(late_hbm, late, sem)
     fetch.start()
-    rows = mixed.shape[0]
+    rows = late.shape[0]
     for updated, target in zip(others, keys):
 
         def step(row, carry):
@@ -300,7 +300,7 @@
     fetch.wait()
 
 
-def attend_body(length, mine, sibling, attn_out, *rest):
+def attend_body(length, mine, sibling, attn_out, late, *rest):
     mixed, (out_hbm, out, bias_held, sems) = rest[:-4], rest[-4:]
     pieces = len(mixed)
     rows, cols, channels = out.shape
@@ -331,13 +331,13 @@
         keys = jnp.concatenate([part[row, :, :channels] for part in mixed], axis=1)
         values = jnp.concatenate([part[row, :, channels : 2 * channels] for part in mixed], axis=0)
         values = jnp.concatenate([values, ones], axis=1)
-        return keys, values, mixed[0][row, :, 2 * channels : 3 * channels]
+        return keys, values, mixed[0][row, :, 2 * channels :]
 
     def finish(row, total):
         attended = total[:, :channels] / total[:, channels:]
-        gate = mixed[0][row, :, 3 * channels : 4 * channels].astype(F32)
+        gate = late[row, :, :channels].astype(F32)
         gated = (attended * gate).astype(BF16)
-        residual = mixed[0][row, :, 4 * channels :].astype(F32)
+        residual = late[row, :, channels:].astype(F32)
         out[row] = (residual + dot(gated, attn_out[...], (1, 0))).astype(BF16)
 
     per_chunk = rows // count
@@ -471,32 +471,32 @@
         dealt, BOTH, split_axis=0, concat_axis=0, axis_index_groups=one_core, tiled=True
     )
 
-    mixed_shape = (rows, cols, 5 * channels)
+    mixed_shape = (rows, cols, 3 * channels)
     key_shape = (rows, cols, 2 * channels)
-    (mixed,) = call(
+    mixed, late = call(
         functools.partial(own_body, score_scale=(channels // heads) ** (-0.5)),
         "own_projections",
-        [shape(mixed_shape, BF16)],
+        [shape(mixed_shape, BF16), shape(key_shape, BF16)],
         2,
-        [pltpu.VMEM(mixed_shape, BF16), pltpu.SemaphoreType.DMA((1, 2))],
-        out_space=HBM,
+        [pltpu.VMEM(key_shape, BF16), pltpu.SemaphoreType.DMA((1, 2))],
+        out_space=[VMEM, HBM],
         flops=3e9,
     )(updated, attn_proj)
     bias, *others = lax.optimization_barrier((bias, *others))
-    mixed = call(
+    late, *keys = call(
         other_body,
         "other_keys",
-        [shape(mixed_shape, BF16)] + [shape(key_shape, BF16)] * len(others),
+        [shape(key_shape, BF16)] * (1 + len(others)),
         2 + len(others),
         [pltpu.SemaphoreType.DMA(())],
         specs=[HBM] + [VMEM] * (1 + len(others)),
         flops=3e9,
-    )(in_hbm(mixed), attn_proj, *others)
+    )(in_hbm(late), attn_proj, *others)
     (result,) = call(
         attend_body,
         "attend",
         [shape(block, BF16)],
-        4 + col_devices,
+        5 + col_devices,
         [
             pltpu.VMEM(block, BF16),
             pltpu.VMEM((heads * cols, col_devices * cols), F32),
@@ -504,7 +504,7 @@
         ],
         smem=1,
         out_space=HBM,
-    )(valid_count, bias, flipped(bias, col_devices), attn_out, *mixed)
+    )(valid_count, bias, flipped(bias, col_devices), attn_out, late, mixed, *keys)
     return result
 
 

time: 76.4 us -> 75.9 us (level)
  Pallas kernels: 19.2 us -> 18.4 us
  transfers between devices with their start and end apart: 14 -> 14, of which waited for: 10 -> 11; matrix products, arithmetic and copies ran while one was open for 0% -> 0% of each run, Pallas kernels for 11% -> 10%
where the time goes in v3:
time: 75.9 us; the launch traced here: 75.5 us
  starting transfers between devices  28.9 us (38%)
  waiting for transfers between devices  27.2 us (36%)
  Pallas kernels  18.4 us (24%)
  between operations  0.79 us (1%)
    ppermute x10, waiting for transfers between devices, flipped(): return lax.ppermute(array, BOTH, [(d, d ^ bits) for d in range(devices)])  17.7 us
    ppermute x10, starting transfers between devices, flipped(): return lax.ppermute(array, BOTH, [(d, d ^ bits) for d in range(devices)])  11.4 us
    all_to_all x1, starting transfers between devices, local(): right = lax.all_to_all(right, BOTH, split_axis=0, concat_axis=0, tiled=True)  7.3 us
    all_to_all x1, waiting for transfers between devices, in_half(): lax.all_to_all(array, BOTH, split_axis=0, concat_axis=0, axis_index_group...  5.43 us
    pallas_call x2, Pallas kernels, edges(): call(functools.partial(edges_body, side=side), 'right_edges' if side else...  5.33 us
    all_to_all x1, starting transfers between devices, in_half(): lax.all_to_all(array, BOTH, split_axis=0, concat_axis=0, axis_index_group...  5.12 us
    pallas_call x1, Pallas kernels, local(): call(attend_body, 'attend', [shape(block, BF16)], 5 + col_devices, [pltpu...  4.67 us
    all_to_all x1, waiting for transfers between devices, local(): lax.all_to_all(dealt, BOTH, split_axis=0, concat_axis=0, axis_index_group...  4.06 us
  transfers between devices with their start and end apart: 14, of which 11 were waited for; matrix products, arithmetic and copies ran while one was open for 0% of the time, Pallas kernels for 10%

profile of v3, /device:TPU:0, one launch (start us, length us, event | category | flops | bytes accessed | tf_op | source)
XLA Modules:
  0.0 75.5 jit_solution(7948910512292185916)
XLA Ops:
  0.7 3.3 %right_edges.1 = (bf16[32,8,16,128]{3,2,1,0:T(8,128)(2,1)}, bf16[16,128,128]{2,1,0:T(8,128)(2,1)}) custom-call(s32[1]{0:T(128)S(6)} %copy.11.length, bf16[16,128,128]{2,1,0:T(8,128)(2,1)} %pair.1, bf16[128,256]{1,0:T(8,128)(2,1)} %proj_hbm.3, bf16[128,256]{1,0:T(8,128)(2,1)} %gate_hbm.3), custom_call_target="tpu_custom_call" | custom-call | flops 3000000000 | bytes 3145728 | tf_op jit(solution)/shard_map/right_edges/pallas_call | solution.py:401
  4.0 7.3 %all-to-all-start = ((bf16[32,8,16,128]{3,2,1,0:T(8,128)(2,1)}), bf16[32,8,16,128]{3,2,1,0:T(8,128)(2,1)S(1)}, u32[]{:S(2)}, u32[]{:S(2)}) async-start(bf16[32,8,16,128]{3,2,1,0:T(8,128)(2,1)} %get-tuple-element.27), calls=%async_computation | async-start | bytes 2097152 | tf_op jit(solution)/shard_map/all_to_all | solution.py:424
  11.3 2.0 %left_edges.1 = (bf16[8,8,16,128]{3,2,1,0:T(8,128)(2,1)S(1)}, bf16[8,8,16,128]{3,2,1,0:T(8,128)(2,1)S(1)}) custom-call(s32[1]{0:T(128)S(6)} %copy.11.length, bf16[16,128,128]{2,1,0:T(8,128)(2,1)} %get-tuple-element.28.source_hbm.normed, bf16[128,256]{1,0:T(8,128)(2,1)} %proj_hbm.3, bf16[128,256]{1,0:T(8,128)(2,1)} %gate_hbm.3), custom_call_target="tpu_custom_call" | custom-call | flops 3000000000 | bytes 1048576 | tf_op jit(solution)/shard_map/left_edges/pallas_call | solution.py:401
  15.0 1.8 %collective-permute-start.1 = (bf16[2,8,16,128]{3,2,1,0:T(8,128)(2,1)S(1)}, bf16[2,8,16,128]{3,2,1,0:T(8,128)(2,1)S(1)}, u32[]{:S(2)}, u32[]{:S(2)}) collective-permute-start(bf16[2,8,16,128]{3,2,1,0:T(8,128)(2,1)S(1)} %get-tuple-element.32), channel_id=1, source_target_pairs={{0,1},{1,0},{2,3},{3,2},{4,5},{5,4},{6,7},{7,6},{8,9},{9,8},{10,11... | collective-permute-start | bytes 196616 | tf_op jit(solution)/shard_map/ppermute | solution.py:421
  16.8 1.5 %collective-permute-start.2 = (bf16[2,8,16,128]{3,2,1,0:T(8,128)(2,1)S(1)}, bf16[2,8,16,128]{3,2,1,0:T(8,128)(2,1)S(1)}, u32[]{:S(2)}, u32[]{:S(2)}) collective-permute-start(bf16[2,8,16,128]{3,2,1,0:T(8,128)(2,1)S(1)} %get-tuple-element.33), channel_id=1, source_target_pairs={{0,4},{1,5},{2,6},{3,7},{4,0},{5,1},{6,2},{7,3},{8,12},{9,13},{10,... | collective-permute-start | bytes 196616 | tf_op jit(solution)/shard_map/ppermute | solution.py:421
  18.5 1.8 %collective-permute-start.4 = (bf16[2,8,16,128]{3,2,1,0:T(8,128)(2,1)S(1)}, bf16[2,8,16,128]{3,2,1,0:T(8,128)(2,1)S(1)}, u32[]{:S(2)}, u32[]{:S(2)}) collective-permute-start(bf16[2,8,16,128]{3,2,1,0:T(8,128)(2,1)S(1)} %get-tuple-element.35), channel_id=1, source_target_pairs={{0,8},{1,9},{2,10},{3,11},{4,12},{5,13},{6,14},{7,15},{8,0},{9,1},... | collective-permute-start | bytes 196616 | tf_op jit(solution)/shard_map/ppermute | solution.py:421
  20.3 1.5 %collective-permute-start.5 = (bf16[2,8,16,128]{3,2,1,0:T(8,128)(2,1)S(1)}, bf16[2,8,16,128]{3,2,1,0:T(8,128)(2,1)S(1)}, u32[]{:S(2)}, u32[]{:S(2)}) collective-permute-start(bf16[2,8,16,128]{3,2,1,0:T(8,128)(2,1)S(1)} %get-tuple-element.36), channel_id=1, source_target_pairs={{0,9},{1,8},{2,11},{3,10},{4,13},{5,12},{6,15},{7,14},{8,1},{9,0},... | collective-permute-start | bytes 196616 | tf_op jit(solution)/shard_map/ppermute | solution.py:421
  21.7 1.6 %collective-permute-done.1.rest_1_ = bf16[2,8,16,128]{3,2,1,0:T(8,128)(2,1)S(1)} collective-permute-done((bf16[2,8,16,128]{3,2,1,0:T(8,128)(2,1)S(1)}, bf16[2,8,16,128]{3,2,1,0:T(8,128)(2,1)S(1)}, u32[]{:S(2)}, u32[]{:S(2)}) %collective-permute-start.1) | collective-permute-done | bytes 65568 | tf_op jit(solution)/shard_map/ppermute | solution.py:421
  25.8 4.9 %collective-permute-done.4.rest_4_ = bf16[2,8,16,128]{3,2,1,0:T(8,128)(2,1)S(1)} collective-permute-done((bf16[2,8,16,128]{3,2,1,0:T(8,128)(2,1)S(1)}, bf16[2,8,16,128]{3,2,1,0:T(8,128)(2,1)S(1)}, u32[]{:S(2)}, u32[]{:S(2)}) %collective-permute-start.4) | collective-permute-done | bytes 65568 | tf_op jit(solution)/shard_map/ppermute | solution.py:421
  30.7 1.5 %collective-permute-done.5.rest_5_ = bf16[2,8,16,128]{3,2,1,0:T(8,128)(2,1)S(1)} collective-permute-done((bf16[2,8,16,128]{3,2,1,0:T(8,128)(2,1)S(1)}, bf16[2,8,16,128]{3,2,1,0:T(8,128)(2,1)S(1)}, u32[]{:S(2)}, u32[]{:S(2)}) %collective-permute-start.5) | collective-permute-done | bytes 65568 | tf_op jit(solution)/shard_map/ppermute | solution.py:421
  32.2 2.7 %collective-permute-done.6.rest_6_ = bf16[2,8,16,128]{3,2,1,0:T(8,128)(2,1)S(1)} collective-permute-done((bf16[2,8,16,128]{3,2,1,0:T(8,128)(2,1)S(1)}, bf16[2,8,16,128]{3,2,1,0:T(8,128)(2,1)S(1)}, u32[]{:S(2)}, u32[]{:S(2)}) %collective-permute-start.6) | collective-permute-done | bytes 65568 | tf_op jit(solution)/shard_map/ppermute | solution.py:421
  34.9 2.9 %collective-permute-done.7.rest_7_ = bf16[2,8,16,128]{3,2,1,0:T(8,128)(2,1)S(1)} collective-permute-done((bf16[2,8,16,128]{3,2,1,0:T(8,128)(2,1)S(1)}, bf16[2,8,16,128]{3,2,1,0:T(8,128)(2,1)S(1)}, u32[]{:S(2)}, u32[]{:S(2)}) %collective-permute-start.7) | collective-permute-done | bytes 65568 | tf_op jit(solution)/shard_map/ppermute | solution.py:421
  37.8 1.3 %triangle.1 = bf16[8,2,8,16,128]{4,3,2,1,0:T(8,128)(2,1)} custom-call(bf16[16,2,8,16,128]{4,3,2,1,0:T(8,128)(2,1)S(1)} %bitcast.3, bf16[2,8,16,128]{3,2,1,0:T(8,128)(2,1)S(1)} %get-tuple-element.31.rest_0_, bf16[2,8,16,128]{3,2,1,0:T(8,128)(2,1)S(1)} %collective-permute-done.1.rest_1_, bf16[2,8,16,128]{3,2,1,0:T(8,128)(2,1)S(1)} %collective-permute-done.2.rest_2_, ...), custom_call_target="tpu_custom_call" | custom-call | flops 2000000000 | bytes 1048576 | tf_op jit(solution)/shard_map/triangle/pallas_call | solution.py:434
  39.1 5.1 %all-to-all-start.1 = ((bf16[16,8,16,128]{3,2,1,0:T(8,128)(2,1)}), bf16[16,8,16,128]{3,2,1,0:T(8,128)(2,1)S(1)}, u32[]{:S(2)}, u32[]{:S(2)}) async-start(bf16[16,8,16,128]{3,2,1,0:T(8,128)(2,1)} %bitcast.5), calls=%async_computation.1 | async-start | bytes 1048576 | tf_op jit(solution)/shard_map/all_to_all | solution.py:390
  44.4 1.6 %tri_gate.1 = (bf16[16,128,128]{2,1,0:T(8,128)(2,1)S(1)}, bf16[16,128,128]{2,1,0:T(8,128)(2,1)S(1)}) custom-call(bf16[16,128,128]{2,1,0:T(8,128)(2,1)S(1)} %copy-done.1, bf16[16,128,128]{2,1,0:T(8,128)(2,1)S(1)} %copy-done.5, bf16[128,128]{1,0:T(8,128)(2,1)S(1)} %copy-done.3), custom_call_target="tpu_custom_call" | custom-call | flops 2000000000 | bytes 2097152 | tf_op jit(solution)/shard_map/tri_gate/pallas_call | solution.py:430
  46.0 5.4 %all-to-all-done.1 = bf16[16,8,16,128]{3,2,1,0:T(8,128)(2,1)S(1)} async-done(((bf16[16,8,16,128]{3,2,1,0:T(8,128)(2,1)}), bf16[16,8,16,128]{3,2,1,0:T(8,128)(2,1)S(1)}, u32[]{:S(2)}, u32[]{:S(2)}) %all-to-all-start.1) | async-done | bytes 524320 | tf_op jit(solution)/shard_map/all_to_all | solution.py:390
  51.4 1.5 %update.1 = (bf16[16,128,128]{2,1,0:T(8,128)(2,1)S(1)}, bf16[4,16,128]{2,1,0:T(8,128)(2,1)S(1)}) custom-call(bf16[128,16,128]{2,1,0:T(8,128)(2,1)S(1)} %bitcast.4, bf16[16,128,128]{2,1,0:T(8,128)(2,1)S(1)} %get-tuple-element.39.source, bf16[16,128,128]{2,1,0:T(8,128)(2,1)S(1)} %get-tuple-element.40.gate, bf16[128,128]{1,0:T(8,128)(2,1)S(1)} %copy-done.4, ...), custom_call_target="tpu_custom_call" | custom-call | flops 2000000000 | bytes 1081344 | tf_op jit(solution)/shard_map/update/pallas_call | solution.py:445
  52.9 1.7 %collective-permute-start.9 = (bf16[16,128,128]{2,1,0:T(8,128)(2,1)S(1)}, bf16[16,128,128]{2,1,0:T(8,128)(2,1)S(1)}, u32[]{:S(2)}, u32[]{:S(2)}) collective-permute-start(bf16[16,128,128]{2,1,0:T(8,128)(2,1)S(1)} %get-tuple-element.42.updated), channel_id=1, source_target_pairs={{1,0},{0,1},{3,2},{2,3},{5,4},{4,5},{7,6},{6,7},{9,8},{8,9},{11,10... | collective-permute-start | bytes 1572872 | tf_op jit(solution)/shard_map/ppermute | solution.py:467
  54.7 3.0 %collective-permute-start.8 = (bf16[4,16,128]{2,1,0:T(8,128)(2,1)S(1)}, bf16[4,16,128]{2,1,0:T(8,128)(2,1)S(1)}, u32[]{:S(2)}, u32[]{:S(2)}) collective-permute-start(bf16[4,16,128]{2,1,0:T(8,128)(2,1)S(1)} %get-tuple-element.41.refs_0_), channel_id=1, source_target_pairs={{0,16},{1,17},{2,18},{3,19},{4,20},{5,21},{6,22},{7,23},{8,24},{9,... | collective-permute-start | bytes 49160 | tf_op jit(solution)/shard_map/ppermute | solution.py:421
  57.6 1.7 %collective-permute-done.8.refs_1_ = bf16[4,16,128]{2,1,0:T(8,128)(2,1)S(1)} collective-permute-done((bf16[4,16,128]{2,1,0:T(8,128)(2,1)S(1)}, bf16[4,16,128]{2,1,0:T(8,128)(2,1)S(1)}, u32[]{:S(2)}, u32[]{:S(2)}) %collective-permute-start.8) | collective-permute-done | bytes 16416 | tf_op jit(solution)/shard_map/ppermute | solution.py:421
  60.0 3.4 %all-to-all-start.2 = ((bf16[8,4,16,128]{3,2,1,0:T(8,128)(2,1)}), bf16[8,4,16,128]{3,2,1,0:T(8,128)(2,1)S(1)}, u32[]{:S(2)}, u32[]{:S(2)}) async-start(bf16[8,4,16,128]{3,2,1,0:T(8,128)(2,1)} %deal_bias.1), calls=%async_computation.2 | async-start | bytes 262144 | tf_op jit(solution)/shard_map/all_to_all | solution.py:470
  63.4 1.9 %own_projections.1 = (bf16[16,128,384]{2,1,0:T(8,128)(2,1)S(1)}, bf16[16,128,256]{2,1,0:T(8,128)(2,1)}) custom-call(bf16[16,128,128]{2,1,0:T(8,128)(2,1)S(1)} %get-tuple-element.42.updated, bf16[128,512]{1,0:T(8,128)(2,1)S(1)} %copy-done.2), custom_call_target="tpu_custom_call" | custom-call | flops 3000000000 | bytes 5242880 | tf_op jit(solution)/shard_map/own_projections/pallas_call | solution.py:476
  65.4 4.1 %all-to-all-done.2.mine = bf16[8,4,16,128]{3,2,1,0:T(8,128)(2,1)S(1)} async-done(((bf16[8,4,16,128]{3,2,1,0:T(8,128)(2,1)}), bf16[8,4,16,128]{3,2,1,0:T(8,128)(2,1)S(1)}, u32[]{:S(2)}, u32[]{:S(2)}) %all-to-all-start.2) | async-done | bytes 131104 | tf_op jit(solution)/shard_map/all_to_all | solution.py:470
  70.8 4.7 %attend.1 = bf16[16,128,128]{2,1,0:T(8,128)(2,1)} custom-call(s32[1]{0:T(128)S(6)} %copy.11.length, bf16[8,4,16,128]{3,2,1,0:T(8,128)(2,1)S(1)} %all-to-all-done.2.mine, bf16[8,4,16,128]{3,2,1,0:T(8,128)(2,1)S(1)} %collective-permute-done.10.sibling, bf16[128,128]{1,0:T(8,128)(2,1)S(1)} %copy-done, bf16[16,128,256]{2,1,0:T(8,128)(2,1)S(1)} %get-tuple-element.46.late, ...), custom_call_target="tpu_custom_call" | custom-call | flops 100000000 | bytes 1048576 | tf_op jit(solution)/shard_map/attend/pallas_call | solution.py:495
  (29 shorter events, 6.6 us)
Async XLA Ops:
  4.0 33.7 %all-to-all-start = ((bf16[32,8,16,128]{3,2,1,0:T(8,128)(2,1)}), bf16[32,8,16,128]{3,2,1,0:T(8,128)(2,1)S(1)}, u32[]{:S(2)}, u32[]{:S(2)}) async-start(bf16[32,8,16,128]{3,2,1,0:T(8,128)(2,1)} %get-tuple-element.27), calls=%async_computation | async-start | bytes 2097152 | tf_op jit(solution)/shard_map/all_to_all | solution.py:424
  13.3 1.6 %collective-permute-start = (bf16[8,8,16,128]{3,2,1,0:T(8,128)(2,1)S(1)}, bf16[8,8,16,128]{3,2,1,0:T(8,128)(2,1)S(1)}, u32[]{:S(2)}, u32[]{:S(2)}) collective-permute-start(bf16[8,8,16,128]{3,2,1,0:T(8,128)(2,1)S(1)} %get-tuple-element.30), channel_id=1, source_target_pairs={{0,2},{1,3},{2,0},{3,1},{4,6},{5,7},{6,4},{7,5},{8,10},{9,11},{10,... | collective-permute-start | bytes 786440 | tf_op jit(solution)/shard_map/ppermute | solution.py:421
  15.0 8.4 %collective-permute-start.1 = (bf16[2,8,16,128]{3,2,1,0:T(8,128)(2,1)S(1)}, bf16[2,8,16,128]{3,2,1,0:T(8,128)(2,1)S(1)}, u32[]{:S(2)}, u32[]{:S(2)}) collective-permute-start(bf16[2,8,16,128]{3,2,1,0:T(8,128)(2,1)S(1)} %get-tuple-element.32), channel_id=1, source_target_pairs={{0,1},{1,0},{2,3},{3,2},{4,5},{5,4},{6,7},{7,6},{8,9},{9,8},{10,11... | collective-permute-start | bytes 196616 | tf_op jit(solution)/shard_map/ppermute | solution.py:421
  16.8 8.5 %collective-permute-start.2 = (bf16[2,8,16,128]{3,2,1,0:T(8,128)(2,1)S(1)}, bf16[2,8,16,128]{3,2,1,0:T(8,128)(2,1)S(1)}, u32[]{:S(2)}, u32[]{:S(2)}) collective-permute-start(bf16[2,8,16,128]{3,2,1,0:T(8,128)(2,1)S(1)} %get-tuple-element.33), channel_id=1, source_target_pairs={{0,4},{1,5},{2,6},{3,7},{4,0},{5,1},{6,2},{7,3},{8,12},{9,13},{10,... | collective-permute-start | bytes 196616 | tf_op jit(solution)/shard_map/ppermute | solution.py:421
  18.3 7.6 %collective-permute-start.3 = (bf16[2,8,16,128]{3,2,1,0:T(8,128)(2,1)S(1)}, bf16[2,8,16,128]{3,2,1,0:T(8,128)(2,1)S(1)}, u32[]{:S(2)}, u32[]{:S(2)}) collective-permute-start(bf16[2,8,16,128]{3,2,1,0:T(8,128)(2,1)S(1)} %get-tuple-element.34), channel_id=1, source_target_pairs={{0,5},{1,4},{2,7},{3,6},{4,1},{5,0},{6,3},{7,2},{8,13},{9,12},{10,... | collective-permute-start | bytes 196616 | tf_op jit(solution)/shard_map/ppermute | solution.py:421
  18.5 12.2 %collective-permute-start.4 = (bf16[2,8,16,128]{3,2,1,0:T(8,128)(2,1)S(1)}, bf16[2,8,16,128]{3,2,1,0:T(8,128)(2,1)S(1)}, u32[]{:S(2)}, u32[]{:S(2)}) collective-permute-start(bf16[2,8,16,128]{3,2,1,0:T(8,128)(2,1)S(1)} %get-tuple-element.35), channel_id=1, source_target_pairs={{0,8},{1,9},{2,10},{3,11},{4,12},{5,13},{6,14},{7,15},{8,0},{9,1},... | collective-permute-start | bytes 196616 | tf_op jit(solution)/shard_map/ppermute | solution.py:421
  20.3 11.9 %collective-permute-start.5 = (bf16[2,8,16,128]{3,2,1,0:T(8,128)(2,1)S(1)}, bf16[2,8,16,128]{3,2,1,0:T(8,128)(2,1)S(1)}, u32[]{:S(2)}, u32[]{:S(2)}) collective-permute-start(bf16[2,8,16,128]{3,2,1,0:T(8,128)(2,1)S(1)} %get-tuple-element.36), channel_id=1, source_target_pairs={{0,9},{1,8},{2,11},{3,10},{4,13},{5,12},{6,15},{7,14},{8,1},{9,0},... | collective-permute-start | bytes 196616 | tf_op jit(solution)/shard_map/ppermute | solution.py:421
  23.3 11.5 %collective-permute-start.6 = (bf16[2,8,16,128]{3,2,1,0:T(8,128)(2,1)S(1)}, bf16[2,8,16,128]{3,2,1,0:T(8,128)(2,1)S(1)}, u32[]{:S(2)}, u32[]{:S(2)}) collective-permute-start(bf16[2,8,16,128]{3,2,1,0:T(8,128)(2,1)S(1)} %get-tuple-element.37), channel_id=1, source_target_pairs={{0,12},{1,13},{2,14},{3,15},{4,8},{5,9},{6,10},{7,11},{8,4},{9,5},... | collective-permute-start | bytes 196616 | tf_op jit(solution)/shard_map/ppermute | solution.py:421
  25.3 12.5 %collective-permute-start.7 = (bf16[2,8,16,128]{3,2,1,0:T(8,128)(2,1)S(1)}, bf16[2,8,16,128]{3,2,1,0:T(8,128)(2,1)S(1)}, u32[]{:S(2)}, u32[]{:S(2)}) collective-permute-start(bf16[2,8,16,128]{3,2,1,0:T(8,128)(2,1)S(1)} %get-tuple-element.38), channel_id=1, source_target_pairs={{0,13},{1,12},{2,15},{3,14},{4,9},{5,8},{6,11},{7,10},{8,5},{9,4},... | collective-permute-start | bytes 196616 | tf_op jit(solution)/shard_map/ppermute | solution.py:421
  37.7 6.5 %copy-start.6 = (bf16[128,4]{0,1:T(4,128)(2,1)S(1)}, bf16[128,4]{0,1:T(4,128)(2,1)}, u32[]{:S(2)}) copy-start(bf16[128,4]{0,1:T(4,128)(2,1)} %param.16) | copy-start | bytes 3076
  37.7 6.6 %copy-start.1 = (bf16[16,128,128]{2,1,0:T(8,128)(2,1)S(1)}, bf16[16,128,128]{2,1,0:T(8,128)(2,1)}, u32[]{:S(2)}) copy-start(bf16[16,128,128]{2,1,0:T(8,128)(2,1)} %pair.1) | copy-start | bytes 1572868
  37.7 6.6 %copy-start.3 = (bf16[128,128]{1,0:T(8,128)(2,1)S(1)}, bf16[128,128]{1,0:T(8,128)(2,1)}, u32[]{:S(2)}) copy-start(bf16[128,128]{1,0:T(8,128)(2,1)} %weights.1) | copy-start | bytes 98308
  37.8 6.6 %copy-start.5 = (bf16[16,128,128]{2,1,0:T(8,128)(2,1)S(1)}, bf16[16,128,128]{2,1,0:T(8,128)(2,1)}, u32[]{:S(2)}) copy-start(bf16[16,128,128]{2,1,0:T(8,128)(2,1)} %get-tuple-element.28.source_hbm.normed) | copy-start | bytes 1572868
  39.1 12.3 %all-to-all-start.1 = ((bf16[16,8,16,128]{3,2,1,0:T(8,128)(2,1)}), bf16[16,8,16,128]{3,2,1,0:T(8,128)(2,1)S(1)}, u32[]{:S(2)}, u32[]{:S(2)}) async-start(bf16[16,8,16,128]{3,2,1,0:T(8,128)(2,1)} %bitcast.5), calls=%async_computation.1 | async-start | bytes 1048576 | tf_op jit(solution)/shard_map/all_to_all | solution.py:390
  44.4 7.0 %copy-start.4 = (bf16[128,128]{1,0:T(8,128)(2,1)S(1)}, bf16[128,128]{1,0:T(8,128)(2,1)}, u32[]{:S(2)}) copy-start(bf16[128,128]{1,0:T(8,128)(2,1)} %tri_out.1) | copy-start | bytes 98308
  51.4 12.0 %copy-start.2 = (bf16[128,512]{1,0:T(8,128)(2,1)S(1)}, bf16[128,512]{1,0:T(8,128)(2,1)}, u32[]{:S(2)}) copy-start(bf16[128,512]{1,0:T(8,128)(2,1)} %attn_proj.3) | copy-start | bytes 393220
  52.9 16.5 %collective-permute-start.9 = (bf16[16,128,128]{2,1,0:T(8,128)(2,1)S(1)}, bf16[16,128,128]{2,1,0:T(8,128)(2,1)S(1)}, u32[]{:S(2)}, u32[]{:S(2)}) collective-permute-start(bf16[16,128,128]{2,1,0:T(8,128)(2,1)S(1)} %get-tuple-element.42.updated), channel_id=1, source_target_pairs={{1,0},{0,1},{3,2},{2,3},{5,4},{4,5},{7,6},{6,7},{9,8},{8,9},{11,10... | collective-permute-start | bytes 1572872 | tf_op jit(solution)/shard_map/ppermute | solution.py:467
  54.7 4.7 %collective-permute-start.8 = (bf16[4,16,128]{2,1,0:T(8,128)(2,1)S(1)}, bf16[4,16,128]{2,1,0:T(8,128)(2,1)S(1)}, u32[]{:S(2)}, u32[]{:S(2)}) collective-permute-start(bf16[4,16,128]{2,1,0:T(8,128)(2,1)S(1)} %get-tuple-element.41.refs_0_), channel_id=1, source_target_pairs={{0,16},{1,17},{2,18},{3,19},{4,20},{5,21},{6,22},{7,23},{8,24},{9,... | collective-permute-start | bytes 49160 | tf_op jit(solution)/shard_map/ppermute | solution.py:421
  60.0 9.4 %all-to-all-start.2 = ((bf16[8,4,16,128]{3,2,1,0:T(8,128)(2,1)}), bf16[8,4,16,128]{3,2,1,0:T(8,128)(2,1)S(1)}, u32[]{:S(2)}, u32[]{:S(2)}) async-start(bf16[8,4,16,128]{3,2,1,0:T(8,128)(2,1)} %deal_bias.1), calls=%async_computation.2 | async-start | bytes 262144 | tf_op jit(solution)/shard_map/all_to_all | solution.py:470
  69.4 1.3 %collective-permute-start.10 = (bf16[8,4,16,128]{3,2,1,0:T(8,128)(2,1)S(1)}, bf16[8,4,16,128]{3,2,1,0:T(8,128)(2,1)S(1)}, u32[]{:S(2)}, u32[]{:S(2)}) collective-permute-start(bf16[8,4,16,128]{3,2,1,0:T(8,128)(2,1)S(1)} %all-to-all-done.2.mine), channel_id=1, source_target_pairs={{0,2},{1,3},{2,0},{3,1},{4,6},{5,7},{6,4},{7,5},{8,10},{9,11},{10,... | collective-permute-start | bytes 393224 | tf_op jit(solution)/shard_map/ppermute | solution.py:421
  69.4 1.3 %copy-start = (bf16[128,128]{1,0:T(8,128)(2,1)S(1)}, bf16[128,128]{1,0:T(8,128)(2,1)}, u32[]{:S(2)}) copy-start(bf16[128,128]{1,0:T(8,128)(2,1)} %attn_out.1) | copy-start | bytes 98308

commit v4 on v3

--- a/solution.py
+++ b/solution.py
@@ -334,37 +334,47 @@
         return keys, values, mixed[0][row, :, 2 * channels :]
 
     def finish(row, total):
-        attended = total[:, :channels] / total[:, channels:]
+        weight = total[:, channels:]
+        inverse = pl.reciprocal(weight, approx=True)
+        attended = total[:, :channels] * (inverse * (2.0 - weight * inverse))
         gate = late[row, :, :channels].astype(F32)
         gated = (attended * gate).astype(BF16)
         residual = late[row, :, channels:].astype(F32)
         out[row] = (residual + dot(gated, attn_out[...], (1, 0))).astype(BF16)
 
     per_chunk = rows // count
-    loaded, logits, weights = {}, {}, {}
-    for time in range(rows + 2):
-        row = time
-        if row < rows:
-            loaded[row] = load(row)
+    loaded, logits, weights, total = {}, {}, {}, None
+    group = 2
+    per_row = heads // group
+    units = rows * per_row
+    for time in range(units + 2):
+        if time < units:
+            row, first = divmod(time, per_row)
+            if first == 0:
+                loaded[row] = load(row)
             keys, _, query = loaded[row]
-            queries = jnp.concatenate([query * mask for mask in masks], axis=0)
-            logits[row] = dot(queries, keys, (1, 0)) + bias_held[...]
-        row = time - 1
-        if 0 <= row < rows:
-            scores = logits.pop(row)
+            mine = masks[first * group : (first + 1) * group]
+            queries = jnp.concatenate([query * mask for mask in mine], axis=0)
+            span = slice(first * group * cols, (first + 1) * group * cols)
+            logits[time] = dot(queries, keys, (1, 0)) + bias_held[span]
+        if 0 <= time - 1 < units:
+            scores = logits.pop(time - 1)
             top = jnp.max(scores, axis=-1, keepdims=True)
-            weights[row] = jnp.exp((scores - top).astype(BF16))
-        row = time - 2
-        if row >= 0:
-            sums = dot(weights.pop(row), loaded.pop(row)[1], (1, 0))
-            total = sums[:cols]
-            for head in range(1, heads):
-                total = jnp.where(both_of == head, sums[head * cols : (head + 1) * cols], total)
-            finish(row, total)
-            chunk, place_in = divmod(row, per_chunk)
-            if place_in == per_chunk - 1:
-                for copy in sends[chunk]:
-                    copy.start()
+            weights[time - 1] = jnp.exp((scores - top).astype(BF16))
+        if time >= 2:
+            row, first = divmod(time - 2, per_row)
+            sums = dot(weights.pop(time - 2), loaded[row][1], (1, 0))
+            for k in range(group):
+                head = first * group + k
+                mine = sums[k * cols : (k + 1) * cols]
+                total = mine if head == 0 else jnp.where(both_of == head, mine, total)
+            if first == per_row - 1:
+                finish(row, total)
+                loaded.pop(row)
+                chunk, place_in = divmod(row, per_chunk)
+                if place_in == per_chunk - 1:
+                    for copy in sends[chunk]:
+                        copy.start()
     for send in sends:
         for copy in send:
             copy.wait()

time: 75.9 us -> 76.2 us (level)
  no operation moved by 1% of the time
where the time goes in v4:
time: 76.2 us; the launch traced here: 75.7 us
  starting transfers between devices  28.9 us (38%)
  waiting for transfers between devices  27.2 us (36%)
  Pallas kernels  18.6 us (24%)
  between operations  0.79 us (1%)
    ppermute x10, waiting for transfers between devices, flipped(): return lax.ppermute(array, BOTH, [(d, d ^ bits) for d in range(devices)])  17.7 us
    ppermute x10, starting transfers between devices, flipped(): return lax.ppermute(array, BOTH, [(d, d ^ bits) for d in range(devices)])  11.4 us
    all_to_all x1, starting transfers between devices, local(): right = lax.all_to_all(right, BOTH, split_axis=0, concat_axis=0, tiled=True)  7.3 us
    all_to_all x1, waiting for transfers between devices, in_half(): lax.all_to_all(array, BOTH, split_axis=0, concat_axis=0, axis_index_group...  5.43 us
    pallas_call x2, Pallas kernels, edges(): call(functools.partial(edges_body, side=side), 'right_edges' if side else...  5.33 us
    all_to_all x1, starting transfers between devices, in_half(): lax.all_to_all(array, BOTH, split_axis=0, concat_axis=0, axis_index_group...  5.12 us
    pallas_call x1, Pallas kernels, local(): call(attend_body, 'attend', [shape(block, BF16)], 5 + col_devices, [pltpu...  4.94 us
    all_to_all x1, waiting for transfers between devices, local(): lax.all_to_all(dealt, BOTH, split_axis=0, concat_axis=0, axis_index_group...  4.06 us
  transfers between devices with their start and end apart: 14, of which 11 were waited for; matrix products, arithmetic and copies ran while one was open for 0% of the time, Pallas kernels for 10%

profile of v4, /device:TPU:0, one launch (start us, length us, event | category | flops | bytes accessed | tf_op | source)
XLA Modules:
  0.0 75.7 jit_solution(4423258054462065862)
XLA Ops:
  0.7 3.3 %right_edges.1 = (bf16[32,8,16,128]{3,2,1,0:T(8,128)(2,1)}, bf16[16,128,128]{2,1,0:T(8,128)(2,1)}) custom-call(s32[1]{0:T(128)S(6)} %copy.11.length, bf16[16,128,128]{2,1,0:T(8,128)(2,1)} %pair.1, bf16[128,256]{1,0:T(8,128)(2,1)} %proj_hbm.3, bf16[128,256]{1,0:T(8,128)(2,1)} %gate_hbm.3), custom_call_target="tpu_custom_call" | custom-call | flops 3000000000 | bytes 3145728 | tf_op jit(solution)/shard_map/right_edges/pallas_call | solution.py:411
  4.0 7.3 %all-to-all-start = ((bf16[32,8,16,128]{3,2,1,0:T(8,128)(2,1)}), bf16[32,8,16,128]{3,2,1,0:T(8,128)(2,1)S(1)}, u32[]{:S(2)}, u32[]{:S(2)}) async-start(bf16[32,8,16,128]{3,2,1,0:T(8,128)(2,1)} %get-tuple-element.27), calls=%async_computation | async-start | bytes 2097152 | tf_op jit(solution)/shard_map/all_to_all | solution.py:434
  11.3 2.0 %left_edges.1 = (bf16[8,8,16,128]{3,2,1,0:T(8,128)(2,1)S(1)}, bf16[8,8,16,128]{3,2,1,0:T(8,128)(2,1)S(1)}) custom-call(s32[1]{0:T(128)S(6)} %copy.11.length, bf16[16,128,128]{2,1,0:T(8,128)(2,1)} %get-tuple-element.28.source_hbm.normed, bf16[128,256]{1,0:T(8,128)(2,1)} %proj_hbm.3, bf16[128,256]{1,0:T(8,128)(2,1)} %gate_hbm.3), custom_call_target="tpu_custom_call" | custom-call | flops 3000000000 | bytes 1048576 | tf_op jit(solution)/shard_map/left_edges/pallas_call | solution.py:411
  15.0 1.8 %collective-permute-start.1 = (bf16[2,8,16,128]{3,2,1,0:T(8,128)(2,1)S(1)}, bf16[2,8,16,128]{3,2,1,0:T(8,128)(2,1)S(1)}, u32[]{:S(2)}, u32[]{:S(2)}) collective-permute-start(bf16[2,8,16,128]{3,2,1,0:T(8,128)(2,1)S(1)} %get-tuple-element.32), channel_id=1, source_target_pairs={{0,1},{1,0},{2,3},{3,2},{4,5},{5,4},{6,7},{7,6},{8,9},{9,8},{10,11... | collective-permute-start | bytes 196616 | tf_op jit(solution)/shard_map/ppermute | solution.py:431
  16.8 1.5 %collective-permute-start.2 = (bf16[2,8,16,128]{3,2,1,0:T(8,128)(2,1)S(1)}, bf16[2,8,16,128]{3,2,1,0:T(8,128)(2,1)S(1)}, u32[]{:S(2)}, u32[]{:S(2)}) collective-permute-start(bf16[2,8,16,128]{3,2,1,0:T(8,128)(2,1)S(1)} %get-tuple-element.33), channel_id=1, source_target_pairs={{0,4},{1,5},{2,6},{3,7},{4,0},{5,1},{6,2},{7,3},{8,12},{9,13},{10,... | collective-permute-start | bytes 196616 | tf_op jit(solution)/shard_map/ppermute | solution.py:431
  18.5 1.8 %collective-permute-start.4 = (bf16[2,8,16,128]{3,2,1,0:T(8,128)(2,1)S(1)}, bf16[2,8,16,128]{3,2,1,0:T(8,128)(2,1)S(1)}, u32[]{:S(2)}, u32[]{:S(2)}) collective-permute-start(bf16[2,8,16,128]{3,2,1,0:T(8,128)(2,1)S(1)} %get-tuple-element.35), channel_id=1, source_target_pairs={{0,8},{1,9},{2,10},{3,11},{4,12},{5,13},{6,14},{7,15},{8,0},{9,1},... | collective-permute-start | bytes 196616 | tf_op jit(solution)/shard_map/ppermute | solution.py:431
  20.3 1.5 %collective-permute-start.5 = (bf16[2,8,16,128]{3,2,1,0:T(8,128)(2,1)S(1)}, bf16[2,8,16,128]{3,2,1,0:T(8,128)(2,1)S(1)}, u32[]{:S(2)}, u32[]{:S(2)}) collective-permute-start(bf16[2,8,16,128]{3,2,1,0:T(8,128)(2,1)S(1)} %get-tuple-element.36), channel_id=1, source_target_pairs={{0,9},{1,8},{2,11},{3,10},{4,13},{5,12},{6,15},{7,14},{8,1},{9,0},... | collective-permute-start | bytes 196616 | tf_op jit(solution)/shard_map/ppermute | solution.py:431
  21.7 1.6 %collective-permute-done.1.rest_1_ = bf16[2,8,16,128]{3,2,1,0:T(8,128)(2,1)S(1)} collective-permute-done((bf16[2,8,16,128]{3,2,1,0:T(8,128)(2,1)S(1)}, bf16[2,8,16,128]{3,2,1,0:T(8,128)(2,1)S(1)}, u32[]{:S(2)}, u32[]{:S(2)}) %collective-permute-start.1) | collective-permute-done | bytes 65568 | tf_op jit(solution)/shard_map/ppermute | solution.py:431
  25.8 4.9 %collective-permute-done.4.rest_4_ = bf16[2,8,16,128]{3,2,1,0:T(8,128)(2,1)S(1)} collective-permute-done((bf16[2,8,16,128]{3,2,1,0:T(8,128)(2,1)S(1)}, bf16[2,8,16,128]{3,2,1,0:T(8,128)(2,1)S(1)}, u32[]{:S(2)}, u32[]{:S(2)}) %collective-permute-start.4) | collective-permute-done | bytes 65568 | tf_op jit(solution)/shard_map/ppermute | solution.py:431
  30.7 1.5 %collective-permute-done.5.rest_5_ = bf16[2,8,16,128]{3,2,1,0:T(8,128)(2,1)S(1)} collective-permute-done((bf16[2,8,16,128]{3,2,1,0:T(8,128)(2,1)S(1)}, bf16[2,8,16,128]{3,2,1,0:T(8,128)(2,1)S(1)}, u32[]{:S(2)}, u32[]{:S(2)}) %collective-permute-start.5) | collective-permute-done | bytes 65568 | tf_op jit(solution)/shard_map/ppermute | solution.py:431
  32.2 2.7 %collective-permute-done.6.rest_6_ = bf16[2,8,16,128]{3,2,1,0:T(8,128)(2,1)S(1)} collective-permute-done((bf16[2,8,16,128]{3,2,1,0:T(8,128)(2,1)S(1)}, bf16[2,8,16,128]{3,2,1,0:T(8,128)(2,1)S(1)}, u32[]{:S(2)}, u32[]{:S(2)}) %collective-permute-start.6) | collective-permute-done | bytes 65568 | tf_op jit(solution)/shard_map/ppermute | solution.py:431
  34.9 2.9 %collective-permute-done.7.rest_7_ = bf16[2,8,16,128]{3,2,1,0:T(8,128)(2,1)S(1)} collective-permute-done((bf16[2,8,16,128]{3,2,1,0:T(8,128)(2,1)S(1)}, bf16[2,8,16,128]{3,2,1,0:T(8,128)(2,1)S(1)}, u32[]{:S(2)}, u32[]{:S(2)}) %collective-permute-start.7) | collective-permute-done | bytes 65568 | tf_op jit(solution)/shard_map/ppermute | solution.py:431
  37.8 1.3 %triangle.1 = bf16[8,2,8,16,128]{4,3,2,1,0:T(8,128)(2,1)} custom-call(bf16[16,2,8,16,128]{4,3,2,1,0:T(8,128)(2,1)S(1)} %bitcast.3, bf16[2,8,16,128]{3,2,1,0:T(8,128)(2,1)S(1)} %get-tuple-element.31.rest_0_, bf16[2,8,16,128]{3,2,1,0:T(8,128)(2,1)S(1)} %collective-permute-done.1.rest_1_, bf16[2,8,16,128]{3,2,1,0:T(8,128)(2,1)S(1)} %collective-permute-done.2.rest_2_, ...), custom_call_target="tpu_custom_call" | custom-call | flops 2000000000 | bytes 1048576 | tf_op jit(solution)/shard_map/triangle/pallas_call | solution.py:444
  39.1 5.1 %all-to-all-start.1 = ((bf16[16,8,16,128]{3,2,1,0:T(8,128)(2,1)}), bf16[16,8,16,128]{3,2,1,0:T(8,128)(2,1)S(1)}, u32[]{:S(2)}, u32[]{:S(2)}) async-start(bf16[16,8,16,128]{3,2,1,0:T(8,128)(2,1)} %bitcast.5), calls=%async_computation.1 | async-start | bytes 1048576 | tf_op jit(solution)/shard_map/all_to_all | solution.py:400
  44.4 1.6 %tri_gate.1 = (bf16[16,128,128]{2,1,0:T(8,128)(2,1)S(1)}, bf16[16,128,128]{2,1,0:T(8,128)(2,1)S(1)}) custom-call(bf16[16,128,128]{2,1,0:T(8,128)(2,1)S(1)} %copy-done.1, bf16[16,128,128]{2,1,0:T(8,128)(2,1)S(1)} %copy-done.5, bf16[128,128]{1,0:T(8,128)(2,1)S(1)} %copy-done.3), custom_call_target="tpu_custom_call" | custom-call | flops 2000000000 | bytes 2097152 | tf_op jit(solution)/shard_map/tri_gate/pallas_call | solution.py:440
  46.0 5.4 %all-to-all-done.1 = bf16[16,8,16,128]{3,2,1,0:T(8,128)(2,1)S(1)} async-done(((bf16[16,8,16,128]{3,2,1,0:T(8,128)(2,1)}), bf16[16,8,16,128]{3,2,1,0:T(8,128)(2,1)S(1)}, u32[]{:S(2)}, u32[]{:S(2)}) %all-to-all-start.1) | async-done | bytes 524320 | tf_op jit(solution)/shard_map/all_to_all | solution.py:400
  51.4 1.5 %update.1 = (bf16[16,128,128]{2,1,0:T(8,128)(2,1)S(1)}, bf16[4,16,128]{2,1,0:T(8,128)(2,1)S(1)}) custom-call(bf16[128,16,128]{2,1,0:T(8,128)(2,1)S(1)} %bitcast.4, bf16[16,128,128]{2,1,0:T(8,128)(2,1)S(1)} %get-tuple-element.39.source, bf16[16,128,128]{2,1,0:T(8,128)(2,1)S(1)} %get-tuple-element.40.gate, bf16[128,128]{1,0:T(8,128)(2,1)S(1)} %copy-done.4, ...), custom_call_target="tpu_custom_call" | custom-call | flops 2000000000 | bytes 1081344 | tf_op jit(solution)/shard_map/update/pallas_call | solution.py:455
  52.9 1.7 %collective-permute-start.9 = (bf16[16,128,128]{2,1,0:T(8,128)(2,1)S(1)}, bf16[16,128,128]{2,1,0:T(8,128)(2,1)S(1)}, u32[]{:S(2)}, u32[]{:S(2)}) collective-permute-start(bf16[16,128,128]{2,1,0:T(8,128)(2,1)S(1)} %get-tuple-element.42.updated), channel_id=1, source_target_pairs={{1,0},{0,1},{3,2},{2,3},{5,4},{4,5},{7,6},{6,7},{9,8},{8,9},{11,10... | collective-permute-start | bytes 1572872 | tf_op jit(solution)/shard_map/ppermute | solution.py:477
  54.7 3.0 %collective-permute-start.8 = (bf16[4,16,128]{2,1,0:T(8,128)(2,1)S(1)}, bf16[4,16,128]{2,1,0:T(8,128)(2,1)S(1)}, u32[]{:S(2)}, u32[]{:S(2)}) collective-permute-start(bf16[4,16,128]{2,1,0:T(8,128)(2,1)S(1)} %get-tuple-element.41.refs_0_), channel_id=1, source_target_pairs={{0,16},{1,17},{2,18},{3,19},{4,20},{5,21},{6,22},{7,23},{8,24},{9,... | collective-permute-start | bytes 49160 | tf_op jit(solution)/shard_map/ppermute | solution.py:431
  57.6 1.7 %collective-permute-done.8.refs_1_ = bf16[4,16,128]{2,1,0:T(8,128)(2,1)S(1)} collective-permute-done((bf16[4,16,128]{2,1,0:T(8,128)(2,1)S(1)}, bf16[4,16,128]{2,1,0:T(8,128)(2,1)S(1)}, u32[]{:S(2)}, u32[]{:S(2)}) %collective-permute-start.8) | collective-permute-done | bytes 16416 | tf_op jit(solution)/shard_map/ppermute | solution.py:431
  60.0 3.4 %all-to-all-start.2 = ((bf16[8,4,16,128]{3,2,1,0:T(8,128)(2,1)}), bf16[8,4,16,128]{3,2,1,0:T(8,128)(2,1)S(1)}, u32[]{:S(2)}, u32[]{:S(2)}) async-start(bf16[8,4,16,128]{3,2,1,0:T(8,128)(2,1)} %deal_bias.1), calls=%async_computation.2 | async-start | bytes 262144 | tf_op jit(solution)/shard_map/all_to_all | solution.py:480
  63.4 1.9 %own_projections.1 = (bf16[16,128,384]{2,1,0:T(8,128)(2,1)S(1)}, bf16[16,128,256]{2,1,0:T(8,128)(2,1)}) custom-call(bf16[16,128,128]{2,1,0:T(8,128)(2,1)S(1)} %get-tuple-element.42.updated, bf16[128,512]{1,0:T(8,128)(2,1)S(1)} %copy-done.2), custom_call_target="tpu_custom_call" | custom-call | flops 3000000000 | bytes 5242880 | tf_op jit(solution)/shard_map/own_projections/pallas_call | solution.py:486
  65.4 4.1 %all-to-all-done.2.mine = bf16[8,4,16,128]{3,2,1,0:T(8,128)(2,1)S(1)} async-done(((bf16[8,4,16,128]{3,2,1,0:T(8,128)(2,1)}), bf16[8,4,16,128]{3,2,1,0:T(8,128)(2,1)S(1)}, u32[]{:S(2)}, u32[]{:S(2)}) %all-to-all-start.2) | async-done | bytes 131104 | tf_op jit(solution)/shard_map/all_to_all | solution.py:480
  70.8 4.9 %attend.1 = bf16[16,128,128]{2,1,0:T(8,128)(2,1)} custom-call(s32[1]{0:T(128)S(6)} %copy.11.length, bf16[8,4,16,128]{3,2,1,0:T(8,128)(2,1)S(1)} %all-to-all-done.2.mine, bf16[8,4,16,128]{3,2,1,0:T(8,128)(2,1)S(1)} %collective-permute-done.10.sibling, bf16[128,128]{1,0:T(8,128)(2,1)S(1)} %copy-done, bf16[16,128,256]{2,1,0:T(8,128)(2,1)S(1)} %get-tuple-element.46.late, ...), custom_call_target="tpu_custom_call" | custom-call | flops 100000000 | bytes 1048576 | tf_op jit(solution)/shard_map/attend/pallas_call | solution.py:505
  (29 shorter events, 6.6 us)
Async XLA Ops:
  4.0 33.7 %all-to-all-start = ((bf16[32,8,16,128]{3,2,1,0:T(8,128)(2,1)}), bf16[32,8,16,128]{3,2,1,0:T(8,128)(2,1)S(1)}, u32[]{:S(2)}, u32[]{:S(2)}) async-start(bf16[32,8,16,128]{3,2,1,0:T(8,128)(2,1)} %get-tuple-element.27), calls=%async_computation | async-start | bytes 2097152 | tf_op jit(solution)/shard_map/all_to_all | solution.py:434
  13.3 1.6 %collective-permute-start = (bf16[8,8,16,128]{3,2,1,0:T(8,128)(2,1)S(1)}, bf16[8,8,16,128]{3,2,1,0:T(8,128)(2,1)S(1)}, u32[]{:S(2)}, u32[]{:S(2)}) collective-permute-start(bf16[8,8,16,128]{3,2,1,0:T(8,128)(2,1)S(1)} %get-tuple-element.30), channel_id=1, source_target_pairs={{0,2},{1,3},{2,0},{3,1},{4,6},{5,7},{6,4},{7,5},{8,10},{9,11},{10,... | collective-permute-start | bytes 786440 | tf_op jit(solution)/shard_map/ppermute | solution.py:431
  15.0 8.4 %collective-permute-start.1 = (bf16[2,8,16,128]{3,2,1,0:T(8,128)(2,1)S(1)}, bf16[2,8,16,128]{3,2,1,0:T(8,128)(2,1)S(1)}, u32[]{:S(2)}, u32[]{:S(2)}) collective-permute-start(bf16[2,8,16,128]{3,2,1,0:T(8,128)(2,1)S(1)} %get-tuple-element.32), channel_id=1, source_target_pairs={{0,1},{1,0},{2,3},{3,2},{4,5},{5,4},{6,7},{7,6},{8,9},{9,8},{10,11... | collective-permute-start | bytes 196616 | tf_op jit(solution)/shard_map/ppermute | solution.py:431
  16.8 8.5 %collective-permute-start.2 = (bf16[2,8,16,128]{3,2,1,0:T(8,128)(2,1)S(1)}, bf16[2,8,16,128]{3,2,1,0:T(8,128)(2,1)S(1)}, u32[]{:S(2)}, u32[]{:S(2)}) collective-permute-start(bf16[2,8,16,128]{3,2,1,0:T(8,128)(2,1)S(1)} %get-tuple-element.33), channel_id=1, source_target_pairs={{0,4},{1,5},{2,6},{3,7},{4,0},{5,1},{6,2},{7,3},{8,12},{9,13},{10,... | collective-permute-start | bytes 196616 | tf_op jit(solution)/shard_map/ppermute | solution.py:431
  18.3 7.6 %collective-permute-start.3 = (bf16[2,8,16,128]{3,2,1,0:T(8,128)(2,1)S(1)}, bf16[2,8,16,128]{3,2,1,0:T(8,128)(2,1)S(1)}, u32[]{:S(2)}, u32[]{:S(2)}) collective-permute-start(bf16[2,8,16,128]{3,2,1,0:T(8,128)(2,1)S(1)} %get-tuple-element.34), channel_id=1, source_target_pairs={{0,5},{1,4},{2,7},{3,6},{4,1},{5,0},{6,3},{7,2},{8,13},{9,12},{10,... | collective-permute-start | bytes 196616 | tf_op jit(solution)/shard_map/ppermute | solution.py:431
  18.5 12.2 %collective-permute-start.4 = (bf16[2,8,16,128]{3,2,1,0:T(8,128)(2,1)S(1)}, bf16[2,8,16,128]{3,2,1,0:T(8,128)(2,1)S(1)}, u32[]{:S(2)}, u32[]{:S(2)}) collective-permute-start(bf16[2,8,16,128]{3,2,1,0:T(8,128)(2,1)S(1)} %get-tuple-element.35), channel_id=1, source_target_pairs={{0,8},{1,9},{2,10},{3,11},{4,12},{5,13},{6,14},{7,15},{8,0},{9,1},... | collective-permute-start | bytes 196616 | tf_op jit(solution)/shard_map/ppermute | solution.py:431
  20.3 11.9 %collective-permute-start.5 = (bf16[2,8,16,128]{3,2,1,0:T(8,128)(2,1)S(1)}, bf16[2,8,16,128]{3,2,1,0:T(8,128)(2,1)S(1)}, u32[]{:S(2)}, u32[]{:S(2)}) collective-permute-start(bf16[2,8,16,128]{3,2,1,0:T(8,128)(2,1)S(1)} %get-tuple-element.36), channel_id=1, source_target_pairs={{0,9},{1,8},{2,11},{3,10},{4,13},{5,12},{6,15},{7,14},{8,1},{9,0},... | collective-permute-start | bytes 196616 | tf_op jit(solution)/shard_map/ppermute | solution.py:431
  23.3 11.5 %collective-permute-start.6 = (bf16[2,8,16,128]{3,2,1,0:T(8,128)(2,1)S(1)}, bf16[2,8,16,128]{3,2,1,0:T(8,128)(2,1)S(1)}, u32[]{:S(2)}, u32[]{:S(2)}) collective-permute-start(bf16[2,8,16,128]{3,2,1,0:T(8,128)(2,1)S(1)} %get-tuple-element.37), channel_id=1, source_target_pairs={{0,12},{1,13},{2,14},{3,15},{4,8},{5,9},{6,10},{7,11},{8,4},{9,5},... | collective-permute-start | bytes 196616 | tf_op jit(solution)/shard_map/ppermute | solution.py:431
  25.3 12.5 %collective-permute-start.7 = (bf16[2,8,16,128]{3,2,1,0:T(8,128)(2,1)S(1)}, bf16[2,8,16,128]{3,2,1,0:T(8,128)(2,1)S(1)}, u32[]{:S(2)}, u32[]{:S(2)}) collective-permute-start(bf16[2,8,16,128]{3,2,1,0:T(8,128)(2,1)S(1)} %get-tuple-element.38), channel_id=1, source_target_pairs={{0,13},{1,12},{2,15},{3,14},{4,9},{5,8},{6,11},{7,10},{8,5},{9,4},... | collective-permute-start | bytes 196616 | tf_op jit(solution)/shard_map/ppermute | solution.py:431
  37.7 6.5 %copy-start.6 = (bf16[128,4]{0,1:T(4,128)(2,1)S(1)}, bf16[128,4]{0,1:T(4,128)(2,1)}, u32[]{:S(2)}) copy-start(bf16[128,4]{0,1:T(4,128)(2,1)} %param.16) | copy-start | bytes 3076
  37.7 6.6 %copy-start.1 = (bf16[16,128,128]{2,1,0:T(8,128)(2,1)S(1)}, bf16[16,128,128]{2,1,0:T(8,128)(2,1)}, u32[]{:S(2)}) copy-start(bf16[16,128,128]{2,1,0:T(8,128)(2,1)} %pair.1) | copy-start | bytes 1572868
  37.7 6.6 %copy-start.3 = (bf16[128,128]{1,0:T(8,128)(2,1)S(1)}, bf16[128,128]{1,0:T(8,128)(2,1)}, u32[]{:S(2)}) copy-start(bf16[128,128]{1,0:T(8,128)(2,1)} %weights.1) | copy-start | bytes 98308
  37.8 6.6 %copy-start.5 = (bf16[16,128,128]{2,1,0:T(8,128)(2,1)S(1)}, bf16[16,128,128]{2,1,0:T(8,128)(2,1)}, u32[]{:S(2)}) copy-start(bf16[16,128,128]{2,1,0:T(8,128)(2,1)} %get-tuple-element.28.source_hbm.normed) | copy-start | bytes 1572868
  39.1 12.3 %all-to-all-start.1 = ((bf16[16,8,16,128]{3,2,1,0:T(8,128)(2,1)}), bf16[16,8,16,128]{3,2,1,0:T(8,128)(2,1)S(1)}, u32[]{:S(2)}, u32[]{:S(2)}) async-start(bf16[16,8,16,128]{3,2,1,0:T(8,128)(2,1)} %bitcast.5), calls=%async_computation.1 | async-start | bytes 1048576 | tf_op jit(solution)/shard_map/all_to_all | solution.py:400
  44.4 7.0 %copy-start.4 = (bf16[128,128]{1,0:T(8,128)(2,1)S(1)}, bf16[128,128]{1,0:T(8,128)(2,1)}, u32[]{:S(2)}) copy-start(bf16[128,128]{1,0:T(8,128)(2,1)} %tri_out.1) | copy-start | bytes 98308
  51.4 12.0 %copy-start.2 = (bf16[128,512]{1,0:T(8,128)(2,1)S(1)}, bf16[128,512]{1,0:T(8,128)(2,1)}, u32[]{:S(2)}) copy-start(bf16[128,512]{1,0:T(8,128)(2,1)} %attn_proj.3) | copy-start | bytes 393220
  52.9 16.5 %collective-permute-start.9 = (bf16[16,128,128]{2,1,0:T(8,128)(2,1)S(1)}, bf16[16,128,128]{2,1,0:T(8,128)(2,1)S(1)}, u32[]{:S(2)}, u32[]{:S(2)}) collective-permute-start(bf16[16,128,128]{2,1,0:T(8,128)(2,1)S(1)} %get-tuple-element.42.updated), channel_id=1, source_target_pairs={{1,0},{0,1},{3,2},{2,3},{5,4},{4,5},{7,6},{6,7},{9,8},{8,9},{11,10... | collective-permute-start | bytes 1572872 | tf_op jit(solution)/shard_map/ppermute | solution.py:477
  54.7 4.7 %collective-permute-start.8 = (bf16[4,16,128]{2,1,0:T(8,128)(2,1)S(1)}, bf16[4,16,128]{2,1,0:T(8,128)(2,1)S(1)}, u32[]{:S(2)}, u32[]{:S(2)}) collective-permute-start(bf16[4,16,128]{2,1,0:T(8,128)(2,1)S(1)} %get-tuple-element.41.refs_0_), channel_id=1, source_target_pairs={{0,16},{1,17},{2,18},{3,19},{4,20},{5,21},{6,22},{7,23},{8,24},{9,... | collective-permute-start | bytes 49160 | tf_op jit(solution)/shard_map/ppermute | solution.py:431
  60.0 9.4 %all-to-all-start.2 = ((bf16[8,4,16,128]{3,2,1,0:T(8,128)(2,1)}), bf16[8,4,16,128]{3,2,1,0:T(8,128)(2,1)S(1)}, u32[]{:S(2)}, u32[]{:S(2)}) async-start(bf16[8,4,16,128]{3,2,1,0:T(8,128)(2,1)} %deal_bias.1), calls=%async_computation.2 | async-start | bytes 262144 | tf_op jit(solution)/shard_map/all_to_all | solution.py:480
  69.4 1.3 %collective-permute-start.10 = (bf16[8,4,16,128]{3,2,1,0:T(8,128)(2,1)S(1)}, bf16[8,4,16,128]{3,2,1,0:T(8,128)(2,1)S(1)}, u32[]{:S(2)}, u32[]{:S(2)}) collective-permute-start(bf16[8,4,16,128]{3,2,1,0:T(8,128)(2,1)S(1)} %all-to-all-done.2.mine), channel_id=1, source_target_pairs={{0,2},{1,3},{2,0},{3,1},{4,6},{5,7},{6,4},{7,5},{8,10},{9,11},{10,... | collective-permute-start | bytes 393224 | tf_op jit(solution)/shard_map/ppermute | solution.py:431
  69.4 1.3 %copy-start = (bf16[128,128]{1,0:T(8,128)(2,1)S(1)}, bf16[128,128]{1,0:T(8,128)(2,1)}, u32[]{:S(2)}) copy-start(bf16[128,128]{1,0:T(8,128)(2,1)} %attn_out.1) | copy-start | bytes 98308

commit v5 on v3

--- a/solution.py
+++ b/solution.py
@@ -178,7 +178,7 @@
 
 
 def triangle_body(right, *rest):
-    parts, out, held, sent = rest[:-3], rest[-3], rest[-2], rest[-1]
+    parts, held = rest[:-1], rest[-1]
     row_devices, col_devices, own, rows, cols = right.shape
     chip, _ = place()
     chip_row = lax.div(chip, col_devices)
@@ -207,7 +207,6 @@
                 held[row, col_devices - 1 - part, channel] = triangle[
                     k * rows : (k + 1) * rows, part * cols : (part + 1) * cols
                 ]
-    run([pltpu.make_async_copy(held, out, sent)])
 
 
 def deal_body(*refs):
@@ -430,14 +429,13 @@
     tri_gating, source = call(
         gate_body, "tri_gate", [shape(turned_block, BF16)] * 2, 3, flops=2e9
     )(pair_act, normed, tri_gate)
+    tri_gating, source, *left = lax.optimization_barrier((tri_gating, source, *left))
     triangle_shape = (row_devices // 2, col_devices, own, rows, cols)
     (triangle,) = call(
         triangle_body,
         "triangle",
         [shape(triangle_shape, BF16)],
         1 + len(left),
-        [pltpu.VMEM(triangle_shape, BF16), pltpu.SemaphoreType.DMA(())],
-        out_space=HBM,
         flops=2e9,
     )(right.reshape((row_devices,) + triangle_shape[1:]), *left)
     triangle = in_half(triangle.reshape(share, own, rows, cols))

time: 75.9 us -> 75.8 us (level)
    ppermute x10, waiting for transfers between devices: 17.7 us -> 15.9 us  [flipped(): return lax.ppermute(array, BOTH, [(d, d ^ bits) for d in range(devices)])]
    all_to_all x1, waiting for transfers between devices: 5.43 us -> 7.05 us  [in_half(): lax.all_to_all(array, BOTH, split_axis=0, concat_axis=0, axis_index_group...]
where the time goes in v5:
time: 75.8 us; the launch traced here: 75.4 us
  starting transfers between devices  29 us (38%)
  waiting for transfers between devices  27 us (36%)
  Pallas kernels  18.4 us (24%)
  between operations  0.78 us (1%)
    ppermute x10, waiting for transfers between devices, flipped(): return lax.ppermute(array, BOTH, [(d, d ^ bits) for d in range(devices)])  15.9 us
    ppermute x10, starting transfers between devices, flipped(): return lax.ppermute(array, BOTH, [(d, d ^ bits) for d in range(devices)])  11.5 us
    all_to_all x1, starting transfers between devices, local(): right = lax.all_to_all(right, BOTH, split_axis=0, concat_axis=0, tiled=True)  7.3 us
    all_to_all x1, waiting for transfers between devices, in_half(): lax.all_to_all(array, BOTH, split_axis=0, concat_axis=0, axis_index_group...  7.05 us
    pallas_call x2, Pallas kernels, edges(): call(functools.partial(edges_body, side=side), 'right_edges' if side else...  5.41 us
    all_to_all x1, starting transfers between devices, in_half(): lax.all_to_all(array, BOTH, split_axis=0, concat_axis=0, axis_index_group...  5.1 us
    pallas_call x1, Pallas kernels, local(): call(attend_body, 'attend', [shape(block, BF16)], 5 + col_devices, [pltpu...  4.67 us
    all_to_all x1, waiting for transfers between devices, local(): lax.all_to_all(dealt, BOTH, split_axis=0, concat_axis=0, axis_index_group...  4.06 us
  transfers between devices with their start and end apart: 14, of which 11 were waited for; matrix products, arithmetic and copies ran while one was open for 0% of the time, Pallas kernels for 10%

profile of v5, /device:TPU:0, one launch (start us, length us, event | category | flops | bytes accessed | tf_op | source)
XLA Modules:
  0.0 75.4 jit_solution(15715537336380571008)
XLA Ops:
  0.7 3.3 %right_edges.1 = (bf16[32,8,16,128]{3,2,1,0:T(8,128)(2,1)}, bf16[16,128,128]{2,1,0:T(8,128)(2,1)}) custom-call(s32[1]{0:T(128)S(6)} %copy.11.length, bf16[16,128,128]{2,1,0:T(8,128)(2,1)} %pair.1, bf16[128,256]{1,0:T(8,128)(2,1)} %proj_hbm.3, bf16[128,256]{1,0:T(8,128)(2,1)} %gate_hbm.3), custom_call_target="tpu_custom_call" | custom-call | flops 3000000000 | bytes 3145728 | tf_op jit(solution)/shard_map/right_edges/pallas_call | solution.py:400
  4.0 7.3 %all-to-all-start = ((bf16[32,8,16,128]{3,2,1,0:T(8,128)(2,1)}), bf16[32,8,16,128]{3,2,1,0:T(8,128)(2,1)S(1)}, u32[]{:S(2)}, u32[]{:S(2)}) async-start(bf16[32,8,16,128]{3,2,1,0:T(8,128)(2,1)} %get-tuple-element.37), calls=%async_computation | async-start | bytes 2097152 | tf_op jit(solution)/shard_map/all_to_all | solution.py:423
  11.3 2.1 %left_edges.1 = (bf16[8,8,16,128]{3,2,1,0:T(8,128)(2,1)S(1)}, bf16[8,8,16,128]{3,2,1,0:T(8,128)(2,1)S(1)}) custom-call(s32[1]{0:T(128)S(6)} %copy.11.length, bf16[16,128,128]{2,1,0:T(8,128)(2,1)} %get-tuple-element.38.normed.source_hbm, bf16[128,256]{1,0:T(8,128)(2,1)} %proj_hbm.3, bf16[128,256]{1,0:T(8,128)(2,1)} %gate_hbm.3), custom_call_target="tpu_custom_call" | custom-call | flops 3000000000 | bytes 1048576 | tf_op jit(solution)/shard_map/left_edges/pallas_call | solution.py:400
  13.7 1.3 %collective-permute-done.sibling = bf16[8,8,16,128]{3,2,1,0:T(8,128)(2,1)S(1)} collective-permute-done((bf16[8,8,16,128]{3,2,1,0:T(8,128)(2,1)S(1)}, bf16[8,8,16,128]{3,2,1,0:T(8,128)(2,1)S(1)}, u32[]{:S(2)}, u32[]{:S(2)}) %collective-permute-start) | collective-permute-done | bytes 262176 | tf_op jit(solution)/shard_map/ppermute | solution.py:420
  15.1 1.8 %collective-permute-start.1 = (bf16[2,8,16,128]{3,2,1,0:T(8,128)(2,1)S(1)}, bf16[2,8,16,128]{3,2,1,0:T(8,128)(2,1)S(1)}, u32[]{:S(2)}, u32[]{:S(2)}) collective-permute-start(bf16[2,8,16,128]{3,2,1,0:T(8,128)(2,1)S(1)} %get-tuple-element.44), channel_id=1, source_target_pairs={{0,1},{1,0},{2,3},{3,2},{4,5},{5,4},{6,7},{7,6},{8,9},{9,8},{10,11... | collective-permute-start | bytes 196616 | tf_op jit(solution)/shard_map/ppermute | solution.py:420
  16.9 1.5 %collective-permute-start.2 = (bf16[2,8,16,128]{3,2,1,0:T(8,128)(2,1)S(1)}, bf16[2,8,16,128]{3,2,1,0:T(8,128)(2,1)S(1)}, u32[]{:S(2)}, u32[]{:S(2)}) collective-permute-start(bf16[2,8,16,128]{3,2,1,0:T(8,128)(2,1)S(1)} %get-tuple-element.45), channel_id=1, source_target_pairs={{0,4},{1,5},{2,6},{3,7},{4,0},{5,1},{6,2},{7,3},{8,12},{9,13},{10,... | collective-permute-start | bytes 196616 | tf_op jit(solution)/shard_map/ppermute | solution.py:420
  18.6 1.8 %collective-permute-start.4 = (bf16[2,8,16,128]{3,2,1,0:T(8,128)(2,1)S(1)}, bf16[2,8,16,128]{3,2,1,0:T(8,128)(2,1)S(1)}, u32[]{:S(2)}, u32[]{:S(2)}) collective-permute-start(bf16[2,8,16,128]{3,2,1,0:T(8,128)(2,1)S(1)} %get-tuple-element.47), channel_id=1, source_target_pairs={{0,8},{1,9},{2,10},{3,11},{4,12},{5,13},{6,14},{7,15},{8,0},{9,1},... | collective-permute-start | bytes 196616 | tf_op jit(solution)/shard_map/ppermute | solution.py:420
  20.4 1.5 %collective-permute-start.5 = (bf16[2,8,16,128]{3,2,1,0:T(8,128)(2,1)S(1)}, bf16[2,8,16,128]{3,2,1,0:T(8,128)(2,1)S(1)}, u32[]{:S(2)}, u32[]{:S(2)}) collective-permute-start(bf16[2,8,16,128]{3,2,1,0:T(8,128)(2,1)S(1)} %get-tuple-element.48), channel_id=1, source_target_pairs={{0,9},{1,8},{2,11},{3,10},{4,13},{5,12},{6,15},{7,14},{8,1},{9,0},... | collective-permute-start | bytes 196616 | tf_op jit(solution)/shard_map/ppermute | solution.py:420
  21.9 1.5 %collective-permute-done.1.rest_1_ = bf16[2,8,16,128]{3,2,1,0:T(8,128)(2,1)S(1)} collective-permute-done((bf16[2,8,16,128]{3,2,1,0:T(8,128)(2,1)S(1)}, bf16[2,8,16,128]{3,2,1,0:T(8,128)(2,1)S(1)}, u32[]{:S(2)}, u32[]{:S(2)}) %collective-permute-start.1) | collective-permute-done | bytes 65568 | tf_op jit(solution)/shard_map/ppermute | solution.py:420
  25.9 1.6 %tri_gate.1 = (bf16[16,128,128]{2,1,0:T(8,128)(2,1)S(1)}, bf16[16,128,128]{2,1,0:T(8,128)(2,1)S(1)}) custom-call(bf16[16,128,128]{2,1,0:T(8,128)(2,1)S(1)} %copy-done.1, bf16[16,128,128]{2,1,0:T(8,128)(2,1)S(1)} %copy-done.5, bf16[128,128]{1,0:T(8,128)(2,1)S(1)} %copy-done.3), custom_call_target="tpu_custom_call" | custom-call | flops 2000000000 | bytes 2097152 | tf_op jit(solution)/shard_map/tri_gate/pallas_call | solution.py:429
  27.5 3.2 %collective-permute-done.4.rest_4_ = bf16[2,8,16,128]{3,2,1,0:T(8,128)(2,1)S(1)} collective-permute-done((bf16[2,8,16,128]{3,2,1,0:T(8,128)(2,1)S(1)}, bf16[2,8,16,128]{3,2,1,0:T(8,128)(2,1)S(1)}, u32[]{:S(2)}, u32[]{:S(2)}) %collective-permute-start.4) | collective-permute-done | bytes 65568 | tf_op jit(solution)/shard_map/ppermute | solution.py:420
  30.7 1.5 %collective-permute-done.5.rest_5_ = bf16[2,8,16,128]{3,2,1,0:T(8,128)(2,1)S(1)} collective-permute-done((bf16[2,8,16,128]{3,2,1,0:T(8,128)(2,1)S(1)}, bf16[2,8,16,128]{3,2,1,0:T(8,128)(2,1)S(1)}, u32[]{:S(2)}, u32[]{:S(2)}) %collective-permute-start.5) | collective-permute-done | bytes 65568 | tf_op jit(solution)/shard_map/ppermute | solution.py:420
  32.2 2.7 %collective-permute-done.6.rest_6_ = bf16[2,8,16,128]{3,2,1,0:T(8,128)(2,1)S(1)} collective-permute-done((bf16[2,8,16,128]{3,2,1,0:T(8,128)(2,1)S(1)}, bf16[2,8,16,128]{3,2,1,0:T(8,128)(2,1)S(1)}, u32[]{:S(2)}, u32[]{:S(2)}) %collective-permute-start.6) | collective-permute-done | bytes 65568 | tf_op jit(solution)/shard_map/ppermute | solution.py:420
  34.9 2.9 %collective-permute-done.7.rest_7_ = bf16[2,8,16,128]{3,2,1,0:T(8,128)(2,1)S(1)} collective-permute-done((bf16[2,8,16,128]{3,2,1,0:T(8,128)(2,1)S(1)}, bf16[2,8,16,128]{3,2,1,0:T(8,128)(2,1)S(1)}, u32[]{:S(2)}, u32[]{:S(2)}) %collective-permute-start.7) | collective-permute-done | bytes 65568 | tf_op jit(solution)/shard_map/ppermute | solution.py:420
  39.0 5.1 %all-to-all-start.1 = ((bf16[16,8,16,128]{3,2,1,0:T(8,128)(2,1)}), bf16[16,8,16,128]{3,2,1,0:T(8,128)(2,1)S(1)}, u32[]{:S(2)}, u32[]{:S(2)}) async-start(bf16[16,8,16,128]{3,2,1,0:T(8,128)(2,1)} %bitcast.1), calls=%async_computation.1 | async-start | bytes 1048576 | tf_op jit(solution)/shard_map/all_to_all | solution.py:389
  44.3 7.0 %all-to-all-done.1 = bf16[16,8,16,128]{3,2,1,0:T(8,128)(2,1)S(1)} async-done(((bf16[16,8,16,128]{3,2,1,0:T(8,128)(2,1)}), bf16[16,8,16,128]{3,2,1,0:T(8,128)(2,1)S(1)}, u32[]{:S(2)}, u32[]{:S(2)}) %all-to-all-start.1) | async-done | bytes 524320 | tf_op jit(solution)/shard_map/all_to_all | solution.py:389
  51.3 1.5 %update.1 = (bf16[16,128,128]{2,1,0:T(8,128)(2,1)S(1)}, bf16[4,16,128]{2,1,0:T(8,128)(2,1)S(1)}) custom-call(bf16[128,16,128]{2,1,0:T(8,128)(2,1)S(1)} %bitcast.4, bf16[16,128,128]{2,1,0:T(8,128)(2,1)S(1)} %get-tuple-element.59.source, bf16[16,128,128]{2,1,0:T(8,128)(2,1)S(1)} %get-tuple-element.60.gate, bf16[128,128]{1,0:T(8,128)(2,1)S(1)} %copy-done.4, ...), custom_call_target="tpu_custom_call" | custom-call | flops 2000000000 | bytes 1081344 | tf_op jit(solution)/shard_map/update/pallas_call | solution.py:443
  52.9 1.7 %collective-permute-start.9 = (bf16[16,128,128]{2,1,0:T(8,128)(2,1)S(1)}, bf16[16,128,128]{2,1,0:T(8,128)(2,1)S(1)}, u32[]{:S(2)}, u32[]{:S(2)}) collective-permute-start(bf16[16,128,128]{2,1,0:T(8,128)(2,1)S(1)} %get-tuple-element.62.updated), channel_id=1, source_target_pairs={{1,0},{0,1},{3,2},{2,3},{5,4},{4,5},{7,6},{6,7},{9,8},{8,9},{11,10... | collective-permute-start | bytes 1572872 | tf_op jit(solution)/shard_map/ppermute | solution.py:465
  54.6 3.0 %collective-permute-start.8 = (bf16[4,16,128]{2,1,0:T(8,128)(2,1)S(1)}, bf16[4,16,128]{2,1,0:T(8,128)(2,1)S(1)}, u32[]{:S(2)}, u32[]{:S(2)}) collective-permute-start(bf16[4,16,128]{2,1,0:T(8,128)(2,1)S(1)} %get-tuple-element.61.refs_0_), channel_id=1, source_target_pairs={{0,16},{1,17},{2,18},{3,19},{4,20},{5,21},{6,22},{7,23},{8,24},{9,... | collective-permute-start | bytes 49160 | tf_op jit(solution)/shard_map/ppermute | solution.py:420
  57.5 1.7 %collective-permute-done.8.refs_1_ = bf16[4,16,128]{2,1,0:T(8,128)(2,1)S(1)} collective-permute-done((bf16[4,16,128]{2,1,0:T(8,128)(2,1)S(1)}, bf16[4,16,128]{2,1,0:T(8,128)(2,1)S(1)}, u32[]{:S(2)}, u32[]{:S(2)}) %collective-permute-start.8) | collective-permute-done | bytes 16416 | tf_op jit(solution)/shard_map/ppermute | solution.py:420
  59.9 3.4 %all-to-all-start.2 = ((bf16[8,4,16,128]{3,2,1,0:T(8,128)(2,1)}), bf16[8,4,16,128]{3,2,1,0:T(8,128)(2,1)S(1)}, u32[]{:S(2)}, u32[]{:S(2)}) async-start(bf16[8,4,16,128]{3,2,1,0:T(8,128)(2,1)} %deal_bias.1), calls=%async_computation.2 | async-start | bytes 262144 | tf_op jit(solution)/shard_map/all_to_all | solution.py:468
  63.3 1.9 %own_projections.1 = (bf16[16,128,384]{2,1,0:T(8,128)(2,1)S(1)}, bf16[16,128,256]{2,1,0:T(8,128)(2,1)}) custom-call(bf16[16,128,128]{2,1,0:T(8,128)(2,1)S(1)} %get-tuple-element.62.updated, bf16[128,512]{1,0:T(8,128)(2,1)S(1)} %copy-done.2), custom_call_target="tpu_custom_call" | custom-call | flops 3000000000 | bytes 5242880 | tf_op jit(solution)/shard_map/own_projections/pallas_call | solution.py:474
  65.3 4.1 %all-to-all-done.2.mine = bf16[8,4,16,128]{3,2,1,0:T(8,128)(2,1)S(1)} async-done(((bf16[8,4,16,128]{3,2,1,0:T(8,128)(2,1)}), bf16[8,4,16,128]{3,2,1,0:T(8,128)(2,1)S(1)}, u32[]{:S(2)}, u32[]{:S(2)}) %all-to-all-start.2) | async-done | bytes 131104 | tf_op jit(solution)/shard_map/all_to_all | solution.py:468
  70.7 4.7 %attend.1 = bf16[16,128,128]{2,1,0:T(8,128)(2,1)} custom-call(s32[1]{0:T(128)S(6)} %copy.11.length, bf16[8,4,16,128]{3,2,1,0:T(8,128)(2,1)S(1)} %all-to-all-done.2.mine, bf16[8,4,16,128]{3,2,1,0:T(8,128)(2,1)S(1)} %collective-permute-done.10.sibling, bf16[128,128]{1,0:T(8,128)(2,1)S(1)} %copy-done, bf16[16,128,256]{2,1,0:T(8,128)(2,1)S(1)} %get-tuple-element.66.late, ...), custom_call_target="tpu_custom_call" | custom-call | flops 100000000 | bytes 1048576 | tf_op jit(solution)/shard_map/attend/pallas_call | solution.py:493
  (29 shorter events, 6.6 us)
Async XLA Ops:
  4.0 33.7 %all-to-all-start = ((bf16[32,8,16,128]{3,2,1,0:T(8,128)(2,1)}), bf16[32,8,16,128]{3,2,1,0:T(8,128)(2,1)S(1)}, u32[]{:S(2)}, u32[]{:S(2)}) async-start(bf16[32,8,16,128]{3,2,1,0:T(8,128)(2,1)} %get-tuple-element.37), calls=%async_computation | async-start | bytes 2097152 | tf_op jit(solution)/shard_map/all_to_all | solution.py:423
  11.3 14.5 %copy-start.1 = (bf16[16,128,128]{2,1,0:T(8,128)(2,1)S(1)}, bf16[16,128,128]{2,1,0:T(8,128)(2,1)}, u32[]{:S(2)}) copy-start(bf16[16,128,128]{2,1,0:T(8,128)(2,1)} %pair.1) | copy-start | bytes 1572868
  11.3 14.5 %copy-start.3 = (bf16[128,128]{1,0:T(8,128)(2,1)S(1)}, bf16[128,128]{1,0:T(8,128)(2,1)}, u32[]{:S(2)}) copy-start(bf16[128,128]{1,0:T(8,128)(2,1)} %weights.1) | copy-start | bytes 98308
  11.3 14.5 %copy-start.5 = (bf16[16,128,128]{2,1,0:T(8,128)(2,1)S(1)}, bf16[16,128,128]{2,1,0:T(8,128)(2,1)}, u32[]{:S(2)}) copy-start(bf16[16,128,128]{2,1,0:T(8,128)(2,1)} %get-tuple-element.38.normed.source_hbm) | copy-start | bytes 1572868
  13.4 1.6 %collective-permute-start = (bf16[8,8,16,128]{3,2,1,0:T(8,128)(2,1)S(1)}, bf16[8,8,16,128]{3,2,1,0:T(8,128)(2,1)S(1)}, u32[]{:S(2)}, u32[]{:S(2)}) collective-permute-start(bf16[8,8,16,128]{3,2,1,0:T(8,128)(2,1)S(1)} %get-tuple-element.42), channel_id=1, source_target_pairs={{0,2},{1,3},{2,0},{3,1},{4,6},{5,7},{6,4},{7,5},{8,10},{9,11},{10,... | collective-permute-start | bytes 786440 | tf_op jit(solution)/shard_map/ppermute | solution.py:420
  15.1 8.3 %collective-permute-start.1 = (bf16[2,8,16,128]{3,2,1,0:T(8,128)(2,1)S(1)}, bf16[2,8,16,128]{3,2,1,0:T(8,128)(2,1)S(1)}, u32[]{:S(2)}, u32[]{:S(2)}) collective-permute-start(bf16[2,8,16,128]{3,2,1,0:T(8,128)(2,1)S(1)} %get-tuple-element.44), channel_id=1, source_target_pairs={{0,1},{1,0},{2,3},{3,2},{4,5},{5,4},{6,7},{7,6},{8,9},{9,8},{10,11... | collective-permute-start | bytes 196616 | tf_op jit(solution)/shard_map/ppermute | solution.py:420
  16.9 8.4 %collective-permute-start.2 = (bf16[2,8,16,128]{3,2,1,0:T(8,128)(2,1)S(1)}, bf16[2,8,16,128]{3,2,1,0:T(8,128)(2,1)S(1)}, u32[]{:S(2)}, u32[]{:S(2)}) collective-permute-start(bf16[2,8,16,128]{3,2,1,0:T(8,128)(2,1)S(1)} %get-tuple-element.45), channel_id=1, source_target_pairs={{0,4},{1,5},{2,6},{3,7},{4,0},{5,1},{6,2},{7,3},{8,12},{9,13},{10,... | collective-permute-start | bytes 196616 | tf_op jit(solution)/shard_map/ppermute | solution.py:420
  18.4 9.1 %collective-permute-start.3 = (bf16[2,8,16,128]{3,2,1,0:T(8,128)(2,1)S(1)}, bf16[2,8,16,128]{3,2,1,0:T(8,128)(2,1)S(1)}, u32[]{:S(2)}, u32[]{:S(2)}) collective-permute-start(bf16[2,8,16,128]{3,2,1,0:T(8,128)(2,1)S(1)} %get-tuple-element.46), channel_id=1, source_target_pairs={{0,5},{1,4},{2,7},{3,6},{4,1},{5,0},{6,3},{7,2},{8,13},{9,12},{10,... | collective-permute-start | bytes 196616 | tf_op jit(solution)/shard_map/ppermute | solution.py:420
  18.6 12.1 %collective-permute-start.4 = (bf16[2,8,16,128]{3,2,1,0:T(8,128)(2,1)S(1)}, bf16[2,8,16,128]{3,2,1,0:T(8,128)(2,1)S(1)}, u32[]{:S(2)}, u32[]{:S(2)}) collective-permute-start(bf16[2,8,16,128]{3,2,1,0:T(8,128)(2,1)S(1)} %get-tuple-element.47), channel_id=1, source_target_pairs={{0,8},{1,9},{2,10},{3,11},{4,12},{5,13},{6,14},{7,15},{8,0},{9,1},... | collective-permute-start | bytes 196616 | tf_op jit(solution)/shard_map/ppermute | solution.py:420
  20.4 11.8 %collective-permute-start.5 = (bf16[2,8,16,128]{3,2,1,0:T(8,128)(2,1)S(1)}, bf16[2,8,16,128]{3,2,1,0:T(8,128)(2,1)S(1)}, u32[]{:S(2)}, u32[]{:S(2)}) collective-permute-start(bf16[2,8,16,128]{3,2,1,0:T(8,128)(2,1)S(1)} %get-tuple-element.48), channel_id=1, source_target_pairs={{0,9},{1,8},{2,11},{3,10},{4,13},{5,12},{6,15},{7,14},{8,1},{9,0},... | collective-permute-start | bytes 196616 | tf_op jit(solution)/shard_map/ppermute | solution.py:420
  23.3 11.5 %collective-permute-start.6 = (bf16[2,8,16,128]{3,2,1,0:T(8,128)(2,1)S(1)}, bf16[2,8,16,128]{3,2,1,0:T(8,128)(2,1)S(1)}, u32[]{:S(2)}, u32[]{:S(2)}) collective-permute-start(bf16[2,8,16,128]{3,2,1,0:T(8,128)(2,1)S(1)} %get-tuple-element.49), channel_id=1, source_target_pairs={{0,12},{1,13},{2,14},{3,15},{4,8},{5,9},{6,10},{7,11},{8,4},{9,5},... | collective-permute-start | bytes 196616 | tf_op jit(solution)/shard_map/ppermute | solution.py:420
  25.3 12.5 %collective-permute-start.7 = (bf16[2,8,16,128]{3,2,1,0:T(8,128)(2,1)S(1)}, bf16[2,8,16,128]{3,2,1,0:T(8,128)(2,1)S(1)}, u32[]{:S(2)}, u32[]{:S(2)}) collective-permute-start(bf16[2,8,16,128]{3,2,1,0:T(8,128)(2,1)S(1)} %get-tuple-element.50), channel_id=1, source_target_pairs={{0,13},{1,12},{2,15},{3,14},{4,9},{5,8},{6,11},{7,10},{8,5},{9,4},... | collective-permute-start | bytes 196616 | tf_op jit(solution)/shard_map/ppermute | solution.py:420
  37.7 6.4 %copy-start.6 = (bf16[128,4]{0,1:T(4,128)(2,1)S(1)}, bf16[128,4]{0,1:T(4,128)(2,1)}, u32[]{:S(2)}) copy-start(bf16[128,4]{0,1:T(4,128)(2,1)} %param.16) | copy-start | bytes 3076
  37.7 13.6 %copy-start.4 = (bf16[128,128]{1,0:T(8,128)(2,1)S(1)}, bf16[128,128]{1,0:T(8,128)(2,1)}, u32[]{:S(2)}) copy-start(bf16[128,128]{1,0:T(8,128)(2,1)} %tri_out.1) | copy-start | bytes 98308
  39.0 12.3 %all-to-all-start.1 = ((bf16[16,8,16,128]{3,2,1,0:T(8,128)(2,1)}), bf16[16,8,16,128]{3,2,1,0:T(8,128)(2,1)S(1)}, u32[]{:S(2)}, u32[]{:S(2)}) async-start(bf16[16,8,16,128]{3,2,1,0:T(8,128)(2,1)} %bitcast.1), calls=%async_computation.1 | async-start | bytes 1048576 | tf_op jit(solution)/shard_map/all_to_all | solution.py:389
  51.3 12.0 %copy-start.2 = (bf16[128,512]{1,0:T(8,128)(2,1)S(1)}, bf16[128,512]{1,0:T(8,128)(2,1)}, u32[]{:S(2)}) copy-start(bf16[128,512]{1,0:T(8,128)(2,1)} %attn_proj.3) | copy-start | bytes 393220
  52.9 16.5 %collective-permute-start.9 = (bf16[16,128,128]{2,1,0:T(8,128)(2,1)S(1)}, bf16[16,128,128]{2,1,0:T(8,128)(2,1)S(1)}, u32[]{:S(2)}, u32[]{:S(2)}) collective-permute-start(bf16[16,128,128]{2,1,0:T(8,128)(2,1)S(1)} %get-tuple-element.62.updated), channel_id=1, source_target_pairs={{1,0},{0,1},{3,2},{2,3},{5,4},{4,5},{7,6},{6,7},{9,8},{8,9},{11,10... | collective-permute-start | bytes 1572872 | tf_op jit(solution)/shard_map/ppermute | solution.py:465
  54.6 4.7 %collective-permute-start.8 = (bf16[4,16,128]{2,1,0:T(8,128)(2,1)S(1)}, bf16[4,16,128]{2,1,0:T(8,128)(2,1)S(1)}, u32[]{:S(2)}, u32[]{:S(2)}) collective-permute-start(bf16[4,16,128]{2,1,0:T(8,128)(2,1)S(1)} %get-tuple-element.61.refs_0_), channel_id=1, source_target_pairs={{0,16},{1,17},{2,18},{3,19},{4,20},{5,21},{6,22},{7,23},{8,24},{9,... | collective-permute-start | bytes 49160 | tf_op jit(solution)/shard_map/ppermute | solution.py:420
  59.9 9.4 %all-to-all-start.2 = ((bf16[8,4,16,128]{3,2,1,0:T(8,128)(2,1)}), bf16[8,4,16,128]{3,2,1,0:T(8,128)(2,1)S(1)}, u32[]{:S(2)}, u32[]{:S(2)}) async-start(bf16[8,4,16,128]{3,2,1,0:T(8,128)(2,1)} %deal_bias.1), calls=%async_computation.2 | async-start | bytes 262144 | tf_op jit(solution)/shard_map/all_to_all | solution.py:468
  69.4 1.3 %collective-permute-start.10 = (bf16[8,4,16,128]{3,2,1,0:T(8,128)(2,1)S(1)}, bf16[8,4,16,128]{3,2,1,0:T(8,128)(2,1)S(1)}, u32[]{:S(2)}, u32[]{:S(2)}) collective-permute-start(bf16[8,4,16,128]{3,2,1,0:T(8,128)(2,1)S(1)} %all-to-all-done.2.mine), channel_id=1, source_target_pairs={{0,2},{1,3},{2,0},{3,1},{4,6},{5,7},{6,4},{7,5},{8,10},{9,11},{10,... | collective-permute-start | bytes 393224 | tf_op jit(solution)/shard_map/ppermute | solution.py:420
  69.4 1.3 %copy-start = (bf16[128,128]{1,0:T(8,128)(2,1)S(1)}, bf16[128,128]{1,0:T(8,128)(2,1)}, u32[]{:S(2)}) copy-start(bf16[128,128]{1,0:T(8,128)(2,1)} %attn_out.1) | copy-start | bytes 98308

commit v6 on v5

--- a/solution.py
+++ b/solution.py
@@ -166,8 +166,9 @@
         out[1 - core] = sibling[k]
 
 
-def gate_body(pair, normed, weights, out, source):
+def gate_body(pair, normed, weights, bias_proj, out, source, bias_weights):
     turned_weights = turned(weights[...])
+    bias_weights[...] = turned(bias_proj[...])
 
     def step(row, carry):
         out[row] = sigmoid(dot(turned_weights, normed[row], (1, 1))).astype(BF16)
@@ -230,13 +231,13 @@
 
 def update_body(triangle, source, gate, tri_out, bias_proj, updated, bias, held, bias_held):
     channels, rows, cols = triangle.shape
-    heads = bias_proj.shape[1]
+    heads = bias_proj.shape[0]
     values = triangle[...].astype(F32)
     centre = values - spread_sum(values) * (1.0 / channels)
     spread = spread_sum(centre * centre) * (1.0 / channels)
     held[...] = (centre * lax.rsqrt(spread + EPS)).reshape(channels * rows, cols)
     out_weights = turned(tri_out[...])
-    bias_weights = turned(bias_proj[...])
+    bias_weights = bias_proj[...]
 
     def step(row, carry):
         tri_normed = held[pl.ds(row, channels, stride=rows), :].astype(BF16)
@@ -426,10 +427,16 @@
         mine, flipped(theirs, col_devices)
     )
     left = [flipped(part, offset) if offset else part for part, offset in zip(left, offsets)]
-    tri_gating, source = call(
-        gate_body, "tri_gate", [shape(turned_block, BF16)] * 2, 3, flops=2e9
-    )(pair_act, normed, tri_gate)
-    tri_gating, source, *left = lax.optimization_barrier((tri_gating, source, *left))
+    tri_gating, source, bias_weights = call(
+        gate_body,
+        "tri_gate",
+        [shape(turned_block, BF16)] * 2 + [shape((heads, channels), BF16)],
+        4,
+        flops=2e9,
+    )(pair_act, normed, tri_gate, bias_proj)
+    tri_gating, source, bias_weights, *left = lax.optimization_barrier(
+        (tri_gating, source, bias_weights, *left)
+    )
     triangle_shape = (row_devices // 2, col_devices, own, rows, cols)
     (triangle,) = call(
         triangle_body,
@@ -447,7 +454,7 @@
         5,
         [pltpu.VMEM((channels * rows, cols), F32), pltpu.VMEM((heads * rows, cols), F32)],
         flops=2e9,
-    )(triangle.reshape(channels, rows, cols), source, tri_gating, tri_out, bias_proj)
+    )(triangle.reshape(channels, rows, cols), source, tri_gating, tri_out, bias_weights)
     per_part = row_devices // col_devices
     parts = [bias] + [
         flipped(bias, flip * per_part * col_devices) for flip in range(1, col_devices)

time: 75.8 us -> 74.9 us (0.988)
  blocking collectives: 0 us -> 12.1 us
  waiting for transfers between devices: 27 us -> 17.8 us
  starting transfers between devices: 29 us -> 24.2 us
  local copies, waits for them, and re-layouts: 0.17 us -> 2 us
  Pallas kernels: 18.4 us -> 17.6 us
    all_to_all x0 -> x1, blocking collectives: none -> 12.1 us  [in_half(): lax.all_to_all(array, BOTH, split_axis=0, concat_axis=0, axis_index_group...]
    all_to_all x1 -> x0, waiting for transfers between devices: 7.05 us -> none  [in_half(): lax.all_to_all(array, BOTH, split_axis=0, concat_axis=0, axis_index_group...]
    all_to_all x1 -> x0, starting transfers between devices: 5.1 us -> none  [in_half(): lax.all_to_all(array, BOTH, split_axis=0, concat_axis=0, axis_index_group...]
    ppermute x10, waiting for transfers between devices: 15.9 us -> 13.7 us  [flipped(): return lax.ppermute(array, BOTH, [(d, d ^ bits) for d in range(devices)])]
    unnamed x15 -> x19, local copies, waits for them, and re-layouts: 0.17 us -> 2 us
    pallas_call x1, Pallas kernels: 1.28 us -> 0.49 us  [local(): call(triangle_body, 'triangle', [shape(triangle_shape, BF16)], 1 + len(le...]
  transfers between devices with their start and end apart: 14 -> 13, of which waited for: 11 -> 10; matrix products, arithmetic and copies ran while one was open for 0% -> 0% of each run, Pallas kernels for 10% -> 10%
where the time goes in v6:
time: 74.9 us; the launch traced here: 74.4 us
  starting transfers between devices  24.2 us (32%)
  waiting for transfers between devices  17.8 us (24%)
  Pallas kernels  17.6 us (23%)
  blocking collectives  12.1 us (16%)
  local copies, waits for them, and re-layouts  2 us (3%)
  between operations  0.79 us (1%)
    ppermute x10, waiting for transfers between devices, flipped(): return lax.ppermute(array, BOTH, [(d, d ^ bits) for d in range(devices)])  13.7 us
    all_to_all x1, blocking collectives, in_half(): lax.all_to_all(array, BOTH, split_axis=0, concat_axis=0, axis_index_group...  12.1 us
    ppermute x10, starting transfers between devices, flipped(): return lax.ppermute(array, BOTH, [(d, d ^ bits) for d in range(devices)])  11.7 us
    all_to_all x1, starting transfers between devices, local(): right = lax.all_to_all(right, BOTH, split_axis=0, concat_axis=0, tiled=True)  7.3 us
    pallas_call x2, Pallas kernels, edges(): call(functools.partial(edges_body, side=side), 'right_edges' if side else...  5.38 us
    pallas_call x1, Pallas kernels, local(): call(attend_body, 'attend', [shape(block, BF16)], 5 + col_devices, [pltpu...  4.69 us
    all_to_all x1, waiting for transfers between devices, local(): lax.all_to_all(dealt, BOTH, split_axis=0, concat_axis=0, axis_index_group...  4.07 us
    all_to_all x1, starting transfers between devices, local(): lax.all_to_all(dealt, BOTH, split_axis=0, concat_axis=0, axis_index_group...  3.37 us
  transfers between devices with their start and end apart: 13, of which 10 were waited for; matrix products, arithmetic and copies ran while one was open for 0% of the time, Pallas kernels for 10%

profile of v6, /device:TPU:0, one launch (start us, length us, event | category | flops | bytes accessed | tf_op | source)
XLA Modules:
  0.0 74.4 jit_solution(14265326988079250872)
XLA Ops:
  0.7 3.3 %right_edges.1 = (bf16[32,8,16,128]{3,2,1,0:T(8,128)(2,1)}, bf16[16,128,128]{2,1,0:T(8,128)(2,1)}) custom-call(s32[1]{0:T(128)S(6)} %copy.11.length, bf16[16,128,128]{2,1,0:T(8,128)(2,1)} %pair.1, bf16[128,256]{1,0:T(8,128)(2,1)} %proj_hbm.3, bf16[128,256]{1,0:T(8,128)(2,1)} %gate_hbm.3), custom_call_target="tpu_custom_call" | custom-call | flops 3000000000 | bytes 3145728 | tf_op jit(solution)/shard_map/right_edges/pallas_call | solution.py:401
  4.0 7.3 %all-to-all-start = ((bf16[32,8,16,128]{3,2,1,0:T(8,128)(2,1)}), bf16[32,8,16,128]{3,2,1,0:T(8,128)(2,1)S(1)}, u32[]{:S(2)}, u32[]{:S(2)}) async-start(bf16[32,8,16,128]{3,2,1,0:T(8,128)(2,1)} %get-tuple-element.39), calls=%async_computation | async-start | bytes 2097152 | tf_op jit(solution)/shard_map/all_to_all | solution.py:424
  11.3 2.0 %left_edges.1 = (bf16[8,8,16,128]{3,2,1,0:T(8,128)(2,1)S(1)}, bf16[8,8,16,128]{3,2,1,0:T(8,128)(2,1)S(1)}) custom-call(s32[1]{0:T(128)S(6)} %copy.11.length, bf16[16,128,128]{2,1,0:T(8,128)(2,1)} %get-tuple-element.40.normed.source_hbm, bf16[128,256]{1,0:T(8,128)(2,1)} %proj_hbm.3, bf16[128,256]{1,0:T(8,128)(2,1)} %gate_hbm.3), custom_call_target="tpu_custom_call" | custom-call | flops 3000000000 | bytes 1048576 | tf_op jit(solution)/shard_map/left_edges/pallas_call | solution.py:401
  13.7 1.3 %collective-permute-done.sibling = bf16[8,8,16,128]{3,2,1,0:T(8,128)(2,1)S(1)} collective-permute-done((bf16[8,8,16,128]{3,2,1,0:T(8,128)(2,1)S(1)}, bf16[8,8,16,128]{3,2,1,0:T(8,128)(2,1)S(1)}, u32[]{:S(2)}, u32[]{:S(2)}) %collective-permute-start) | collective-permute-done | bytes 262176 | tf_op jit(solution)/shard_map/ppermute | solution.py:421
  15.0 1.8 %collective-permute-start.1 = (bf16[2,8,16,128]{3,2,1,0:T(8,128)(2,1)S(1)}, bf16[2,8,16,128]{3,2,1,0:T(8,128)(2,1)S(1)}, u32[]{:S(2)}, u32[]{:S(2)}) collective-permute-start(bf16[2,8,16,128]{3,2,1,0:T(8,128)(2,1)S(1)} %get-tuple-element.47), channel_id=1, source_target_pairs={{0,1},{1,0},{2,3},{3,2},{4,5},{5,4},{6,7},{7,6},{8,9},{9,8},{10,11... | collective-permute-start | bytes 196616 | tf_op jit(solution)/shard_map/ppermute | solution.py:421
  16.9 1.5 %collective-permute-start.2 = (bf16[2,8,16,128]{3,2,1,0:T(8,128)(2,1)S(1)}, bf16[2,8,16,128]{3,2,1,0:T(8,128)(2,1)S(1)}, u32[]{:S(2)}, u32[]{:S(2)}) collective-permute-start(bf16[2,8,16,128]{3,2,1,0:T(8,128)(2,1)S(1)} %get-tuple-element.48), channel_id=1, source_target_pairs={{0,4},{1,5},{2,6},{3,7},{4,0},{5,1},{6,2},{7,3},{8,12},{9,13},{10,... | collective-permute-start | bytes 196616 | tf_op jit(solution)/shard_map/ppermute | solution.py:421
  18.8 1.8 %collective-permute-start.4 = (bf16[2,8,16,128]{3,2,1,0:T(8,128)(2,1)S(1)}, bf16[2,8,16,128]{3,2,1,0:T(8,128)(2,1)S(1)}, u32[]{:S(2)}, u32[]{:S(2)}) collective-permute-start(bf16[2,8,16,128]{3,2,1,0:T(8,128)(2,1)S(1)} %get-tuple-element.50), channel_id=1, source_target_pairs={{0,8},{1,9},{2,10},{3,11},{4,12},{5,13},{6,14},{7,15},{8,0},{9,1},... | collective-permute-start | bytes 196616 | tf_op jit(solution)/shard_map/ppermute | solution.py:421
  20.6 1.5 %collective-permute-start.5 = (bf16[2,8,16,128]{3,2,1,0:T(8,128)(2,1)S(1)}, bf16[2,8,16,128]{3,2,1,0:T(8,128)(2,1)S(1)}, u32[]{:S(2)}, u32[]{:S(2)}) collective-permute-start(bf16[2,8,16,128]{3,2,1,0:T(8,128)(2,1)S(1)} %get-tuple-element.51), channel_id=1, source_target_pairs={{0,9},{1,8},{2,11},{3,10},{4,13},{5,12},{6,15},{7,14},{8,1},{9,0},... | collective-permute-start | bytes 196616 | tf_op jit(solution)/shard_map/ppermute | solution.py:421
  22.0 1.3 %collective-permute-done.1.rest_1_ = bf16[2,8,16,128]{3,2,1,0:T(8,128)(2,1)S(1)} collective-permute-done((bf16[2,8,16,128]{3,2,1,0:T(8,128)(2,1)S(1)}, bf16[2,8,16,128]{3,2,1,0:T(8,128)(2,1)S(1)}, u32[]{:S(2)}, u32[]{:S(2)}) %collective-permute-start.1) | collective-permute-done | bytes 65568 | tf_op jit(solution)/shard_map/ppermute | solution.py:421
  26.9 1.6 %tri_gate.1 = (bf16[16,128,128]{2,1,0:T(8,128)(2,1)S(1)}, bf16[16,128,128]{2,1,0:T(8,128)(2,1)S(1)}, bf16[4,128]{1,0:T(4,128)(2,1)S(1)}) custom-call(bf16[16,128,128]{2,1,0:T(8,128)(2,1)S(1)} %copy-done.1, bf16[16,128,128]{2,1,0:T(8,128)(2,1)S(1)} %copy-done.7, bf16[128,128]{1,0:T(8,128)(2,1)S(1)} %copy-done.3, bf16[128,4]{1,0:T(8,128)(2,1)S(1)} %copy.10.bias_proj), custom_call_target="tpu_custom_call" | custom-call | flops 2000000000 | bytes 2099200 | tf_op jit(solution)/shard_map/tri_gate/pallas_call | solution.py:430
  29.3 1.4 %collective-permute-done.4.rest_4_ = bf16[2,8,16,128]{3,2,1,0:T(8,128)(2,1)S(1)} collective-permute-done((bf16[2,8,16,128]{3,2,1,0:T(8,128)(2,1)S(1)}, bf16[2,8,16,128]{3,2,1,0:T(8,128)(2,1)S(1)}, u32[]{:S(2)}, u32[]{:S(2)}) %collective-permute-start.4) | collective-permute-done | bytes 65568 | tf_op jit(solution)/shard_map/ppermute | solution.py:421
  30.7 1.5 %collective-permute-done.5.rest_5_ = bf16[2,8,16,128]{3,2,1,0:T(8,128)(2,1)S(1)} collective-permute-done((bf16[2,8,16,128]{3,2,1,0:T(8,128)(2,1)S(1)}, bf16[2,8,16,128]{3,2,1,0:T(8,128)(2,1)S(1)}, u32[]{:S(2)}, u32[]{:S(2)}) %collective-permute-start.5) | collective-permute-done | bytes 65568 | tf_op jit(solution)/shard_map/ppermute | solution.py:421
  32.2 2.7 %collective-permute-done.6.rest_6_ = bf16[2,8,16,128]{3,2,1,0:T(8,128)(2,1)S(1)} collective-permute-done((bf16[2,8,16,128]{3,2,1,0:T(8,128)(2,1)S(1)}, bf16[2,8,16,128]{3,2,1,0:T(8,128)(2,1)S(1)}, u32[]{:S(2)}, u32[]{:S(2)}) %collective-permute-start.6) | collective-permute-done | bytes 65568 | tf_op jit(solution)/shard_map/ppermute | solution.py:421
  34.9 2.9 %collective-permute-done.7.rest_7_ = bf16[2,8,16,128]{3,2,1,0:T(8,128)(2,1)S(1)} collective-permute-done((bf16[2,8,16,128]{3,2,1,0:T(8,128)(2,1)S(1)}, bf16[2,8,16,128]{3,2,1,0:T(8,128)(2,1)S(1)}, u32[]{:S(2)}, u32[]{:S(2)}) %collective-permute-start.7) | collective-permute-done | bytes 65568 | tf_op jit(solution)/shard_map/ppermute | solution.py:421
  38.2 12.1 %all_to_all.15 = bf16[16,8,16,128]{3,2,1,0:T(8,128)(2,1)S(1)} all-to-all(bf16[16,8,16,128]{3,2,1,0:T(8,128)(2,1)S(1)} %bitcast.4), channel_id=1, replica_groups={{15,14,13,12,11,10,9,8,7,6,5,4,3,2,1,0},{31,30,29,28,27,26,25,24,23,22,..., dimensions={0} | all-to-all | bytes 1048576 | tf_op jit(solution)/shard_map/all_to_all | solution.py:390
  50.3 1.6 %update.1 = (bf16[16,128,128]{2,1,0:T(8,128)(2,1)S(1)}, bf16[4,16,128]{2,1,0:T(8,128)(2,1)S(1)}) custom-call(bf16[128,16,128]{2,1,0:T(8,128)(2,1)S(1)} %bitcast.5, bf16[16,128,128]{2,1,0:T(8,128)(2,1)S(1)} %copy-done.6, bf16[16,128,128]{2,1,0:T(8,128)(2,1)S(1)} %get-tuple-element.63.gate, bf16[128,128]{1,0:T(8,128)(2,1)S(1)} %copy-done.4, ...), custom_call_target="tpu_custom_call" | custom-call | flops 2000000000 | bytes 1081344 | tf_op jit(solution)/shard_map/update/pallas_call | solution.py:450
  51.9 1.7 %collective-permute-start.9 = (bf16[16,128,128]{2,1,0:T(8,128)(2,1)S(1)}, bf16[16,128,128]{2,1,0:T(8,128)(2,1)S(1)}, u32[]{:S(2)}, u32[]{:S(2)}) collective-permute-start(bf16[16,128,128]{2,1,0:T(8,128)(2,1)S(1)} %get-tuple-element.66.updated), channel_id=1, source_target_pairs={{1,0},{0,1},{3,2},{2,3},{5,4},{4,5},{7,6},{6,7},{9,8},{8,9},{11,10... | collective-permute-start | bytes 1572872 | tf_op jit(solution)/shard_map/ppermute | solution.py:472
  53.6 2.9 %collective-permute-start.8 = (bf16[4,16,128]{2,1,0:T(8,128)(2,1)S(1)}, bf16[4,16,128]{2,1,0:T(8,128)(2,1)S(1)}, u32[]{:S(2)}, u32[]{:S(2)}) collective-permute-start(bf16[4,16,128]{2,1,0:T(8,128)(2,1)S(1)} %get-tuple-element.65.refs_0_), channel_id=1, source_target_pairs={{0,16},{1,17},{2,18},{3,19},{4,20},{5,21},{6,22},{7,23},{8,24},{9,... | collective-permute-start | bytes 49160 | tf_op jit(solution)/shard_map/ppermute | solution.py:421
  56.6 1.7 %collective-permute-done.8.refs_1_ = bf16[4,16,128]{2,1,0:T(8,128)(2,1)S(1)} collective-permute-done((bf16[4,16,128]{2,1,0:T(8,128)(2,1)S(1)}, bf16[4,16,128]{2,1,0:T(8,128)(2,1)S(1)}, u32[]{:S(2)}, u32[]{:S(2)}) %collective-permute-start.8) | collective-permute-done | bytes 16416 | tf_op jit(solution)/shard_map/ppermute | solution.py:421
  59.0 3.4 %all-to-all-start.2 = ((bf16[8,4,16,128]{3,2,1,0:T(8,128)(2,1)}), bf16[8,4,16,128]{3,2,1,0:T(8,128)(2,1)S(1)}, u32[]{:S(2)}, u32[]{:S(2)}) async-start(bf16[8,4,16,128]{3,2,1,0:T(8,128)(2,1)} %deal_bias.1), calls=%async_computation.2 | async-start | bytes 262144 | tf_op jit(solution)/shard_map/all_to_all | solution.py:475
  62.4 1.9 %own_projections.1 = (bf16[16,128,384]{2,1,0:T(8,128)(2,1)S(1)}, bf16[16,128,256]{2,1,0:T(8,128)(2,1)}) custom-call(bf16[16,128,128]{2,1,0:T(8,128)(2,1)S(1)} %get-tuple-element.66.updated, bf16[128,512]{1,0:T(8,128)(2,1)S(1)} %copy-done.2), custom_call_target="tpu_custom_call" | custom-call | flops 3000000000 | bytes 5242880 | tf_op jit(solution)/shard_map/own_projections/pallas_call | solution.py:481
  64.3 4.1 %all-to-all-done.2.mine = bf16[8,4,16,128]{3,2,1,0:T(8,128)(2,1)S(1)} async-done(((bf16[8,4,16,128]{3,2,1,0:T(8,128)(2,1)}), bf16[8,4,16,128]{3,2,1,0:T(8,128)(2,1)S(1)}, u32[]{:S(2)}, u32[]{:S(2)}) %all-to-all-start.2) | async-done | bytes 131104 | tf_op jit(solution)/shard_map/all_to_all | solution.py:475
  68.4 1.2 %other_keys.1 = (bf16[16,128,256]{2,1,0:T(8,128)(2,1)S(1)}, bf16[16,128,256]{2,1,0:T(8,128)(2,1)S(1)}) custom-call(bf16[16,128,256]{2,1,0:T(8,128)(2,1)} %get-tuple-element.68.late_hbm, bf16[128,512]{1,0:T(8,128)(2,1)S(1)} %copy-done.2, bf16[16,128,128]{2,1,0:T(8,128)(2,1)S(1)} %collective-permute-done.9.rest_0_), custom_call_target="tpu_custom_call" | custom-call | flops 3000000000 | bytes 4194304 | tf_op jit(solution)/shard_map/other_keys/pallas_call | solution.py:491
  69.7 4.7 %attend.1 = bf16[16,128,128]{2,1,0:T(8,128)(2,1)} custom-call(s32[1]{0:T(128)S(6)} %copy.11.length, bf16[8,4,16,128]{3,2,1,0:T(8,128)(2,1)S(1)} %all-to-all-done.2.mine, bf16[8,4,16,128]{3,2,1,0:T(8,128)(2,1)S(1)} %collective-permute-done.10.sibling, bf16[128,128]{1,0:T(8,128)(2,1)S(1)} %copy-done, bf16[16,128,256]{2,1,0:T(8,128)(2,1)S(1)} %get-tuple-element.70.late, ...), custom_call_target="tpu_custom_call" | custom-call | flops 100000000 | bytes 1048576 | tf_op jit(solution)/shard_map/attend/pallas_call | solution.py:500
  (32 shorter events, 6.4 us)
Async XLA Ops:
  4.0 33.7 %all-to-all-start = ((bf16[32,8,16,128]{3,2,1,0:T(8,128)(2,1)}), bf16[32,8,16,128]{3,2,1,0:T(8,128)(2,1)S(1)}, u32[]{:S(2)}, u32[]{:S(2)}) async-start(bf16[32,8,16,128]{3,2,1,0:T(8,128)(2,1)} %get-tuple-element.39), calls=%async_computation | async-start | bytes 2097152 | tf_op jit(solution)/shard_map/all_to_all | solution.py:424
  11.3 7.0 %copy-start.8 = (bf16[128,4]{0,1:T(4,128)(2,1)S(1)}, bf16[128,4]{0,1:T(4,128)(2,1)}, u32[]{:S(2)}) copy-start(bf16[128,4]{0,1:T(4,128)(2,1)} %param.16) | copy-start | bytes 3076
  11.3 14.5 %copy-start.1 = (bf16[16,128,128]{2,1,0:T(8,128)(2,1)S(1)}, bf16[16,128,128]{2,1,0:T(8,128)(2,1)}, u32[]{:S(2)}) copy-start(bf16[16,128,128]{2,1,0:T(8,128)(2,1)} %pair.1) | copy-start | bytes 1572868
  11.3 14.5 %copy-start.3 = (bf16[128,128]{1,0:T(8,128)(2,1)S(1)}, bf16[128,128]{1,0:T(8,128)(2,1)}, u32[]{:S(2)}) copy-start(bf16[128,128]{1,0:T(8,128)(2,1)} %weights.1) | copy-start | bytes 98308
  13.4 1.6 %collective-permute-start = (bf16[8,8,16,128]{3,2,1,0:T(8,128)(2,1)S(1)}, bf16[8,8,16,128]{3,2,1,0:T(8,128)(2,1)S(1)}, u32[]{:S(2)}, u32[]{:S(2)}) collective-permute-start(bf16[8,8,16,128]{3,2,1,0:T(8,128)(2,1)S(1)} %get-tuple-element.45), channel_id=1, source_target_pairs={{0,2},{1,3},{2,0},{3,1},{4,6},{5,7},{6,4},{7,5},{8,10},{9,11},{10,... | collective-permute-start | bytes 786440 | tf_op jit(solution)/shard_map/ppermute | solution.py:421
  15.0 8.3 %collective-permute-start.1 = (bf16[2,8,16,128]{3,2,1,0:T(8,128)(2,1)S(1)}, bf16[2,8,16,128]{3,2,1,0:T(8,128)(2,1)S(1)}, u32[]{:S(2)}, u32[]{:S(2)}) collective-permute-start(bf16[2,8,16,128]{3,2,1,0:T(8,128)(2,1)S(1)} %get-tuple-element.47), channel_id=1, source_target_pairs={{0,1},{1,0},{2,3},{3,2},{4,5},{5,4},{6,7},{7,6},{8,9},{9,8},{10,11... | collective-permute-start | bytes 196616 | tf_op jit(solution)/shard_map/ppermute | solution.py:421
  16.9 8.4 %collective-permute-start.2 = (bf16[2,8,16,128]{3,2,1,0:T(8,128)(2,1)S(1)}, bf16[2,8,16,128]{3,2,1,0:T(8,128)(2,1)S(1)}, u32[]{:S(2)}, u32[]{:S(2)}) collective-permute-start(bf16[2,8,16,128]{3,2,1,0:T(8,128)(2,1)S(1)} %get-tuple-element.48), channel_id=1, source_target_pairs={{0,4},{1,5},{2,6},{3,7},{4,0},{5,1},{6,2},{7,3},{8,12},{9,13},{10,... | collective-permute-start | bytes 196616 | tf_op jit(solution)/shard_map/ppermute | solution.py:421
  18.5 10.8 %collective-permute-start.3 = (bf16[2,8,16,128]{3,2,1,0:T(8,128)(2,1)S(1)}, bf16[2,8,16,128]{3,2,1,0:T(8,128)(2,1)S(1)}, u32[]{:S(2)}, u32[]{:S(2)}) collective-permute-start(bf16[2,8,16,128]{3,2,1,0:T(8,128)(2,1)S(1)} %get-tuple-element.49), channel_id=1, source_target_pairs={{0,5},{1,4},{2,7},{3,6},{4,1},{5,0},{6,3},{7,2},{8,13},{9,12},{10,... | collective-permute-start | bytes 196616 | tf_op jit(solution)/shard_map/ppermute | solution.py:421
  18.8 11.9 %collective-permute-start.4 = (bf16[2,8,16,128]{3,2,1,0:T(8,128)(2,1)S(1)}, bf16[2,8,16,128]{3,2,1,0:T(8,128)(2,1)S(1)}, u32[]{:S(2)}, u32[]{:S(2)}) collective-permute-start(bf16[2,8,16,128]{3,2,1,0:T(8,128)(2,1)S(1)} %get-tuple-element.50), channel_id=1, source_target_pairs={{0,8},{1,9},{2,10},{3,11},{4,12},{5,13},{6,14},{7,15},{8,0},{9,1},... | collective-permute-start | bytes 196616 | tf_op jit(solution)/shard_map/ppermute | solution.py:421
  20.6 11.6 %collective-permute-start.5 = (bf16[2,8,16,128]{3,2,1,0:T(8,128)(2,1)S(1)}, bf16[2,8,16,128]{3,2,1,0:T(8,128)(2,1)S(1)}, u32[]{:S(2)}, u32[]{:S(2)}) collective-permute-start(bf16[2,8,16,128]{3,2,1,0:T(8,128)(2,1)S(1)} %get-tuple-element.51), channel_id=1, source_target_pairs={{0,9},{1,8},{2,11},{3,10},{4,13},{5,12},{6,15},{7,14},{8,1},{9,0},... | collective-permute-start | bytes 196616 | tf_op jit(solution)/shard_map/ppermute | solution.py:421
  23.3 11.5 %collective-permute-start.6 = (bf16[2,8,16,128]{3,2,1,0:T(8,128)(2,1)S(1)}, bf16[2,8,16,128]{3,2,1,0:T(8,128)(2,1)S(1)}, u32[]{:S(2)}, u32[]{:S(2)}) collective-permute-start(bf16[2,8,16,128]{3,2,1,0:T(8,128)(2,1)S(1)} %get-tuple-element.52), channel_id=1, source_target_pairs={{0,12},{1,13},{2,14},{3,15},{4,8},{5,9},{6,10},{7,11},{8,4},{9,5},... | collective-permute-start | bytes 196616 | tf_op jit(solution)/shard_map/ppermute | solution.py:421
  25.3 12.5 %collective-permute-start.7 = (bf16[2,8,16,128]{3,2,1,0:T(8,128)(2,1)S(1)}, bf16[2,8,16,128]{3,2,1,0:T(8,128)(2,1)S(1)}, u32[]{:S(2)}, u32[]{:S(2)}) collective-permute-start(bf16[2,8,16,128]{3,2,1,0:T(8,128)(2,1)S(1)} %get-tuple-element.53), channel_id=1, source_target_pairs={{0,13},{1,12},{2,15},{3,14},{4,9},{5,8},{6,11},{7,10},{8,5},{9,4},... | collective-permute-start | bytes 196616 | tf_op jit(solution)/shard_map/ppermute | solution.py:421
  25.8 1.0 %copy-start.7 = (bf16[16,128,128]{2,1,0:T(8,128)(2,1)S(1)}, bf16[16,128,128]{2,1,0:T(8,128)(2,1)}, u32[]{:S(2)}) copy-start(bf16[16,128,128]{2,1,0:T(8,128)(2,1)} %get-tuple-element.40.normed.source_hbm) | copy-start | bytes 1572868
  28.5 0.8 %copy-start.5 = (bf16[16,128,128]{2,1,0:T(8,128)(2,1)}, bf16[16,128,128]{2,1,0:T(8,128)(2,1)S(1)}, u32[]{:S(2)}) copy-start(bf16[16,128,128]{2,1,0:T(8,128)(2,1)S(1)} %get-tuple-element.62.source) | copy-start | bytes 1572868
  37.7 12.6 %copy-start.4 = (bf16[128,128]{1,0:T(8,128)(2,1)S(1)}, bf16[128,128]{1,0:T(8,128)(2,1)}, u32[]{:S(2)}) copy-start(bf16[128,128]{1,0:T(8,128)(2,1)} %tri_out.1) | copy-start | bytes 98308
  37.7 12.6 %copy-start.6 = (bf16[16,128,128]{2,1,0:T(8,128)(2,1)S(1)}, bf16[16,128,128]{2,1,0:T(8,128)(2,1)}, u32[]{:S(2)}) copy-start(bf16[16,128,128]{2,1,0:T(8,128)(2,1)} %copy-done.5) | copy-start | bytes 1572868
  50.3 12.0 %copy-start.2 = (bf16[128,512]{1,0:T(8,128)(2,1)S(1)}, bf16[128,512]{1,0:T(8,128)(2,1)}, u32[]{:S(2)}) copy-start(bf16[128,512]{1,0:T(8,128)(2,1)} %attn_proj.3) | copy-start | bytes 393220
  51.9 16.5 %collective-permute-start.9 = (bf16[16,128,128]{2,1,0:T(8,128)(2,1)S(1)}, bf16[16,128,128]{2,1,0:T(8,128)(2,1)S(1)}, u32[]{:S(2)}, u32[]{:S(2)}) collective-permute-start(bf16[16,128,128]{2,1,0:T(8,128)(2,1)S(1)} %get-tuple-element.66.updated), channel_id=1, source_target_pairs={{1,0},{0,1},{3,2},{2,3},{5,4},{4,5},{7,6},{6,7},{9,8},{8,9},{11,10... | collective-permute-start | bytes 1572872 | tf_op jit(solution)/shard_map/ppermute | solution.py:472
  53.6 4.7 %collective-permute-start.8 = (bf16[4,16,128]{2,1,0:T(8,128)(2,1)S(1)}, bf16[4,16,128]{2,1,0:T(8,128)(2,1)S(1)}, u32[]{:S(2)}, u32[]{:S(2)}) collective-permute-start(bf16[4,16,128]{2,1,0:T(8,128)(2,1)S(1)} %get-tuple-element.65.refs_0_), channel_id=1, source_target_pairs={{0,16},{1,17},{2,18},{3,19},{4,20},{5,21},{6,22},{7,23},{8,24},{9,... | collective-permute-start | bytes 49160 | tf_op jit(solution)/shard_map/ppermute | solution.py:421
  59.0 9.4 %all-to-all-start.2 = ((bf16[8,4,16,128]{3,2,1,0:T(8,128)(2,1)}), bf16[8,4,16,128]{3,2,1,0:T(8,128)(2,1)S(1)}, u32[]{:S(2)}, u32[]{:S(2)}) async-start(bf16[8,4,16,128]{3,2,1,0:T(8,128)(2,1)} %deal_bias.1), calls=%async_computation.2 | async-start | bytes 262144 | tf_op jit(solution)/shard_map/all_to_all | solution.py:475
  68.4 1.3 %collective-permute-start.10 = (bf16[8,4,16,128]{3,2,1,0:T(8,128)(2,1)S(1)}, bf16[8,4,16,128]{3,2,1,0:T(8,128)(2,1)S(1)}, u32[]{:S(2)}, u32[]{:S(2)}) collective-permute-start(bf16[8,4,16,128]{3,2,1,0:T(8,128)(2,1)S(1)} %all-to-all-done.2.mine), channel_id=1, source_target_pairs={{0,2},{1,3},{2,0},{3,1},{4,6},{5,7},{6,4},{7,5},{8,10},{9,11},{10,... | collective-permute-start | bytes 393224 | tf_op jit(solution)/shard_map/ppermute | solution.py:421
  68.4 1.3 %copy-start = (bf16[128,128]{1,0:T(8,128)(2,1)S(1)}, bf16[128,128]{1,0:T(8,128)(2,1)}, u32[]{:S(2)}) copy-start(bf16[128,128]{1,0:T(8,128)(2,1)} %attn_out.1) | copy-start | bytes 98308

commit v7 on v6

--- a/solution.py
+++ b/solution.py
@@ -269,35 +269,23 @@
         put(late, 1, values.T)
 
 
-def own_body(updated, attn_proj, mixed, late_hbm, late, sems, *, score_scale):
-    rows = updated.shape[0]
-
+def own_body(updated, attn_proj, mixed, late, *, score_scale):
     def step(row, carry):
         project(updated, attn_proj, mixed, row, score_scale, late)
         return carry
 
-    sends = chunked([(late, late_hbm)], sems, 0, 2)
-    for chunk in range(2):
-        lax.fori_loop(chunk * rows // 2, (chunk + 1) * rows // 2, step, 0, unroll=rows // 2)
-        sends[chunk][0].start()
-    for (copy,) in sends:
-        copy.wait()
-
-
-def other_body(late_hbm, attn_proj, *rest):
-    pieces = (len(rest) - 2) // 2
-    others, late, keys, sem = rest[:pieces], rest[pieces], rest[pieces + 1 : -1], rest[-1]
-    fetch = pltpu.make_async_copy(late_hbm, late, sem)
-    fetch.start()
-    rows = late.shape[0]
-    for updated, target in zip(others, keys):
+    lax.fori_loop(0, updated.shape[0], step, 0, unroll=8)
+
+
+def other_body(attn_proj, *rest):
+    pieces = len(rest) // 2
+    for updated, target in zip(rest[:pieces], rest[pieces:]):
 
         def step(row, carry):
             project(updated, attn_proj, target, row, None)
             return carry
 
-        lax.fori_loop(0, rows, step, 0, unroll=rows // 2)
-    fetch.wait()
+        lax.fori_loop(0, updated.shape[0], step, 0, unroll=8)
 
 
 def attend_body(length, mine, sibling, attn_out, late, *rest):
@@ -472,10 +460,6 @@
         lax.ppermute(updated, "ch", [((c + s) % col_devices, c) for c in range(col_devices)])
         for s in range(1, col_devices)
     ]
-    bias = lax.all_to_all(
-        dealt, BOTH, split_axis=0, concat_axis=0, axis_index_groups=one_core, tiled=True
-    )
-
     mixed_shape = (rows, cols, 3 * channels)
     key_shape = (rows, cols, 2 * channels)
     mixed, late = call(
@@ -483,20 +467,20 @@
         "own_projections",
         [shape(mixed_shape, BF16), shape(key_shape, BF16)],
         2,
-        [pltpu.VMEM(key_shape, BF16), pltpu.SemaphoreType.DMA((1, 2))],
-        out_space=[VMEM, HBM],
-        flops=3e9,
+        flops=2e9,
     )(updated, attn_proj)
+    dealt, mixed, late = lax.optimization_barrier((dealt, mixed, late))
+    bias = lax.all_to_all(
+        dealt, BOTH, split_axis=0, concat_axis=0, axis_index_groups=one_core, tiled=True
+    )
     bias, *others = lax.optimization_barrier((bias, *others))
-    late, *keys = call(
+    keys = call(
         other_body,
         "other_keys",
-        [shape(key_shape, BF16)] * (1 + len(others)),
-        2 + len(others),
-        [pltpu.SemaphoreType.DMA(())],
-        specs=[HBM] + [VMEM] * (1 + len(others)),
+        [shape(key_shape, BF16)] * len(others),
+        1 + len(others),
         flops=3e9,
-    )(in_hbm(late), attn_proj, *others)
+    )(attn_proj, *others)
     (result,) = call(
         attend_body,
         "attend",

time: 74.9 us -> 74.5 us (level)
  blocking collectives: 12.1 us -> 21.8 us
  waiting for transfers between devices: 17.8 us -> 13.7 us
  starting transfers between devices: 24.2 us -> 20.8 us
  Pallas kernels: 17.6 us -> 15.8 us
  local copies, waits for them, and re-layouts: 2 us -> 1.21 us
    all_to_all x0 -> x1, blocking collectives: none -> 9.75 us  [local(): lax.all_to_all(dealt, BOTH, split_axis=0, concat_axis=0, axis_index_group...]
    all_to_all x1 -> x0, waiting for transfers between devices: 4.07 us -> none  [local(): lax.all_to_all(dealt, BOTH, split_axis=0, concat_axis=0, axis_index_group...]
    all_to_all x1 -> x0, starting transfers between devices: 3.37 us -> none  [local(): lax.all_to_all(dealt, BOTH, split_axis=0, concat_axis=0, axis_index_group...]
    unnamed x19 -> x15, local copies, waits for them, and re-layouts: 2 us -> 1.21 us
    pallas_call x1, Pallas kernels: 1.95 us -> 1.16 us  [local(): call(functools.partial(own_body, score_scale=(channels // heads) ** (-0.5...]
  transfers between devices with their start and end apart: 13 -> 12, of which waited for: 10 -> 9; matrix products, arithmetic and copies ran while one was open for 0% -> 0% of each run, Pallas kernels for 10% -> 8%
where the time goes in v7:
time: 74.5 us; the launch traced here: 74.1 us
  blocking collectives  21.8 us (29%)
  starting transfers between devices  20.8 us (28%)
  Pallas kernels  15.8 us (21%)
  waiting for transfers between devices  13.7 us (18%)
  local copies, waits for them, and re-layouts  1.21 us (2%)
  between operations  0.77 us (1%)
    ppermute x10, waiting for transfers between devices, flipped(): return lax.ppermute(array, BOTH, [(d, d ^ bits) for d in range(devices)])  13.7 us
    all_to_all x1, blocking collectives, in_half(): lax.all_to_all(array, BOTH, split_axis=0, concat_axis=0, axis_index_group...  12.1 us
    ppermute x10, starting transfers between devices, flipped(): return lax.ppermute(array, BOTH, [(d, d ^ bits) for d in range(devices)])  11.7 us
    all_to_all x1, blocking collectives, local(): lax.all_to_all(dealt, BOTH, split_axis=0, concat_axis=0, axis_index_group...  9.75 us
    all_to_all x1, starting transfers between devices, local(): right = lax.all_to_all(right, BOTH, split_axis=0, concat_axis=0, tiled=True)  7.3 us
    pallas_call x2, Pallas kernels, edges(): call(functools.partial(edges_body, side=side), 'right_edges' if side else...  5.38 us
    pallas_call x1, Pallas kernels, local(): call(attend_body, 'attend', [shape(block, BF16)], 5 + col_devices, [pltpu...  4.67 us
    ppermute x1, starting transfers between devices, local(): lax.ppermute(updated, 'ch', [((c + s) % col_devices, c) for c in range(co...  1.75 us
  transfers between devices with their start and end apart: 12, of which 9 were waited for; matrix products, arithmetic and copies ran while one was open for 0% of the time, Pallas kernels for 8%

profile of v7, /device:TPU:0, one launch (start us, length us, event | category | flops | bytes accessed | tf_op | source)
XLA Modules:
  0.0 74.1 jit_solution(1880339007628160521)
XLA Ops:
  0.7 3.3 %right_edges.1 = (bf16[32,8,16,128]{3,2,1,0:T(8,128)(2,1)}, bf16[16,128,128]{2,1,0:T(8,128)(2,1)}) custom-call(s32[1]{0:T(128)S(6)} %copy.11.length, bf16[16,128,128]{2,1,0:T(8,128)(2,1)} %pair.1, bf16[128,256]{1,0:T(8,128)(2,1)} %proj_hbm.3, bf16[128,256]{1,0:T(8,128)(2,1)} %gate_hbm.3), custom_call_target="tpu_custom_call" | custom-call | flops 3000000000 | bytes 3145728 | tf_op jit(solution)/shard_map/right_edges/pallas_call | solution.py:389
  4.0 7.3 %all-to-all-start = ((bf16[32,8,16,128]{3,2,1,0:T(8,128)(2,1)}), bf16[32,8,16,128]{3,2,1,0:T(8,128)(2,1)S(1)}, u32[]{:S(2)}, u32[]{:S(2)}) async-start(bf16[32,8,16,128]{3,2,1,0:T(8,128)(2,1)} %get-tuple-element.40), calls=%async_computation | async-start | bytes 2097152 | tf_op jit(solution)/shard_map/all_to_all | solution.py:412
  11.3 2.0 %left_edges.1 = (bf16[8,8,16,128]{3,2,1,0:T(8,128)(2,1)S(1)}, bf16[8,8,16,128]{3,2,1,0:T(8,128)(2,1)S(1)}) custom-call(s32[1]{0:T(128)S(6)} %copy.11.length, bf16[16,128,128]{2,1,0:T(8,128)(2,1)} %get-tuple-element.41.normed.source_hbm, bf16[128,256]{1,0:T(8,128)(2,1)} %proj_hbm.3, bf16[128,256]{1,0:T(8,128)(2,1)} %gate_hbm.3), custom_call_target="tpu_custom_call" | custom-call | flops 3000000000 | bytes 1048576 | tf_op jit(solution)/shard_map/left_edges/pallas_call | solution.py:389
  13.7 1.3 %collective-permute-done.sibling = bf16[8,8,16,128]{3,2,1,0:T(8,128)(2,1)S(1)} collective-permute-done((bf16[8,8,16,128]{3,2,1,0:T(8,128)(2,1)S(1)}, bf16[8,8,16,128]{3,2,1,0:T(8,128)(2,1)S(1)}, u32[]{:S(2)}, u32[]{:S(2)}) %collective-permute-start) | collective-permute-done | bytes 262176 | tf_op jit(solution)/shard_map/ppermute | solution.py:409
  15.1 1.8 %collective-permute-start.1 = (bf16[2,8,16,128]{3,2,1,0:T(8,128)(2,1)S(1)}, bf16[2,8,16,128]{3,2,1,0:T(8,128)(2,1)S(1)}, u32[]{:S(2)}, u32[]{:S(2)}) collective-permute-start(bf16[2,8,16,128]{3,2,1,0:T(8,128)(2,1)S(1)} %get-tuple-element.48), channel_id=1, source_target_pairs={{0,1},{1,0},{2,3},{3,2},{4,5},{5,4},{6,7},{7,6},{8,9},{9,8},{10,11... | collective-permute-start | bytes 196616 | tf_op jit(solution)/shard_map/ppermute | solution.py:409
  16.9 1.5 %collective-permute-start.2 = (bf16[2,8,16,128]{3,2,1,0:T(8,128)(2,1)S(1)}, bf16[2,8,16,128]{3,2,1,0:T(8,128)(2,1)S(1)}, u32[]{:S(2)}, u32[]{:S(2)}) collective-permute-start(bf16[2,8,16,128]{3,2,1,0:T(8,128)(2,1)S(1)} %get-tuple-element.49), channel_id=1, source_target_pairs={{0,4},{1,5},{2,6},{3,7},{4,0},{5,1},{6,2},{7,3},{8,12},{9,13},{10,... | collective-permute-start | bytes 196616 | tf_op jit(solution)/shard_map/ppermute | solution.py:409
  18.8 1.8 %collective-permute-start.4 = (bf16[2,8,16,128]{3,2,1,0:T(8,128)(2,1)S(1)}, bf16[2,8,16,128]{3,2,1,0:T(8,128)(2,1)S(1)}, u32[]{:S(2)}, u32[]{:S(2)}) collective-permute-start(bf16[2,8,16,128]{3,2,1,0:T(8,128)(2,1)S(1)} %get-tuple-element.51), channel_id=1, source_target_pairs={{0,8},{1,9},{2,10},{3,11},{4,12},{5,13},{6,14},{7,15},{8,0},{9,1},... | collective-permute-start | bytes 196616 | tf_op jit(solution)/shard_map/ppermute | solution.py:409
  20.6 1.5 %collective-permute-start.5 = (bf16[2,8,16,128]{3,2,1,0:T(8,128)(2,1)S(1)}, bf16[2,8,16,128]{3,2,1,0:T(8,128)(2,1)S(1)}, u32[]{:S(2)}, u32[]{:S(2)}) collective-permute-start(bf16[2,8,16,128]{3,2,1,0:T(8,128)(2,1)S(1)} %get-tuple-element.52), channel_id=1, source_target_pairs={{0,9},{1,8},{2,11},{3,10},{4,13},{5,12},{6,15},{7,14},{8,1},{9,0},... | collective-permute-start | bytes 196616 | tf_op jit(solution)/shard_map/ppermute | solution.py:409
  22.0 1.3 %collective-permute-done.1.rest_1_ = bf16[2,8,16,128]{3,2,1,0:T(8,128)(2,1)S(1)} collective-permute-done((bf16[2,8,16,128]{3,2,1,0:T(8,128)(2,1)S(1)}, bf16[2,8,16,128]{3,2,1,0:T(8,128)(2,1)S(1)}, u32[]{:S(2)}, u32[]{:S(2)}) %collective-permute-start.1) | collective-permute-done | bytes 65568 | tf_op jit(solution)/shard_map/ppermute | solution.py:409
  23.3 1.1 %collective-permute-start.6 = (bf16[2,8,16,128]{3,2,1,0:T(8,128)(2,1)S(1)}, bf16[2,8,16,128]{3,2,1,0:T(8,128)(2,1)S(1)}, u32[]{:S(2)}, u32[]{:S(2)}) collective-permute-start(bf16[2,8,16,128]{3,2,1,0:T(8,128)(2,1)S(1)} %get-tuple-element.53), channel_id=1, source_target_pairs={{0,12},{1,13},{2,14},{3,15},{4,8},{5,9},{6,10},{7,11},{8,4},{9,5},... | collective-permute-start | bytes 196616 | tf_op jit(solution)/shard_map/ppermute | solution.py:409
  25.9 1.0 %copy-done.5 = bf16[16,128,128]{2,1,0:T(8,128)(2,1)S(1)} copy-done((bf16[16,128,128]{2,1,0:T(8,128)(2,1)S(1)}, bf16[16,128,128]{2,1,0:T(8,128)(2,1)}, u32[]{:S(2)}) %copy-start.5) | copy-done | bytes 524312
  26.9 1.6 %tri_gate.1 = (bf16[16,128,128]{2,1,0:T(8,128)(2,1)S(1)}, bf16[16,128,128]{2,1,0:T(8,128)(2,1)S(1)}, bf16[4,128]{1,0:T(4,128)(2,1)S(1)}) custom-call(bf16[16,128,128]{2,1,0:T(8,128)(2,1)S(1)} %copy-done.1, bf16[16,128,128]{2,1,0:T(8,128)(2,1)S(1)} %copy-done.5, bf16[128,128]{1,0:T(8,128)(2,1)S(1)} %copy-done.3, bf16[128,4]{1,0:T(8,128)(2,1)S(1)} %copy.10.bias_proj), custom_call_target="tpu_custom_call" | custom-call | flops 2000000000 | bytes 2099200 | tf_op jit(solution)/shard_map/tri_gate/pallas_call | solution.py:418
  28.5 2.2 %collective-permute-done.4.rest_4_ = bf16[2,8,16,128]{3,2,1,0:T(8,128)(2,1)S(1)} collective-permute-done((bf16[2,8,16,128]{3,2,1,0:T(8,128)(2,1)S(1)}, bf16[2,8,16,128]{3,2,1,0:T(8,128)(2,1)S(1)}, u32[]{:S(2)}, u32[]{:S(2)}) %collective-permute-start.4) | collective-permute-done | bytes 65568 | tf_op jit(solution)/shard_map/ppermute | solution.py:409
  30.7 1.5 %collective-permute-done.5.rest_5_ = bf16[2,8,16,128]{3,2,1,0:T(8,128)(2,1)S(1)} collective-permute-done((bf16[2,8,16,128]{3,2,1,0:T(8,128)(2,1)S(1)}, bf16[2,8,16,128]{3,2,1,0:T(8,128)(2,1)S(1)}, u32[]{:S(2)}, u32[]{:S(2)}) %collective-permute-start.5) | collective-permute-done | bytes 65568 | tf_op jit(solution)/shard_map/ppermute | solution.py:409
  32.2 2.7 %collective-permute-done.6.rest_6_ = bf16[2,8,16,128]{3,2,1,0:T(8,128)(2,1)S(1)} collective-permute-done((bf16[2,8,16,128]{3,2,1,0:T(8,128)(2,1)S(1)}, bf16[2,8,16,128]{3,2,1,0:T(8,128)(2,1)S(1)}, u32[]{:S(2)}, u32[]{:S(2)}) %collective-permute-start.6) | collective-permute-done | bytes 65568 | tf_op jit(solution)/shard_map/ppermute | solution.py:409
  34.9 2.9 %collective-permute-done.7.rest_7_ = bf16[2,8,16,128]{3,2,1,0:T(8,128)(2,1)S(1)} collective-permute-done((bf16[2,8,16,128]{3,2,1,0:T(8,128)(2,1)S(1)}, bf16[2,8,16,128]{3,2,1,0:T(8,128)(2,1)S(1)}, u32[]{:S(2)}, u32[]{:S(2)}) %collective-permute-start.7) | collective-permute-done | bytes 65568 | tf_op jit(solution)/shard_map/ppermute | solution.py:409
  38.2 12.1 %all_to_all.15 = bf16[16,8,16,128]{3,2,1,0:T(8,128)(2,1)S(1)} all-to-all(bf16[16,8,16,128]{3,2,1,0:T(8,128)(2,1)S(1)} %bitcast.4), channel_id=1, replica_groups={{15,14,13,12,11,10,9,8,7,6,5,4,3,2,1,0},{31,30,29,28,27,26,25,24,23,22,..., dimensions={0} | all-to-all | bytes 1048576 | tf_op jit(solution)/shard_map/all_to_all | solution.py:378
  50.3 1.6 %update.1 = (bf16[16,128,128]{2,1,0:T(8,128)(2,1)S(1)}, bf16[4,16,128]{2,1,0:T(8,128)(2,1)S(1)}) custom-call(bf16[128,16,128]{2,1,0:T(8,128)(2,1)S(1)} %bitcast.5, bf16[16,128,128]{2,1,0:T(8,128)(2,1)S(1)} %get-tuple-element.63.source, bf16[16,128,128]{2,1,0:T(8,128)(2,1)S(1)} %get-tuple-element.64.gate, bf16[128,128]{1,0:T(8,128)(2,1)S(1)} %copy-done.4, ...), custom_call_target="tpu_custom_call" | custom-call | flops 2000000000 | bytes 1081344 | tf_op jit(solution)/shard_map/update/pallas_call | solution.py:438
  51.9 1.7 %collective-permute-start.9 = (bf16[16,128,128]{2,1,0:T(8,128)(2,1)S(1)}, bf16[16,128,128]{2,1,0:T(8,128)(2,1)S(1)}, u32[]{:S(2)}, u32[]{:S(2)}) collective-permute-start(bf16[16,128,128]{2,1,0:T(8,128)(2,1)S(1)} %get-tuple-element.67.updated), channel_id=1, source_target_pairs={{1,0},{0,1},{3,2},{2,3},{5,4},{4,5},{7,6},{6,7},{9,8},{8,9},{11,10... | collective-permute-start | bytes 1572872 | tf_op jit(solution)/shard_map/ppermute | solution.py:460
  53.6 2.9 %collective-permute-start.8 = (bf16[4,16,128]{2,1,0:T(8,128)(2,1)S(1)}, bf16[4,16,128]{2,1,0:T(8,128)(2,1)S(1)}, u32[]{:S(2)}, u32[]{:S(2)}) collective-permute-start(bf16[4,16,128]{2,1,0:T(8,128)(2,1)S(1)} %get-tuple-element.66.refs_0_), channel_id=1, source_target_pairs={{0,16},{1,17},{2,18},{3,19},{4,20},{5,21},{6,22},{7,23},{8,24},{9,... | collective-permute-start | bytes 49160 | tf_op jit(solution)/shard_map/ppermute | solution.py:409
  56.6 1.2 %own_projections.1 = (bf16[16,128,384]{2,1,0:T(8,128)(2,1)S(1)}, bf16[16,128,256]{2,1,0:T(8,128)(2,1)S(1)}) custom-call(bf16[16,128,128]{2,1,0:T(8,128)(2,1)S(1)} %get-tuple-element.67.updated, bf16[128,512]{1,0:T(8,128)(2,1)S(1)} %copy-done.2), custom_call_target="tpu_custom_call" | custom-call | flops 2000000000 | bytes 5242880 | tf_op jit(solution)/shard_map/own_projections/pallas_call | solution.py:465
  58.3 9.8 %all_to_all.16.mine = bf16[8,4,16,128]{3,2,1,0:T(8,128)(2,1)S(1)} all-to-all(bf16[8,4,16,128]{3,2,1,0:T(8,128)(2,1)S(1)} %deal_bias.1), channel_id=1, replica_groups={{0,1,4,5,8,9,12,13},{2,3,6,7,10,11,14,15},{16,17,20,21,24,25,28,29},{18..., dimensions={0} | all-to-all | bytes 262144 | tf_op jit(solution)/shard_map/all_to_all | solution.py:473
  68.1 0.9 %other_keys.1.rest_1_ = bf16[16,128,256]{2,1,0:T(8,128)(2,1)S(1)} custom-call(bf16[128,512]{1,0:T(8,128)(2,1)S(1)} %copy-done.2, bf16[16,128,128]{2,1,0:T(8,128)(2,1)S(1)} %collective-permute-done.9.rest_0_), custom_call_target="tpu_custom_call" | custom-call | flops 3000000000 | bytes 2097152 | tf_op jit(solution)/shard_map/other_keys/pallas_call | solution.py:477
  69.4 4.7 %attend.1 = bf16[16,128,128]{2,1,0:T(8,128)(2,1)} custom-call(s32[1]{0:T(128)S(6)} %copy.11.length, bf16[8,4,16,128]{3,2,1,0:T(8,128)(2,1)S(1)} %all_to_all.16.mine, bf16[8,4,16,128]{3,2,1,0:T(8,128)(2,1)S(1)} %collective-permute-done.10.sibling, bf16[128,128]{1,0:T(8,128)(2,1)S(1)} %copy-done, bf16[16,128,256]{2,1,0:T(8,128)(2,1)S(1)} %get-tuple-element.72.late, ...), custom_call_target="tpu_custom_call" | custom-call | flops 100000000 | bytes 1048576 | tf_op jit(solution)/shard_map/attend/pallas_call | solution.py:484
  (27 shorter events, 3.8 us)
Async XLA Ops:
  4.0 33.7 %all-to-all-start = ((bf16[32,8,16,128]{3,2,1,0:T(8,128)(2,1)}), bf16[32,8,16,128]{3,2,1,0:T(8,128)(2,1)S(1)}, u32[]{:S(2)}, u32[]{:S(2)}) async-start(bf16[32,8,16,128]{3,2,1,0:T(8,128)(2,1)} %get-tuple-element.40), calls=%async_computation | async-start | bytes 2097152 | tf_op jit(solution)/shard_map/all_to_all | solution.py:412
  11.3 7.0 %copy-start.6 = (bf16[128,4]{0,1:T(4,128)(2,1)S(1)}, bf16[128,4]{0,1:T(4,128)(2,1)}, u32[]{:S(2)}) copy-start(bf16[128,4]{0,1:T(4,128)(2,1)} %param.16) | copy-start | bytes 3076
  11.3 14.5 %copy-start.1 = (bf16[16,128,128]{2,1,0:T(8,128)(2,1)S(1)}, bf16[16,128,128]{2,1,0:T(8,128)(2,1)}, u32[]{:S(2)}) copy-start(bf16[16,128,128]{2,1,0:T(8,128)(2,1)} %pair.1) | copy-start | bytes 1572868
  11.3 14.5 %copy-start.3 = (bf16[128,128]{1,0:T(8,128)(2,1)S(1)}, bf16[128,128]{1,0:T(8,128)(2,1)}, u32[]{:S(2)}) copy-start(bf16[128,128]{1,0:T(8,128)(2,1)} %weights.1) | copy-start | bytes 98308
  13.4 1.6 %collective-permute-start = (bf16[8,8,16,128]{3,2,1,0:T(8,128)(2,1)S(1)}, bf16[8,8,16,128]{3,2,1,0:T(8,128)(2,1)S(1)}, u32[]{:S(2)}, u32[]{:S(2)}) collective-permute-start(bf16[8,8,16,128]{3,2,1,0:T(8,128)(2,1)S(1)} %get-tuple-element.46), channel_id=1, source_target_pairs={{0,2},{1,3},{2,0},{3,1},{4,6},{5,7},{6,4},{7,5},{8,10},{9,11},{10,... | collective-permute-start | bytes 786440 | tf_op jit(solution)/shard_map/ppermute | solution.py:409
  15.1 8.3 %collective-permute-start.1 = (bf16[2,8,16,128]{3,2,1,0:T(8,128)(2,1)S(1)}, bf16[2,8,16,128]{3,2,1,0:T(8,128)(2,1)S(1)}, u32[]{:S(2)}, u32[]{:S(2)}) collective-permute-start(bf16[2,8,16,128]{3,2,1,0:T(8,128)(2,1)S(1)} %get-tuple-element.48), channel_id=1, source_target_pairs={{0,1},{1,0},{2,3},{3,2},{4,5},{5,4},{6,7},{7,6},{8,9},{9,8},{10,11... | collective-permute-start | bytes 196616 | tf_op jit(solution)/shard_map/ppermute | solution.py:409
  16.9 8.4 %collective-permute-start.2 = (bf16[2,8,16,128]{3,2,1,0:T(8,128)(2,1)S(1)}, bf16[2,8,16,128]{3,2,1,0:T(8,128)(2,1)S(1)}, u32[]{:S(2)}, u32[]{:S(2)}) collective-permute-start(bf16[2,8,16,128]{3,2,1,0:T(8,128)(2,1)S(1)} %get-tuple-element.49), channel_id=1, source_target_pairs={{0,4},{1,5},{2,6},{3,7},{4,0},{5,1},{6,2},{7,3},{8,12},{9,13},{10,... | collective-permute-start | bytes 196616 | tf_op jit(solution)/shard_map/ppermute | solution.py:409
  18.5 10.0 %collective-permute-start.3 = (bf16[2,8,16,128]{3,2,1,0:T(8,128)(2,1)S(1)}, bf16[2,8,16,128]{3,2,1,0:T(8,128)(2,1)S(1)}, u32[]{:S(2)}, u32[]{:S(2)}) collective-permute-start(bf16[2,8,16,128]{3,2,1,0:T(8,128)(2,1)S(1)} %get-tuple-element.50), channel_id=1, source_target_pairs={{0,5},{1,4},{2,7},{3,6},{4,1},{5,0},{6,3},{7,2},{8,13},{9,12},{10,... | collective-permute-start | bytes 196616 | tf_op jit(solution)/shard_map/ppermute | solution.py:409
  18.8 11.9 %collective-permute-start.4 = (bf16[2,8,16,128]{3,2,1,0:T(8,128)(2,1)S(1)}, bf16[2,8,16,128]{3,2,1,0:T(8,128)(2,1)S(1)}, u32[]{:S(2)}, u32[]{:S(2)}) collective-permute-start(bf16[2,8,16,128]{3,2,1,0:T(8,128)(2,1)S(1)} %get-tuple-element.51), channel_id=1, source_target_pairs={{0,8},{1,9},{2,10},{3,11},{4,12},{5,13},{6,14},{7,15},{8,0},{9,1},... | collective-permute-start | bytes 196616 | tf_op jit(solution)/shard_map/ppermute | solution.py:409
  20.6 11.6 %collective-permute-start.5 = (bf16[2,8,16,128]{3,2,1,0:T(8,128)(2,1)S(1)}, bf16[2,8,16,128]{3,2,1,0:T(8,128)(2,1)S(1)}, u32[]{:S(2)}, u32[]{:S(2)}) collective-permute-start(bf16[2,8,16,128]{3,2,1,0:T(8,128)(2,1)S(1)} %get-tuple-element.52), channel_id=1, source_target_pairs={{0,9},{1,8},{2,11},{3,10},{4,13},{5,12},{6,15},{7,14},{8,1},{9,0},... | collective-permute-start | bytes 196616 | tf_op jit(solution)/shard_map/ppermute | solution.py:409
  23.3 11.5 %collective-permute-start.6 = (bf16[2,8,16,128]{3,2,1,0:T(8,128)(2,1)S(1)}, bf16[2,8,16,128]{3,2,1,0:T(8,128)(2,1)S(1)}, u32[]{:S(2)}, u32[]{:S(2)}) collective-permute-start(bf16[2,8,16,128]{3,2,1,0:T(8,128)(2,1)S(1)} %get-tuple-element.53), channel_id=1, source_target_pairs={{0,12},{1,13},{2,14},{3,15},{4,8},{5,9},{6,10},{7,11},{8,4},{9,5},... | collective-permute-start | bytes 196616 | tf_op jit(solution)/shard_map/ppermute | solution.py:409
  25.3 12.5 %collective-permute-start.7 = (bf16[2,8,16,128]{3,2,1,0:T(8,128)(2,1)S(1)}, bf16[2,8,16,128]{3,2,1,0:T(8,128)(2,1)S(1)}, u32[]{:S(2)}, u32[]{:S(2)}) collective-permute-start(bf16[2,8,16,128]{3,2,1,0:T(8,128)(2,1)S(1)} %get-tuple-element.54), channel_id=1, source_target_pairs={{0,13},{1,12},{2,15},{3,14},{4,9},{5,8},{6,11},{7,10},{8,5},{9,4},... | collective-permute-start | bytes 196616 | tf_op jit(solution)/shard_map/ppermute | solution.py:409
  25.9 1.0 %copy-start.5 = (bf16[16,128,128]{2,1,0:T(8,128)(2,1)S(1)}, bf16[16,128,128]{2,1,0:T(8,128)(2,1)}, u32[]{:S(2)}) copy-start(bf16[16,128,128]{2,1,0:T(8,128)(2,1)} %get-tuple-element.41.normed.source_hbm) | copy-start | bytes 1572868
  37.7 12.6 %copy-start.4 = (bf16[128,128]{1,0:T(8,128)(2,1)S(1)}, bf16[128,128]{1,0:T(8,128)(2,1)}, u32[]{:S(2)}) copy-start(bf16[128,128]{1,0:T(8,128)(2,1)} %tri_out.1) | copy-start | bytes 98308
  50.3 6.2 %copy-start.2 = (bf16[128,512]{1,0:T(8,128)(2,1)S(1)}, bf16[128,512]{1,0:T(8,128)(2,1)}, u32[]{:S(2)}) copy-start(bf16[128,512]{1,0:T(8,128)(2,1)} %attn_proj.3) | copy-start | bytes 393220
  51.9 16.2 %collective-permute-start.9 = (bf16[16,128,128]{2,1,0:T(8,128)(2,1)S(1)}, bf16[16,128,128]{2,1,0:T(8,128)(2,1)S(1)}, u32[]{:S(2)}, u32[]{:S(2)}) collective-permute-start(bf16[16,128,128]{2,1,0:T(8,128)(2,1)S(1)} %get-tuple-element.67.updated), channel_id=1, source_target_pairs={{1,0},{0,1},{3,2},{2,3},{5,4},{4,5},{7,6},{6,7},{9,8},{8,9},{11,10... | collective-permute-start | bytes 1572872 | tf_op jit(solution)/shard_map/ppermute | solution.py:460
  53.6 4.6 %collective-permute-start.8 = (bf16[4,16,128]{2,1,0:T(8,128)(2,1)S(1)}, bf16[4,16,128]{2,1,0:T(8,128)(2,1)S(1)}, u32[]{:S(2)}, u32[]{:S(2)}) collective-permute-start(bf16[4,16,128]{2,1,0:T(8,128)(2,1)S(1)} %get-tuple-element.66.refs_0_), channel_id=1, source_target_pairs={{0,16},{1,17},{2,18},{3,19},{4,20},{5,21},{6,22},{7,23},{8,24},{9,... | collective-permute-start | bytes 49160 | tf_op jit(solution)/shard_map/ppermute | solution.py:409
  68.1 1.4 %copy-start = (bf16[128,128]{1,0:T(8,128)(2,1)S(1)}, bf16[128,128]{1,0:T(8,128)(2,1)}, u32[]{:S(2)}) copy-start(bf16[128,128]{1,0:T(8,128)(2,1)} %attn_out.1) | copy-start | bytes 98308
  68.1 1.3 %collective-permute-start.10 = (bf16[8,4,16,128]{3,2,1,0:T(8,128)(2,1)S(1)}, bf16[8,4,16,128]{3,2,1,0:T(8,128)(2,1)S(1)}, u32[]{:S(2)}, u32[]{:S(2)}) collective-permute-start(bf16[8,4,16,128]{3,2,1,0:T(8,128)(2,1)S(1)} %all_to_all.16.mine), channel_id=1, source_target_pairs={{0,2},{1,3},{2,0},{3,1},{4,6},{5,7},{6,4},{7,5},{8,10},{9,11},{10,... | collective-permute-start | bytes 393224 | tf_op jit(solution)/shard_map/ppermute | solution.py:409

commit v8 on v7

--- a/solution.py
+++ b/solution.py
@@ -248,7 +248,7 @@
         bias_held[pl.ds(row, heads, stride=rows), :] = dot(bias_weights, normed, (1, 0))
         return carry
 
-    lax.fori_loop(0, rows, step, 0, unroll=8)
+    lax.fori_loop(0, rows, step, 0, unroll=rows)
     bias[...] = bias_held[...].astype(BF16).reshape(heads, rows, cols)
 
 
@@ -331,17 +331,6 @@
     per_chunk = rows // count
     loaded, logits, weights = {}, {}, {}
     for time in range(rows + 2):
-        row = time
-        if row < rows:
-            loaded[row] = load(row)
-            keys, _, query = loaded[row]
-            queries = jnp.concatenate([query * mask for mask in masks], axis=0)
-            logits[row] = dot(queries, keys, (1, 0)) + bias_held[...]
-        row = time - 1
-        if 0 <= row < rows:
-            scores = logits.pop(row)
-            top = jnp.max(scores, axis=-1, keepdims=True)
-            weights[row] = jnp.exp((scores - top).astype(BF16))
         row = time - 2
         if row >= 0:
             sums = dot(weights.pop(row), loaded.pop(row)[1], (1, 0))
@@ -353,6 +342,17 @@
             if place_in == per_chunk - 1:
                 for copy in sends[chunk]:
                     copy.start()
+        row = time - 1
+        if 0 <= row < rows:
+            scores = logits.pop(row)
+            top = jnp.max(scores, axis=-1, keepdims=True)
+            weights[row] = jnp.exp((scores - top).astype(BF16))
+        row = time
+        if row < rows:
+            loaded[row] = load(row)
+            keys, _, query = loaded[row]
+            queries = jnp.concatenate([query * mask for mask in masks], axis=0)
+            logits[row] = dot(queries, keys, (1, 0)) + bias_held[...]
     for send in sends:
         for copy in send:
             copy.wait()

time: 74.5 us -> 74.4 us (level)
  no operation moved by 1% of the time
where the time goes in v8:
time: 74.4 us; the launch traced here: 74 us
  blocking collectives  21.8 us (29%)
  starting transfers between devices  20.8 us (28%)
  Pallas kernels  15.7 us (21%)
  waiting for transfers between devices  13.7 us (18%)
  local copies, waits for them, and re-layouts  1.21 us (2%)
  between operations  0.77 us (1%)
    ppermute x10, waiting for transfers between devices, flipped(): return lax.ppermute(array, BOTH, [(d, d ^ bits) for d in range(devices)])  13.7 us
    all_to_all x1, blocking collectives, in_half(): lax.all_to_all(array, BOTH, split_axis=0, concat_axis=0, axis_index_group...  12.1 us
    ppermute x10, starting transfers between devices, flipped(): return lax.ppermute(array, BOTH, [(d, d ^ bits) for d in range(devices)])  11.7 us
    all_to_all x1, blocking collectives, local(): lax.all_to_all(dealt, BOTH, split_axis=0, concat_axis=0, axis_index_group...  9.75 us
    all_to_all x1, starting transfers between devices, local(): right = lax.all_to_all(right, BOTH, split_axis=0, concat_axis=0, tiled=True)  7.3 us
    pallas_call x2, Pallas kernels, edges(): call(functools.partial(edges_body, side=side), 'right_edges' if side else...  5.38 us
    pallas_call x1, Pallas kernels, local(): call(attend_body, 'attend', [shape(block, BF16)], 5 + col_devices, [pltpu...  4.79 us
    ppermute x1, starting transfers between devices, local(): lax.ppermute(updated, 'ch', [((c + s) % col_devices, c) for c in range(co...  1.74 us
  transfers between devices with their start and end apart: 12, of which 9 were waited for; matrix products, arithmetic and copies ran while one was open for 0% of the time, Pallas kernels for 8%

profile of v8, /device:TPU:0, one launch (start us, length us, event | category | flops | bytes accessed | tf_op | source)
XLA Modules:
  0.0 74.0 jit_solution(16424321157265127370)
XLA Ops:
  0.7 3.3 %right_edges.1 = (bf16[32,8,16,128]{3,2,1,0:T(8,128)(2,1)}, bf16[16,128,128]{2,1,0:T(8,128)(2,1)}) custom-call(s32[1]{0:T(128)S(6)} %copy.11.length, bf16[16,128,128]{2,1,0:T(8,128)(2,1)} %pair.1, bf16[128,256]{1,0:T(8,128)(2,1)} %proj_hbm.3, bf16[128,256]{1,0:T(8,128)(2,1)} %gate_hbm.3), custom_call_target="tpu_custom_call" | custom-call | flops 3000000000 | bytes 3145728 | tf_op jit(solution)/shard_map/right_edges/pallas_call | solution.py:389
  4.0 7.3 %all-to-all-start = ((bf16[32,8,16,128]{3,2,1,0:T(8,128)(2,1)}), bf16[32,8,16,128]{3,2,1,0:T(8,128)(2,1)S(1)}, u32[]{:S(2)}, u32[]{:S(2)}) async-start(bf16[32,8,16,128]{3,2,1,0:T(8,128)(2,1)} %get-tuple-element.40), calls=%async_computation | async-start | bytes 2097152 | tf_op jit(solution)/shard_map/all_to_all | solution.py:412
  11.3 2.0 %left_edges.1 = (bf16[8,8,16,128]{3,2,1,0:T(8,128)(2,1)S(1)}, bf16[8,8,16,128]{3,2,1,0:T(8,128)(2,1)S(1)}) custom-call(s32[1]{0:T(128)S(6)} %copy.11.length, bf16[16,128,128]{2,1,0:T(8,128)(2,1)} %get-tuple-element.41.normed.source_hbm, bf16[128,256]{1,0:T(8,128)(2,1)} %proj_hbm.3, bf16[128,256]{1,0:T(8,128)(2,1)} %gate_hbm.3), custom_call_target="tpu_custom_call" | custom-call | flops 3000000000 | bytes 1048576 | tf_op jit(solution)/shard_map/left_edges/pallas_call | solution.py:389
  13.7 1.3 %collective-permute-done.sibling = bf16[8,8,16,128]{3,2,1,0:T(8,128)(2,1)S(1)} collective-permute-done((bf16[8,8,16,128]{3,2,1,0:T(8,128)(2,1)S(1)}, bf16[8,8,16,128]{3,2,1,0:T(8,128)(2,1)S(1)}, u32[]{:S(2)}, u32[]{:S(2)}) %collective-permute-start) | collective-permute-done | bytes 262176 | tf_op jit(solution)/shard_map/ppermute | solution.py:409
  15.1 1.8 %collective-permute-start.1 = (bf16[2,8,16,128]{3,2,1,0:T(8,128)(2,1)S(1)}, bf16[2,8,16,128]{3,2,1,0:T(8,128)(2,1)S(1)}, u32[]{:S(2)}, u32[]{:S(2)}) collective-permute-start(bf16[2,8,16,128]{3,2,1,0:T(8,128)(2,1)S(1)} %get-tuple-element.48), channel_id=1, source_target_pairs={{0,1},{1,0},{2,3},{3,2},{4,5},{5,4},{6,7},{7,6},{8,9},{9,8},{10,11... | collective-permute-start | bytes 196616 | tf_op jit(solution)/shard_map/ppermute | solution.py:409
  16.9 1.5 %collective-permute-start.2 = (bf16[2,8,16,128]{3,2,1,0:T(8,128)(2,1)S(1)}, bf16[2,8,16,128]{3,2,1,0:T(8,128)(2,1)S(1)}, u32[]{:S(2)}, u32[]{:S(2)}) collective-permute-start(bf16[2,8,16,128]{3,2,1,0:T(8,128)(2,1)S(1)} %get-tuple-element.49), channel_id=1, source_target_pairs={{0,4},{1,5},{2,6},{3,7},{4,0},{5,1},{6,2},{7,3},{8,12},{9,13},{10,... | collective-permute-start | bytes 196616 | tf_op jit(solution)/shard_map/ppermute | solution.py:409
  18.8 1.8 %collective-permute-start.4 = (bf16[2,8,16,128]{3,2,1,0:T(8,128)(2,1)S(1)}, bf16[2,8,16,128]{3,2,1,0:T(8,128)(2,1)S(1)}, u32[]{:S(2)}, u32[]{:S(2)}) collective-permute-start(bf16[2,8,16,128]{3,2,1,0:T(8,128)(2,1)S(1)} %get-tuple-element.51), channel_id=1, source_target_pairs={{0,8},{1,9},{2,10},{3,11},{4,12},{5,13},{6,14},{7,15},{8,0},{9,1},... | collective-permute-start | bytes 196616 | tf_op jit(solution)/shard_map/ppermute | solution.py:409
  20.6 1.5 %collective-permute-start.5 = (bf16[2,8,16,128]{3,2,1,0:T(8,128)(2,1)S(1)}, bf16[2,8,16,128]{3,2,1,0:T(8,128)(2,1)S(1)}, u32[]{:S(2)}, u32[]{:S(2)}) collective-permute-start(bf16[2,8,16,128]{3,2,1,0:T(8,128)(2,1)S(1)} %get-tuple-element.52), channel_id=1, source_target_pairs={{0,9},{1,8},{2,11},{3,10},{4,13},{5,12},{6,15},{7,14},{8,1},{9,0},... | collective-permute-start | bytes 196616 | tf_op jit(solution)/shard_map/ppermute | solution.py:409
  22.0 1.3 %collective-permute-done.1.rest_1_ = bf16[2,8,16,128]{3,2,1,0:T(8,128)(2,1)S(1)} collective-permute-done((bf16[2,8,16,128]{3,2,1,0:T(8,128)(2,1)S(1)}, bf16[2,8,16,128]{3,2,1,0:T(8,128)(2,1)S(1)}, u32[]{:S(2)}, u32[]{:S(2)}) %collective-permute-start.1) | collective-permute-done | bytes 65568 | tf_op jit(solution)/shard_map/ppermute | solution.py:409
  23.3 1.1 %collective-permute-start.6 = (bf16[2,8,16,128]{3,2,1,0:T(8,128)(2,1)S(1)}, bf16[2,8,16,128]{3,2,1,0:T(8,128)(2,1)S(1)}, u32[]{:S(2)}, u32[]{:S(2)}) collective-permute-start(bf16[2,8,16,128]{3,2,1,0:T(8,128)(2,1)S(1)} %get-tuple-element.53), channel_id=1, source_target_pairs={{0,12},{1,13},{2,14},{3,15},{4,8},{5,9},{6,10},{7,11},{8,4},{9,5},... | collective-permute-start | bytes 196616 | tf_op jit(solution)/shard_map/ppermute | solution.py:409
  25.9 1.0 %copy-done.5 = bf16[16,128,128]{2,1,0:T(8,128)(2,1)S(1)} copy-done((bf16[16,128,128]{2,1,0:T(8,128)(2,1)S(1)}, bf16[16,128,128]{2,1,0:T(8,128)(2,1)}, u32[]{:S(2)}) %copy-start.5) | copy-done | bytes 524312
  26.9 1.6 %tri_gate.1 = (bf16[16,128,128]{2,1,0:T(8,128)(2,1)S(1)}, bf16[16,128,128]{2,1,0:T(8,128)(2,1)S(1)}, bf16[4,128]{1,0:T(4,128)(2,1)S(1)}) custom-call(bf16[16,128,128]{2,1,0:T(8,128)(2,1)S(1)} %copy-done.1, bf16[16,128,128]{2,1,0:T(8,128)(2,1)S(1)} %copy-done.5, bf16[128,128]{1,0:T(8,128)(2,1)S(1)} %copy-done.3, bf16[128,4]{1,0:T(8,128)(2,1)S(1)} %copy.10.bias_proj), custom_call_target="tpu_custom_call" | custom-call | flops 2000000000 | bytes 2099200 | tf_op jit(solution)/shard_map/tri_gate/pallas_call | solution.py:418
  28.5 2.2 %collective-permute-done.4.rest_4_ = bf16[2,8,16,128]{3,2,1,0:T(8,128)(2,1)S(1)} collective-permute-done((bf16[2,8,16,128]{3,2,1,0:T(8,128)(2,1)S(1)}, bf16[2,8,16,128]{3,2,1,0:T(8,128)(2,1)S(1)}, u32[]{:S(2)}, u32[]{:S(2)}) %collective-permute-start.4) | collective-permute-done | bytes 65568 | tf_op jit(solution)/shard_map/ppermute | solution.py:409
  30.7 1.5 %collective-permute-done.5.rest_5_ = bf16[2,8,16,128]{3,2,1,0:T(8,128)(2,1)S(1)} collective-permute-done((bf16[2,8,16,128]{3,2,1,0:T(8,128)(2,1)S(1)}, bf16[2,8,16,128]{3,2,1,0:T(8,128)(2,1)S(1)}, u32[]{:S(2)}, u32[]{:S(2)}) %collective-permute-start.5) | collective-permute-done | bytes 65568 | tf_op jit(solution)/shard_map/ppermute | solution.py:409
  32.2 2.7 %collective-permute-done.6.rest_6_ = bf16[2,8,16,128]{3,2,1,0:T(8,128)(2,1)S(1)} collective-permute-done((bf16[2,8,16,128]{3,2,1,0:T(8,128)(2,1)S(1)}, bf16[2,8,16,128]{3,2,1,0:T(8,128)(2,1)S(1)}, u32[]{:S(2)}, u32[]{:S(2)}) %collective-permute-start.6) | collective-permute-done | bytes 65568 | tf_op jit(solution)/shard_map/ppermute | solution.py:409
  34.9 2.9 %collective-permute-done.7.rest_7_ = bf16[2,8,16,128]{3,2,1,0:T(8,128)(2,1)S(1)} collective-permute-done((bf16[2,8,16,128]{3,2,1,0:T(8,128)(2,1)S(1)}, bf16[2,8,16,128]{3,2,1,0:T(8,128)(2,1)S(1)}, u32[]{:S(2)}, u32[]{:S(2)}) %collective-permute-start.7) | collective-permute-done | bytes 65568 | tf_op jit(solution)/shard_map/ppermute | solution.py:409
  38.2 12.1 %all_to_all.15 = bf16[16,8,16,128]{3,2,1,0:T(8,128)(2,1)S(1)} all-to-all(bf16[16,8,16,128]{3,2,1,0:T(8,128)(2,1)S(1)} %bitcast.4), channel_id=1, replica_groups={{15,14,13,12,11,10,9,8,7,6,5,4,3,2,1,0},{31,30,29,28,27,26,25,24,23,22,..., dimensions={0} | all-to-all | bytes 1048576 | tf_op jit(solution)/shard_map/all_to_all | solution.py:378
  50.3 1.3 %update.1 = (bf16[16,128,128]{2,1,0:T(8,128)(2,1)S(1)}, bf16[4,16,128]{2,1,0:T(8,128)(2,1)S(1)}) custom-call(bf16[128,16,128]{2,1,0:T(8,128)(2,1)S(1)} %bitcast.5, bf16[16,128,128]{2,1,0:T(8,128)(2,1)S(1)} %get-tuple-element.63.source, bf16[16,128,128]{2,1,0:T(8,128)(2,1)S(1)} %get-tuple-element.64.gate, bf16[128,128]{1,0:T(8,128)(2,1)S(1)} %copy-done.4, ...), custom_call_target="tpu_custom_call" | custom-call | flops 2000000000 | bytes 1081344 | tf_op jit(solution)/shard_map/update/pallas_call | solution.py:438
  51.7 1.7 %collective-permute-start.9 = (bf16[16,128,128]{2,1,0:T(8,128)(2,1)S(1)}, bf16[16,128,128]{2,1,0:T(8,128)(2,1)S(1)}, u32[]{:S(2)}, u32[]{:S(2)}) collective-permute-start(bf16[16,128,128]{2,1,0:T(8,128)(2,1)S(1)} %get-tuple-element.67.updated), channel_id=1, source_target_pairs={{1,0},{0,1},{3,2},{2,3},{5,4},{4,5},{7,6},{6,7},{9,8},{8,9},{11,10... | collective-permute-start | bytes 1572872 | tf_op jit(solution)/shard_map/ppermute | solution.py:460
  53.4 2.9 %collective-permute-start.8 = (bf16[4,16,128]{2,1,0:T(8,128)(2,1)S(1)}, bf16[4,16,128]{2,1,0:T(8,128)(2,1)S(1)}, u32[]{:S(2)}, u32[]{:S(2)}) collective-permute-start(bf16[4,16,128]{2,1,0:T(8,128)(2,1)S(1)} %get-tuple-element.66.refs_0_), channel_id=1, source_target_pairs={{0,16},{1,17},{2,18},{3,19},{4,20},{5,21},{6,22},{7,23},{8,24},{9,... | collective-permute-start | bytes 49160 | tf_op jit(solution)/shard_map/ppermute | solution.py:409
  56.3 1.2 %own_projections.1 = (bf16[16,128,384]{2,1,0:T(8,128)(2,1)S(1)}, bf16[16,128,256]{2,1,0:T(8,128)(2,1)S(1)}) custom-call(bf16[16,128,128]{2,1,0:T(8,128)(2,1)S(1)} %get-tuple-element.67.updated, bf16[128,512]{1,0:T(8,128)(2,1)S(1)} %copy-done.2), custom_call_target="tpu_custom_call" | custom-call | flops 2000000000 | bytes 5242880 | tf_op jit(solution)/shard_map/own_projections/pallas_call | solution.py:465
  58.1 9.8 %all_to_all.16.mine = bf16[8,4,16,128]{3,2,1,0:T(8,128)(2,1)S(1)} all-to-all(bf16[8,4,16,128]{3,2,1,0:T(8,128)(2,1)S(1)} %deal_bias.1), channel_id=1, replica_groups={{0,1,4,5,8,9,12,13},{2,3,6,7,10,11,14,15},{16,17,20,21,24,25,28,29},{18..., dimensions={0} | all-to-all | bytes 262144 | tf_op jit(solution)/shard_map/all_to_all | solution.py:473
  67.8 0.9 %other_keys.1.rest_1_ = bf16[16,128,256]{2,1,0:T(8,128)(2,1)S(1)} custom-call(bf16[128,512]{1,0:T(8,128)(2,1)S(1)} %copy-done.2, bf16[16,128,128]{2,1,0:T(8,128)(2,1)S(1)} %collective-permute-done.9.rest_0_), custom_call_target="tpu_custom_call" | custom-call | flops 3000000000 | bytes 2097152 | tf_op jit(solution)/shard_map/other_keys/pallas_call | solution.py:477
  69.2 4.8 %attend.1 = bf16[16,128,128]{2,1,0:T(8,128)(2,1)} custom-call(s32[1]{0:T(128)S(6)} %copy.11.length, bf16[8,4,16,128]{3,2,1,0:T(8,128)(2,1)S(1)} %all_to_all.16.mine, bf16[8,4,16,128]{3,2,1,0:T(8,128)(2,1)S(1)} %collective-permute-done.10.sibling, bf16[128,128]{1,0:T(8,128)(2,1)S(1)} %copy-done, bf16[16,128,256]{2,1,0:T(8,128)(2,1)S(1)} %get-tuple-element.72.late, ...), custom_call_target="tpu_custom_call" | custom-call | flops 100000000 | bytes 1048576 | tf_op jit(solution)/shard_map/attend/pallas_call | solution.py:484
  (27 shorter events, 3.8 us)
Async XLA Ops:
  4.0 33.7 %all-to-all-start = ((bf16[32,8,16,128]{3,2,1,0:T(8,128)(2,1)}), bf16[32,8,16,128]{3,2,1,0:T(8,128)(2,1)S(1)}, u32[]{:S(2)}, u32[]{:S(2)}) async-start(bf16[32,8,16,128]{3,2,1,0:T(8,128)(2,1)} %get-tuple-element.40), calls=%async_computation | async-start | bytes 2097152 | tf_op jit(solution)/shard_map/all_to_all | solution.py:412
  11.3 7.0 %copy-start.6 = (bf16[128,4]{0,1:T(4,128)(2,1)S(1)}, bf16[128,4]{0,1:T(4,128)(2,1)}, u32[]{:S(2)}) copy-start(bf16[128,4]{0,1:T(4,128)(2,1)} %param.16) | copy-start | bytes 3076
  11.3 14.5 %copy-start.1 = (bf16[16,128,128]{2,1,0:T(8,128)(2,1)S(1)}, bf16[16,128,128]{2,1,0:T(8,128)(2,1)}, u32[]{:S(2)}) copy-start(bf16[16,128,128]{2,1,0:T(8,128)(2,1)} %pair.1) | copy-start | bytes 1572868
  11.3 14.5 %copy-start.3 = (bf16[128,128]{1,0:T(8,128)(2,1)S(1)}, bf16[128,128]{1,0:T(8,128)(2,1)}, u32[]{:S(2)}) copy-start(bf16[128,128]{1,0:T(8,128)(2,1)} %weights.1) | copy-start | bytes 98308
  13.4 1.6 %collective-permute-start = (bf16[8,8,16,128]{3,2,1,0:T(8,128)(2,1)S(1)}, bf16[8,8,16,128]{3,2,1,0:T(8,128)(2,1)S(1)}, u32[]{:S(2)}, u32[]{:S(2)}) collective-permute-start(bf16[8,8,16,128]{3,2,1,0:T(8,128)(2,1)S(1)} %get-tuple-element.46), channel_id=1, source_target_pairs={{0,2},{1,3},{2,0},{3,1},{4,6},{5,7},{6,4},{7,5},{8,10},{9,11},{10,... | collective-permute-start | bytes 786440 | tf_op jit(solution)/shard_map/ppermute | solution.py:409
  15.1 8.3 %collective-permute-start.1 = (bf16[2,8,16,128]{3,2,1,0:T(8,128)(2,1)S(1)}, bf16[2,8,16,128]{3,2,1,0:T(8,128)(2,1)S(1)}, u32[]{:S(2)}, u32[]{:S(2)}) collective-permute-start(bf16[2,8,16,128]{3,2,1,0:T(8,128)(2,1)S(1)} %get-tuple-element.48), channel_id=1, source_target_pairs={{0,1},{1,0},{2,3},{3,2},{4,5},{5,4},{6,7},{7,6},{8,9},{9,8},{10,11... | collective-permute-start | bytes 196616 | tf_op jit(solution)/shard_map/ppermute | solution.py:409
  16.9 8.4 %collective-permute-start.2 = (bf16[2,8,16,128]{3,2,1,0:T(8,128)(2,1)S(1)}, bf16[2,8,16,128]{3,2,1,0:T(8,128)(2,1)S(1)}, u32[]{:S(2)}, u32[]{:S(2)}) collective-permute-start(bf16[2,8,16,128]{3,2,1,0:T(8,128)(2,1)S(1)} %get-tuple-element.49), channel_id=1, source_target_pairs={{0,4},{1,5},{2,6},{3,7},{4,0},{5,1},{6,2},{7,3},{8,12},{9,13},{10,... | collective-permute-start | bytes 196616 | tf_op jit(solution)/shard_map/ppermute | solution.py:409
  18.5 10.0 %collective-permute-start.3 = (bf16[2,8,16,128]{3,2,1,0:T(8,128)(2,1)S(1)}, bf16[2,8,16,128]{3,2,1,0:T(8,128)(2,1)S(1)}, u32[]{:S(2)}, u32[]{:S(2)}) collective-permute-start(bf16[2,8,16,128]{3,2,1,0:T(8,128)(2,1)S(1)} %get-tuple-element.50), channel_id=1, source_target_pairs={{0,5},{1,4},{2,7},{3,6},{4,1},{5,0},{6,3},{7,2},{8,13},{9,12},{10,... | collective-permute-start | bytes 196616 | tf_op jit(solution)/shard_map/ppermute | solution.py:409
  18.8 11.9 %collective-permute-start.4 = (bf16[2,8,16,128]{3,2,1,0:T(8,128)(2,1)S(1)}, bf16[2,8,16,128]{3,2,1,0:T(8,128)(2,1)S(1)}, u32[]{:S(2)}, u32[]{:S(2)}) collective-permute-start(bf16[2,8,16,128]{3,2,1,0:T(8,128)(2,1)S(1)} %get-tuple-element.51), channel_id=1, source_target_pairs={{0,8},{1,9},{2,10},{3,11},{4,12},{5,13},{6,14},{7,15},{8,0},{9,1},... | collective-permute-start | bytes 196616 | tf_op jit(solution)/shard_map/ppermute | solution.py:409
  20.6 11.6 %collective-permute-start.5 = (bf16[2,8,16,128]{3,2,1,0:T(8,128)(2,1)S(1)}, bf16[2,8,16,128]{3,2,1,0:T(8,128)(2,1)S(1)}, u32[]{:S(2)}, u32[]{:S(2)}) collective-permute-start(bf16[2,8,16,128]{3,2,1,0:T(8,128)(2,1)S(1)} %get-tuple-element.52), channel_id=1, source_target_pairs={{0,9},{1,8},{2,11},{3,10},{4,13},{5,12},{6,15},{7,14},{8,1},{9,0},... | collective-permute-start | bytes 196616 | tf_op jit(solution)/shard_map/ppermute | solution.py:409
  23.3 11.5 %collective-permute-start.6 = (bf16[2,8,16,128]{3,2,1,0:T(8,128)(2,1)S(1)}, bf16[2,8,16,128]{3,2,1,0:T(8,128)(2,1)S(1)}, u32[]{:S(2)}, u32[]{:S(2)}) collective-permute-start(bf16[2,8,16,128]{3,2,1,0:T(8,128)(2,1)S(1)} %get-tuple-element.53), channel_id=1, source_target_pairs={{0,12},{1,13},{2,14},{3,15},{4,8},{5,9},{6,10},{7,11},{8,4},{9,5},... | collective-permute-start | bytes 196616 | tf_op jit(solution)/shard_map/ppermute | solution.py:409
  25.3 12.5 %collective-permute-start.7 = (bf16[2,8,16,128]{3,2,1,0:T(8,128)(2,1)S(1)}, bf16[2,8,16,128]{3,2,1,0:T(8,128)(2,1)S(1)}, u32[]{:S(2)}, u32[]{:S(2)}) collective-permute-start(bf16[2,8,16,128]{3,2,1,0:T(8,128)(2,1)S(1)} %get-tuple-element.54), channel_id=1, source_target_pairs={{0,13},{1,12},{2,15},{3,14},{4,9},{5,8},{6,11},{7,10},{8,5},{9,4},... | collective-permute-start | bytes 196616 | tf_op jit(solution)/shard_map/ppermute | solution.py:409
  25.9 1.0 %copy-start.5 = (bf16[16,128,128]{2,1,0:T(8,128)(2,1)S(1)}, bf16[16,128,128]{2,1,0:T(8,128)(2,1)}, u32[]{:S(2)}) copy-start(bf16[16,128,128]{2,1,0:T(8,128)(2,1)} %get-tuple-element.41.normed.source_hbm) | copy-start | bytes 1572868
  37.7 12.6 %copy-start.4 = (bf16[128,128]{1,0:T(8,128)(2,1)S(1)}, bf16[128,128]{1,0:T(8,128)(2,1)}, u32[]{:S(2)}) copy-start(bf16[128,128]{1,0:T(8,128)(2,1)} %tri_out.1) | copy-start | bytes 98308
  50.3 6.0 %copy-start.2 = (bf16[128,512]{1,0:T(8,128)(2,1)S(1)}, bf16[128,512]{1,0:T(8,128)(2,1)}, u32[]{:S(2)}) copy-start(bf16[128,512]{1,0:T(8,128)(2,1)} %attn_proj.3) | copy-start | bytes 393220
  51.7 16.2 %collective-permute-start.9 = (bf16[16,128,128]{2,1,0:T(8,128)(2,1)S(1)}, bf16[16,128,128]{2,1,0:T(8,128)(2,1)S(1)}, u32[]{:S(2)}, u32[]{:S(2)}) collective-permute-start(bf16[16,128,128]{2,1,0:T(8,128)(2,1)S(1)} %get-tuple-element.67.updated), channel_id=1, source_target_pairs={{1,0},{0,1},{3,2},{2,3},{5,4},{4,5},{7,6},{6,7},{9,8},{8,9},{11,10... | collective-permute-start | bytes 1572872 | tf_op jit(solution)/shard_map/ppermute | solution.py:460
  53.4 4.6 %collective-permute-start.8 = (bf16[4,16,128]{2,1,0:T(8,128)(2,1)S(1)}, bf16[4,16,128]{2,1,0:T(8,128)(2,1)S(1)}, u32[]{:S(2)}, u32[]{:S(2)}) collective-permute-start(bf16[4,16,128]{2,1,0:T(8,128)(2,1)S(1)} %get-tuple-element.66.refs_0_), channel_id=1, source_target_pairs={{0,16},{1,17},{2,18},{3,19},{4,20},{5,21},{6,22},{7,23},{8,24},{9,... | collective-permute-start | bytes 49160 | tf_op jit(solution)/shard_map/ppermute | solution.py:409
  67.8 1.4 %copy-start = (bf16[128,128]{1,0:T(8,128)(2,1)S(1)}, bf16[128,128]{1,0:T(8,128)(2,1)}, u32[]{:S(2)}) copy-start(bf16[128,128]{1,0:T(8,128)(2,1)} %attn_out.1) | copy-start | bytes 98308
  67.8 1.3 %collective-permute-start.10 = (bf16[8,4,16,128]{3,2,1,0:T(8,128)(2,1)S(1)}, bf16[8,4,16,128]{3,2,1,0:T(8,128)(2,1)S(1)}, u32[]{:S(2)}, u32[]{:S(2)}) collective-permute-start(bf16[8,4,16,128]{3,2,1,0:T(8,128)(2,1)S(1)} %all_to_all.16.mine), channel_id=1, source_target_pairs={{0,2},{1,3},{2,0},{3,1},{4,6},{5,7},{6,4},{7,5},{8,10},{9,11},{10,... | collective-permute-start | bytes 393224 | tf_op jit(solution)/shard_map/ppermute | solution.py:409

commit v9 on v7

--- a/solution.py
+++ b/solution.py
@@ -248,7 +248,7 @@
         bias_held[pl.ds(row, heads, stride=rows), :] = dot(bias_weights, normed, (1, 0))
         return carry
 
-    lax.fori_loop(0, rows, step, 0, unroll=8)
+    lax.fori_loop(0, rows, step, 0, unroll=rows)
     bias[...] = bias_held[...].astype(BF16).reshape(heads, rows, cols)
 
 

time: 74.5 us -> 74.3 us (level)
  no operation moved by 1% of the time
where the time goes in v9:
time: 74.3 us; the launch traced here: 73.9 us
  blocking collectives  21.8 us (29%)
  starting transfers between devices  20.8 us (28%)
  Pallas kernels  15.6 us (21%)
  waiting for transfers between devices  13.7 us (18%)
  local copies, waits for them, and re-layouts  1.21 us (2%)
  between operations  0.77 us (1%)
    ppermute x10, waiting for transfers between devices, flipped(): return lax.ppermute(array, BOTH, [(d, d ^ bits) for d in range(devices)])  13.7 us
    all_to_all x1, blocking collectives, in_half(): lax.all_to_all(array, BOTH, split_axis=0, concat_axis=0, axis_index_group...  12.1 us
    ppermute x10, starting transfers between devices, flipped(): return lax.ppermute(array, BOTH, [(d, d ^ bits) for d in range(devices)])  11.7 us
    all_to_all x1, blocking collectives, local(): lax.all_to_all(dealt, BOTH, split_axis=0, concat_axis=0, axis_index_group...  9.75 us
    all_to_all x1, starting transfers between devices, local(): right = lax.all_to_all(right, BOTH, split_axis=0, concat_axis=0, tiled=True)  7.3 us
    pallas_call x2, Pallas kernels, edges(): call(functools.partial(edges_body, side=side), 'right_edges' if side else...  5.38 us
    pallas_call x1, Pallas kernels, local(): call(attend_body, 'attend', [shape(block, BF16)], 5 + col_devices, [pltpu...  4.67 us
    ppermute x1, starting transfers between devices, local(): lax.ppermute(updated, 'ch', [((c + s) % col_devices, c) for c in range(co...  1.74 us
  transfers between devices with their start and end apart: 12, of which 9 were waited for; matrix products, arithmetic and copies ran while one was open for 0% of the time, Pallas kernels for 8%

profile of v9, /device:TPU:0, one launch (start us, length us, event | category | flops | bytes accessed | tf_op | source)
XLA Modules:
  0.0 73.9 jit_solution(4427276942435970712)
XLA Ops:
  0.7 3.3 %right_edges.1 = (bf16[32,8,16,128]{3,2,1,0:T(8,128)(2,1)}, bf16[16,128,128]{2,1,0:T(8,128)(2,1)}) custom-call(s32[1]{0:T(128)S(6)} %copy.11.length, bf16[16,128,128]{2,1,0:T(8,128)(2,1)} %pair.1, bf16[128,256]{1,0:T(8,128)(2,1)} %proj_hbm.3, bf16[128,256]{1,0:T(8,128)(2,1)} %gate_hbm.3), custom_call_target="tpu_custom_call" | custom-call | flops 3000000000 | bytes 3145728 | tf_op jit(solution)/shard_map/right_edges/pallas_call | solution.py:389
  4.0 7.3 %all-to-all-start = ((bf16[32,8,16,128]{3,2,1,0:T(8,128)(2,1)}), bf16[32,8,16,128]{3,2,1,0:T(8,128)(2,1)S(1)}, u32[]{:S(2)}, u32[]{:S(2)}) async-start(bf16[32,8,16,128]{3,2,1,0:T(8,128)(2,1)} %get-tuple-element.40), calls=%async_computation | async-start | bytes 2097152 | tf_op jit(solution)/shard_map/all_to_all | solution.py:412
  11.3 2.0 %left_edges.1 = (bf16[8,8,16,128]{3,2,1,0:T(8,128)(2,1)S(1)}, bf16[8,8,16,128]{3,2,1,0:T(8,128)(2,1)S(1)}) custom-call(s32[1]{0:T(128)S(6)} %copy.11.length, bf16[16,128,128]{2,1,0:T(8,128)(2,1)} %get-tuple-element.41.normed.source_hbm, bf16[128,256]{1,0:T(8,128)(2,1)} %proj_hbm.3, bf16[128,256]{1,0:T(8,128)(2,1)} %gate_hbm.3), custom_call_target="tpu_custom_call" | custom-call | flops 3000000000 | bytes 1048576 | tf_op jit(solution)/shard_map/left_edges/pallas_call | solution.py:389
  13.7 1.3 %collective-permute-done.sibling = bf16[8,8,16,128]{3,2,1,0:T(8,128)(2,1)S(1)} collective-permute-done((bf16[8,8,16,128]{3,2,1,0:T(8,128)(2,1)S(1)}, bf16[8,8,16,128]{3,2,1,0:T(8,128)(2,1)S(1)}, u32[]{:S(2)}, u32[]{:S(2)}) %collective-permute-start) | collective-permute-done | bytes 262176 | tf_op jit(solution)/shard_map/ppermute | solution.py:409
  15.1 1.8 %collective-permute-start.1 = (bf16[2,8,16,128]{3,2,1,0:T(8,128)(2,1)S(1)}, bf16[2,8,16,128]{3,2,1,0:T(8,128)(2,1)S(1)}, u32[]{:S(2)}, u32[]{:S(2)}) collective-permute-start(bf16[2,8,16,128]{3,2,1,0:T(8,128)(2,1)S(1)} %get-tuple-element.48), channel_id=1, source_target_pairs={{0,1},{1,0},{2,3},{3,2},{4,5},{5,4},{6,7},{7,6},{8,9},{9,8},{10,11... | collective-permute-start | bytes 196616 | tf_op jit(solution)/shard_map/ppermute | solution.py:409
  16.9 1.5 %collective-permute-start.2 = (bf16[2,8,16,128]{3,2,1,0:T(8,128)(2,1)S(1)}, bf16[2,8,16,128]{3,2,1,0:T(8,128)(2,1)S(1)}, u32[]{:S(2)}, u32[]{:S(2)}) collective-permute-start(bf16[2,8,16,128]{3,2,1,0:T(8,128)(2,1)S(1)} %get-tuple-element.49), channel_id=1, source_target_pairs={{0,4},{1,5},{2,6},{3,7},{4,0},{5,1},{6,2},{7,3},{8,12},{9,13},{10,... | collective-permute-start | bytes 196616 | tf_op jit(solution)/shard_map/ppermute | solution.py:409
  18.8 1.8 %collective-permute-start.4 = (bf16[2,8,16,128]{3,2,1,0:T(8,128)(2,1)S(1)}, bf16[2,8,16,128]{3,2,1,0:T(8,128)(2,1)S(1)}, u32[]{:S(2)}, u32[]{:S(2)}) collective-permute-start(bf16[2,8,16,128]{3,2,1,0:T(8,128)(2,1)S(1)} %get-tuple-element.51), channel_id=1, source_target_pairs={{0,8},{1,9},{2,10},{3,11},{4,12},{5,13},{6,14},{7,15},{8,0},{9,1},... | collective-permute-start | bytes 196616 | tf_op jit(solution)/shard_map/ppermute | solution.py:409
  20.6 1.5 %collective-permute-start.5 = (bf16[2,8,16,128]{3,2,1,0:T(8,128)(2,1)S(1)}, bf16[2,8,16,128]{3,2,1,0:T(8,128)(2,1)S(1)}, u32[]{:S(2)}, u32[]{:S(2)}) collective-permute-start(bf16[2,8,16,128]{3,2,1,0:T(8,128)(2,1)S(1)} %get-tuple-element.52), channel_id=1, source_target_pairs={{0,9},{1,8},{2,11},{3,10},{4,13},{5,12},{6,15},{7,14},{8,1},{9,0},... | collective-permute-start | bytes 196616 | tf_op jit(solution)/shard_map/ppermute | solution.py:409
  22.0 1.3 %collective-permute-done.1.rest_1_ = bf16[2,8,16,128]{3,2,1,0:T(8,128)(2,1)S(1)} collective-permute-done((bf16[2,8,16,128]{3,2,1,0:T(8,128)(2,1)S(1)}, bf16[2,8,16,128]{3,2,1,0:T(8,128)(2,1)S(1)}, u32[]{:S(2)}, u32[]{:S(2)}) %collective-permute-start.1) | collective-permute-done | bytes 65568 | tf_op jit(solution)/shard_map/ppermute | solution.py:409
  23.3 1.1 %collective-permute-start.6 = (bf16[2,8,16,128]{3,2,1,0:T(8,128)(2,1)S(1)}, bf16[2,8,16,128]{3,2,1,0:T(8,128)(2,1)S(1)}, u32[]{:S(2)}, u32[]{:S(2)}) collective-permute-start(bf16[2,8,16,128]{3,2,1,0:T(8,128)(2,1)S(1)} %get-tuple-element.53), channel_id=1, source_target_pairs={{0,12},{1,13},{2,14},{3,15},{4,8},{5,9},{6,10},{7,11},{8,4},{9,5},... | collective-permute-start | bytes 196616 | tf_op jit(solution)/shard_map/ppermute | solution.py:409
  25.9 1.0 %copy-done.5 = bf16[16,128,128]{2,1,0:T(8,128)(2,1)S(1)} copy-done((bf16[16,128,128]{2,1,0:T(8,128)(2,1)S(1)}, bf16[16,128,128]{2,1,0:T(8,128)(2,1)}, u32[]{:S(2)}) %copy-start.5) | copy-done | bytes 524312
  26.9 1.6 %tri_gate.1 = (bf16[16,128,128]{2,1,0:T(8,128)(2,1)S(1)}, bf16[16,128,128]{2,1,0:T(8,128)(2,1)S(1)}, bf16[4,128]{1,0:T(4,128)(2,1)S(1)}) custom-call(bf16[16,128,128]{2,1,0:T(8,128)(2,1)S(1)} %copy-done.1, bf16[16,128,128]{2,1,0:T(8,128)(2,1)S(1)} %copy-done.5, bf16[128,128]{1,0:T(8,128)(2,1)S(1)} %copy-done.3, bf16[128,4]{1,0:T(8,128)(2,1)S(1)} %copy.10.bias_proj), custom_call_target="tpu_custom_call" | custom-call | flops 2000000000 | bytes 2099200 | tf_op jit(solution)/shard_map/tri_gate/pallas_call | solution.py:418
  28.5 2.2 %collective-permute-done.4.rest_4_ = bf16[2,8,16,128]{3,2,1,0:T(8,128)(2,1)S(1)} collective-permute-done((bf16[2,8,16,128]{3,2,1,0:T(8,128)(2,1)S(1)}, bf16[2,8,16,128]{3,2,1,0:T(8,128)(2,1)S(1)}, u32[]{:S(2)}, u32[]{:S(2)}) %collective-permute-start.4) | collective-permute-done | bytes 65568 | tf_op jit(solution)/shard_map/ppermute | solution.py:409
  30.7 1.5 %collective-permute-done.5.rest_5_ = bf16[2,8,16,128]{3,2,1,0:T(8,128)(2,1)S(1)} collective-permute-done((bf16[2,8,16,128]{3,2,1,0:T(8,128)(2,1)S(1)}, bf16[2,8,16,128]{3,2,1,0:T(8,128)(2,1)S(1)}, u32[]{:S(2)}, u32[]{:S(2)}) %collective-permute-start.5) | collective-permute-done | bytes 65568 | tf_op jit(solution)/shard_map/ppermute | solution.py:409
  32.2 2.7 %collective-permute-done.6.rest_6_ = bf16[2,8,16,128]{3,2,1,0:T(8,128)(2,1)S(1)} collective-permute-done((bf16[2,8,16,128]{3,2,1,0:T(8,128)(2,1)S(1)}, bf16[2,8,16,128]{3,2,1,0:T(8,128)(2,1)S(1)}, u32[]{:S(2)}, u32[]{:S(2)}) %collective-permute-start.6) | collective-permute-done | bytes 65568 | tf_op jit(solution)/shard_map/ppermute | solution.py:409
  34.9 2.9 %collective-permute-done.7.rest_7_ = bf16[2,8,16,128]{3,2,1,0:T(8,128)(2,1)S(1)} collective-permute-done((bf16[2,8,16,128]{3,2,1,0:T(8,128)(2,1)S(1)}, bf16[2,8,16,128]{3,2,1,0:T(8,128)(2,1)S(1)}, u32[]{:S(2)}, u32[]{:S(2)}) %collective-permute-start.7) | collective-permute-done | bytes 65568 | tf_op jit(solution)/shard_map/ppermute | solution.py:409
  38.2 12.1 %all_to_all.15 = bf16[16,8,16,128]{3,2,1,0:T(8,128)(2,1)S(1)} all-to-all(bf16[16,8,16,128]{3,2,1,0:T(8,128)(2,1)S(1)} %bitcast.4), channel_id=1, replica_groups={{15,14,13,12,11,10,9,8,7,6,5,4,3,2,1,0},{31,30,29,28,27,26,25,24,23,22,..., dimensions={0} | all-to-all | bytes 1048576 | tf_op jit(solution)/shard_map/all_to_all | solution.py:378
  50.3 1.3 %update.1 = (bf16[16,128,128]{2,1,0:T(8,128)(2,1)S(1)}, bf16[4,16,128]{2,1,0:T(8,128)(2,1)S(1)}) custom-call(bf16[128,16,128]{2,1,0:T(8,128)(2,1)S(1)} %bitcast.5, bf16[16,128,128]{2,1,0:T(8,128)(2,1)S(1)} %get-tuple-element.63.source, bf16[16,128,128]{2,1,0:T(8,128)(2,1)S(1)} %get-tuple-element.64.gate, bf16[128,128]{1,0:T(8,128)(2,1)S(1)} %copy-done.4, ...), custom_call_target="tpu_custom_call" | custom-call | flops 2000000000 | bytes 1081344 | tf_op jit(solution)/shard_map/update/pallas_call | solution.py:438
  51.7 1.7 %collective-permute-start.9 = (bf16[16,128,128]{2,1,0:T(8,128)(2,1)S(1)}, bf16[16,128,128]{2,1,0:T(8,128)(2,1)S(1)}, u32[]{:S(2)}, u32[]{:S(2)}) collective-permute-start(bf16[16,128,128]{2,1,0:T(8,128)(2,1)S(1)} %get-tuple-element.67.updated), channel_id=1, source_target_pairs={{1,0},{0,1},{3,2},{2,3},{5,4},{4,5},{7,6},{6,7},{9,8},{8,9},{11,10... | collective-permute-start | bytes 1572872 | tf_op jit(solution)/shard_map/ppermute | solution.py:460
  53.4 2.9 %collective-permute-start.8 = (bf16[4,16,128]{2,1,0:T(8,128)(2,1)S(1)}, bf16[4,16,128]{2,1,0:T(8,128)(2,1)S(1)}, u32[]{:S(2)}, u32[]{:S(2)}) collective-permute-start(bf16[4,16,128]{2,1,0:T(8,128)(2,1)S(1)} %get-tuple-element.66.refs_0_), channel_id=1, source_target_pairs={{0,16},{1,17},{2,18},{3,19},{4,20},{5,21},{6,22},{7,23},{8,24},{9,... | collective-permute-start | bytes 49160 | tf_op jit(solution)/shard_map/ppermute | solution.py:409
  56.3 1.2 %own_projections.1 = (bf16[16,128,384]{2,1,0:T(8,128)(2,1)S(1)}, bf16[16,128,256]{2,1,0:T(8,128)(2,1)S(1)}) custom-call(bf16[16,128,128]{2,1,0:T(8,128)(2,1)S(1)} %get-tuple-element.67.updated, bf16[128,512]{1,0:T(8,128)(2,1)S(1)} %copy-done.2), custom_call_target="tpu_custom_call" | custom-call | flops 2000000000 | bytes 5242880 | tf_op jit(solution)/shard_map/own_projections/pallas_call | solution.py:465
  58.1 9.8 %all_to_all.16.mine = bf16[8,4,16,128]{3,2,1,0:T(8,128)(2,1)S(1)} all-to-all(bf16[8,4,16,128]{3,2,1,0:T(8,128)(2,1)S(1)} %deal_bias.1), channel_id=1, replica_groups={{0,1,4,5,8,9,12,13},{2,3,6,7,10,11,14,15},{16,17,20,21,24,25,28,29},{18..., dimensions={0} | all-to-all | bytes 262144 | tf_op jit(solution)/shard_map/all_to_all | solution.py:473
  67.8 0.9 %other_keys.1.rest_1_ = bf16[16,128,256]{2,1,0:T(8,128)(2,1)S(1)} custom-call(bf16[128,512]{1,0:T(8,128)(2,1)S(1)} %copy-done.2, bf16[16,128,128]{2,1,0:T(8,128)(2,1)S(1)} %collective-permute-done.9.rest_0_), custom_call_target="tpu_custom_call" | custom-call | flops 3000000000 | bytes 2097152 | tf_op jit(solution)/shard_map/other_keys/pallas_call | solution.py:477
  69.2 4.7 %attend.1 = bf16[16,128,128]{2,1,0:T(8,128)(2,1)} custom-call(s32[1]{0:T(128)S(6)} %copy.11.length, bf16[8,4,16,128]{3,2,1,0:T(8,128)(2,1)S(1)} %all_to_all.16.mine, bf16[8,4,16,128]{3,2,1,0:T(8,128)(2,1)S(1)} %collective-permute-done.10.sibling, bf16[128,128]{1,0:T(8,128)(2,1)S(1)} %copy-done, bf16[16,128,256]{2,1,0:T(8,128)(2,1)S(1)} %get-tuple-element.72.late, ...), custom_call_target="tpu_custom_call" | custom-call | flops 100000000 | bytes 1048576 | tf_op jit(solution)/shard_map/attend/pallas_call | solution.py:484
  (27 shorter events, 3.8 us)
Async XLA Ops:
  4.0 33.7 %all-to-all-start = ((bf16[32,8,16,128]{3,2,1,0:T(8,128)(2,1)}), bf16[32,8,16,128]{3,2,1,0:T(8,128)(2,1)S(1)}, u32[]{:S(2)}, u32[]{:S(2)}) async-start(bf16[32,8,16,128]{3,2,1,0:T(8,128)(2,1)} %get-tuple-element.40), calls=%async_computation | async-start | bytes 2097152 | tf_op jit(solution)/shard_map/all_to_all | solution.py:412
  11.3 7.0 %copy-start.6 = (bf16[128,4]{0,1:T(4,128)(2,1)S(1)}, bf16[128,4]{0,1:T(4,128)(2,1)}, u32[]{:S(2)}) copy-start(bf16[128,4]{0,1:T(4,128)(2,1)} %param.16) | copy-start | bytes 3076
  11.3 14.5 %copy-start.1 = (bf16[16,128,128]{2,1,0:T(8,128)(2,1)S(1)}, bf16[16,128,128]{2,1,0:T(8,128)(2,1)}, u32[]{:S(2)}) copy-start(bf16[16,128,128]{2,1,0:T(8,128)(2,1)} %pair.1) | copy-start | bytes 1572868
  11.3 14.5 %copy-start.3 = (bf16[128,128]{1,0:T(8,128)(2,1)S(1)}, bf16[128,128]{1,0:T(8,128)(2,1)}, u32[]{:S(2)}) copy-start(bf16[128,128]{1,0:T(8,128)(2,1)} %weights.1) | copy-start | bytes 98308
  13.4 1.6 %collective-permute-start = (bf16[8,8,16,128]{3,2,1,0:T(8,128)(2,1)S(1)}, bf16[8,8,16,128]{3,2,1,0:T(8,128)(2,1)S(1)}, u32[]{:S(2)}, u32[]{:S(2)}) collective-permute-start(bf16[8,8,16,128]{3,2,1,0:T(8,128)(2,1)S(1)} %get-tuple-element.46), channel_id=1, source_target_pairs={{0,2},{1,3},{2,0},{3,1},{4,6},{5,7},{6,4},{7,5},{8,10},{9,11},{10,... | collective-permute-start | bytes 786440 | tf_op jit(solution)/shard_map/ppermute | solution.py:409
  15.1 8.3 %collective-permute-start.1 = (bf16[2,8,16,128]{3,2,1,0:T(8,128)(2,1)S(1)}, bf16[2,8,16,128]{3,2,1,0:T(8,128)(2,1)S(1)}, u32[]{:S(2)}, u32[]{:S(2)}) collective-permute-start(bf16[2,8,16,128]{3,2,1,0:T(8,128)(2,1)S(1)} %get-tuple-element.48), channel_id=1, source_target_pairs={{0,1},{1,0},{2,3},{3,2},{4,5},{5,4},{6,7},{7,6},{8,9},{9,8},{10,11... | collective-permute-start | bytes 196616 | tf_op jit(solution)/shard_map/ppermute | solution.py:409
  16.9 8.4 %collective-permute-start.2 = (bf16[2,8,16,128]{3,2,1,0:T(8,128)(2,1)S(1)}, bf16[2,8,16,128]{3,2,1,0:T(8,128)(2,1)S(1)}, u32[]{:S(2)}, u32[]{:S(2)}) collective-permute-start(bf16[2,8,16,128]{3,2,1,0:T(8,128)(2,1)S(1)} %get-tuple-element.49), channel_id=1, source_target_pairs={{0,4},{1,5},{2,6},{3,7},{4,0},{5,1},{6,2},{7,3},{8,12},{9,13},{10,... | collective-permute-start | bytes 196616 | tf_op jit(solution)/shard_map/ppermute | solution.py:409
  18.5 10.0 %collective-permute-start.3 = (bf16[2,8,16,128]{3,2,1,0:T(8,128)(2,1)S(1)}, bf16[2,8,16,128]{3,2,1,0:T(8,128)(2,1)S(1)}, u32[]{:S(2)}, u32[]{:S(2)}) collective-permute-start(bf16[2,8,16,128]{3,2,1,0:T(8,128)(2,1)S(1)} %get-tuple-element.50), channel_id=1, source_target_pairs={{0,5},{1,4},{2,7},{3,6},{4,1},{5,0},{6,3},{7,2},{8,13},{9,12},{10,... | collective-permute-start | bytes 196616 | tf_op jit(solution)/shard_map/ppermute | solution.py:409
  18.8 11.9 %collective-permute-start.4 = (bf16[2,8,16,128]{3,2,1,0:T(8,128)(2,1)S(1)}, bf16[2,8,16,128]{3,2,1,0:T(8,128)(2,1)S(1)}, u32[]{:S(2)}, u32[]{:S(2)}) collective-permute-start(bf16[2,8,16,128]{3,2,1,0:T(8,128)(2,1)S(1)} %get-tuple-element.51), channel_id=1, source_target_pairs={{0,8},{1,9},{2,10},{3,11},{4,12},{5,13},{6,14},{7,15},{8,0},{9,1},... | collective-permute-start | bytes 196616 | tf_op jit(solution)/shard_map/ppermute | solution.py:409
  20.6 11.6 %collective-permute-start.5 = (bf16[2,8,16,128]{3,2,1,0:T(8,128)(2,1)S(1)}, bf16[2,8,16,128]{3,2,1,0:T(8,128)(2,1)S(1)}, u32[]{:S(2)}, u32[]{:S(2)}) collective-permute-start(bf16[2,8,16,128]{3,2,1,0:T(8,128)(2,1)S(1)} %get-tuple-element.52), channel_id=1, source_target_pairs={{0,9},{1,8},{2,11},{3,10},{4,13},{5,12},{6,15},{7,14},{8,1},{9,0},... | collective-permute-start | bytes 196616 | tf_op jit(solution)/shard_map/ppermute | solution.py:409
  23.3 11.5 %collective-permute-start.6 = (bf16[2,8,16,128]{3,2,1,0:T(8,128)(2,1)S(1)}, bf16[2,8,16,128]{3,2,1,0:T(8,128)(2,1)S(1)}, u32[]{:S(2)}, u32[]{:S(2)}) collective-permute-start(bf16[2,8,16,128]{3,2,1,0:T(8,128)(2,1)S(1)} %get-tuple-element.53), channel_id=1, source_target_pairs={{0,12},{1,13},{2,14},{3,15},{4,8},{5,9},{6,10},{7,11},{8,4},{9,5},... | collective-permute-start | bytes 196616 | tf_op jit(solution)/shard_map/ppermute | solution.py:409
  25.3 12.5 %collective-permute-start.7 = (bf16[2,8,16,128]{3,2,1,0:T(8,128)(2,1)S(1)}, bf16[2,8,16,128]{3,2,1,0:T(8,128)(2,1)S(1)}, u32[]{:S(2)}, u32[]{:S(2)}) collective-permute-start(bf16[2,8,16,128]{3,2,1,0:T(8,128)(2,1)S(1)} %get-tuple-element.54), channel_id=1, source_target_pairs={{0,13},{1,12},{2,15},{3,14},{4,9},{5,8},{6,11},{7,10},{8,5},{9,4},... | collective-permute-start | bytes 196616 | tf_op jit(solution)/shard_map/ppermute | solution.py:409
  25.9 1.0 %copy-start.5 = (bf16[16,128,128]{2,1,0:T(8,128)(2,1)S(1)}, bf16[16,128,128]{2,1,0:T(8,128)(2,1)}, u32[]{:S(2)}) copy-start(bf16[16,128,128]{2,1,0:T(8,128)(2,1)} %get-tuple-element.41.normed.source_hbm) | copy-start | bytes 1572868
  37.7 12.6 %copy-start.4 = (bf16[128,128]{1,0:T(8,128)(2,1)S(1)}, bf16[128,128]{1,0:T(8,128)(2,1)}, u32[]{:S(2)}) copy-start(bf16[128,128]{1,0:T(8,128)(2,1)} %tri_out.1) | copy-start | bytes 98308
  50.3 6.0 %copy-start.2 = (bf16[128,512]{1,0:T(8,128)(2,1)S(1)}, bf16[128,512]{1,0:T(8,128)(2,1)}, u32[]{:S(2)}) copy-start(bf16[128,512]{1,0:T(8,128)(2,1)} %attn_proj.3) | copy-start | bytes 393220
  51.7 16.2 %collective-permute-start.9 = (bf16[16,128,128]{2,1,0:T(8,128)(2,1)S(1)}, bf16[16,128,128]{2,1,0:T(8,128)(2,1)S(1)}, u32[]{:S(2)}, u32[]{:S(2)}) collective-permute-start(bf16[16,128,128]{2,1,0:T(8,128)(2,1)S(1)} %get-tuple-element.67.updated), channel_id=1, source_target_pairs={{1,0},{0,1},{3,2},{2,3},{5,4},{4,5},{7,6},{6,7},{9,8},{8,9},{11,10... | collective-permute-start | bytes 1572872 | tf_op jit(solution)/shard_map/ppermute | solution.py:460
  53.4 4.6 %collective-permute-start.8 = (bf16[4,16,128]{2,1,0:T(8,128)(2,1)S(1)}, bf16[4,16,128]{2,1,0:T(8,128)(2,1)S(1)}, u32[]{:S(2)}, u32[]{:S(2)}) collective-permute-start(bf16[4,16,128]{2,1,0:T(8,128)(2,1)S(1)} %get-tuple-element.66.refs_0_), channel_id=1, source_target_pairs={{0,16},{1,17},{2,18},{3,19},{4,20},{5,21},{6,22},{7,23},{8,24},{9,... | collective-permute-start | bytes 49160 | tf_op jit(solution)/shard_map/ppermute | solution.py:409
  67.8 1.4 %copy-start = (bf16[128,128]{1,0:T(8,128)(2,1)S(1)}, bf16[128,128]{1,0:T(8,128)(2,1)}, u32[]{:S(2)}) copy-start(bf16[128,128]{1,0:T(8,128)(2,1)} %attn_out.1) | copy-start | bytes 98308
  67.8 1.3 %collective-permute-start.10 = (bf16[8,4,16,128]{3,2,1,0:T(8,128)(2,1)S(1)}, bf16[8,4,16,128]{3,2,1,0:T(8,128)(2,1)S(1)}, u32[]{:S(2)}, u32[]{:S(2)}) collective-permute-start(bf16[8,4,16,128]{3,2,1,0:T(8,128)(2,1)S(1)} %all_to_all.16.mine), channel_id=1, source_target_pairs={{0,2},{1,3},{2,0},{3,1},{4,6},{5,7},{6,4},{7,5},{8,10},{9,11},{10,... | collective-permute-start | bytes 393224 | tf_op jit(solution)/shard_map/ppermute | solution.py:409

commit v10 on v9

--- a/solution.py
+++ b/solution.py
@@ -220,7 +220,7 @@
         for flip in range(1, columns):
             value = jnp.where(jnp.bitwise_xor(part, col) == flip, parts[flip][...], value)
         for chip in range(out.shape[0] // columns):
-            out[chip * columns + col] = value
+            out[out.shape[0] - 1 - chip * columns - col] = value
 
 
 def spread_sum(values):
@@ -305,7 +305,7 @@
         key_term = jnp.where(token < length[0], 0.0, -1e9)
         for part, core in ((mine, its_core), (sibling, 1 - its_core)):
             for chip in range(chips):
-                tiles = part[chip * pieces + block]
+                tiles = part[part.shape[0] - 1 - chip * pieces - block]
                 for head in range(heads):
                     first = pl.multiple_of(head * cols + (chip * 2 + core) * rows, rows)
                     bias_held[pl.ds(first, rows), piece * cols : (piece + 1) * cols] = (
@@ -454,7 +454,8 @@
     for part in range(col_devices):
         for core in range(2):
             members = range(part * per_part + core, (part + 1) * per_part, 2)
-            one_core.append([r * col_devices + c for r in members for c in range(col_devices)])
+            group = [r * col_devices + c for r in members for c in range(col_devices)]
+            one_core.append(group[::-1])
 
     others = [
         lax.ppermute(updated, "ch", [((c + s) % col_devices, c) for c in range(col_devices)])

time: 74.3 us -> 74.1 us (level)
  no operation moved by 1% of the time
where the time goes in v10:
time: 74.1 us; the launch traced here: 73.7 us
  blocking collectives  21.7 us (29%)
  starting transfers between devices  20.8 us (28%)
  Pallas kernels  15.6 us (21%)
  waiting for transfers between devices  13.7 us (18%)
  local copies, waits for them, and re-layouts  1.21 us (2%)
  between operations  0.77 us (1%)
    ppermute x10, waiting for transfers between devices, flipped(): return lax.ppermute(array, BOTH, [(d, d ^ bits) for d in range(devices)])  13.7 us
    all_to_all x1, blocking collectives, in_half(): lax.all_to_all(array, BOTH, split_axis=0, concat_axis=0, axis_index_group...  12.1 us
    ppermute x10, starting transfers between devices, flipped(): return lax.ppermute(array, BOTH, [(d, d ^ bits) for d in range(devices)])  11.7 us
    all_to_all x1, blocking collectives, local(): lax.all_to_all(dealt, BOTH, split_axis=0, concat_axis=0, axis_index_group...  9.58 us
    all_to_all x1, starting transfers between devices, local(): right = lax.all_to_all(right, BOTH, split_axis=0, concat_axis=0, tiled=True)  7.3 us
    pallas_call x2, Pallas kernels, edges(): call(functools.partial(edges_body, side=side), 'right_edges' if side else...  5.38 us
    pallas_call x1, Pallas kernels, local(): call(attend_body, 'attend', [shape(block, BF16)], 5 + col_devices, [pltpu...  4.68 us
    ppermute x1, starting transfers between devices, local(): lax.ppermute(updated, 'ch', [((c + s) % col_devices, c) for c in range(co...  1.74 us
  transfers between devices with their start and end apart: 12, of which 9 were waited for; matrix products, arithmetic and copies ran while one was open for 0% of the time, Pallas kernels for 8%

profile of v10, /device:TPU:0, one launch (start us, length us, event | category | flops | bytes accessed | tf_op | source)
XLA Modules:
  0.0 73.7 jit_solution(10232669352069236422)
XLA Ops:
  0.7 3.3 %right_edges.1 = (bf16[32,8,16,128]{3,2,1,0:T(8,128)(2,1)}, bf16[16,128,128]{2,1,0:T(8,128)(2,1)}) custom-call(s32[1]{0:T(128)S(6)} %copy.11.length, bf16[16,128,128]{2,1,0:T(8,128)(2,1)} %pair.1, bf16[128,256]{1,0:T(8,128)(2,1)} %proj_hbm.3, bf16[128,256]{1,0:T(8,128)(2,1)} %gate_hbm.3), custom_call_target="tpu_custom_call" | custom-call | flops 3000000000 | bytes 3145728 | tf_op jit(solution)/shard_map/right_edges/pallas_call | solution.py:389
  4.0 7.3 %all-to-all-start = ((bf16[32,8,16,128]{3,2,1,0:T(8,128)(2,1)}), bf16[32,8,16,128]{3,2,1,0:T(8,128)(2,1)S(1)}, u32[]{:S(2)}, u32[]{:S(2)}) async-start(bf16[32,8,16,128]{3,2,1,0:T(8,128)(2,1)} %get-tuple-element.40), calls=%async_computation | async-start | bytes 2097152 | tf_op jit(solution)/shard_map/all_to_all | solution.py:412
  11.3 2.0 %left_edges.1 = (bf16[8,8,16,128]{3,2,1,0:T(8,128)(2,1)S(1)}, bf16[8,8,16,128]{3,2,1,0:T(8,128)(2,1)S(1)}) custom-call(s32[1]{0:T(128)S(6)} %copy.11.length, bf16[16,128,128]{2,1,0:T(8,128)(2,1)} %get-tuple-element.41.normed.source_hbm, bf16[128,256]{1,0:T(8,128)(2,1)} %proj_hbm.3, bf16[128,256]{1,0:T(8,128)(2,1)} %gate_hbm.3), custom_call_target="tpu_custom_call" | custom-call | flops 3000000000 | bytes 1048576 | tf_op jit(solution)/shard_map/left_edges/pallas_call | solution.py:389
  13.7 1.3 %collective-permute-done.sibling = bf16[8,8,16,128]{3,2,1,0:T(8,128)(2,1)S(1)} collective-permute-done((bf16[8,8,16,128]{3,2,1,0:T(8,128)(2,1)S(1)}, bf16[8,8,16,128]{3,2,1,0:T(8,128)(2,1)S(1)}, u32[]{:S(2)}, u32[]{:S(2)}) %collective-permute-start) | collective-permute-done | bytes 262176 | tf_op jit(solution)/shard_map/ppermute | solution.py:409
  15.1 1.8 %collective-permute-start.1 = (bf16[2,8,16,128]{3,2,1,0:T(8,128)(2,1)S(1)}, bf16[2,8,16,128]{3,2,1,0:T(8,128)(2,1)S(1)}, u32[]{:S(2)}, u32[]{:S(2)}) collective-permute-start(bf16[2,8,16,128]{3,2,1,0:T(8,128)(2,1)S(1)} %get-tuple-element.48), channel_id=1, source_target_pairs={{0,1},{1,0},{2,3},{3,2},{4,5},{5,4},{6,7},{7,6},{8,9},{9,8},{10,11... | collective-permute-start | bytes 196616 | tf_op jit(solution)/shard_map/ppermute | solution.py:409
  16.9 1.5 %collective-permute-start.2 = (bf16[2,8,16,128]{3,2,1,0:T(8,128)(2,1)S(1)}, bf16[2,8,16,128]{3,2,1,0:T(8,128)(2,1)S(1)}, u32[]{:S(2)}, u32[]{:S(2)}) collective-permute-start(bf16[2,8,16,128]{3,2,1,0:T(8,128)(2,1)S(1)} %get-tuple-element.49), channel_id=1, source_target_pairs={{0,4},{1,5},{2,6},{3,7},{4,0},{5,1},{6,2},{7,3},{8,12},{9,13},{10,... | collective-permute-start | bytes 196616 | tf_op jit(solution)/shard_map/ppermute | solution.py:409
  18.8 1.8 %collective-permute-start.4 = (bf16[2,8,16,128]{3,2,1,0:T(8,128)(2,1)S(1)}, bf16[2,8,16,128]{3,2,1,0:T(8,128)(2,1)S(1)}, u32[]{:S(2)}, u32[]{:S(2)}) collective-permute-start(bf16[2,8,16,128]{3,2,1,0:T(8,128)(2,1)S(1)} %get-tuple-element.51), channel_id=1, source_target_pairs={{0,8},{1,9},{2,10},{3,11},{4,12},{5,13},{6,14},{7,15},{8,0},{9,1},... | collective-permute-start | bytes 196616 | tf_op jit(solution)/shard_map/ppermute | solution.py:409
  20.6 1.5 %collective-permute-start.5 = (bf16[2,8,16,128]{3,2,1,0:T(8,128)(2,1)S(1)}, bf16[2,8,16,128]{3,2,1,0:T(8,128)(2,1)S(1)}, u32[]{:S(2)}, u32[]{:S(2)}) collective-permute-start(bf16[2,8,16,128]{3,2,1,0:T(8,128)(2,1)S(1)} %get-tuple-element.52), channel_id=1, source_target_pairs={{0,9},{1,8},{2,11},{3,10},{4,13},{5,12},{6,15},{7,14},{8,1},{9,0},... | collective-permute-start | bytes 196616 | tf_op jit(solution)/shard_map/ppermute | solution.py:409
  22.0 1.3 %collective-permute-done.1.rest_1_ = bf16[2,8,16,128]{3,2,1,0:T(8,128)(2,1)S(1)} collective-permute-done((bf16[2,8,16,128]{3,2,1,0:T(8,128)(2,1)S(1)}, bf16[2,8,16,128]{3,2,1,0:T(8,128)(2,1)S(1)}, u32[]{:S(2)}, u32[]{:S(2)}) %collective-permute-start.1) | collective-permute-done | bytes 65568 | tf_op jit(solution)/shard_map/ppermute | solution.py:409
  23.3 1.1 %collective-permute-start.6 = (bf16[2,8,16,128]{3,2,1,0:T(8,128)(2,1)S(1)}, bf16[2,8,16,128]{3,2,1,0:T(8,128)(2,1)S(1)}, u32[]{:S(2)}, u32[]{:S(2)}) collective-permute-start(bf16[2,8,16,128]{3,2,1,0:T(8,128)(2,1)S(1)} %get-tuple-element.53), channel_id=1, source_target_pairs={{0,12},{1,13},{2,14},{3,15},{4,8},{5,9},{6,10},{7,11},{8,4},{9,5},... | collective-permute-start | bytes 196616 | tf_op jit(solution)/shard_map/ppermute | solution.py:409
  25.9 1.0 %copy-done.5 = bf16[16,128,128]{2,1,0:T(8,128)(2,1)S(1)} copy-done((bf16[16,128,128]{2,1,0:T(8,128)(2,1)S(1)}, bf16[16,128,128]{2,1,0:T(8,128)(2,1)}, u32[]{:S(2)}) %copy-start.5) | copy-done | bytes 524312
  26.9 1.6 %tri_gate.1 = (bf16[16,128,128]{2,1,0:T(8,128)(2,1)S(1)}, bf16[16,128,128]{2,1,0:T(8,128)(2,1)S(1)}, bf16[4,128]{1,0:T(4,128)(2,1)S(1)}) custom-call(bf16[16,128,128]{2,1,0:T(8,128)(2,1)S(1)} %copy-done.1, bf16[16,128,128]{2,1,0:T(8,128)(2,1)S(1)} %copy-done.5, bf16[128,128]{1,0:T(8,128)(2,1)S(1)} %copy-done.3, bf16[128,4]{1,0:T(8,128)(2,1)S(1)} %copy.10.bias_proj), custom_call_target="tpu_custom_call" | custom-call | flops 2000000000 | bytes 2099200 | tf_op jit(solution)/shard_map/tri_gate/pallas_call | solution.py:418
  28.5 2.2 %collective-permute-done.4.rest_4_ = bf16[2,8,16,128]{3,2,1,0:T(8,128)(2,1)S(1)} collective-permute-done((bf16[2,8,16,128]{3,2,1,0:T(8,128)(2,1)S(1)}, bf16[2,8,16,128]{3,2,1,0:T(8,128)(2,1)S(1)}, u32[]{:S(2)}, u32[]{:S(2)}) %collective-permute-start.4) | collective-permute-done | bytes 65568 | tf_op jit(solution)/shard_map/ppermute | solution.py:409
  30.7 1.5 %collective-permute-done.5.rest_5_ = bf16[2,8,16,128]{3,2,1,0:T(8,128)(2,1)S(1)} collective-permute-done((bf16[2,8,16,128]{3,2,1,0:T(8,128)(2,1)S(1)}, bf16[2,8,16,128]{3,2,1,0:T(8,128)(2,1)S(1)}, u32[]{:S(2)}, u32[]{:S(2)}) %collective-permute-start.5) | collective-permute-done | bytes 65568 | tf_op jit(solution)/shard_map/ppermute | solution.py:409
  32.2 2.7 %collective-permute-done.6.rest_6_ = bf16[2,8,16,128]{3,2,1,0:T(8,128)(2,1)S(1)} collective-permute-done((bf16[2,8,16,128]{3,2,1,0:T(8,128)(2,1)S(1)}, bf16[2,8,16,128]{3,2,1,0:T(8,128)(2,1)S(1)}, u32[]{:S(2)}, u32[]{:S(2)}) %collective-permute-start.6) | collective-permute-done | bytes 65568 | tf_op jit(solution)/shard_map/ppermute | solution.py:409
  34.9 2.9 %collective-permute-done.7.rest_7_ = bf16[2,8,16,128]{3,2,1,0:T(8,128)(2,1)S(1)} collective-permute-done((bf16[2,8,16,128]{3,2,1,0:T(8,128)(2,1)S(1)}, bf16[2,8,16,128]{3,2,1,0:T(8,128)(2,1)S(1)}, u32[]{:S(2)}, u32[]{:S(2)}) %collective-permute-start.7) | collective-permute-done | bytes 65568 | tf_op jit(solution)/shard_map/ppermute | solution.py:409
  38.2 12.1 %all_to_all.15 = bf16[16,8,16,128]{3,2,1,0:T(8,128)(2,1)S(1)} all-to-all(bf16[16,8,16,128]{3,2,1,0:T(8,128)(2,1)S(1)} %bitcast.4), channel_id=1, replica_groups={{15,14,13,12,11,10,9,8,7,6,5,4,3,2,1,0},{31,30,29,28,27,26,25,24,23,22,..., dimensions={0} | all-to-all | bytes 1048576 | tf_op jit(solution)/shard_map/all_to_all | solution.py:378
  50.3 1.3 %update.1 = (bf16[16,128,128]{2,1,0:T(8,128)(2,1)S(1)}, bf16[4,16,128]{2,1,0:T(8,128)(2,1)S(1)}) custom-call(bf16[128,16,128]{2,1,0:T(8,128)(2,1)S(1)} %bitcast.5, bf16[16,128,128]{2,1,0:T(8,128)(2,1)S(1)} %get-tuple-element.63.source, bf16[16,128,128]{2,1,0:T(8,128)(2,1)S(1)} %get-tuple-element.64.gate, bf16[128,128]{1,0:T(8,128)(2,1)S(1)} %copy-done.4, ...), custom_call_target="tpu_custom_call" | custom-call | flops 2000000000 | bytes 1081344 | tf_op jit(solution)/shard_map/update/pallas_call | solution.py:438
  51.7 1.7 %collective-permute-start.9 = (bf16[16,128,128]{2,1,0:T(8,128)(2,1)S(1)}, bf16[16,128,128]{2,1,0:T(8,128)(2,1)S(1)}, u32[]{:S(2)}, u32[]{:S(2)}) collective-permute-start(bf16[16,128,128]{2,1,0:T(8,128)(2,1)S(1)} %get-tuple-element.67.updated), channel_id=1, source_target_pairs={{1,0},{0,1},{3,2},{2,3},{5,4},{4,5},{7,6},{6,7},{9,8},{8,9},{11,10... | collective-permute-start | bytes 1572872 | tf_op jit(solution)/shard_map/ppermute | solution.py:461
  53.4 2.9 %collective-permute-start.8 = (bf16[4,16,128]{2,1,0:T(8,128)(2,1)S(1)}, bf16[4,16,128]{2,1,0:T(8,128)(2,1)S(1)}, u32[]{:S(2)}, u32[]{:S(2)}) collective-permute-start(bf16[4,16,128]{2,1,0:T(8,128)(2,1)S(1)} %get-tuple-element.66.refs_0_), channel_id=1, source_target_pairs={{0,16},{1,17},{2,18},{3,19},{4,20},{5,21},{6,22},{7,23},{8,24},{9,... | collective-permute-start | bytes 49160 | tf_op jit(solution)/shard_map/ppermute | solution.py:409
  56.3 1.2 %own_projections.1 = (bf16[16,128,384]{2,1,0:T(8,128)(2,1)S(1)}, bf16[16,128,256]{2,1,0:T(8,128)(2,1)S(1)}) custom-call(bf16[16,128,128]{2,1,0:T(8,128)(2,1)S(1)} %get-tuple-element.67.updated, bf16[128,512]{1,0:T(8,128)(2,1)S(1)} %copy-done.2), custom_call_target="tpu_custom_call" | custom-call | flops 2000000000 | bytes 5242880 | tf_op jit(solution)/shard_map/own_projections/pallas_call | solution.py:466
  58.1 9.6 %all_to_all.16.mine = bf16[8,4,16,128]{3,2,1,0:T(8,128)(2,1)S(1)} all-to-all(bf16[8,4,16,128]{3,2,1,0:T(8,128)(2,1)S(1)} %deal_bias.1), channel_id=1, replica_groups={{13,12,9,8,5,4,1,0},{15,14,11,10,7,6,3,2},{29,28,25,24,21,20,17,16},{31..., dimensions={0} | all-to-all | bytes 262144 | tf_op jit(solution)/shard_map/all_to_all | solution.py:474
  67.7 0.9 %other_keys.1.rest_1_ = bf16[16,128,256]{2,1,0:T(8,128)(2,1)S(1)} custom-call(bf16[128,512]{1,0:T(8,128)(2,1)S(1)} %copy-done.2, bf16[16,128,128]{2,1,0:T(8,128)(2,1)S(1)} %collective-permute-done.9.rest_0_), custom_call_target="tpu_custom_call" | custom-call | flops 3000000000 | bytes 2097152 | tf_op jit(solution)/shard_map/other_keys/pallas_call | solution.py:478
  69.0 4.7 %attend.1 = bf16[16,128,128]{2,1,0:T(8,128)(2,1)} custom-call(s32[1]{0:T(128)S(6)} %copy.11.length, bf16[8,4,16,128]{3,2,1,0:T(8,128)(2,1)S(1)} %all_to_all.16.mine, bf16[8,4,16,128]{3,2,1,0:T(8,128)(2,1)S(1)} %collective-permute-done.10.sibling, bf16[128,128]{1,0:T(8,128)(2,1)S(1)} %copy-done, bf16[16,128,256]{2,1,0:T(8,128)(2,1)S(1)} %get-tuple-element.72.late, ...), custom_call_target="tpu_custom_call" | custom-call | flops 100000000 | bytes 1048576 | tf_op jit(solution)/shard_map/attend/pallas_call | solution.py:485
  (27 shorter events, 3.8 us)
Async XLA Ops:
  4.0 33.7 %all-to-all-start = ((bf16[32,8,16,128]{3,2,1,0:T(8,128)(2,1)}), bf16[32,8,16,128]{3,2,1,0:T(8,128)(2,1)S(1)}, u32[]{:S(2)}, u32[]{:S(2)}) async-start(bf16[32,8,16,128]{3,2,1,0:T(8,128)(2,1)} %get-tuple-element.40), calls=%async_computation | async-start | bytes 2097152 | tf_op jit(solution)/shard_map/all_to_all | solution.py:412
  11.3 7.0 %copy-start.6 = (bf16[128,4]{0,1:T(4,128)(2,1)S(1)}, bf16[128,4]{0,1:T(4,128)(2,1)}, u32[]{:S(2)}) copy-start(bf16[128,4]{0,1:T(4,128)(2,1)} %param.16) | copy-start | bytes 3076
  11.3 14.5 %copy-start.1 = (bf16[16,128,128]{2,1,0:T(8,128)(2,1)S(1)}, bf16[16,128,128]{2,1,0:T(8,128)(2,1)}, u32[]{:S(2)}) copy-start(bf16[16,128,128]{2,1,0:T(8,128)(2,1)} %pair.1) | copy-start | bytes 1572868
  11.3 14.5 %copy-start.3 = (bf16[128,128]{1,0:T(8,128)(2,1)S(1)}, bf16[128,128]{1,0:T(8,128)(2,1)}, u32[]{:S(2)}) copy-start(bf16[128,128]{1,0:T(8,128)(2,1)} %weights.1) | copy-start | bytes 98308
  13.4 1.6 %collective-permute-start = (bf16[8,8,16,128]{3,2,1,0:T(8,128)(2,1)S(1)}, bf16[8,8,16,128]{3,2,1,0:T(8,128)(2,1)S(1)}, u32[]{:S(2)}, u32[]{:S(2)}) collective-permute-start(bf16[8,8,16,128]{3,2,1,0:T(8,128)(2,1)S(1)} %get-tuple-element.46), channel_id=1, source_target_pairs={{0,2},{1,3},{2,0},{3,1},{4,6},{5,7},{6,4},{7,5},{8,10},{9,11},{10,... | collective-permute-start | bytes 786440 | tf_op jit(solution)/shard_map/ppermute | solution.py:409
  15.1 8.3 %collective-permute-start.1 = (bf16[2,8,16,128]{3,2,1,0:T(8,128)(2,1)S(1)}, bf16[2,8,16,128]{3,2,1,0:T(8,128)(2,1)S(1)}, u32[]{:S(2)}, u32[]{:S(2)}) collective-permute-start(bf16[2,8,16,128]{3,2,1,0:T(8,128)(2,1)S(1)} %get-tuple-element.48), channel_id=1, source_target_pairs={{0,1},{1,0},{2,3},{3,2},{4,5},{5,4},{6,7},{7,6},{8,9},{9,8},{10,11... | collective-permute-start | bytes 196616 | tf_op jit(solution)/shard_map/ppermute | solution.py:409
  16.9 8.4 %collective-permute-start.2 = (bf16[2,8,16,128]{3,2,1,0:T(8,128)(2,1)S(1)}, bf16[2,8,16,128]{3,2,1,0:T(8,128)(2,1)S(1)}, u32[]{:S(2)}, u32[]{:S(2)}) collective-permute-start(bf16[2,8,16,128]{3,2,1,0:T(8,128)(2,1)S(1)} %get-tuple-element.49), channel_id=1, source_target_pairs={{0,4},{1,5},{2,6},{3,7},{4,0},{5,1},{6,2},{7,3},{8,12},{9,13},{10,... | collective-permute-start | bytes 196616 | tf_op jit(solution)/shard_map/ppermute | solution.py:409
  18.5 10.0 %collective-permute-start.3 = (bf16[2,8,16,128]{3,2,1,0:T(8,128)(2,1)S(1)}, bf16[2,8,16,128]{3,2,1,0:T(8,128)(2,1)S(1)}, u32[]{:S(2)}, u32[]{:S(2)}) collective-permute-start(bf16[2,8,16,128]{3,2,1,0:T(8,128)(2,1)S(1)} %get-tuple-element.50), channel_id=1, source_target_pairs={{0,5},{1,4},{2,7},{3,6},{4,1},{5,0},{6,3},{7,2},{8,13},{9,12},{10,... | collective-permute-start | bytes 196616 | tf_op jit(solution)/shard_map/ppermute | solution.py:409
  18.8 11.9 %collective-permute-start.4 = (bf16[2,8,16,128]{3,2,1,0:T(8,128)(2,1)S(1)}, bf16[2,8,16,128]{3,2,1,0:T(8,128)(2,1)S(1)}, u32[]{:S(2)}, u32[]{:S(2)}) collective-permute-start(bf16[2,8,16,128]{3,2,1,0:T(8,128)(2,1)S(1)} %get-tuple-element.51), channel_id=1, source_target_pairs={{0,8},{1,9},{2,10},{3,11},{4,12},{5,13},{6,14},{7,15},{8,0},{9,1},... | collective-permute-start | bytes 196616 | tf_op jit(solution)/shard_map/ppermute | solution.py:409
  20.6 11.6 %collective-permute-start.5 = (bf16[2,8,16,128]{3,2,1,0:T(8,128)(2,1)S(1)}, bf16[2,8,16,128]{3,2,1,0:T(8,128)(2,1)S(1)}, u32[]{:S(2)}, u32[]{:S(2)}) collective-permute-start(bf16[2,8,16,128]{3,2,1,0:T(8,128)(2,1)S(1)} %get-tuple-element.52), channel_id=1, source_target_pairs={{0,9},{1,8},{2,11},{3,10},{4,13},{5,12},{6,15},{7,14},{8,1},{9,0},... | collective-permute-start | bytes 196616 | tf_op jit(solution)/shard_map/ppermute | solution.py:409
  23.3 11.5 %collective-permute-start.6 = (bf16[2,8,16,128]{3,2,1,0:T(8,128)(2,1)S(1)}, bf16[2,8,16,128]{3,2,1,0:T(8,128)(2,1)S(1)}, u32[]{:S(2)}, u32[]{:S(2)}) collective-permute-start(bf16[2,8,16,128]{3,2,1,0:T(8,128)(2,1)S(1)} %get-tuple-element.53), channel_id=1, source_target_pairs={{0,12},{1,13},{2,14},{3,15},{4,8},{5,9},{6,10},{7,11},{8,4},{9,5},... | collective-permute-start | bytes 196616 | tf_op jit(solution)/shard_map/ppermute | solution.py:409
  25.3 12.5 %collective-permute-start.7 = (bf16[2,8,16,128]{3,2,1,0:T(8,128)(2,1)S(1)}, bf16[2,8,16,128]{3,2,1,0:T(8,128)(2,1)S(1)}, u32[]{:S(2)}, u32[]{:S(2)}) collective-permute-start(bf16[2,8,16,128]{3,2,1,0:T(8,128)(2,1)S(1)} %get-tuple-element.54), channel_id=1, source_target_pairs={{0,13},{1,12},{2,15},{3,14},{4,9},{5,8},{6,11},{7,10},{8,5},{9,4},... | collective-permute-start | bytes 196616 | tf_op jit(solution)/shard_map/ppermute | solution.py:409
  25.9 1.0 %copy-start.5 = (bf16[16,128,128]{2,1,0:T(8,128)(2,1)S(1)}, bf16[16,128,128]{2,1,0:T(8,128)(2,1)}, u32[]{:S(2)}) copy-start(bf16[16,128,128]{2,1,0:T(8,128)(2,1)} %get-tuple-element.41.normed.source_hbm) | copy-start | bytes 1572868
  37.7 12.6 %copy-start.4 = (bf16[128,128]{1,0:T(8,128)(2,1)S(1)}, bf16[128,128]{1,0:T(8,128)(2,1)}, u32[]{:S(2)}) copy-start(bf16[128,128]{1,0:T(8,128)(2,1)} %tri_out.1) | copy-start | bytes 98308
  50.3 6.0 %copy-start.2 = (bf16[128,512]{1,0:T(8,128)(2,1)S(1)}, bf16[128,512]{1,0:T(8,128)(2,1)}, u32[]{:S(2)}) copy-start(bf16[128,512]{1,0:T(8,128)(2,1)} %attn_proj.3) | copy-start | bytes 393220
  51.7 16.0 %collective-permute-start.9 = (bf16[16,128,128]{2,1,0:T(8,128)(2,1)S(1)}, bf16[16,128,128]{2,1,0:T(8,128)(2,1)S(1)}, u32[]{:S(2)}, u32[]{:S(2)}) collective-permute-start(bf16[16,128,128]{2,1,0:T(8,128)(2,1)S(1)} %get-tuple-element.67.updated), channel_id=1, source_target_pairs={{1,0},{0,1},{3,2},{2,3},{5,4},{4,5},{7,6},{6,7},{9,8},{8,9},{11,10... | collective-permute-start | bytes 1572872 | tf_op jit(solution)/shard_map/ppermute | solution.py:461
  53.4 4.6 %collective-permute-start.8 = (bf16[4,16,128]{2,1,0:T(8,128)(2,1)S(1)}, bf16[4,16,128]{2,1,0:T(8,128)(2,1)S(1)}, u32[]{:S(2)}, u32[]{:S(2)}) collective-permute-start(bf16[4,16,128]{2,1,0:T(8,128)(2,1)S(1)} %get-tuple-element.66.refs_0_), channel_id=1, source_target_pairs={{0,16},{1,17},{2,18},{3,19},{4,20},{5,21},{6,22},{7,23},{8,24},{9,... | collective-permute-start | bytes 49160 | tf_op jit(solution)/shard_map/ppermute | solution.py:409
  67.7 1.4 %copy-start = (bf16[128,128]{1,0:T(8,128)(2,1)S(1)}, bf16[128,128]{1,0:T(8,128)(2,1)}, u32[]{:S(2)}) copy-start(bf16[128,128]{1,0:T(8,128)(2,1)} %attn_out.1) | copy-start | bytes 98308
  67.7 1.3 %collective-permute-start.10 = (bf16[8,4,16,128]{3,2,1,0:T(8,128)(2,1)S(1)}, bf16[8,4,16,128]{3,2,1,0:T(8,128)(2,1)S(1)}, u32[]{:S(2)}, u32[]{:S(2)}) collective-permute-start(bf16[8,4,16,128]{3,2,1,0:T(8,128)(2,1)S(1)} %all_to_all.16.mine), channel_id=1, source_target_pairs={{0,2},{1,3},{2,0},{3,1},{4,6},{5,7},{6,4},{7,5},{8,10},{9,11},{10,... | collective-permute-start | bytes 393224 | tf_op jit(solution)/shard_map/ppermute | solution.py:409

commit v11 on v10

--- a/solution.py
+++ b/solution.py
@@ -95,16 +95,15 @@
     ]
 
 
-def edges_body(length, source_hbm, proj_hbm, gate_hbm, *rest, side):
-    outs = rest[:-6]
-    source, proj, gate, held, out, sems = rest[-6:]
+def edges_body(
+    length, source_hbm, proj_hbm, gate_hbm, right, normed, mine, theirs, source, proj, gate, held, out, sems
+):
     rows, cols, channels = source.shape
     share, own = out.shape[:2]
     columns = lax.axis_size("ch")
-    span = pl.ds(side * channels, channels)
     fetches = [
-        pltpu.make_async_copy(proj_hbm.at[:, span], proj, sems.at[0, 2]),
-        pltpu.make_async_copy(gate_hbm.at[:, span], gate, sems.at[0, 3]),
+        pltpu.make_async_copy(proj_hbm, proj, sems.at[0, 2]),
+        pltpu.make_async_copy(gate_hbm, gate, sems.at[0, 3]),
     ]
     chunks = chunked([(source_hbm, source)], sems, 0, 2)
     for copy in fetches + chunks[0] + chunks[1]:
@@ -116,47 +115,68 @@
     col_valid = jnp.where(tokens < count, 0.5, 0.0)
     for copy in fetches:
         copy.wait()
-    weights = jnp.concatenate([turned(proj[...]), turned(gate[...])], axis=0)
-
-    def step(row, carry):
-        values = source[row]
-        if side:
-            values = layer_norm(values.astype(F32), -1).astype(BF16)
-            source[row] = values
-        mixed = dot(weights, values, (1, 1))
-        valid = col_valid * (row_offset + row < count).astype(F32)
-        twice = jnp.tanh(0.5 * mixed[channels:]) + 1.0
-        held[pl.ds(row, channels, stride=rows), :] = twice * (mixed[:channels] * valid)
-        return carry
-
+    spans = [slice(side * channels, (side + 1) * channels) for side in range(2)]
+    weights = [
+        jnp.concatenate([turned(proj[:, span]), turned(gate[:, span])], axis=0) for span in spans
+    ]
     for (copy,) in chunks:
         copy.wait()
-    lax.fori_loop(0, rows, step, 0, unroll=rows)
     sends = []
-    if side:
-        sends.append(pltpu.make_async_copy(source, outs[1], sems.at[1, 0]))
-        sends[0].start()
-    group = share // 4
-    for device in range(share):
-        part = held[device * own * rows : (device + 1) * own * rows, :].astype(BF16)
-        position = share - 1 - device
-        out[position] = part.reshape(own, rows, cols)
-        if side and device % group == group - 1:
-            for k in range(2):
-                source_part = out.at[pl.ds(position, group)]
-                target = outs[0].at[pl.ds(k * share + position, group)]
-                sends.append(
-                    pltpu.make_async_copy(source_part, target, sems.at[1 + k, 1 + device // group])
-                )
-                sends[-1].start()
-    if not side:
-        chip, core = place()
-        for k, offset in enumerate(chip_offsets()):
-            for other in range(2):
-                index = jnp.bitwise_xor(chip, offset) + lax.rem(core + other, 2) * columns
-                outs[other][k] = out[index]
+    for side in (1, 0):
+
+        def step(row, carry):
+            values = source[row]
+            if side:
+                values = layer_norm(values.astype(F32), -1).astype(BF16)
+                source[row] = values
+            mixed = dot(weights[side], values, (1, 1))
+            valid = col_valid * (row_offset + row < count).astype(F32)
+            twice = jnp.tanh(0.5 * mixed[channels:]) + 1.0
+            held[side, pl.ds(row, channels, stride=rows), :] = twice * (mixed[:channels] * valid)
+            return carry
+
+        lax.fori_loop(0, rows, step, 0, unroll=rows)
+        if side:
+            sends.append(pltpu.make_async_copy(source, normed, sems.at[1, 0]))
+            sends[0].start()
+        group = share // 4
+        for device in range(share):
+            part = held[side, device * own * rows : (device + 1) * own * rows, :].astype(BF16)
+            position = share - 1 - device
+            if side:
+                out[position] = part.reshape(own, rows, cols)
+            else:
+                held_left = part.reshape(own, rows, cols)
+                theirs_at = position % (2 * columns) // columns
+                place_of(position, theirs_at, held_left, mine, theirs)
+            if side and device % group == group - 1:
+                for k in range(2):
+                    source_part = out.at[pl.ds(position, group)]
+                    target = right.at[pl.ds(k * share + position, group)]
+                    sends.append(
+                        pltpu.make_async_copy(
+                            source_part, target, sems.at[1 + k, 1 + device // group]
+                        )
+                    )
+                    sends[-1].start()
     for copy in sends:
         copy.wait()
+
+
+def place_of(position, its_core, block, mine, theirs):
+    columns = lax.axis_size("ch")
+    chip, core = place()
+    offset = jnp.bitwise_xor(chip, position - its_core * columns)
+    col = lax.rem(offset, columns)
+    index = lax.div(offset, 2 * columns) * columns + col
+
+    @pl.when(core == its_core)
+    def _():
+        mine[index] = block
+
+    @pl.when(core != its_core)
+    def _():
+        theirs[index] = block
 
 
 def pack_body(mine, sibling, *outs):
@@ -380,37 +400,33 @@
         )
 
 
-    weight = pltpu.VMEM((channels, channels), BF16)
     offsets = chip_offsets()
     tile = (own, rows, cols)
-
-    def edges(side, source):
-        outs = [shape((devices,) + tile, BF16), shape(block, BF16)]
-        return call(
-            functools.partial(edges_body, side=side),
-            "right_edges" if side else "left_edges",
-            outs if side else [shape((len(offsets),) + tile, BF16)] * 2,
-            4,
-            [
-                pltpu.VMEM(block, BF16),
-                weight,
-                weight,
-                pltpu.VMEM((channels * rows, cols), F32),
-                pltpu.VMEM((share,) + tile, BF16),
-                pltpu.SemaphoreType.DMA((3, 5)),
-            ],
-            smem=1,
-            space=HBM,
-            out_space=HBM if side else VMEM,
-            flops=3e9,
-        )(valid_count, *[in_hbm(a) for a in (source, edge_proj, edge_gate)])
+    both = pltpu.VMEM(edge_proj.shape, BF16)
+    right, normed, mine, theirs = call(
+        edges_body,
+        "edges",
+        [shape((devices,) + tile, BF16), shape(block, BF16)]
+        + [shape((len(offsets),) + tile, BF16)] * 2,
+        4,
+        [
+            pltpu.VMEM(block, BF16),
+            both,
+            both,
+            pltpu.VMEM((2, channels * rows, cols), F32),
+            pltpu.VMEM((share,) + tile, BF16),
+            pltpu.SemaphoreType.DMA((3, 5)),
+        ],
+        smem=1,
+        space=HBM,
+        out_space=[HBM, HBM, VMEM, VMEM],
+        flops=4e9,
+    )(valid_count, *[in_hbm(a) for a in (pair_act, edge_proj, edge_gate)])
 
     def flipped(array, bits):
         return lax.ppermute(array, BOTH, [(d, d ^ bits) for d in range(devices)])
 
-    right, normed = edges(1, pair_act)
     right = lax.all_to_all(right, BOTH, split_axis=0, concat_axis=0, tiled=True)
-    mine, theirs = edges(0, normed)
     left = call(pack_body, "pack", [shape((2,) + tile, BF16)] * len(offsets), 2)(
         mine, flipped(theirs, col_devices)
     )

time: 74.1 us -> 74.2 us (level)
  Pallas kernels: 15.6 us -> 13.7 us
  waiting for transfers between devices: 13.7 us -> 15.4 us
  local copies, waits for them, and re-layouts: 1.21 us -> 2 us
    pallas_call x2 -> x1, Pallas kernels: 5.38 us -> 3.46 us  [local(): call(edges_body, 'edges', [shape((devices,) + tile, BF16), shape(block, B...]
    ppermute x10, waiting for transfers between devices: 13.7 us -> 15.4 us  [flipped(): return lax.ppermute(array, BOTH, [(d, d ^ bits) for d in range(devices)])]
    unnamed x15 -> x19, local copies, waits for them, and re-layouts: 1.21 us -> 2 us
  transfers between devices with their start and end apart: 12 -> 12, of which waited for: 9 -> 9; matrix products, arithmetic and copies ran while one was open for 0% -> 0% of each run, Pallas kernels for 8% -> 5%
where the time goes in v11:
time: 74.2 us; the launch traced here: 73.8 us
  blocking collectives  21.7 us (29%)
  starting transfers between devices  20.3 us (27%)
  waiting for transfers between devices  15.4 us (21%)
  Pallas kernels  13.7 us (18%)
  local copies, waits for them, and re-layouts  2 us (3%)
  between operations  0.76 us (1%)
    ppermute x10, waiting for transfers between devices, flipped(): return lax.ppermute(array, BOTH, [(d, d ^ bits) for d in range(devices)])  15.4 us
    all_to_all x1, blocking collectives, in_half(): lax.all_to_all(array, BOTH, split_axis=0, concat_axis=0, axis_index_group...  12.1 us
    ppermute x10, starting transfers between devices, flipped(): return lax.ppermute(array, BOTH, [(d, d ^ bits) for d in range(devices)])  11.3 us
    all_to_all x1, blocking collectives, local(): lax.all_to_all(dealt, BOTH, split_axis=0, concat_axis=0, axis_index_group...  9.58 us
    all_to_all x1, starting transfers between devices, local(): right = lax.all_to_all(right, BOTH, split_axis=0, concat_axis=0, tiled=True)  7.3 us
    pallas_call x1, Pallas kernels, local(): call(attend_body, 'attend', [shape(block, BF16)], 5 + col_devices, [pltpu...  4.67 us
    pallas_call x1, Pallas kernels, local(): call(edges_body, 'edges', [shape((devices,) + tile, BF16), shape(block, B...  3.46 us
    unnamed x19, local copies, waits for them, and re-layouts  2 us
  transfers between devices with their start and end apart: 12, of which 9 were waited for; matrix products, arithmetic and copies ran while one was open for 0% of the time, Pallas kernels for 5%

profile of v11, /device:TPU:0, one launch (start us, length us, event | category | flops | bytes accessed | tf_op | source)
XLA Modules:
  0.0 73.8 jit_solution(5077724308190857714)
XLA Ops:
  0.7 3.5 %edges.1 = (bf16[32,8,16,128]{3,2,1,0:T(8,128)(2,1)}, bf16[16,128,128]{2,1,0:T(8,128)(2,1)}, bf16[8,8,16,128]{3,2,1,0:T(8,128)(2,1)S(1)}, bf16[8,8,16,128]{3,2,1,0:T(8,128)(2,1)S(1)}) custom-call(s32[1]{0:T(128)S(6)} %copy.11.length, bf16[16,128,128]{2,1,0:T(8,128)(2,1)} %pair.1, bf16[128,256]{1,0:T(8,128)(2,1)} %proj_hbm.1, bf16[128,256]{1,0:T(8,128)(2,1)} %gate_hbm.1), custom_call_target="tpu_custom_call" | custom-call | flops 4000000000 | bytes 4194304 | tf_op jit(solution)/shard_map/edges/pallas_call | solution.py:406
  4.2 7.3 %all-to-all-start = ((bf16[32,8,16,128]{3,2,1,0:T(8,128)(2,1)}), bf16[32,8,16,128]{3,2,1,0:T(8,128)(2,1)S(1)}, u32[]{:S(2)}, u32[]{:S(2)}) async-start(bf16[32,8,16,128]{3,2,1,0:T(8,128)(2,1)} %get-tuple-element.40), calls=%async_computation | async-start | bytes 2097152 | tf_op jit(solution)/shard_map/all_to_all | solution.py:429
  11.8 1.3 %collective-permute-done.sibling = bf16[8,8,16,128]{3,2,1,0:T(8,128)(2,1)S(1)} collective-permute-done((bf16[8,8,16,128]{3,2,1,0:T(8,128)(2,1)S(1)}, bf16[8,8,16,128]{3,2,1,0:T(8,128)(2,1)S(1)}, u32[]{:S(2)}, u32[]{:S(2)}) %collective-permute-start) | collective-permute-done | bytes 262176 | tf_op jit(solution)/shard_map/ppermute | solution.py:427
  13.1 1.8 %collective-permute-start.1 = (bf16[2,8,16,128]{3,2,1,0:T(8,128)(2,1)S(1)}, bf16[2,8,16,128]{3,2,1,0:T(8,128)(2,1)S(1)}, u32[]{:S(2)}, u32[]{:S(2)}) collective-permute-start(bf16[2,8,16,128]{3,2,1,0:T(8,128)(2,1)S(1)} %get-tuple-element.48), channel_id=1, source_target_pairs={{0,1},{1,0},{2,3},{3,2},{4,5},{5,4},{6,7},{7,6},{8,9},{9,8},{10,11... | collective-permute-start | bytes 196616 | tf_op jit(solution)/shard_map/ppermute | solution.py:427
  15.0 1.5 %collective-permute-start.2 = (bf16[2,8,16,128]{3,2,1,0:T(8,128)(2,1)S(1)}, bf16[2,8,16,128]{3,2,1,0:T(8,128)(2,1)S(1)}, u32[]{:S(2)}, u32[]{:S(2)}) collective-permute-start(bf16[2,8,16,128]{3,2,1,0:T(8,128)(2,1)S(1)} %get-tuple-element.49), channel_id=1, source_target_pairs={{0,4},{1,5},{2,6},{3,7},{4,0},{5,1},{6,2},{7,3},{8,12},{9,13},{10,... | collective-permute-start | bytes 196616 | tf_op jit(solution)/shard_map/ppermute | solution.py:427
  16.9 1.8 %collective-permute-start.4 = (bf16[2,8,16,128]{3,2,1,0:T(8,128)(2,1)S(1)}, bf16[2,8,16,128]{3,2,1,0:T(8,128)(2,1)S(1)}, u32[]{:S(2)}, u32[]{:S(2)}) collective-permute-start(bf16[2,8,16,128]{3,2,1,0:T(8,128)(2,1)S(1)} %get-tuple-element.51), channel_id=1, source_target_pairs={{0,8},{1,9},{2,10},{3,11},{4,12},{5,13},{6,14},{7,15},{8,0},{9,1},... | collective-permute-start | bytes 196616 | tf_op jit(solution)/shard_map/ppermute | solution.py:427
  18.6 1.5 %collective-permute-start.5 = (bf16[2,8,16,128]{3,2,1,0:T(8,128)(2,1)S(1)}, bf16[2,8,16,128]{3,2,1,0:T(8,128)(2,1)S(1)}, u32[]{:S(2)}, u32[]{:S(2)}) collective-permute-start(bf16[2,8,16,128]{3,2,1,0:T(8,128)(2,1)S(1)} %get-tuple-element.52), channel_id=1, source_target_pairs={{0,9},{1,8},{2,11},{3,10},{4,13},{5,12},{6,15},{7,14},{8,1},{9,0},... | collective-permute-start | bytes 196616 | tf_op jit(solution)/shard_map/ppermute | solution.py:427
  20.1 3.4 %collective-permute-done.1.rest_1_ = bf16[2,8,16,128]{3,2,1,0:T(8,128)(2,1)S(1)} collective-permute-done((bf16[2,8,16,128]{3,2,1,0:T(8,128)(2,1)S(1)}, bf16[2,8,16,128]{3,2,1,0:T(8,128)(2,1)S(1)}, u32[]{:S(2)}, u32[]{:S(2)}) %collective-permute-start.1) | collective-permute-done | bytes 65568 | tf_op jit(solution)/shard_map/ppermute | solution.py:427
  23.8 1.4 %collective-permute-done.2.rest_2_ = bf16[2,8,16,128]{3,2,1,0:T(8,128)(2,1)S(1)} collective-permute-done((bf16[2,8,16,128]{3,2,1,0:T(8,128)(2,1)S(1)}, bf16[2,8,16,128]{3,2,1,0:T(8,128)(2,1)S(1)}, u32[]{:S(2)}, u32[]{:S(2)}) %collective-permute-start.2) | collective-permute-done | bytes 65568 | tf_op jit(solution)/shard_map/ppermute | solution.py:427
  25.3 0.8 %collective-permute-start.7 = (bf16[2,8,16,128]{3,2,1,0:T(8,128)(2,1)S(1)}, bf16[2,8,16,128]{3,2,1,0:T(8,128)(2,1)S(1)}, u32[]{:S(2)}, u32[]{:S(2)}) collective-permute-start(bf16[2,8,16,128]{3,2,1,0:T(8,128)(2,1)S(1)} %get-tuple-element.54), channel_id=1, source_target_pairs={{0,13},{1,12},{2,15},{3,14},{4,9},{5,8},{6,11},{7,10},{8,5},{9,4},... | collective-permute-start | bytes 196616 | tf_op jit(solution)/shard_map/ppermute | solution.py:427
  26.1 1.0 %copy-done.7 = bf16[16,128,128]{2,1,0:T(8,128)(2,1)S(1)} copy-done((bf16[16,128,128]{2,1,0:T(8,128)(2,1)S(1)}, bf16[16,128,128]{2,1,0:T(8,128)(2,1)}, u32[]{:S(2)}) %copy-start.7) | copy-done | bytes 524312
  27.1 1.6 %tri_gate.1 = (bf16[16,128,128]{2,1,0:T(8,128)(2,1)S(1)}, bf16[16,128,128]{2,1,0:T(8,128)(2,1)S(1)}, bf16[4,128]{1,0:T(4,128)(2,1)S(1)}) custom-call(bf16[16,128,128]{2,1,0:T(8,128)(2,1)S(1)} %copy-done.1, bf16[16,128,128]{2,1,0:T(8,128)(2,1)S(1)} %copy-done.7, bf16[128,128]{1,0:T(8,128)(2,1)S(1)} %copy-done.3, bf16[128,4]{1,0:T(8,128)(2,1)S(1)} %copy.10.bias_proj), custom_call_target="tpu_custom_call" | custom-call | flops 2000000000 | bytes 2099200 | tf_op jit(solution)/shard_map/tri_gate/pallas_call | solution.py:434
  29.5 1.3 %collective-permute-done.4.rest_4_ = bf16[2,8,16,128]{3,2,1,0:T(8,128)(2,1)S(1)} collective-permute-done((bf16[2,8,16,128]{3,2,1,0:T(8,128)(2,1)S(1)}, bf16[2,8,16,128]{3,2,1,0:T(8,128)(2,1)S(1)}, u32[]{:S(2)}, u32[]{:S(2)}) %collective-permute-start.4) | collective-permute-done | bytes 65568 | tf_op jit(solution)/shard_map/ppermute | solution.py:427
  30.9 1.5 %collective-permute-done.5.rest_5_ = bf16[2,8,16,128]{3,2,1,0:T(8,128)(2,1)S(1)} collective-permute-done((bf16[2,8,16,128]{3,2,1,0:T(8,128)(2,1)S(1)}, bf16[2,8,16,128]{3,2,1,0:T(8,128)(2,1)S(1)}, u32[]{:S(2)}, u32[]{:S(2)}) %collective-permute-start.5) | collective-permute-done | bytes 65568 | tf_op jit(solution)/shard_map/ppermute | solution.py:427
  32.4 2.7 %collective-permute-done.6.rest_6_ = bf16[2,8,16,128]{3,2,1,0:T(8,128)(2,1)S(1)} collective-permute-done((bf16[2,8,16,128]{3,2,1,0:T(8,128)(2,1)S(1)}, bf16[2,8,16,128]{3,2,1,0:T(8,128)(2,1)S(1)}, u32[]{:S(2)}, u32[]{:S(2)}) %collective-permute-start.6) | collective-permute-done | bytes 65568 | tf_op jit(solution)/shard_map/ppermute | solution.py:427
  35.0 2.9 %collective-permute-done.7.rest_7_ = bf16[2,8,16,128]{3,2,1,0:T(8,128)(2,1)S(1)} collective-permute-done((bf16[2,8,16,128]{3,2,1,0:T(8,128)(2,1)S(1)}, bf16[2,8,16,128]{3,2,1,0:T(8,128)(2,1)S(1)}, u32[]{:S(2)}, u32[]{:S(2)}) %collective-permute-start.7) | collective-permute-done | bytes 65568 | tf_op jit(solution)/shard_map/ppermute | solution.py:427
  38.4 12.1 %all_to_all.15 = bf16[16,8,16,128]{3,2,1,0:T(8,128)(2,1)S(1)} all-to-all(bf16[16,8,16,128]{3,2,1,0:T(8,128)(2,1)S(1)} %bitcast.4), channel_id=1, replica_groups={{15,14,13,12,11,10,9,8,7,6,5,4,3,2,1,0},{31,30,29,28,27,26,25,24,23,22,..., dimensions={0} | all-to-all | bytes 1048576 | tf_op jit(solution)/shard_map/all_to_all | solution.py:398
  50.5 1.3 %update.1 = (bf16[16,128,128]{2,1,0:T(8,128)(2,1)S(1)}, bf16[4,16,128]{2,1,0:T(8,128)(2,1)S(1)}) custom-call(bf16[128,16,128]{2,1,0:T(8,128)(2,1)S(1)} %bitcast.5, bf16[16,128,128]{2,1,0:T(8,128)(2,1)S(1)} %copy-done.6, bf16[16,128,128]{2,1,0:T(8,128)(2,1)S(1)} %get-tuple-element.64.gate, bf16[128,128]{1,0:T(8,128)(2,1)S(1)} %copy-done.4, ...), custom_call_target="tpu_custom_call" | custom-call | flops 2000000000 | bytes 1081344 | tf_op jit(solution)/shard_map/update/pallas_call | solution.py:454
  51.8 1.7 %collective-permute-start.9 = (bf16[16,128,128]{2,1,0:T(8,128)(2,1)S(1)}, bf16[16,128,128]{2,1,0:T(8,128)(2,1)S(1)}, u32[]{:S(2)}, u32[]{:S(2)}) collective-permute-start(bf16[16,128,128]{2,1,0:T(8,128)(2,1)S(1)} %get-tuple-element.67.updated), channel_id=1, source_target_pairs={{1,0},{0,1},{3,2},{2,3},{5,4},{4,5},{7,6},{6,7},{9,8},{8,9},{11,10... | collective-permute-start | bytes 1572872 | tf_op jit(solution)/shard_map/ppermute | solution.py:477
  53.6 2.9 %collective-permute-start.8 = (bf16[4,16,128]{2,1,0:T(8,128)(2,1)S(1)}, bf16[4,16,128]{2,1,0:T(8,128)(2,1)S(1)}, u32[]{:S(2)}, u32[]{:S(2)}) collective-permute-start(bf16[4,16,128]{2,1,0:T(8,128)(2,1)S(1)} %get-tuple-element.66.refs_0_), channel_id=1, source_target_pairs={{0,16},{1,17},{2,18},{3,19},{4,20},{5,21},{6,22},{7,23},{8,24},{9,... | collective-permute-start | bytes 49160 | tf_op jit(solution)/shard_map/ppermute | solution.py:427
  56.5 1.2 %own_projections.1 = (bf16[16,128,384]{2,1,0:T(8,128)(2,1)S(1)}, bf16[16,128,256]{2,1,0:T(8,128)(2,1)S(1)}) custom-call(bf16[16,128,128]{2,1,0:T(8,128)(2,1)S(1)} %get-tuple-element.67.updated, bf16[128,512]{1,0:T(8,128)(2,1)S(1)} %copy-done.2), custom_call_target="tpu_custom_call" | custom-call | flops 2000000000 | bytes 5242880 | tf_op jit(solution)/shard_map/own_projections/pallas_call | solution.py:482
  58.2 9.6 %all_to_all.16.mine = bf16[8,4,16,128]{3,2,1,0:T(8,128)(2,1)S(1)} all-to-all(bf16[8,4,16,128]{3,2,1,0:T(8,128)(2,1)S(1)} %deal_bias.1), channel_id=1, replica_groups={{13,12,9,8,5,4,1,0},{15,14,11,10,7,6,3,2},{29,28,25,24,21,20,17,16},{31..., dimensions={0} | all-to-all | bytes 262144 | tf_op jit(solution)/shard_map/all_to_all | solution.py:490
  67.8 0.9 %other_keys.1.rest_1_ = bf16[16,128,256]{2,1,0:T(8,128)(2,1)S(1)} custom-call(bf16[128,512]{1,0:T(8,128)(2,1)S(1)} %copy-done.2, bf16[16,128,128]{2,1,0:T(8,128)(2,1)S(1)} %collective-permute-done.9.rest_0_), custom_call_target="tpu_custom_call" | custom-call | flops 3000000000 | bytes 2097152 | tf_op jit(solution)/shard_map/other_keys/pallas_call | solution.py:494
  69.2 4.7 %attend.1 = bf16[16,128,128]{2,1,0:T(8,128)(2,1)} custom-call(s32[1]{0:T(128)S(6)} %copy.11.length, bf16[8,4,16,128]{3,2,1,0:T(8,128)(2,1)S(1)} %all_to_all.16.mine, bf16[8,4,16,128]{3,2,1,0:T(8,128)(2,1)S(1)} %collective-permute-done.10.sibling, bf16[128,128]{1,0:T(8,128)(2,1)S(1)} %copy-done, bf16[16,128,256]{2,1,0:T(8,128)(2,1)S(1)} %get-tuple-element.72.late, ...), custom_call_target="tpu_custom_call" | custom-call | flops 100000000 | bytes 1048576 | tf_op jit(solution)/shard_map/attend/pallas_call | solution.py:501
  (30 shorter events, 3.5 us)
Async XLA Ops:
  4.1 12.3 %copy-start.8 = (bf16[128,4]{0,1:T(4,128)(2,1)S(1)}, bf16[128,4]{0,1:T(4,128)(2,1)}, u32[]{:S(2)}) copy-start(bf16[128,4]{0,1:T(4,128)(2,1)} %param.16) | copy-start | bytes 3076
  4.1 22.0 %copy-start.1 = (bf16[16,128,128]{2,1,0:T(8,128)(2,1)S(1)}, bf16[16,128,128]{2,1,0:T(8,128)(2,1)}, u32[]{:S(2)}) copy-start(bf16[16,128,128]{2,1,0:T(8,128)(2,1)} %pair.1) | copy-start | bytes 1572868
  4.1 22.0 %copy-start.3 = (bf16[128,128]{1,0:T(8,128)(2,1)S(1)}, bf16[128,128]{1,0:T(8,128)(2,1)}, u32[]{:S(2)}) copy-start(bf16[128,128]{1,0:T(8,128)(2,1)} %weights.1) | copy-start | bytes 98308
  4.2 33.7 %all-to-all-start = ((bf16[32,8,16,128]{3,2,1,0:T(8,128)(2,1)}), bf16[32,8,16,128]{3,2,1,0:T(8,128)(2,1)S(1)}, u32[]{:S(2)}, u32[]{:S(2)}) async-start(bf16[32,8,16,128]{3,2,1,0:T(8,128)(2,1)} %get-tuple-element.40), calls=%async_computation | async-start | bytes 2097152 | tf_op jit(solution)/shard_map/all_to_all | solution.py:429
  11.5 1.6 %collective-permute-start = (bf16[8,8,16,128]{3,2,1,0:T(8,128)(2,1)S(1)}, bf16[8,8,16,128]{3,2,1,0:T(8,128)(2,1)S(1)}, u32[]{:S(2)}, u32[]{:S(2)}) collective-permute-start(bf16[8,8,16,128]{3,2,1,0:T(8,128)(2,1)S(1)} %get-tuple-element.46), channel_id=1, source_target_pairs={{0,2},{1,3},{2,0},{3,1},{4,6},{5,7},{6,4},{7,5},{8,10},{9,11},{10,... | collective-permute-start | bytes 786440 | tf_op jit(solution)/shard_map/ppermute | solution.py:427
  13.1 10.4 %collective-permute-start.1 = (bf16[2,8,16,128]{3,2,1,0:T(8,128)(2,1)S(1)}, bf16[2,8,16,128]{3,2,1,0:T(8,128)(2,1)S(1)}, u32[]{:S(2)}, u32[]{:S(2)}) collective-permute-start(bf16[2,8,16,128]{3,2,1,0:T(8,128)(2,1)S(1)} %get-tuple-element.48), channel_id=1, source_target_pairs={{0,1},{1,0},{2,3},{3,2},{4,5},{5,4},{6,7},{7,6},{8,9},{9,8},{10,11... | collective-permute-start | bytes 196616 | tf_op jit(solution)/shard_map/ppermute | solution.py:427
  15.0 10.3 %collective-permute-start.2 = (bf16[2,8,16,128]{3,2,1,0:T(8,128)(2,1)S(1)}, bf16[2,8,16,128]{3,2,1,0:T(8,128)(2,1)S(1)}, u32[]{:S(2)}, u32[]{:S(2)}) collective-permute-start(bf16[2,8,16,128]{3,2,1,0:T(8,128)(2,1)S(1)} %get-tuple-element.49), channel_id=1, source_target_pairs={{0,4},{1,5},{2,6},{3,7},{4,0},{5,1},{6,2},{7,3},{8,12},{9,13},{10,... | collective-permute-start | bytes 196616 | tf_op jit(solution)/shard_map/ppermute | solution.py:427
  16.6 13.0 %collective-permute-start.3 = (bf16[2,8,16,128]{3,2,1,0:T(8,128)(2,1)S(1)}, bf16[2,8,16,128]{3,2,1,0:T(8,128)(2,1)S(1)}, u32[]{:S(2)}, u32[]{:S(2)}) collective-permute-start(bf16[2,8,16,128]{3,2,1,0:T(8,128)(2,1)S(1)} %get-tuple-element.50), channel_id=1, source_target_pairs={{0,5},{1,4},{2,7},{3,6},{4,1},{5,0},{6,3},{7,2},{8,13},{9,12},{10,... | collective-permute-start | bytes 196616 | tf_op jit(solution)/shard_map/ppermute | solution.py:427
  16.9 14.0 %collective-permute-start.4 = (bf16[2,8,16,128]{3,2,1,0:T(8,128)(2,1)S(1)}, bf16[2,8,16,128]{3,2,1,0:T(8,128)(2,1)S(1)}, u32[]{:S(2)}, u32[]{:S(2)}) collective-permute-start(bf16[2,8,16,128]{3,2,1,0:T(8,128)(2,1)S(1)} %get-tuple-element.51), channel_id=1, source_target_pairs={{0,8},{1,9},{2,10},{3,11},{4,12},{5,13},{6,14},{7,15},{8,0},{9,1},... | collective-permute-start | bytes 196616 | tf_op jit(solution)/shard_map/ppermute | solution.py:427
  18.6 13.7 %collective-permute-start.5 = (bf16[2,8,16,128]{3,2,1,0:T(8,128)(2,1)S(1)}, bf16[2,8,16,128]{3,2,1,0:T(8,128)(2,1)S(1)}, u32[]{:S(2)}, u32[]{:S(2)}) collective-permute-start(bf16[2,8,16,128]{3,2,1,0:T(8,128)(2,1)S(1)} %get-tuple-element.52), channel_id=1, source_target_pairs={{0,9},{1,8},{2,11},{3,10},{4,13},{5,12},{6,15},{7,14},{8,1},{9,0},... | collective-permute-start | bytes 196616 | tf_op jit(solution)/shard_map/ppermute | solution.py:427
  23.5 11.5 %collective-permute-start.6 = (bf16[2,8,16,128]{3,2,1,0:T(8,128)(2,1)S(1)}, bf16[2,8,16,128]{3,2,1,0:T(8,128)(2,1)S(1)}, u32[]{:S(2)}, u32[]{:S(2)}) collective-permute-start(bf16[2,8,16,128]{3,2,1,0:T(8,128)(2,1)S(1)} %get-tuple-element.53), channel_id=1, source_target_pairs={{0,12},{1,13},{2,14},{3,15},{4,8},{5,9},{6,10},{7,11},{8,4},{9,5},... | collective-permute-start | bytes 196616 | tf_op jit(solution)/shard_map/ppermute | solution.py:427
  25.3 12.6 %collective-permute-start.7 = (bf16[2,8,16,128]{3,2,1,0:T(8,128)(2,1)S(1)}, bf16[2,8,16,128]{3,2,1,0:T(8,128)(2,1)S(1)}, u32[]{:S(2)}, u32[]{:S(2)}) collective-permute-start(bf16[2,8,16,128]{3,2,1,0:T(8,128)(2,1)S(1)} %get-tuple-element.54), channel_id=1, source_target_pairs={{0,13},{1,12},{2,15},{3,14},{4,9},{5,8},{6,11},{7,10},{8,5},{9,4},... | collective-permute-start | bytes 196616 | tf_op jit(solution)/shard_map/ppermute | solution.py:427
  26.1 1.0 %copy-start.7 = (bf16[16,128,128]{2,1,0:T(8,128)(2,1)S(1)}, bf16[16,128,128]{2,1,0:T(8,128)(2,1)}, u32[]{:S(2)}) copy-start(bf16[16,128,128]{2,1,0:T(8,128)(2,1)} %get-tuple-element.41.normed) | copy-start | bytes 1572868
  28.7 0.8 %copy-start.5 = (bf16[16,128,128]{2,1,0:T(8,128)(2,1)}, bf16[16,128,128]{2,1,0:T(8,128)(2,1)S(1)}, u32[]{:S(2)}) copy-start(bf16[16,128,128]{2,1,0:T(8,128)(2,1)S(1)} %get-tuple-element.63.source) | copy-start | bytes 1572868
  37.9 12.6 %copy-start.4 = (bf16[128,128]{1,0:T(8,128)(2,1)S(1)}, bf16[128,128]{1,0:T(8,128)(2,1)}, u32[]{:S(2)}) copy-start(bf16[128,128]{1,0:T(8,128)(2,1)} %tri_out.1) | copy-start | bytes 98308
  37.9 12.6 %copy-start.6 = (bf16[16,128,128]{2,1,0:T(8,128)(2,1)S(1)}, bf16[16,128,128]{2,1,0:T(8,128)(2,1)}, u32[]{:S(2)}) copy-start(bf16[16,128,128]{2,1,0:T(8,128)(2,1)} %copy-done.5) | copy-start | bytes 1572868
  50.5 6.0 %copy-start.2 = (bf16[128,512]{1,0:T(8,128)(2,1)S(1)}, bf16[128,512]{1,0:T(8,128)(2,1)}, u32[]{:S(2)}) copy-start(bf16[128,512]{1,0:T(8,128)(2,1)} %attn_proj.3) | copy-start | bytes 393220
  51.8 16.0 %collective-permute-start.9 = (bf16[16,128,128]{2,1,0:T(8,128)(2,1)S(1)}, bf16[16,128,128]{2,1,0:T(8,128)(2,1)S(1)}, u32[]{:S(2)}, u32[]{:S(2)}) collective-permute-start(bf16[16,128,128]{2,1,0:T(8,128)(2,1)S(1)} %get-tuple-element.67.updated), channel_id=1, source_target_pairs={{1,0},{0,1},{3,2},{2,3},{5,4},{4,5},{7,6},{6,7},{9,8},{8,9},{11,10... | collective-permute-start | bytes 1572872 | tf_op jit(solution)/shard_map/ppermute | solution.py:477
  53.6 4.6 %collective-permute-start.8 = (bf16[4,16,128]{2,1,0:T(8,128)(2,1)S(1)}, bf16[4,16,128]{2,1,0:T(8,128)(2,1)S(1)}, u32[]{:S(2)}, u32[]{:S(2)}) collective-permute-start(bf16[4,16,128]{2,1,0:T(8,128)(2,1)S(1)} %get-tuple-element.66.refs_0_), channel_id=1, source_target_pairs={{0,16},{1,17},{2,18},{3,19},{4,20},{5,21},{6,22},{7,23},{8,24},{9,... | collective-permute-start | bytes 49160 | tf_op jit(solution)/shard_map/ppermute | solution.py:427
  67.8 1.4 %copy-start = (bf16[128,128]{1,0:T(8,128)(2,1)S(1)}, bf16[128,128]{1,0:T(8,128)(2,1)}, u32[]{:S(2)}) copy-start(bf16[128,128]{1,0:T(8,128)(2,1)} %attn_out.1) | copy-start | bytes 98308
  67.8 1.3 %collective-permute-start.10 = (bf16[8,4,16,128]{3,2,1,0:T(8,128)(2,1)S(1)}, bf16[8,4,16,128]{3,2,1,0:T(8,128)(2,1)S(1)}, u32[]{:S(2)}, u32[]{:S(2)}) collective-permute-start(bf16[8,4,16,128]{3,2,1,0:T(8,128)(2,1)S(1)} %all_to_all.16.mine), channel_id=1, source_target_pairs={{0,2},{1,3},{2,0},{3,1},{4,6},{5,7},{6,4},{7,5},{8,10},{9,11},{10,... | collective-permute-start | bytes 393224 | tf_op jit(solution)/shard_map/ppermute | solution.py:427

commit v12 on v11

--- a/solution.py
+++ b/solution.py
@@ -272,7 +272,7 @@
     bias[...] = bias_held[...].astype(BF16).reshape(heads, rows, cols)
 
 
-def project(updated, attn_proj, mixed, row, score_scale, late=None):
+def project(updated, attn_proj, mixed, row, score_scale, late=None, query=None):
     channels = updated.shape[1]
     values = updated[row].astype(F32)
     normed = layer_norm(values, 0)
@@ -284,14 +284,20 @@
     put(mixed, 0, dot(turned(attn_proj[:, channels : 2 * channels]), normed.astype(BF16), (1, 0)))
     put(mixed, 1, dot(natural, attn_proj[:, 2 * channels : 3 * channels], (1, 0)))
     if late is not None:
-        put(mixed, 2, dot(natural, attn_proj[:, :channels], (1, 0)) * score_scale)
+        scaled = (dot(natural, attn_proj[:, :channels], (1, 0)) * score_scale).astype(BF16)
+        cols = natural.shape[0]
+        heads = query.shape[1] // cols
+        head_of = lax.broadcasted_iota(jnp.int32, (1, channels), 1) // (channels // heads)
+        for head in range(heads):
+            mask = (head_of == head).astype(BF16)
+            query[row, head * cols : (head + 1) * cols, :] = scaled * mask
         put(late, 0, sigmoid(dot(natural, attn_proj[:, 3 * channels :], (1, 0))))
         put(late, 1, values.T)
 
 
-def own_body(updated, attn_proj, mixed, late, *, score_scale):
+def own_body(updated, attn_proj, mixed, late, query, *, score_scale):
     def step(row, carry):
-        project(updated, attn_proj, mixed, row, score_scale, late)
+        project(updated, attn_proj, mixed, row, score_scale, late, query)
         return carry
 
     lax.fori_loop(0, updated.shape[0], step, 0, unroll=8)
@@ -308,7 +314,7 @@
         lax.fori_loop(0, updated.shape[0], step, 0, unroll=8)
 
 
-def attend_body(length, mine, sibling, attn_out, late, *rest):
+def attend_body(length, mine, sibling, attn_out, late, query, *rest):
     mixed, (out_hbm, out, bias_held, sems) = rest[:-4], rest[-4:]
     pieces = len(mixed)
     rows, cols, channels = out.shape
@@ -332,17 +338,18 @@
                         tiles[head].astype(F32) + key_term
                     )
     both_of = jnp.concatenate([head_of, head_of], axis=1)
-    masks = [(head_of == head).astype(BF16) for head in range(heads)]
     ones = jnp.ones((pieces * cols, channels), BF16)
 
     def load(row):
         keys = jnp.concatenate([part[row, :, :channels] for part in mixed], axis=1)
         values = jnp.concatenate([part[row, :, channels : 2 * channels] for part in mixed], axis=0)
         values = jnp.concatenate([values, ones], axis=1)
-        return keys, values, mixed[0][row, :, 2 * channels :]
+        return keys, values
 
     def finish(row, total):
-        attended = total[:, :channels] / total[:, channels:]
+        weight = total[:, channels:]
+        inverse = pl.reciprocal(weight, approx=True)
+        attended = total[:, :channels] * (inverse * (2.0 - weight * inverse))
         gate = late[row, :, :channels].astype(F32)
         gated = (attended * gate).astype(BF16)
         residual = late[row, :, channels:].astype(F32)
@@ -354,9 +361,7 @@
         row = time
         if row < rows:
             loaded[row] = load(row)
-            keys, _, query = loaded[row]
-            queries = jnp.concatenate([query * mask for mask in masks], axis=0)
-            logits[row] = dot(queries, keys, (1, 0)) + bias_held[...]
+            logits[row] = dot(query[row], loaded[row][0], (1, 0)) + bias_held[...]
         row = time - 1
         if 0 <= row < rows:
             scores = logits.pop(row)
@@ -477,16 +482,15 @@
         lax.ppermute(updated, "ch", [((c + s) % col_devices, c) for c in range(col_devices)])
         for s in range(1, col_devices)
     ]
-    mixed_shape = (rows, cols, 3 * channels)
     key_shape = (rows, cols, 2 * channels)
-    mixed, late = call(
+    mixed, late, query = call(
         functools.partial(own_body, score_scale=(channels // heads) ** (-0.5)),
         "own_projections",
-        [shape(mixed_shape, BF16), shape(key_shape, BF16)],
+        [shape(key_shape, BF16)] * 2 + [shape((rows, heads * cols, channels), BF16)],
         2,
         flops=2e9,
     )(updated, attn_proj)
-    dealt, mixed, late = lax.optimization_barrier((dealt, mixed, late))
+    dealt, mixed, late, query = lax.optimization_barrier((dealt, mixed, late, query))
     bias = lax.all_to_all(
         dealt, BOTH, split_axis=0, concat_axis=0, axis_index_groups=one_core, tiled=True
     )
@@ -502,7 +506,7 @@
         attend_body,
         "attend",
         [shape(block, BF16)],
-        5 + col_devices,
+        6 + col_devices,
         [
             pltpu.VMEM(block, BF16),
             pltpu.VMEM((heads * cols, col_devices * cols), F32),
@@ -510,7 +514,7 @@
         ],
         smem=1,
         out_space=HBM,
-    )(valid_count, bias, flipped(bias, col_devices), attn_out, late, mixed, *keys)
+    )(valid_count, bias, flipped(bias, col_devices), attn_out, late, query, mixed, *keys)
     return result
 
 

time: 74.2 us -> 74.2 us (level)
  no operation moved by 1% of the time
where the time goes in v12:
time: 74.2 us; the launch traced here: 73.9 us
  blocking collectives  21.7 us (29%)
  starting transfers between devices  20.3 us (27%)
  waiting for transfers between devices  15.2 us (20%)
  Pallas kernels  14 us (19%)
  local copies, waits for them, and re-layouts  2 us (3%)
  between operations  0.76 us (1%)
    ppermute x10, waiting for transfers between devices, flipped(): return lax.ppermute(array, BOTH, [(d, d ^ bits) for d in range(devices)])  15.2 us
    all_to_all x1, blocking collectives, in_half(): lax.all_to_all(array, BOTH, split_axis=0, concat_axis=0, axis_index_group...  12.1 us
    ppermute x10, starting transfers between devices, flipped(): return lax.ppermute(array, BOTH, [(d, d ^ bits) for d in range(devices)])  11.3 us
    all_to_all x1, blocking collectives, local(): lax.all_to_all(dealt, BOTH, split_axis=0, concat_axis=0, axis_index_group...  9.58 us
    all_to_all x1, starting transfers between devices, local(): right = lax.all_to_all(right, BOTH, split_axis=0, concat_axis=0, tiled=True)  7.3 us
    pallas_call x1, Pallas kernels, local(): call(attend_body, 'attend', [shape(block, BF16)], 6 + col_devices, [pltpu...  4.71 us
    pallas_call x1, Pallas kernels, local(): call(edges_body, 'edges', [shape((devices,) + tile, BF16), shape(block, B...  3.46 us
    unnamed x19, local copies, waits for them, and re-layouts  2 us
  transfers between devices with their start and end apart: 12, of which 9 were waited for; matrix products, arithmetic and copies ran while one was open for 0% of the time, Pallas kernels for 5%

profile of v12, /device:TPU:0, one launch (start us, length us, event | category | flops | bytes accessed | tf_op | source)
XLA Modules:
  0.0 73.9 jit_solution(9466562451568214)
XLA Ops:
  0.7 3.5 %edges.1 = (bf16[32,8,16,128]{3,2,1,0:T(8,128)(2,1)}, bf16[16,128,128]{2,1,0:T(8,128)(2,1)}, bf16[8,8,16,128]{3,2,1,0:T(8,128)(2,1)S(1)}, bf16[8,8,16,128]{3,2,1,0:T(8,128)(2,1)S(1)}) custom-call(s32[1]{0:T(128)S(6)} %copy.11.length, bf16[16,128,128]{2,1,0:T(8,128)(2,1)} %pair.1, bf16[128,256]{1,0:T(8,128)(2,1)} %proj_hbm.1, bf16[128,256]{1,0:T(8,128)(2,1)} %gate_hbm.1), custom_call_target="tpu_custom_call" | custom-call | flops 4000000000 | bytes 4194304 | tf_op jit(solution)/shard_map/edges/pallas_call | solution.py:411
  4.2 7.3 %all-to-all-start = ((bf16[32,8,16,128]{3,2,1,0:T(8,128)(2,1)}), bf16[32,8,16,128]{3,2,1,0:T(8,128)(2,1)S(1)}, u32[]{:S(2)}, u32[]{:S(2)}) async-start(bf16[32,8,16,128]{3,2,1,0:T(8,128)(2,1)} %get-tuple-element.42), calls=%async_computation | async-start | bytes 2097152 | tf_op jit(solution)/shard_map/all_to_all | solution.py:434
  11.8 1.3 %collective-permute-done.sibling = bf16[8,8,16,128]{3,2,1,0:T(8,128)(2,1)S(1)} collective-permute-done((bf16[8,8,16,128]{3,2,1,0:T(8,128)(2,1)S(1)}, bf16[8,8,16,128]{3,2,1,0:T(8,128)(2,1)S(1)}, u32[]{:S(2)}, u32[]{:S(2)}) %collective-permute-start) | collective-permute-done | bytes 262176 | tf_op jit(solution)/shard_map/ppermute | solution.py:432
  13.1 1.8 %collective-permute-start.1 = (bf16[2,8,16,128]{3,2,1,0:T(8,128)(2,1)S(1)}, bf16[2,8,16,128]{3,2,1,0:T(8,128)(2,1)S(1)}, u32[]{:S(2)}, u32[]{:S(2)}) collective-permute-start(bf16[2,8,16,128]{3,2,1,0:T(8,128)(2,1)S(1)} %get-tuple-element.50), channel_id=1, source_target_pairs={{0,1},{1,0},{2,3},{3,2},{4,5},{5,4},{6,7},{7,6},{8,9},{9,8},{10,11... | collective-permute-start | bytes 196616 | tf_op jit(solution)/shard_map/ppermute | solution.py:432
  15.0 1.5 %collective-permute-start.2 = (bf16[2,8,16,128]{3,2,1,0:T(8,128)(2,1)S(1)}, bf16[2,8,16,128]{3,2,1,0:T(8,128)(2,1)S(1)}, u32[]{:S(2)}, u32[]{:S(2)}) collective-permute-start(bf16[2,8,16,128]{3,2,1,0:T(8,128)(2,1)S(1)} %get-tuple-element.51), channel_id=1, source_target_pairs={{0,4},{1,5},{2,6},{3,7},{4,0},{5,1},{6,2},{7,3},{8,12},{9,13},{10,... | collective-permute-start | bytes 196616 | tf_op jit(solution)/shard_map/ppermute | solution.py:432
  16.9 1.8 %collective-permute-start.4 = (bf16[2,8,16,128]{3,2,1,0:T(8,128)(2,1)S(1)}, bf16[2,8,16,128]{3,2,1,0:T(8,128)(2,1)S(1)}, u32[]{:S(2)}, u32[]{:S(2)}) collective-permute-start(bf16[2,8,16,128]{3,2,1,0:T(8,128)(2,1)S(1)} %get-tuple-element.53), channel_id=1, source_target_pairs={{0,8},{1,9},{2,10},{3,11},{4,12},{5,13},{6,14},{7,15},{8,0},{9,1},... | collective-permute-start | bytes 196616 | tf_op jit(solution)/shard_map/ppermute | solution.py:432
  18.6 1.5 %collective-permute-start.5 = (bf16[2,8,16,128]{3,2,1,0:T(8,128)(2,1)S(1)}, bf16[2,8,16,128]{3,2,1,0:T(8,128)(2,1)S(1)}, u32[]{:S(2)}, u32[]{:S(2)}) collective-permute-start(bf16[2,8,16,128]{3,2,1,0:T(8,128)(2,1)S(1)} %get-tuple-element.54), channel_id=1, source_target_pairs={{0,9},{1,8},{2,11},{3,10},{4,13},{5,12},{6,15},{7,14},{8,1},{9,0},... | collective-permute-start | bytes 196616 | tf_op jit(solution)/shard_map/ppermute | solution.py:432
  20.1 3.4 %collective-permute-done.1.rest_1_ = bf16[2,8,16,128]{3,2,1,0:T(8,128)(2,1)S(1)} collective-permute-done((bf16[2,8,16,128]{3,2,1,0:T(8,128)(2,1)S(1)}, bf16[2,8,16,128]{3,2,1,0:T(8,128)(2,1)S(1)}, u32[]{:S(2)}, u32[]{:S(2)}) %collective-permute-start.1) | collective-permute-done | bytes 65568 | tf_op jit(solution)/shard_map/ppermute | solution.py:432
  23.8 1.4 %collective-permute-done.2.rest_2_ = bf16[2,8,16,128]{3,2,1,0:T(8,128)(2,1)S(1)} collective-permute-done((bf16[2,8,16,128]{3,2,1,0:T(8,128)(2,1)S(1)}, bf16[2,8,16,128]{3,2,1,0:T(8,128)(2,1)S(1)}, u32[]{:S(2)}, u32[]{:S(2)}) %collective-permute-start.2) | collective-permute-done | bytes 65568 | tf_op jit(solution)/shard_map/ppermute | solution.py:432
  25.3 0.8 %collective-permute-start.7 = (bf16[2,8,16,128]{3,2,1,0:T(8,128)(2,1)S(1)}, bf16[2,8,16,128]{3,2,1,0:T(8,128)(2,1)S(1)}, u32[]{:S(2)}, u32[]{:S(2)}) collective-permute-start(bf16[2,8,16,128]{3,2,1,0:T(8,128)(2,1)S(1)} %get-tuple-element.56), channel_id=1, source_target_pairs={{0,13},{1,12},{2,15},{3,14},{4,9},{5,8},{6,11},{7,10},{8,5},{9,4},... | collective-permute-start | bytes 196616 | tf_op jit(solution)/shard_map/ppermute | solution.py:432
  26.1 1.0 %copy-done.7 = bf16[16,128,128]{2,1,0:T(8,128)(2,1)S(1)} copy-done((bf16[16,128,128]{2,1,0:T(8,128)(2,1)S(1)}, bf16[16,128,128]{2,1,0:T(8,128)(2,1)}, u32[]{:S(2)}) %copy-start.7) | copy-done | bytes 524312
  27.1 1.6 %tri_gate.1 = (bf16[16,128,128]{2,1,0:T(8,128)(2,1)S(1)}, bf16[16,128,128]{2,1,0:T(8,128)(2,1)S(1)}, bf16[4,128]{1,0:T(4,128)(2,1)S(1)}) custom-call(bf16[16,128,128]{2,1,0:T(8,128)(2,1)S(1)} %copy-done.1, bf16[16,128,128]{2,1,0:T(8,128)(2,1)S(1)} %copy-done.7, bf16[128,128]{1,0:T(8,128)(2,1)S(1)} %copy-done.3, bf16[128,4]{1,0:T(8,128)(2,1)S(1)} %copy.10.bias_proj), custom_call_target="tpu_custom_call" | custom-call | flops 2000000000 | bytes 2099200 | tf_op jit(solution)/shard_map/tri_gate/pallas_call | solution.py:439
  29.5 1.3 %collective-permute-done.4.rest_4_ = bf16[2,8,16,128]{3,2,1,0:T(8,128)(2,1)S(1)} collective-permute-done((bf16[2,8,16,128]{3,2,1,0:T(8,128)(2,1)S(1)}, bf16[2,8,16,128]{3,2,1,0:T(8,128)(2,1)S(1)}, u32[]{:S(2)}, u32[]{:S(2)}) %collective-permute-start.4) | collective-permute-done | bytes 65568 | tf_op jit(solution)/shard_map/ppermute | solution.py:432
  30.9 1.5 %collective-permute-done.5.rest_5_ = bf16[2,8,16,128]{3,2,1,0:T(8,128)(2,1)S(1)} collective-permute-done((bf16[2,8,16,128]{3,2,1,0:T(8,128)(2,1)S(1)}, bf16[2,8,16,128]{3,2,1,0:T(8,128)(2,1)S(1)}, u32[]{:S(2)}, u32[]{:S(2)}) %collective-permute-start.5) | collective-permute-done | bytes 65568 | tf_op jit(solution)/shard_map/ppermute | solution.py:432
  32.4 2.7 %collective-permute-done.6.rest_6_ = bf16[2,8,16,128]{3,2,1,0:T(8,128)(2,1)S(1)} collective-permute-done((bf16[2,8,16,128]{3,2,1,0:T(8,128)(2,1)S(1)}, bf16[2,8,16,128]{3,2,1,0:T(8,128)(2,1)S(1)}, u32[]{:S(2)}, u32[]{:S(2)}) %collective-permute-start.6) | collective-permute-done | bytes 65568 | tf_op jit(solution)/shard_map/ppermute | solution.py:432
  35.0 2.9 %collective-permute-done.7.rest_7_ = bf16[2,8,16,128]{3,2,1,0:T(8,128)(2,1)S(1)} collective-permute-done((bf16[2,8,16,128]{3,2,1,0:T(8,128)(2,1)S(1)}, bf16[2,8,16,128]{3,2,1,0:T(8,128)(2,1)S(1)}, u32[]{:S(2)}, u32[]{:S(2)}) %collective-permute-start.7) | collective-permute-done | bytes 65568 | tf_op jit(solution)/shard_map/ppermute | solution.py:432
  38.4 12.1 %all_to_all.15 = bf16[16,8,16,128]{3,2,1,0:T(8,128)(2,1)S(1)} all-to-all(bf16[16,8,16,128]{3,2,1,0:T(8,128)(2,1)S(1)} %bitcast.4), channel_id=1, replica_groups={{15,14,13,12,11,10,9,8,7,6,5,4,3,2,1,0},{31,30,29,28,27,26,25,24,23,22,..., dimensions={0} | all-to-all | bytes 1048576 | tf_op jit(solution)/shard_map/all_to_all | solution.py:403
  50.5 1.3 %update.1 = (bf16[16,128,128]{2,1,0:T(8,128)(2,1)S(1)}, bf16[4,16,128]{2,1,0:T(8,128)(2,1)S(1)}) custom-call(bf16[128,16,128]{2,1,0:T(8,128)(2,1)S(1)} %bitcast.5, bf16[16,128,128]{2,1,0:T(8,128)(2,1)S(1)} %copy-done.6, bf16[16,128,128]{2,1,0:T(8,128)(2,1)S(1)} %get-tuple-element.66.gate, bf16[128,128]{1,0:T(8,128)(2,1)S(1)} %copy-done.4, ...), custom_call_target="tpu_custom_call" | custom-call | flops 2000000000 | bytes 1081344 | tf_op jit(solution)/shard_map/update/pallas_call | solution.py:459
  51.8 1.7 %collective-permute-start.9 = (bf16[16,128,128]{2,1,0:T(8,128)(2,1)S(1)}, bf16[16,128,128]{2,1,0:T(8,128)(2,1)S(1)}, u32[]{:S(2)}, u32[]{:S(2)}) collective-permute-start(bf16[16,128,128]{2,1,0:T(8,128)(2,1)S(1)} %get-tuple-element.69.updated), channel_id=1, source_target_pairs={{1,0},{0,1},{3,2},{2,3},{5,4},{4,5},{7,6},{6,7},{9,8},{8,9},{11,10... | collective-permute-start | bytes 1572872 | tf_op jit(solution)/shard_map/ppermute | solution.py:482
  53.6 2.9 %collective-permute-start.8 = (bf16[4,16,128]{2,1,0:T(8,128)(2,1)S(1)}, bf16[4,16,128]{2,1,0:T(8,128)(2,1)S(1)}, u32[]{:S(2)}, u32[]{:S(2)}) collective-permute-start(bf16[4,16,128]{2,1,0:T(8,128)(2,1)S(1)} %get-tuple-element.68.refs_0_), channel_id=1, source_target_pairs={{0,16},{1,17},{2,18},{3,19},{4,20},{5,21},{6,22},{7,23},{8,24},{9,... | collective-permute-start | bytes 49160 | tf_op jit(solution)/shard_map/ppermute | solution.py:432
  56.5 1.4 %own_projections.1 = (bf16[16,128,256]{2,1,0:T(8,128)(2,1)S(1)}, bf16[16,128,256]{2,1,0:T(8,128)(2,1)S(1)}, bf16[16,512,128]{2,1,0:T(8,128)(2,1)S(1)}) custom-call(bf16[16,128,128]{2,1,0:T(8,128)(2,1)S(1)} %get-tuple-element.69.updated, bf16[128,512]{1,0:T(8,128)(2,1)S(1)} %copy-done.2), custom_call_target="tpu_custom_call" | custom-call | flops 2000000000 | bytes 8388608 | tf_op jit(solution)/shard_map/own_projections/pallas_call | solution.py:486
  58.2 9.6 %all_to_all.16.mine = bf16[8,4,16,128]{3,2,1,0:T(8,128)(2,1)S(1)} all-to-all(bf16[8,4,16,128]{3,2,1,0:T(8,128)(2,1)S(1)} %deal_bias.1), channel_id=1, replica_groups={{13,12,9,8,5,4,1,0},{15,14,11,10,7,6,3,2},{29,28,25,24,21,20,17,16},{31..., dimensions={0} | all-to-all | bytes 262144 | tf_op jit(solution)/shard_map/all_to_all | solution.py:494
  67.8 0.9 %other_keys.1.rest_1_ = bf16[16,128,256]{2,1,0:T(8,128)(2,1)S(1)} custom-call(bf16[128,512]{1,0:T(8,128)(2,1)S(1)} %copy-done.2, bf16[16,128,128]{2,1,0:T(8,128)(2,1)S(1)} %collective-permute-done.9.rest_0_), custom_call_target="tpu_custom_call" | custom-call | flops 3000000000 | bytes 2097152 | tf_op jit(solution)/shard_map/other_keys/pallas_call | solution.py:498
  69.2 4.7 %attend.1 = bf16[16,128,128]{2,1,0:T(8,128)(2,1)} custom-call(s32[1]{0:T(128)S(6)} %copy.11.length, bf16[8,4,16,128]{3,2,1,0:T(8,128)(2,1)S(1)} %all_to_all.16.mine, bf16[8,4,16,128]{3,2,1,0:T(8,128)(2,1)S(1)} %collective-permute-done.10.sibling, bf16[128,128]{1,0:T(8,128)(2,1)S(1)} %copy-done, bf16[16,128,256]{2,1,0:T(8,128)(2,1)S(1)} %get-tuple-element.75.late, ...), custom_call_target="tpu_custom_call" | custom-call | flops 100000000 | bytes 1048576 | tf_op jit(solution)/shard_map/attend/pallas_call | solution.py:505
  (30 shorter events, 3.2 us)
Async XLA Ops:
  4.1 12.3 %copy-start.8 = (bf16[128,4]{0,1:T(4,128)(2,1)S(1)}, bf16[128,4]{0,1:T(4,128)(2,1)}, u32[]{:S(2)}) copy-start(bf16[128,4]{0,1:T(4,128)(2,1)} %param.16) | copy-start | bytes 3076
  4.1 22.0 %copy-start.1 = (bf16[16,128,128]{2,1,0:T(8,128)(2,1)S(1)}, bf16[16,128,128]{2,1,0:T(8,128)(2,1)}, u32[]{:S(2)}) copy-start(bf16[16,128,128]{2,1,0:T(8,128)(2,1)} %pair.1) | copy-start | bytes 1572868
  4.1 22.0 %copy-start.3 = (bf16[128,128]{1,0:T(8,128)(2,1)S(1)}, bf16[128,128]{1,0:T(8,128)(2,1)}, u32[]{:S(2)}) copy-start(bf16[128,128]{1,0:T(8,128)(2,1)} %weights.1) | copy-start | bytes 98308
  4.2 33.7 %all-to-all-start = ((bf16[32,8,16,128]{3,2,1,0:T(8,128)(2,1)}), bf16[32,8,16,128]{3,2,1,0:T(8,128)(2,1)S(1)}, u32[]{:S(2)}, u32[]{:S(2)}) async-start(bf16[32,8,16,128]{3,2,1,0:T(8,128)(2,1)} %get-tuple-element.42), calls=%async_computation | async-start | bytes 2097152 | tf_op jit(solution)/shard_map/all_to_all | solution.py:434
  11.5 1.6 %collective-permute-start = (bf16[8,8,16,128]{3,2,1,0:T(8,128)(2,1)S(1)}, bf16[8,8,16,128]{3,2,1,0:T(8,128)(2,1)S(1)}, u32[]{:S(2)}, u32[]{:S(2)}) collective-permute-start(bf16[8,8,16,128]{3,2,1,0:T(8,128)(2,1)S(1)} %get-tuple-element.48), channel_id=1, source_target_pairs={{0,2},{1,3},{2,0},{3,1},{4,6},{5,7},{6,4},{7,5},{8,10},{9,11},{10,... | collective-permute-start | bytes 786440 | tf_op jit(solution)/shard_map/ppermute | solution.py:432
  13.1 10.4 %collective-permute-start.1 = (bf16[2,8,16,128]{3,2,1,0:T(8,128)(2,1)S(1)}, bf16[2,8,16,128]{3,2,1,0:T(8,128)(2,1)S(1)}, u32[]{:S(2)}, u32[]{:S(2)}) collective-permute-start(bf16[2,8,16,128]{3,2,1,0:T(8,128)(2,1)S(1)} %get-tuple-element.50), channel_id=1, source_target_pairs={{0,1},{1,0},{2,3},{3,2},{4,5},{5,4},{6,7},{7,6},{8,9},{9,8},{10,11... | collective-permute-start | bytes 196616 | tf_op jit(solution)/shard_map/ppermute | solution.py:432
  15.0 10.3 %collective-permute-start.2 = (bf16[2,8,16,128]{3,2,1,0:T(8,128)(2,1)S(1)}, bf16[2,8,16,128]{3,2,1,0:T(8,128)(2,1)S(1)}, u32[]{:S(2)}, u32[]{:S(2)}) collective-permute-start(bf16[2,8,16,128]{3,2,1,0:T(8,128)(2,1)S(1)} %get-tuple-element.51), channel_id=1, source_target_pairs={{0,4},{1,5},{2,6},{3,7},{4,0},{5,1},{6,2},{7,3},{8,12},{9,13},{10,... | collective-permute-start | bytes 196616 | tf_op jit(solution)/shard_map/ppermute | solution.py:432
  16.6 13.0 %collective-permute-start.3 = (bf16[2,8,16,128]{3,2,1,0:T(8,128)(2,1)S(1)}, bf16[2,8,16,128]{3,2,1,0:T(8,128)(2,1)S(1)}, u32[]{:S(2)}, u32[]{:S(2)}) collective-permute-start(bf16[2,8,16,128]{3,2,1,0:T(8,128)(2,1)S(1)} %get-tuple-element.52), channel_id=1, source_target_pairs={{0,5},{1,4},{2,7},{3,6},{4,1},{5,0},{6,3},{7,2},{8,13},{9,12},{10,... | collective-permute-start | bytes 196616 | tf_op jit(solution)/shard_map/ppermute | solution.py:432
  16.9 14.0 %collective-permute-start.4 = (bf16[2,8,16,128]{3,2,1,0:T(8,128)(2,1)S(1)}, bf16[2,8,16,128]{3,2,1,0:T(8,128)(2,1)S(1)}, u32[]{:S(2)}, u32[]{:S(2)}) collective-permute-start(bf16[2,8,16,128]{3,2,1,0:T(8,128)(2,1)S(1)} %get-tuple-element.53), channel_id=1, source_target_pairs={{0,8},{1,9},{2,10},{3,11},{4,12},{5,13},{6,14},{7,15},{8,0},{9,1},... | collective-permute-start | bytes 196616 | tf_op jit(solution)/shard_map/ppermute | solution.py:432
  18.6 13.7 %collective-permute-start.5 = (bf16[2,8,16,128]{3,2,1,0:T(8,128)(2,1)S(1)}, bf16[2,8,16,128]{3,2,1,0:T(8,128)(2,1)S(1)}, u32[]{:S(2)}, u32[]{:S(2)}) collective-permute-start(bf16[2,8,16,128]{3,2,1,0:T(8,128)(2,1)S(1)} %get-tuple-element.54), channel_id=1, source_target_pairs={{0,9},{1,8},{2,11},{3,10},{4,13},{5,12},{6,15},{7,14},{8,1},{9,0},... | collective-permute-start | bytes 196616 | tf_op jit(solution)/shard_map/ppermute | solution.py:432
  23.5 11.5 %collective-permute-start.6 = (bf16[2,8,16,128]{3,2,1,0:T(8,128)(2,1)S(1)}, bf16[2,8,16,128]{3,2,1,0:T(8,128)(2,1)S(1)}, u32[]{:S(2)}, u32[]{:S(2)}) collective-permute-start(bf16[2,8,16,128]{3,2,1,0:T(8,128)(2,1)S(1)} %get-tuple-element.55), channel_id=1, source_target_pairs={{0,12},{1,13},{2,14},{3,15},{4,8},{5,9},{6,10},{7,11},{8,4},{9,5},... | collective-permute-start | bytes 196616 | tf_op jit(solution)/shard_map/ppermute | solution.py:432
  25.3 12.6 %collective-permute-start.7 = (bf16[2,8,16,128]{3,2,1,0:T(8,128)(2,1)S(1)}, bf16[2,8,16,128]{3,2,1,0:T(8,128)(2,1)S(1)}, u32[]{:S(2)}, u32[]{:S(2)}) collective-permute-start(bf16[2,8,16,128]{3,2,1,0:T(8,128)(2,1)S(1)} %get-tuple-element.56), channel_id=1, source_target_pairs={{0,13},{1,12},{2,15},{3,14},{4,9},{5,8},{6,11},{7,10},{8,5},{9,4},... | collective-permute-start | bytes 196616 | tf_op jit(solution)/shard_map/ppermute | solution.py:432
  26.1 1.0 %copy-start.7 = (bf16[16,128,128]{2,1,0:T(8,128)(2,1)S(1)}, bf16[16,128,128]{2,1,0:T(8,128)(2,1)}, u32[]{:S(2)}) copy-start(bf16[16,128,128]{2,1,0:T(8,128)(2,1)} %get-tuple-element.43.normed) | copy-start | bytes 1572868
  28.7 0.8 %copy-start.5 = (bf16[16,128,128]{2,1,0:T(8,128)(2,1)}, bf16[16,128,128]{2,1,0:T(8,128)(2,1)S(1)}, u32[]{:S(2)}) copy-start(bf16[16,128,128]{2,1,0:T(8,128)(2,1)S(1)} %get-tuple-element.65.source) | copy-start | bytes 1572868
  37.9 12.6 %copy-start.4 = (bf16[128,128]{1,0:T(8,128)(2,1)S(1)}, bf16[128,128]{1,0:T(8,128)(2,1)}, u32[]{:S(2)}) copy-start(bf16[128,128]{1,0:T(8,128)(2,1)} %tri_out.1) | copy-start | bytes 98308
  37.9 12.6 %copy-start.6 = (bf16[16,128,128]{2,1,0:T(8,128)(2,1)S(1)}, bf16[16,128,128]{2,1,0:T(8,128)(2,1)}, u32[]{:S(2)}) copy-start(bf16[16,128,128]{2,1,0:T(8,128)(2,1)} %copy-done.5) | copy-start | bytes 1572868
  50.5 6.0 %copy-start.2 = (bf16[128,512]{1,0:T(8,128)(2,1)S(1)}, bf16[128,512]{1,0:T(8,128)(2,1)}, u32[]{:S(2)}) copy-start(bf16[128,512]{1,0:T(8,128)(2,1)} %attn_proj.3) | copy-start | bytes 393220
  51.8 16.0 %collective-permute-start.9 = (bf16[16,128,128]{2,1,0:T(8,128)(2,1)S(1)}, bf16[16,128,128]{2,1,0:T(8,128)(2,1)S(1)}, u32[]{:S(2)}, u32[]{:S(2)}) collective-permute-start(bf16[16,128,128]{2,1,0:T(8,128)(2,1)S(1)} %get-tuple-element.69.updated), channel_id=1, source_target_pairs={{1,0},{0,1},{3,2},{2,3},{5,4},{4,5},{7,6},{6,7},{9,8},{8,9},{11,10... | collective-permute-start | bytes 1572872 | tf_op jit(solution)/shard_map/ppermute | solution.py:482
  53.6 4.6 %collective-permute-start.8 = (bf16[4,16,128]{2,1,0:T(8,128)(2,1)S(1)}, bf16[4,16,128]{2,1,0:T(8,128)(2,1)S(1)}, u32[]{:S(2)}, u32[]{:S(2)}) collective-permute-start(bf16[4,16,128]{2,1,0:T(8,128)(2,1)S(1)} %get-tuple-element.68.refs_0_), channel_id=1, source_target_pairs={{0,16},{1,17},{2,18},{3,19},{4,20},{5,21},{6,22},{7,23},{8,24},{9,... | collective-permute-start | bytes 49160 | tf_op jit(solution)/shard_map/ppermute | solution.py:432
  67.8 1.4 %copy-start = (bf16[128,128]{1,0:T(8,128)(2,1)S(1)}, bf16[128,128]{1,0:T(8,128)(2,1)}, u32[]{:S(2)}) copy-start(bf16[128,128]{1,0:T(8,128)(2,1)} %attn_out.1) | copy-start | bytes 98308
  67.8 1.3 %collective-permute-start.10 = (bf16[8,4,16,128]{3,2,1,0:T(8,128)(2,1)S(1)}, bf16[8,4,16,128]{3,2,1,0:T(8,128)(2,1)S(1)}, u32[]{:S(2)}, u32[]{:S(2)}) collective-permute-start(bf16[8,4,16,128]{3,2,1,0:T(8,128)(2,1)S(1)} %all_to_all.16.mine), channel_id=1, source_target_pairs={{0,2},{1,3},{2,0},{3,1},{4,6},{5,7},{6,4},{7,5},{8,10},{9,11},{10,... | collective-permute-start | bytes 393224 | tf_op jit(solution)/shard_map/ppermute | solution.py:432

commit v13 on v11

--- a/solution.py
+++ b/solution.py
@@ -506,7 +506,7 @@
         [
             pltpu.VMEM(block, BF16),
             pltpu.VMEM((heads * cols, col_devices * cols), F32),
-            pltpu.SemaphoreType.DMA((1, rows // 2)),
+            pltpu.SemaphoreType.DMA((1, rows)),
         ],
         smem=1,
         out_space=HBM,

time: 74.2 us -> 74.2 us (level)
  no operation moved by 1% of the time
where the time goes in v13:
time: 74.2 us; the launch traced here: 73.9 us
  blocking collectives  21.7 us (29%)
  starting transfers between devices  20.3 us (27%)
  waiting for transfers between devices  15.4 us (21%)
  Pallas kernels  13.7 us (18%)
  local copies, waits for them, and re-layouts  2 us (3%)
  between operations  0.76 us (1%)
    ppermute x10, waiting for transfers between devices, flipped(): return lax.ppermute(array, BOTH, [(d, d ^ bits) for d in range(devices)])  15.4 us
    all_to_all x1, blocking collectives, in_half(): lax.all_to_all(array, BOTH, split_axis=0, concat_axis=0, axis_index_group...  12.1 us
    ppermute x10, starting transfers between devices, flipped(): return lax.ppermute(array, BOTH, [(d, d ^ bits) for d in range(devices)])  11.3 us
    all_to_all x1, blocking collectives, local(): lax.all_to_all(dealt, BOTH, split_axis=0, concat_axis=0, axis_index_group...  9.58 us
    all_to_all x1, starting transfers between devices, local(): right = lax.all_to_all(right, BOTH, split_axis=0, concat_axis=0, tiled=True)  7.3 us
    pallas_call x1, Pallas kernels, local(): call(attend_body, 'attend', [shape(block, BF16)], 5 + col_devices, [pltpu...  4.73 us
    pallas_call x1, Pallas kernels, local(): call(edges_body, 'edges', [shape((devices,) + tile, BF16), shape(block, B...  3.46 us
    unnamed x19, local copies, waits for them, and re-layouts  2 us
  transfers between devices with their start and end apart: 12, of which 9 were waited for; matrix products, arithmetic and copies ran while one was open for 0% of the time, Pallas kernels for 5%

profile of v13, /device:TPU:0, one launch (start us, length us, event | category | flops | bytes accessed | tf_op | source)
XLA Modules:
  0.0 73.9 jit_solution(11992024101829581839)
XLA Ops:
  0.7 3.5 %edges.1 = (bf16[32,8,16,128]{3,2,1,0:T(8,128)(2,1)}, bf16[16,128,128]{2,1,0:T(8,128)(2,1)}, bf16[8,8,16,128]{3,2,1,0:T(8,128)(2,1)S(1)}, bf16[8,8,16,128]{3,2,1,0:T(8,128)(2,1)S(1)}) custom-call(s32[1]{0:T(128)S(6)} %copy.11.length, bf16[16,128,128]{2,1,0:T(8,128)(2,1)} %pair.1, bf16[128,256]{1,0:T(8,128)(2,1)} %proj_hbm.1, bf16[128,256]{1,0:T(8,128)(2,1)} %gate_hbm.1), custom_call_target="tpu_custom_call" | custom-call | flops 4000000000 | bytes 4194304 | tf_op jit(solution)/shard_map/edges/pallas_call | solution.py:406
  4.2 7.3 %all-to-all-start = ((bf16[32,8,16,128]{3,2,1,0:T(8,128)(2,1)}), bf16[32,8,16,128]{3,2,1,0:T(8,128)(2,1)S(1)}, u32[]{:S(2)}, u32[]{:S(2)}) async-start(bf16[32,8,16,128]{3,2,1,0:T(8,128)(2,1)} %get-tuple-element.40), calls=%async_computation | async-start | bytes 2097152 | tf_op jit(solution)/shard_map/all_to_all | solution.py:429
  11.8 1.3 %collective-permute-done.sibling = bf16[8,8,16,128]{3,2,1,0:T(8,128)(2,1)S(1)} collective-permute-done((bf16[8,8,16,128]{3,2,1,0:T(8,128)(2,1)S(1)}, bf16[8,8,16,128]{3,2,1,0:T(8,128)(2,1)S(1)}, u32[]{:S(2)}, u32[]{:S(2)}) %collective-permute-start) | collective-permute-done | bytes 262176 | tf_op jit(solution)/shard_map/ppermute | solution.py:427
  13.1 1.8 %collective-permute-start.1 = (bf16[2,8,16,128]{3,2,1,0:T(8,128)(2,1)S(1)}, bf16[2,8,16,128]{3,2,1,0:T(8,128)(2,1)S(1)}, u32[]{:S(2)}, u32[]{:S(2)}) collective-permute-start(bf16[2,8,16,128]{3,2,1,0:T(8,128)(2,1)S(1)} %get-tuple-element.48), channel_id=1, source_target_pairs={{0,1},{1,0},{2,3},{3,2},{4,5},{5,4},{6,7},{7,6},{8,9},{9,8},{10,11... | collective-permute-start | bytes 196616 | tf_op jit(solution)/shard_map/ppermute | solution.py:427
  15.0 1.5 %collective-permute-start.2 = (bf16[2,8,16,128]{3,2,1,0:T(8,128)(2,1)S(1)}, bf16[2,8,16,128]{3,2,1,0:T(8,128)(2,1)S(1)}, u32[]{:S(2)}, u32[]{:S(2)}) collective-permute-start(bf16[2,8,16,128]{3,2,1,0:T(8,128)(2,1)S(1)} %get-tuple-element.49), channel_id=1, source_target_pairs={{0,4},{1,5},{2,6},{3,7},{4,0},{5,1},{6,2},{7,3},{8,12},{9,13},{10,... | collective-permute-start | bytes 196616 | tf_op jit(solution)/shard_map/ppermute | solution.py:427
  16.9 1.8 %collective-permute-start.4 = (bf16[2,8,16,128]{3,2,1,0:T(8,128)(2,1)S(1)}, bf16[2,8,16,128]{3,2,1,0:T(8,128)(2,1)S(1)}, u32[]{:S(2)}, u32[]{:S(2)}) collective-permute-start(bf16[2,8,16,128]{3,2,1,0:T(8,128)(2,1)S(1)} %get-tuple-element.51), channel_id=1, source_target_pairs={{0,8},{1,9},{2,10},{3,11},{4,12},{5,13},{6,14},{7,15},{8,0},{9,1},... | collective-permute-start | bytes 196616 | tf_op jit(solution)/shard_map/ppermute | solution.py:427
  18.6 1.5 %collective-permute-start.5 = (bf16[2,8,16,128]{3,2,1,0:T(8,128)(2,1)S(1)}, bf16[2,8,16,128]{3,2,1,0:T(8,128)(2,1)S(1)}, u32[]{:S(2)}, u32[]{:S(2)}) collective-permute-start(bf16[2,8,16,128]{3,2,1,0:T(8,128)(2,1)S(1)} %get-tuple-element.52), channel_id=1, source_target_pairs={{0,9},{1,8},{2,11},{3,10},{4,13},{5,12},{6,15},{7,14},{8,1},{9,0},... | collective-permute-start | bytes 196616 | tf_op jit(solution)/shard_map/ppermute | solution.py:427
  20.1 3.4 %collective-permute-done.1.rest_1_ = bf16[2,8,16,128]{3,2,1,0:T(8,128)(2,1)S(1)} collective-permute-done((bf16[2,8,16,128]{3,2,1,0:T(8,128)(2,1)S(1)}, bf16[2,8,16,128]{3,2,1,0:T(8,128)(2,1)S(1)}, u32[]{:S(2)}, u32[]{:S(2)}) %collective-permute-start.1) | collective-permute-done | bytes 65568 | tf_op jit(solution)/shard_map/ppermute | solution.py:427
  23.8 1.4 %collective-permute-done.2.rest_2_ = bf16[2,8,16,128]{3,2,1,0:T(8,128)(2,1)S(1)} collective-permute-done((bf16[2,8,16,128]{3,2,1,0:T(8,128)(2,1)S(1)}, bf16[2,8,16,128]{3,2,1,0:T(8,128)(2,1)S(1)}, u32[]{:S(2)}, u32[]{:S(2)}) %collective-permute-start.2) | collective-permute-done | bytes 65568 | tf_op jit(solution)/shard_map/ppermute | solution.py:427
  25.3 0.8 %collective-permute-start.7 = (bf16[2,8,16,128]{3,2,1,0:T(8,128)(2,1)S(1)}, bf16[2,8,16,128]{3,2,1,0:T(8,128)(2,1)S(1)}, u32[]{:S(2)}, u32[]{:S(2)}) collective-permute-start(bf16[2,8,16,128]{3,2,1,0:T(8,128)(2,1)S(1)} %get-tuple-element.54), channel_id=1, source_target_pairs={{0,13},{1,12},{2,15},{3,14},{4,9},{5,8},{6,11},{7,10},{8,5},{9,4},... | collective-permute-start | bytes 196616 | tf_op jit(solution)/shard_map/ppermute | solution.py:427
  26.1 1.0 %copy-done.7 = bf16[16,128,128]{2,1,0:T(8,128)(2,1)S(1)} copy-done((bf16[16,128,128]{2,1,0:T(8,128)(2,1)S(1)}, bf16[16,128,128]{2,1,0:T(8,128)(2,1)}, u32[]{:S(2)}) %copy-start.7) | copy-done | bytes 524312
  27.1 1.6 %tri_gate.1 = (bf16[16,128,128]{2,1,0:T(8,128)(2,1)S(1)}, bf16[16,128,128]{2,1,0:T(8,128)(2,1)S(1)}, bf16[4,128]{1,0:T(4,128)(2,1)S(1)}) custom-call(bf16[16,128,128]{2,1,0:T(8,128)(2,1)S(1)} %copy-done.1, bf16[16,128,128]{2,1,0:T(8,128)(2,1)S(1)} %copy-done.7, bf16[128,128]{1,0:T(8,128)(2,1)S(1)} %copy-done.3, bf16[128,4]{1,0:T(8,128)(2,1)S(1)} %copy.10.bias_proj), custom_call_target="tpu_custom_call" | custom-call | flops 2000000000 | bytes 2099200 | tf_op jit(solution)/shard_map/tri_gate/pallas_call | solution.py:434
  29.5 1.3 %collective-permute-done.4.rest_4_ = bf16[2,8,16,128]{3,2,1,0:T(8,128)(2,1)S(1)} collective-permute-done((bf16[2,8,16,128]{3,2,1,0:T(8,128)(2,1)S(1)}, bf16[2,8,16,128]{3,2,1,0:T(8,128)(2,1)S(1)}, u32[]{:S(2)}, u32[]{:S(2)}) %collective-permute-start.4) | collective-permute-done | bytes 65568 | tf_op jit(solution)/shard_map/ppermute | solution.py:427
  30.9 1.5 %collective-permute-done.5.rest_5_ = bf16[2,8,16,128]{3,2,1,0:T(8,128)(2,1)S(1)} collective-permute-done((bf16[2,8,16,128]{3,2,1,0:T(8,128)(2,1)S(1)}, bf16[2,8,16,128]{3,2,1,0:T(8,128)(2,1)S(1)}, u32[]{:S(2)}, u32[]{:S(2)}) %collective-permute-start.5) | collective-permute-done | bytes 65568 | tf_op jit(solution)/shard_map/ppermute | solution.py:427
  32.4 2.7 %collective-permute-done.6.rest_6_ = bf16[2,8,16,128]{3,2,1,0:T(8,128)(2,1)S(1)} collective-permute-done((bf16[2,8,16,128]{3,2,1,0:T(8,128)(2,1)S(1)}, bf16[2,8,16,128]{3,2,1,0:T(8,128)(2,1)S(1)}, u32[]{:S(2)}, u32[]{:S(2)}) %collective-permute-start.6) | collective-permute-done | bytes 65568 | tf_op jit(solution)/shard_map/ppermute | solution.py:427
  35.0 2.9 %collective-permute-done.7.rest_7_ = bf16[2,8,16,128]{3,2,1,0:T(8,128)(2,1)S(1)} collective-permute-done((bf16[2,8,16,128]{3,2,1,0:T(8,128)(2,1)S(1)}, bf16[2,8,16,128]{3,2,1,0:T(8,128)(2,1)S(1)}, u32[]{:S(2)}, u32[]{:S(2)}) %collective-permute-start.7) | collective-permute-done | bytes 65568 | tf_op jit(solution)/shard_map/ppermute | solution.py:427
  38.4 12.1 %all_to_all.15 = bf16[16,8,16,128]{3,2,1,0:T(8,128)(2,1)S(1)} all-to-all(bf16[16,8,16,128]{3,2,1,0:T(8,128)(2,1)S(1)} %bitcast.4), channel_id=1, replica_groups={{15,14,13,12,11,10,9,8,7,6,5,4,3,2,1,0},{31,30,29,28,27,26,25,24,23,22,..., dimensions={0} | all-to-all | bytes 1048576 | tf_op jit(solution)/shard_map/all_to_all | solution.py:398
  50.5 1.3 %update.1 = (bf16[16,128,128]{2,1,0:T(8,128)(2,1)S(1)}, bf16[4,16,128]{2,1,0:T(8,128)(2,1)S(1)}) custom-call(bf16[128,16,128]{2,1,0:T(8,128)(2,1)S(1)} %bitcast.5, bf16[16,128,128]{2,1,0:T(8,128)(2,1)S(1)} %copy-done.6, bf16[16,128,128]{2,1,0:T(8,128)(2,1)S(1)} %get-tuple-element.64.gate, bf16[128,128]{1,0:T(8,128)(2,1)S(1)} %copy-done.4, ...), custom_call_target="tpu_custom_call" | custom-call | flops 2000000000 | bytes 1081344 | tf_op jit(solution)/shard_map/update/pallas_call | solution.py:454
  51.8 1.7 %collective-permute-start.9 = (bf16[16,128,128]{2,1,0:T(8,128)(2,1)S(1)}, bf16[16,128,128]{2,1,0:T(8,128)(2,1)S(1)}, u32[]{:S(2)}, u32[]{:S(2)}) collective-permute-start(bf16[16,128,128]{2,1,0:T(8,128)(2,1)S(1)} %get-tuple-element.67.updated), channel_id=1, source_target_pairs={{1,0},{0,1},{3,2},{2,3},{5,4},{4,5},{7,6},{6,7},{9,8},{8,9},{11,10... | collective-permute-start | bytes 1572872 | tf_op jit(solution)/shard_map/ppermute | solution.py:477
  53.6 2.9 %collective-permute-start.8 = (bf16[4,16,128]{2,1,0:T(8,128)(2,1)S(1)}, bf16[4,16,128]{2,1,0:T(8,128)(2,1)S(1)}, u32[]{:S(2)}, u32[]{:S(2)}) collective-permute-start(bf16[4,16,128]{2,1,0:T(8,128)(2,1)S(1)} %get-tuple-element.66.refs_0_), channel_id=1, source_target_pairs={{0,16},{1,17},{2,18},{3,19},{4,20},{5,21},{6,22},{7,23},{8,24},{9,... | collective-permute-start | bytes 49160 | tf_op jit(solution)/shard_map/ppermute | solution.py:427
  56.5 1.2 %own_projections.1 = (bf16[16,128,384]{2,1,0:T(8,128)(2,1)S(1)}, bf16[16,128,256]{2,1,0:T(8,128)(2,1)S(1)}) custom-call(bf16[16,128,128]{2,1,0:T(8,128)(2,1)S(1)} %get-tuple-element.67.updated, bf16[128,512]{1,0:T(8,128)(2,1)S(1)} %copy-done.2), custom_call_target="tpu_custom_call" | custom-call | flops 2000000000 | bytes 5242880 | tf_op jit(solution)/shard_map/own_projections/pallas_call | solution.py:482
  58.2 9.6 %all_to_all.16.mine = bf16[8,4,16,128]{3,2,1,0:T(8,128)(2,1)S(1)} all-to-all(bf16[8,4,16,128]{3,2,1,0:T(8,128)(2,1)S(1)} %deal_bias.1), channel_id=1, replica_groups={{13,12,9,8,5,4,1,0},{15,14,11,10,7,6,3,2},{29,28,25,24,21,20,17,16},{31..., dimensions={0} | all-to-all | bytes 262144 | tf_op jit(solution)/shard_map/all_to_all | solution.py:490
  67.8 0.9 %other_keys.1.rest_1_ = bf16[16,128,256]{2,1,0:T(8,128)(2,1)S(1)} custom-call(bf16[128,512]{1,0:T(8,128)(2,1)S(1)} %copy-done.2, bf16[16,128,128]{2,1,0:T(8,128)(2,1)S(1)} %collective-permute-done.9.rest_0_), custom_call_target="tpu_custom_call" | custom-call | flops 3000000000 | bytes 2097152 | tf_op jit(solution)/shard_map/other_keys/pallas_call | solution.py:494
  69.2 4.7 %attend.1 = bf16[16,128,128]{2,1,0:T(8,128)(2,1)} custom-call(s32[1]{0:T(128)S(6)} %copy.11.length, bf16[8,4,16,128]{3,2,1,0:T(8,128)(2,1)S(1)} %all_to_all.16.mine, bf16[8,4,16,128]{3,2,1,0:T(8,128)(2,1)S(1)} %collective-permute-done.10.sibling, bf16[128,128]{1,0:T(8,128)(2,1)S(1)} %copy-done, bf16[16,128,256]{2,1,0:T(8,128)(2,1)S(1)} %get-tuple-element.72.late, ...), custom_call_target="tpu_custom_call" | custom-call | flops 100000000 | bytes 1048576 | tf_op jit(solution)/shard_map/attend/pallas_call | solution.py:501
  (30 shorter events, 3.5 us)
Async XLA Ops:
  4.1 12.3 %copy-start.8 = (bf16[128,4]{0,1:T(4,128)(2,1)S(1)}, bf16[128,4]{0,1:T(4,128)(2,1)}, u32[]{:S(2)}) copy-start(bf16[128,4]{0,1:T(4,128)(2,1)} %param.16) | copy-start | bytes 3076
  4.1 22.0 %copy-start.1 = (bf16[16,128,128]{2,1,0:T(8,128)(2,1)S(1)}, bf16[16,128,128]{2,1,0:T(8,128)(2,1)}, u32[]{:S(2)}) copy-start(bf16[16,128,128]{2,1,0:T(8,128)(2,1)} %pair.1) | copy-start | bytes 1572868
  4.1 22.0 %copy-start.3 = (bf16[128,128]{1,0:T(8,128)(2,1)S(1)}, bf16[128,128]{1,0:T(8,128)(2,1)}, u32[]{:S(2)}) copy-start(bf16[128,128]{1,0:T(8,128)(2,1)} %weights.1) | copy-start | bytes 98308
  4.2 33.7 %all-to-all-start = ((bf16[32,8,16,128]{3,2,1,0:T(8,128)(2,1)}), bf16[32,8,16,128]{3,2,1,0:T(8,128)(2,1)S(1)}, u32[]{:S(2)}, u32[]{:S(2)}) async-start(bf16[32,8,16,128]{3,2,1,0:T(8,128)(2,1)} %get-tuple-element.40), calls=%async_computation | async-start | bytes 2097152 | tf_op jit(solution)/shard_map/all_to_all | solution.py:429
  11.5 1.6 %collective-permute-start = (bf16[8,8,16,128]{3,2,1,0:T(8,128)(2,1)S(1)}, bf16[8,8,16,128]{3,2,1,0:T(8,128)(2,1)S(1)}, u32[]{:S(2)}, u32[]{:S(2)}) collective-permute-start(bf16[8,8,16,128]{3,2,1,0:T(8,128)(2,1)S(1)} %get-tuple-element.46), channel_id=1, source_target_pairs={{0,2},{1,3},{2,0},{3,1},{4,6},{5,7},{6,4},{7,5},{8,10},{9,11},{10,... | collective-permute-start | bytes 786440 | tf_op jit(solution)/shard_map/ppermute | solution.py:427
  13.1 10.4 %collective-permute-start.1 = (bf16[2,8,16,128]{3,2,1,0:T(8,128)(2,1)S(1)}, bf16[2,8,16,128]{3,2,1,0:T(8,128)(2,1)S(1)}, u32[]{:S(2)}, u32[]{:S(2)}) collective-permute-start(bf16[2,8,16,128]{3,2,1,0:T(8,128)(2,1)S(1)} %get-tuple-element.48), channel_id=1, source_target_pairs={{0,1},{1,0},{2,3},{3,2},{4,5},{5,4},{6,7},{7,6},{8,9},{9,8},{10,11... | collective-permute-start | bytes 196616 | tf_op jit(solution)/shard_map/ppermute | solution.py:427
  15.0 10.3 %collective-permute-start.2 = (bf16[2,8,16,128]{3,2,1,0:T(8,128)(2,1)S(1)}, bf16[2,8,16,128]{3,2,1,0:T(8,128)(2,1)S(1)}, u32[]{:S(2)}, u32[]{:S(2)}) collective-permute-start(bf16[2,8,16,128]{3,2,1,0:T(8,128)(2,1)S(1)} %get-tuple-element.49), channel_id=1, source_target_pairs={{0,4},{1,5},{2,6},{3,7},{4,0},{5,1},{6,2},{7,3},{8,12},{9,13},{10,... | collective-permute-start | bytes 196616 | tf_op jit(solution)/shard_map/ppermute | solution.py:427
  16.6 13.0 %collective-permute-start.3 = (bf16[2,8,16,128]{3,2,1,0:T(8,128)(2,1)S(1)}, bf16[2,8,16,128]{3,2,1,0:T(8,128)(2,1)S(1)}, u32[]{:S(2)}, u32[]{:S(2)}) collective-permute-start(bf16[2,8,16,128]{3,2,1,0:T(8,128)(2,1)S(1)} %get-tuple-element.50), channel_id=1, source_target_pairs={{0,5},{1,4},{2,7},{3,6},{4,1},{5,0},{6,3},{7,2},{8,13},{9,12},{10,... | collective-permute-start | bytes 196616 | tf_op jit(solution)/shard_map/ppermute | solution.py:427
  16.9 14.0 %collective-permute-start.4 = (bf16[2,8,16,128]{3,2,1,0:T(8,128)(2,1)S(1)}, bf16[2,8,16,128]{3,2,1,0:T(8,128)(2,1)S(1)}, u32[]{:S(2)}, u32[]{:S(2)}) collective-permute-start(bf16[2,8,16,128]{3,2,1,0:T(8,128)(2,1)S(1)} %get-tuple-element.51), channel_id=1, source_target_pairs={{0,8},{1,9},{2,10},{3,11},{4,12},{5,13},{6,14},{7,15},{8,0},{9,1},... | collective-permute-start | bytes 196616 | tf_op jit(solution)/shard_map/ppermute | solution.py:427
  18.6 13.7 %collective-permute-start.5 = (bf16[2,8,16,128]{3,2,1,0:T(8,128)(2,1)S(1)}, bf16[2,8,16,128]{3,2,1,0:T(8,128)(2,1)S(1)}, u32[]{:S(2)}, u32[]{:S(2)}) collective-permute-start(bf16[2,8,16,128]{3,2,1,0:T(8,128)(2,1)S(1)} %get-tuple-element.52), channel_id=1, source_target_pairs={{0,9},{1,8},{2,11},{3,10},{4,13},{5,12},{6,15},{7,14},{8,1},{9,0},... | collective-permute-start | bytes 196616 | tf_op jit(solution)/shard_map/ppermute | solution.py:427
  23.5 11.5 %collective-permute-start.6 = (bf16[2,8,16,128]{3,2,1,0:T(8,128)(2,1)S(1)}, bf16[2,8,16,128]{3,2,1,0:T(8,128)(2,1)S(1)}, u32[]{:S(2)}, u32[]{:S(2)}) collective-permute-start(bf16[2,8,16,128]{3,2,1,0:T(8,128)(2,1)S(1)} %get-tuple-element.53), channel_id=1, source_target_pairs={{0,12},{1,13},{2,14},{3,15},{4,8},{5,9},{6,10},{7,11},{8,4},{9,5},... | collective-permute-start | bytes 196616 | tf_op jit(solution)/shard_map/ppermute | solution.py:427
  25.3 12.6 %collective-permute-start.7 = (bf16[2,8,16,128]{3,2,1,0:T(8,128)(2,1)S(1)}, bf16[2,8,16,128]{3,2,1,0:T(8,128)(2,1)S(1)}, u32[]{:S(2)}, u32[]{:S(2)}) collective-permute-start(bf16[2,8,16,128]{3,2,1,0:T(8,128)(2,1)S(1)} %get-tuple-element.54), channel_id=1, source_target_pairs={{0,13},{1,12},{2,15},{3,14},{4,9},{5,8},{6,11},{7,10},{8,5},{9,4},... | collective-permute-start | bytes 196616 | tf_op jit(solution)/shard_map/ppermute | solution.py:427
  26.1 1.0 %copy-start.7 = (bf16[16,128,128]{2,1,0:T(8,128)(2,1)S(1)}, bf16[16,128,128]{2,1,0:T(8,128)(2,1)}, u32[]{:S(2)}) copy-start(bf16[16,128,128]{2,1,0:T(8,128)(2,1)} %get-tuple-element.41.normed) | copy-start | bytes 1572868
  28.7 0.8 %copy-start.5 = (bf16[16,128,128]{2,1,0:T(8,128)(2,1)}, bf16[16,128,128]{2,1,0:T(8,128)(2,1)S(1)}, u32[]{:S(2)}) copy-start(bf16[16,128,128]{2,1,0:T(8,128)(2,1)S(1)} %get-tuple-element.63.source) | copy-start | bytes 1572868
  37.9 12.6 %copy-start.4 = (bf16[128,128]{1,0:T(8,128)(2,1)S(1)}, bf16[128,128]{1,0:T(8,128)(2,1)}, u32[]{:S(2)}) copy-start(bf16[128,128]{1,0:T(8,128)(2,1)} %tri_out.1) | copy-start | bytes 98308
  37.9 12.6 %copy-start.6 = (bf16[16,128,128]{2,1,0:T(8,128)(2,1)S(1)}, bf16[16,128,128]{2,1,0:T(8,128)(2,1)}, u32[]{:S(2)}) copy-start(bf16[16,128,128]{2,1,0:T(8,128)(2,1)} %copy-done.5) | copy-start | bytes 1572868
  50.5 6.0 %copy-start.2 = (bf16[128,512]{1,0:T(8,128)(2,1)S(1)}, bf16[128,512]{1,0:T(8,128)(2,1)}, u32[]{:S(2)}) copy-start(bf16[128,512]{1,0:T(8,128)(2,1)} %attn_proj.3) | copy-start | bytes 393220
  51.8 16.0 %collective-permute-start.9 = (bf16[16,128,128]{2,1,0:T(8,128)(2,1)S(1)}, bf16[16,128,128]{2,1,0:T(8,128)(2,1)S(1)}, u32[]{:S(2)}, u32[]{:S(2)}) collective-permute-start(bf16[16,128,128]{2,1,0:T(8,128)(2,1)S(1)} %get-tuple-element.67.updated), channel_id=1, source_target_pairs={{1,0},{0,1},{3,2},{2,3},{5,4},{4,5},{7,6},{6,7},{9,8},{8,9},{11,10... | collective-permute-start | bytes 1572872 | tf_op jit(solution)/shard_map/ppermute | solution.py:477
  53.6 4.6 %collective-permute-start.8 = (bf16[4,16,128]{2,1,0:T(8,128)(2,1)S(1)}, bf16[4,16,128]{2,1,0:T(8,128)(2,1)S(1)}, u32[]{:S(2)}, u32[]{:S(2)}) collective-permute-start(bf16[4,16,128]{2,1,0:T(8,128)(2,1)S(1)} %get-tuple-element.66.refs_0_), channel_id=1, source_target_pairs={{0,16},{1,17},{2,18},{3,19},{4,20},{5,21},{6,22},{7,23},{8,24},{9,... | collective-permute-start | bytes 49160 | tf_op jit(solution)/shard_map/ppermute | solution.py:427
  67.8 1.4 %copy-start = (bf16[128,128]{1,0:T(8,128)(2,1)S(1)}, bf16[128,128]{1,0:T(8,128)(2,1)}, u32[]{:S(2)}) copy-start(bf16[128,128]{1,0:T(8,128)(2,1)} %attn_out.1) | copy-start | bytes 98308
  67.8 1.3 %collective-permute-start.10 = (bf16[8,4,16,128]{3,2,1,0:T(8,128)(2,1)S(1)}, bf16[8,4,16,128]{3,2,1,0:T(8,128)(2,1)S(1)}, u32[]{:S(2)}, u32[]{:S(2)}) collective-permute-start(bf16[8,4,16,128]{3,2,1,0:T(8,128)(2,1)S(1)} %all_to_all.16.mine), channel_id=1, source_target_pairs={{0,2},{1,3},{2,0},{3,1},{4,6},{5,7},{6,4},{7,5},{8,10},{9,11},{10,... | collective-permute-start | bytes 393224 | tf_op jit(solution)/shard_map/ppermute | solution.py:427
